TPU v7x, 256 devices: a whole 4x4x8 slice. The times are simulated.
256 devices in a mesh: ctx: 16 (over y, x), exp: 16 (over z, core).
Axes of the slice: x: 4, y: 4, z: 8, core: 2. Of those that a mesh axis runs over, the one named last changes fastest.
Arguments:
- tokens: bfloat16 [128, 4096], P('exp', 'ctx'), may hold values from -4.2 to 4.2, as said below
- attn_gain: float32 [4096], P('ctx'), may hold values from 0.1 to 1.9
- w_qkv: bfloat16 [4096, 5120], P('ctx'), may hold values from -0.09375 to 0.09375
- w_out: bfloat16 [4096, 4096], P(None, 'ctx'), may hold values from -0.09375 to 0.09375
- k_cache: bfloat16 [128, 2048, 512], P('exp', 'ctx'), may hold values from -480 to 480
- value_cache: bfloat16 [128, 2048, 512], P('exp', 'ctx'), may hold values from -24 to 24
- lengths: int32 [128], P('exp'), may hold values from 1 to 2047
- moe_gain: float32 [4096], P('ctx'), may hold values from 0.1 to 1.9
- routes: int32 [128, 8], P('exp'), may hold values from 0 to 63, all different within a row; in each aligned block of 8 rows (0 to 7, 8 to 15, ...) at most 2 rows name the same one
- gates: float32 [128, 8], P('exp'), may hold values from 0.05 to 0.3
- w_in: bfloat16 [64, 4096, 1536], P('exp', 'ctx'), may hold values from -0.09375 to 0.09375
- w_down: bfloat16 [64, 768, 4096], P('exp', None, 'ctx'), may hold values from -0.21875 to 0.21875
Outputs:
- context: bfloat16 [128, 4096], P('exp')
- layer_out: bfloat16 [128, 4096], P('exp', 'ctx')
Inputs may be any that keep to these rules, and one draw needn't show every extreme that they name: Among the 64 routes of the tokens of one index of exp, at most 2 name one expert, and in every draw some expert is named exactly 2 times there. `tokens`: residual features.
All inputs are finite; a program needn't handle non-finite values.
Results may differ from a plain program's by a relative error of at most 0.04.
Values may be sent and summed in bfloat16 or wider, within the bound.
No kernel may reach another device: no remote copies, remote signals or barrier semaphores. Data moves between devices by JAX's collectives and lax.ppermute only.
A program may use at most 64 MiB of HBM per device.

v0:
```python
import jax
import jax.numpy as jnp
from jax import lax
from jax.sharding import PartitionSpec as P

D = 4096
QUERY_HEADS = 32
KEY_VALUE_HEADS = 4
HEAD_DIMENSION = 128


def apply_rotary(vec, pos):
    half = vec.shape[-1] // 2
    freq = jnp.exp(-jnp.log(1000000.0) * jnp.arange(half).astype(jnp.float32) / half)
    angle = pos.astype(jnp.float32)[:, None] * freq[None, :]
    cosine = jnp.cos(angle)[:, None, :]
    sine = jnp.sin(angle)[:, None, :]
    lower = vec[..., :half]
    upper = vec[..., half:]
    return jnp.concatenate([lower * cosine - upper * sine, upper * cosine + lower * sine], -1)


def activate(gate_up, width):
    return (jax.nn.silu(gate_up[..., :width]) * gate_up[..., width:]).astype(jnp.bfloat16)


def local(
    tokens,
    attn_gain,
    w_qkv,
    w_out,
    k_cache,
    value_cache,
    lengths,
    moe_gain,
    routes,
    gates,
    w_in,
    w_down,
):
    seqs, slice_width = tokens.shape
    positions = k_cache.shape[1]
    key_value_heads = KEY_VALUE_HEADS
    head_size = HEAD_DIMENSION
    q_heads = QUERY_HEADS
    query_group = q_heads // key_value_heads
    hidden = w_down.shape[1]
    local_exp = w_in.shape[0]
    n_exp = lax.axis_size("exp")
    experts_all = local_exp * n_exp
    top_k = routes.shape[1]
    capacity = 2 * seqs * top_k // experts_all
    scale = 1.0 / jnp.sqrt(jnp.float32(head_size))
    xf = tokens.astype(jnp.float32)
    scaled = (xf * attn_gain).astype(jnp.bfloat16)
    partial_value = jnp.dot(scaled, w_qkv, preferred_element_type=jnp.float32)
    projection_matrix, sumsq = lax.psum((partial_value, jnp.sum(xf * xf, -1, keepdims=True)), "ctx")
    projection_matrix = projection_matrix * lax.rsqrt(sumsq / D + 1e-06)
    query = apply_rotary(
        projection_matrix[:, : q_heads * head_size].reshape(seqs, q_heads, head_size), lengths
    )
    fresh_key = apply_rotary(
        projection_matrix[:, q_heads * head_size : (q_heads + key_value_heads) * head_size].reshape(
            seqs, key_value_heads, head_size
        ),
        lengths,
    )
    fresh_value = projection_matrix[:, (q_heads + key_value_heads) * head_size :].reshape(
        seqs, key_value_heads, head_size
    )
    grouped_queries = query.reshape(seqs, key_value_heads, query_group, head_size)
    where_pos = lax.axis_index("ctx") * positions + jnp.arange(positions)
    live = (where_pos[None, :] < lengths[:, None])[:, None, None, :]
    cached_keys = k_cache.reshape(seqs, positions, key_value_heads, head_size).astype(jnp.float32)
    cached_values = value_cache.reshape(seqs, positions, key_value_heads, head_size).astype(
        jnp.float32
    )
    scores = jnp.einsum("bhgd,blhd->bhgl", grouped_queries, cached_keys) * scale
    scores = jnp.where(live, scores, -1e30)
    local_top = jnp.max(scores, -1)
    weights = jnp.where(live, jnp.exp(scores - local_top[..., None]), 0.0)
    local_total = jnp.sum(weights, -1)
    local_acc = jnp.einsum("bhgl,blhd->bhgd", weights, cached_values)
    whole_top = lax.pmax(local_top, "ctx")
    factor = jnp.exp(local_top - whole_top)
    whole_total, whole_acc = lax.psum((local_total * factor, local_acc * factor[..., None]), "ctx")
    s_new = jnp.einsum("bhgd,bhd->bhg", grouped_queries, fresh_key) * scale
    final_top = jnp.maximum(whole_top, s_new)
    old_part = jnp.exp(whole_top - final_top)
    new_part = jnp.exp(s_new - final_top)
    total = whole_total * old_part + new_part
    acc = whole_acc * old_part[..., None] + new_part[..., None] * fresh_value[:, :, None, :]
    context = (acc / total[..., None]).reshape(seqs, q_heads * head_size).astype(jnp.bfloat16)
    attn_out = jnp.dot(context, w_out, preferred_element_type=jnp.float32)
    resid = (xf + attn_out).astype(jnp.bfloat16)
    rf = resid.astype(jnp.float32)
    sumsq_two = lax.psum(jnp.sum(rf * rf, -1, keepdims=True), "ctx")
    normed = (rf * lax.rsqrt(sumsq_two / D + 1e-06) * moe_gain).astype(jnp.bfloat16)
    flat_ids = routes.reshape(-1)
    onehot = (flat_ids[:, None] == jnp.arange(experts_all)[None, :]).astype(jnp.int32)
    rank = jnp.sum((jnp.cumsum(onehot, 0) - onehot) * onehot, -1)
    slot_index = flat_ids * capacity + rank
    select = (slot_index[:, None] == jnp.arange(experts_all * capacity)[None, :]).astype(
        jnp.float32
    )
    token_map = (jnp.arange(seqs * top_k)[:, None] // top_k == jnp.arange(seqs)[None, :]).astype(
        jnp.float32
    )
    placing = jnp.dot(select.T, token_map, precision=lax.Precision.HIGHEST).astype(jnp.bfloat16)
    outgoing = jnp.dot(placing, normed, preferred_element_type=jnp.float32).astype(jnp.bfloat16)
    outgoing = outgoing.reshape(n_exp, local_exp, capacity, slice_width)
    incoming = lax.all_to_all(outgoing, "exp", split_axis=0, concat_axis=0, tiled=True)
    gate_up = jnp.einsum("sjcd,jdf->sjcf", incoming, w_in, preferred_element_type=jnp.float32)
    summed = lax.psum(gate_up, "ctx")
    act = activate(summed, hidden)
    expert_out = jnp.einsum(
        "sjcf,jfd->sjcd", act, w_down, preferred_element_type=jnp.float32
    ).astype(jnp.bfloat16)
    returned = lax.all_to_all(expert_out, "exp", split_axis=0, concat_axis=0, tiled=True)
    returned = returned.reshape(experts_all * capacity, slice_width).astype(jnp.float32)
    weighting = jnp.dot(
        token_map.T, select * gates.reshape(-1)[:, None], precision=lax.Precision.HIGHEST
    )
    moe = jnp.dot(weighting, returned, precision=lax.Precision.HIGHEST)
    layer_out = (rf + moe).astype(jnp.bfloat16)
    return (context, layer_out)


def solution(mesh):
    placed = (
        P("exp", "ctx"),
        P("ctx"),
        P("ctx", None),
        P(None, "ctx"),
        P("exp", "ctx", None),
        P("exp", "ctx", None),
        P("exp"),
        P("ctx"),
        P("exp", None),
        P("exp", None),
        P("exp", "ctx", None),
        P("exp", None, "ctx"),
    )
    return jax.shard_map(
        local,
        mesh=mesh,
        in_specs=placed,
        out_specs=(P("exp", None), P("exp", "ctx")),
        check_vma=False,
    )
```

profile of v0, /device:TPU:1, one launch (start us, length us, event | category | flops | bytes accessed | tf_op | source)
XLA Modules:
  0.0 447.3 jit_solution(13924952348790180376)
XLA Ops:
  7.2 0.0 copy-start
  7.2 0.0 copy-start.2
  7.2 0.0 copy-start.6
  7.2 0.0 copy-start.3
  7.2 0.0 all-reduce.4.cloned.1.call-start
  7.3 3.0 fusion.49
  10.3 0.0 all-reduce.4.cloned.1.call-update
  10.3 0.0 all-reduce.6.cloned.1.call-start
  10.4 0.0 copy-done.2
  10.4 0.1 fusion.48
  10.5 0.0 copy-done.6
  10.5 34.3 %psum.43 = f32[8,1]{0,1:T(1,128)S(1)} all-reduce(f32[8,1]{0,1:T(1,128)S(1)} %bitcast.85), channel_id=1, replica_groups=mesh['ctx'=16,'exp'=16] {'ctx'}, use_global_device_ids=true, to_apply=%region_2.0 | all-reduce | flops 8 | bytes 64 | tf_op jit(solution)/shard_map/psum | solution.py:57
  44.8 0.1 broadcast_compare_fusion
  44.9 0.0 copy-done.3
  44.9 0.1 reshape.168
  44.9 0.1 fusion.37
  45.0 0.1 reduce_window_sum.11
  45.1 0.2 select_reduce_fusion
  45.3 0.1 multiply_cosine_fusion
  45.4 0.3 convolution_convert_fusion.1
  45.7 61.2 %all-reduce.4.cloned.1.call-done = f32[8,5120]{1,0:T(8,128)} async-done(((f32[8,5120]{1,0:T(8,128)}), f32[8,5120]{1,0:T(8,128)}) %all-reduce.4.cloned.1.call-update) | async-done | bytes 163856 | tf_op jit(solution)/shard_map/psum | solution.py:57
  106.9 1.0 broadcast_multiply_fusion
  107.9 0.1 multiply_subtract_fusion
  108.0 0.1 pad_maximum_fusion
  108.1 1.9 fusion.60
  110.0 0.0 copy-start.5
  110.0 58.0 %pmax.7 = f32[8,4,8]{2,1,0:T(4,128)S(1)} all-reduce(f32[8,4,8]{2,1,0:T(4,128)S(1)} %get-tuple-element.15), channel_id=1, replica_groups=mesh['ctx'=16,'exp'=16] {'ctx'}, use_global_device_ids=true, to_apply=%region_4.5 | all-reduce | flops 256 | bytes 2048 | tf_op jit(solution)/shard_map/pmax | solution.py:84
  168.1 0.2 fusion.29
  168.3 2.3 convolution_multiply_fusion
  170.6 0.0 all-reduce.6.cloned.1.call-update
  170.7 0.0 all-reduce.8.cloned.1.call-start
  170.7 56.0 %psum.45 = f32[8,4,8]{2,1,0:T(4,128)S(1)} all-reduce(f32[8,4,8]{2,1,0:T(4,128)S(1)} %bitcast.81), channel_id=1, replica_groups=mesh['ctx'=16,'exp'=16] {'ctx'}, use_global_device_ids=true, to_apply=%region_7.8 | all-reduce | flops 256 | bytes 2048 | tf_op jit(solution)/shard_map/psum | solution.py:86
  226.7 0.1 multiply_subtract_fusion.1
  226.8 0.1 maximum_bitcast_fusion
  226.8 0.2 fusion.24
  227.1 47.0 %all-reduce.6.cloned.1.call-done = f32[8,4,8,128]{3,2,1,0:T(8,128)} async-done(((f32[8,4,8,128]{3,2,1,0:T(8,128)}), f32[8,4,8,128]{3,2,1,0:T(8,128)}) %all-reduce.6.cloned.1.call-update) | async-done | bytes 131088 | tf_op jit(solution)/shard_map/psum | solution.py:86
  274.1 1.1 fusion.33
  275.2 0.0 copy-start.1
  275.2 2.1 multiply_reduce_fusion
  277.3 0.0 copy-start.4
  277.3 31.5 %psum.46 = f32[8,1]{0,1:T(1,128)S(1)} all-reduce(f32[8,1]{0,1:T(1,128)S(1)} %bitcast.84), channel_id=1, replica_groups=mesh['ctx'=16,'exp'=16] {'ctx'}, use_global_device_ids=true, to_apply=%region_11.12 | all-reduce | flops 8 | bytes 64 | tf_op jit(solution)/shard_map/psum | solution.py:97
  308.8 0.0 copy-done.5
  308.8 0.3 convolution_convert_fusion
  309.1 23.5 %all_to_all.10 = bf16[16,4,2,256]{3,2,1,0:T(2,128)(2,1)S(1)} all-to-all(bf16[16,4,2,256]{3,2,1,0:T(2,128)(2,1)S(1)} %reshape.169), channel_id=1, replica_groups=mesh['ctx'=16,'exp'=16] {'exp'}, dimensions={0} | all-to-all | bytes 131072 | tf_op jit(solution)/shard_map/all_to_all | solution.py:112
  332.6 0.0 copy-done
  332.6 1.6 fusion.2
  334.2 0.0 copy-done.1
  334.2 0.0 all-reduce.8.cloned.1.call-update
  334.2 0.0 copy-done.4
  334.2 0.1 mul.249
  334.3 86.1 %all-reduce.8.cloned.1.call-done = f32[16,4,2,1536]{3,0,2,1:T(8,128)} async-done(((f32[16,4,2,1536]{3,0,2,1:T(8,128)}), f32[16,4,2,1536]{3,0,2,1:T(8,128)}) %all-reduce.8.cloned.1.call-update) | async-done | bytes 786448 | tf_op jit(solution)/shard_map/psum | solution.py:114
  420.4 2.0 fusion.11
  422.4 0.7 copy.30
  423.1 9.0 %all-to-all-start.1 = ((bf16[16,4,2,256]{3,2,1,0:T(2,128)(2,1)}), bf16[16,4,2,256]{3,2,1,0:T(2,128)(2,1)S(1)}, u32[]{:S(2)}, u32[]{:S(2)}) async-start(bf16[16,4,2,256]{3,2,1,0:T(2,128)(2,1)} %copy.30), calls=%async_computation.1 | async-start | bytes 131072 | tf_op jit(solution)/shard_map/all_to_all | solution.py:119
  432.1 0.3 fusion.35
  432.4 7.5 %all-to-all-done.1 = bf16[16,4,2,256]{3,2,1,0:T(2,128)(2,1)S(1)} async-done(((bf16[16,4,2,256]{3,2,1,0:T(2,128)(2,1)}), bf16[16,4,2,256]{3,2,1,0:T(2,128)(2,1)S(1)}, u32[]{:S(2)}, u32[]{:S(2)}) %all-to-all-start.1) | async-done | bytes 65568 | tf_op jit(solution)/shard_map/all_to_all | solution.py:119
  440.0 0.7 fusion.16
  (14 shorter events, 0.2 us)
Async XLA Ops:
  7.2 325.5 %copy-start = (bf16[4,256,1536]{2,1,0:T(8,128)(2,1)S(1)}, bf16[4,256,1536]{2,1,0:T(8,128)(2,1)}, u32[]{:S(2)}) copy-start(bf16[4,256,1536]{2,1,0:T(8,128)(2,1)} %param.22) | copy-start | bytes 9437188
  7.2 3.2 copy-start.2
  7.2 3.3 copy-start.6
  7.2 37.7 %copy-start.3 = (s32[8,8]{1,0:T(8,128)S(1)}, s32[8,8]{1,0:T(8,128)}, u32[]{:S(2)}) copy-start(s32[8,8]{1,0:T(8,128)} %param.20) | copy-start | bytes 772
  7.2 99.6 %all-reduce.4.cloned.1.call-start = ((), (), s32[]{:S(2)}) async-start(), calls=%async_computation.2 | async-start | bytes 327680 | tf_op jit(solution)/shard_map/psum | solution.py:57
  10.3 263.8 %all-reduce.6.cloned.1.call-start = ((), (), s32[]{:S(2)}) async-start(), calls=%async_computation.3 | async-start | bytes 262144 | tf_op jit(solution)/shard_map/psum | solution.py:86
  110.0 198.8 %copy-start.5 = (f32[256]{0:T(256)S(1)}, f32[256]{0:T(256)}, u32[]{:S(2)}) copy-start(f32[256]{0:T(256)} %param.19) | copy-start | bytes 3076
  170.7 249.8 %all-reduce.8.cloned.1.call-start = ((), (), s32[]{:S(2)}) async-start(), calls=%async_computation.4 | async-start | bytes 1572864 | tf_op jit(solution)/shard_map/psum | solution.py:114
  275.2 59.0 %copy-start.1 = (bf16[1,8,32,128]{3,1,2,0:T(8,128)(2,1)}, bf16[1,8,32,128]{3,1,2,0:T(8,128)(2,1)S(1)}, u32[]{:S(2)}) copy-start(bf16[1,8,32,128]{3,1,2,0:T(8,128)(2,1)S(1)} %copy.63) | copy-start | bytes 196612
  277.3 56.9 %copy-start.4 = (f32[8,8]{1,0:T(8,128)S(1)}, f32[8,8]{1,0:T(8,128)}, u32[]{:S(2)}) copy-start(f32[8,8]{1,0:T(8,128)} %param.21) | copy-start | bytes 772
  423.1 16.8 %all-to-all-start.1 = ((bf16[16,4,2,256]{3,2,1,0:T(2,128)(2,1)}), bf16[16,4,2,256]{3,2,1,0:T(2,128)(2,1)S(1)}, u32[]{:S(2)}, u32[]{:S(2)}) async-start(bf16[16,4,2,256]{3,2,1,0:T(2,128)(2,1)} %copy.30), calls=%async_computation.1 | async-start | bytes 131072 | tf_op jit(solution)/shard_map/all_to_all | solution.py:119
Sparse Core Ops, SparseCore 0:
  11.3 95.5 all-reduce.3
  170.8 103.2 all-reduce.5
  334.3 86.0 all-reduce.7
where the time goes:
time: 448 us; the launch traced here: 447 us
  blocking collectives  203 us (45%)
  waiting for transfers between devices  202 us (45%)
  matrix products  14.7 us (3%)
  between operations  13.9 us (3%)
  starting transfers between devices  9.15 us (2%)
    psum x1, waiting for transfers between devices, local(): summed = lax.psum(gate_up, 'ctx')  86.1 us
    psum x1, waiting for transfers between devices, local(): lax.psum((partial_value, jnp.sum(xf * xf, -1, keepdims=True)), 'ctx')  61.2 us
    pmax x1, blocking collectives, local(): whole_top = lax.pmax(local_top, 'ctx')  58 us
    psum x1, blocking collectives, local(): lax.psum((local_total * factor, local_acc * factor[..., None]), 'ctx')  56 us
    psum x1, waiting for transfers between devices, local(): lax.psum((local_total * factor, local_acc * factor[..., None]), 'ctx')  47 us
    psum x1, blocking collectives, local(): lax.psum((partial_value, jnp.sum(xf * xf, -1, keepdims=True)), 'ctx')  34.3 us
    psum x1, blocking collectives, local(): sumsq_two = lax.psum(jnp.sum(rf * rf, -1, keepdims=True), 'ctx')  31.5 us
    all_to_all x1, blocking collectives, local(): lax.all_to_all(outgoing, 'exp', split_axis=0, concat_axis=0, tiled=True)  23.5 us
  transfers between devices with their start and end apart: 4, of which 4 were waited for; matrix products, arithmetic and copies ran while one was open for 0% of the time, Pallas kernels for 0%

commit v1 on v0

v1 whole, which is shorter than its diff:
```python
import functools

import jax
import jax.numpy as jnp
from jax import lax
from jax.experimental import pallas as pl
from jax.experimental.pallas import tpu as pltpu
from jax.sharding import PartitionSpec as P

D = 4096
QUERY_HEADS = 32
KEY_VALUE_HEADS = 4
HEAD_DIMENSION = 128
AXES = ("ctx", "exp")


def exchange(value, stage, n_ctx, n_exp):
    side = 4
    got = []
    for step in range(1, side):
        pairs = []
        for i in range(n_ctx):
            for e in range(n_exp):
                j = i ^ step if (e & 1) == stage else i ^ (side * step)
                pairs.append((i * n_exp + e, j * n_exp + e))
        got.append(lax.ppermute(value, AXES, pairs))
    return got


def rotation(pos, size):
    half = size // 2
    freq = jnp.exp(-jnp.log(1000000.0) * jnp.arange(half).astype(jnp.float32) / half)
    angle = pos.astype(jnp.float32)[:, None] * freq[None, :]
    cosine, sine = jnp.cos(angle), jnp.sin(angle)
    return jnp.concatenate([cosine, cosine], -1), jnp.concatenate([-sine, sine], -1)


def lane_ids():
    return lax.broadcasted_iota(jnp.int32, (QUERY_HEADS, 128), 1)


def spread(log, seqs):
    log = jnp.where(lane_ids() < seqs, log, 0.0)
    high = log.astype(jnp.bfloat16).astype(jnp.float32)
    rest = log - high
    middle = rest.astype(jnp.bfloat16).astype(jnp.float32)
    low = rest - middle
    terms = high + pltpu.roll(middle, seqs, 1) + pltpu.roll(low, 2 * seqs, 1)
    return terms.astype(jnp.bfloat16)


def gather_terms(block, seqs):
    terms = block.astype(jnp.float32)
    return (terms + pltpu.roll(terms, 128 - seqs, 1)) + pltpu.roll(terms, 128 - 2 * seqs, 1)


def halves(value):
    high = value.astype(jnp.bfloat16).astype(jnp.float32)
    lane = lax.broadcasted_iota(jnp.int32, (value.shape[0], 128), 1)
    return jnp.where(lane < 64, high, value - high).astype(jnp.bfloat16)


def project_kernel(tokens_hbm, gain_hbm, w_hbm, out, tokens, gain, w_ref, small, sems):
    f32, bf16 = jnp.float32, jnp.bfloat16
    chunks = sems.shape[0]
    cols = w_hbm.shape[1]
    width = cols // chunks
    copies = [
        pltpu.make_async_copy(
            w_hbm.at[:, pl.ds(c * width, width)], w_ref.at[:, pl.ds(c * width, width)], sems.at[c]
        )
        for c in range(chunks)
    ]
    first = [
        pltpu.make_async_copy(tokens_hbm, tokens, small.at[0]),
        pltpu.make_async_copy(gain_hbm, gain, small.at[1]),
    ]
    for copy in first + copies:
        copy.start()
    for copy in first:
        copy.wait()
    xf = tokens[...].astype(f32)
    scaled = (xf * gain[...]).astype(bf16)
    out[:, cols:] = halves(jnp.sum(xf * xf, 1, keepdims=True))
    for c, copy in enumerate(copies):
        copy.wait()
        at = slice(c * width, (c + 1) * width)
        out[:, at] = jnp.dot(scaled, w_ref[:, at], preferred_element_type=f32).astype(bf16)


def load_kernel(after, k_hbm, v_hbm, w_hbm, k_out, v_out, w_out, sems):
    copies = [
        pltpu.make_async_copy(source, target, sems.at[i])
        for i, (source, target) in enumerate(((k_hbm, k_out), (v_hbm, v_out), (w_hbm, w_out)))
    ]
    for copy in copies:
        copy.start()
    for copy in copies:
        copy.wait()


def add_kernel(m0, m1, m2, m3, after, out):
    f32, bf16 = jnp.float32, jnp.bfloat16
    cols = out.shape[1] - 128

    def total(at):
        p, q, r, s = (m[:, at].astype(f32) for m in (m0, m1, m2, m3))
        return (p + q) + (r + s)

    out[:, :cols] = total(slice(0, cols)).astype(bf16)
    squares = total(slice(cols, cols + 128))
    out[:, cols:] = halves((squares + pltpu.roll(squares, 64, 1))[:, :1])


def attend_kernel(seqs, m0, m1, m2, m3, cosine, sine, live_ref, owns, k_ref, v_ref, out, rows):
    f32, bf16 = jnp.float32, jnp.bfloat16
    qh, kvh, hd = QUERY_HEADS, KEY_VALUE_HEADS, HEAD_DIMENSION
    group = qh // kvh
    positions = k_ref.shape[1]

    def share(h):
        p, q, r, s = (m[:, h * hd : (h + 1) * hd].astype(f32) for m in (m0, m1, m2, m3))
        return (p + q) + (r + s)

    squares = share(qh + 2 * kvh)
    norm = lax.rsqrt((squares + pltpu.roll(squares, 64, 1)) / D + 1e-06)
    cos, sin = cosine[...] * norm, sine[...] * norm
    scale = hd**-0.5
    cos_q, sin_q = cos * scale, sin * scale
    for h in range(qh):
        v = share(h)
        rows[h * seqs : (h + 1) * seqs, :] = v * cos_q + pltpu.roll(v, hd // 2, 1) * sin_q
    for h in range(qh, qh + kvh):
        v = share(h)
        rows[h * seqs : (h + 1) * seqs, :] = v * cos + pltpu.roll(v, hd // 2, 1) * sin
    for h in range(qh + kvh, qh + 2 * kvh):
        rows[h * seqs : (h + 1) * seqs, :] = share(h) * norm

    def grouped(first, b):
        at = [(first + g) * seqs + b for g in range(kvh)]
        return jnp.concatenate(
            [jnp.broadcast_to(rows[i : i + 1, :], (group, hd)) for i in at], 0
        )

    owns_new = jnp.broadcast_to(owns[0:1, :], (qh, 128))[:, :1] > 0.5
    zero = jnp.zeros((group, hd), f32)
    lanes = lane_ids()
    logs = jnp.zeros((qh, 128), f32)
    for b in range(seqs):
        q = rows[pl.ds(b, qh, stride=seqs), :]
        fresh = jnp.where(owns_new, jnp.sum(q * grouped(qh, b), 1, keepdims=True), -1e30)
        wide = jnp.concatenate(
            [
                jnp.concatenate(
                    [q[g * group : (g + 1) * group] if c == g else zero for c in range(kvh)], 1
                )
                for g in range(kvh)
            ],
            0,
        )
        high = wide.astype(bf16)
        low = (wide - high.astype(f32)).astype(bf16)
        both = lax.dot_general(
            jnp.concatenate([high, low], 0),
            k_ref[b],
            (((1,), (1,)), ((), ())),
            preferred_element_type=f32,
        )
        live = jnp.broadcast_to(live_ref[b : b + 1, :], (qh, positions)) > 0.5
        s = jnp.where(live, both[:qh] + both[qh:], -1e30)
        top = jnp.maximum(jnp.max(s, 1, keepdims=True), fresh)
        p = jnp.where(live, jnp.exp(s - top), 0.0)
        p_new = jnp.where(owns_new, jnp.exp(fresh - top), 0.0)
        total = jnp.sum(p, 1, keepdims=True) + p_new
        acc = jnp.dot(p.astype(bf16), v_ref[b], preferred_element_type=f32)
        acc = jnp.concatenate(
            [acc[g * group : (g + 1) * group, g * hd : (g + 1) * hd] for g in range(kvh)], 0
        )
        some = total > 0
        safe = jnp.where(some, total, 1.0)
        out[b * qh : (b + 1) * qh, :] = ((acc + p_new * grouped(qh + kvh, b)) / safe).astype(bf16)
        log = jnp.where(some, top + jnp.log(safe), -1e30)
        logs = jnp.where(lanes == b, log, logs)
    out[seqs * qh : (seqs + 1) * qh, :] = spread(logs, seqs)


def merged(seqs, parts):
    qh = QUERY_HEADS
    logs = [gather_terms(p[seqs * qh : (seqs + 1) * qh, :], seqs) for p in parts]
    top = jnp.maximum(jnp.maximum(logs[0], logs[1]), jnp.maximum(logs[2], logs[3]))
    weights = [jnp.exp(v - top) for v in logs]
    total = (weights[0] + weights[1]) + (weights[2] + weights[3])
    shares = [w / total for w in weights]
    values = []
    for b in range(seqs):
        v = [
            p[b * qh : (b + 1) * qh, :].astype(jnp.float32) * w[:, b : b + 1]
            for p, w in zip(parts, shares)
        ]
        values.append((v[0] + v[1]) + (v[2] + v[3]))
    return values, top + jnp.log(total)


def merge_kernel(seqs, p0, p1, p2, p3, out):
    qh = QUERY_HEADS
    values, log = merged(seqs, (p0, p1, p2, p3))
    for b in range(seqs):
        out[b * qh : (b + 1) * qh, :] = values[b].astype(jnp.bfloat16)
    out[seqs * qh : (seqs + 1) * qh, :] = spread(log, seqs)


def finish_kernel(seqs, p0, p1, p2, p3, tokens, placing, w_ref, context, resid, outgoing, rows):
    f32, bf16 = jnp.float32, jnp.bfloat16
    qh = QUERY_HEADS
    values, _ = merged(seqs, (p0, p1, p2, p3))
    for b in range(seqs):
        rows[pl.ds(b, qh, stride=seqs), :] = values[b]
    whole = jnp.concatenate([rows[h * seqs : (h + 1) * seqs, :] for h in range(qh)], 1).astype(bf16)
    context[...] = whole
    attn = jnp.dot(whole, w_ref[...], preferred_element_type=f32)
    after = (tokens[...].astype(f32) + attn).astype(bf16)
    resid[...] = after
    padded = jnp.concatenate(
        [after.astype(f32), jnp.zeros((placing.shape[1] - seqs, after.shape[1]), f32)], 0
    ).astype(bf16)
    outgoing[...] = jnp.dot(placing[...], padded, preferred_element_type=f32).astype(bf16)


def own_rows(capacity, per_source, n_rows, width, j):
    row = lax.broadcasted_iota(jnp.int32, (n_rows, width), 0)
    return lax.rem(row, per_source) // capacity == j


def gate_up_kernel(capacity, x_ref, gain, w_ref, out):
    f32, bf16 = jnp.float32, jnp.bfloat16
    n_rows, width = x_ref.shape
    experts, _, cols = w_ref.shape
    xf = x_ref[...].astype(f32)
    out[:, cols:] = halves(jnp.sum(xf * xf, 1, keepdims=True))
    gained = xf * gain[...]
    blocks = [
        jnp.where(own_rows(capacity, experts * capacity, n_rows, width, j), gained, 0.0).astype(bf16)
        for j in range(experts)
    ]
    step = 256
    for c in range(0, cols, step):
        total = jnp.dot(blocks[0], w_ref[0, :, c : c + step], preferred_element_type=f32)
        for j in range(1, experts):
            total += jnp.dot(blocks[j], w_ref[j, :, c : c + step], preferred_element_type=f32)
        out[:, c : c + step] = total.astype(bf16)


def activate_kernel(shares, out):
    f32, bf16 = jnp.float32, jnp.bfloat16
    hidden = out.shape[2]

    def total(at):
        terms = [shares[i, :, at].astype(f32) for i in range(shares.shape[0])]
        while len(terms) > 1:
            terms = [p + q for p, q in zip(terms[::2], terms[1::2])]
        return terms[0]

    squares = total(slice(2 * hidden, 2 * hidden + 128))
    norm = lax.rsqrt((squares + pltpu.roll(squares, 64, 1)) / D + 1e-06)[:, :1]
    gate = total(slice(0, hidden)) * norm
    up = total(slice(hidden, 2 * hidden)) * norm
    act = (gate / (1.0 + jnp.exp(-gate)) * up).astype(bf16)
    for i in range(out.shape[0]):
        out[i] = act


def down_kernel(capacity, x_ref, w_ref, out):
    f32 = jnp.float32
    n_rows, width = x_ref.shape
    experts = w_ref.shape[0]
    xf = x_ref[...].astype(f32)
    total = None
    for j in range(experts):
        mine = own_rows(capacity, experts * capacity, n_rows, width, j)
        block = jnp.where(mine, xf, 0.0).astype(jnp.bfloat16)
        part = jnp.dot(block, w_ref[j], preferred_element_type=f32)
        total = part if total is None else total + part
    out[...] = total.astype(jnp.bfloat16)


def combine_kernel(resid, weighting, returned, out):
    f32, bf16 = jnp.float32, jnp.bfloat16
    weights = weighting[...]
    seqs = weights.shape[0]
    high = weights.astype(bf16).astype(f32)
    rest = weights - high
    middle = rest.astype(bf16).astype(f32)
    low = rest - middle
    stack = jnp.concatenate([high, middle, low, jnp.zeros_like(low)], 0).astype(bf16)
    sums = jnp.dot(stack, returned[...], preferred_element_type=f32)
    moe = (sums[:seqs] + sums[seqs : 2 * seqs]) + sums[2 * seqs : 3 * seqs]
    out[...] = (resid[...].astype(f32) + moe).astype(bf16)


VM = pl.BlockSpec(memory_space=pltpu.VMEM)
ANY = pl.BlockSpec(memory_space=pl.ANY)
HBM = pl.BlockSpec(memory_space=pltpu.HBM)


def shape(dims, dtype=jnp.bfloat16):
    return jax.ShapeDtypeStruct(dims, dtype)


def call(kernel, name, out, inputs, specs, scratch=(), mib=8):
    return pl.pallas_call(
        kernel,
        out_shape=out,
        in_specs=specs,
        out_specs=jax.tree.map(lambda _: VM, out),
        scratch_shapes=list(scratch),
        compiler_params=pltpu.CompilerParams(vmem_limit_bytes=mib << 20),
        name=name,
    )(*inputs)


def local(
    tokens,
    attn_gain,
    w_qkv,
    w_out,
    k_cache,
    value_cache,
    lengths,
    moe_gain,
    routes,
    gates,
    w_in,
    w_down,
):
    f32, bf16 = jnp.float32, jnp.bfloat16
    seqs, slice_width = tokens.shape
    hd = HEAD_DIMENSION
    hidden = w_down.shape[1]
    local_exp = w_in.shape[0]
    n_ctx, n_exp = lax.axis_size("ctx"), lax.axis_size("exp")
    experts_all = local_exp * n_exp
    top_k = routes.shape[1]
    capacity = 2 * seqs * top_k // experts_all
    per_source = local_exp * capacity

    cols = w_qkv.shape[1]
    message = call(
        project_kernel,
        "project",
        shape((seqs, cols + 128)),
        (tokens, attn_gain[None], w_qkv),
        [HBM] * 3,
        [
            pltpu.VMEM(tokens.shape, bf16),
            pltpu.VMEM((1, slice_width), f32),
            pltpu.VMEM(w_qkv.shape, bf16),
            pltpu.SemaphoreType.DMA((2,)),
            pltpu.SemaphoreType.DMA((10,)),
        ],
        mib=62,
    )
    got = exchange(message, 0, n_ctx, n_exp)
    keys, values, w_near = call(
        load_kernel,
        "load",
        (shape(k_cache.shape), shape(value_cache.shape), shape(w_out.shape)),
        (message, k_cache, value_cache, w_out),
        [ANY] + [HBM] * 3,
        [pltpu.SemaphoreType.DMA((3,))],
    )
    message = call(
        add_kernel,
        "add",
        shape(message.shape),
        (message, *got, w_near),
        [VM] * 4 + [ANY],
    )
    shares = [message] + exchange(message, 1, n_ctx, n_exp)
    cosine, sine = rotation(lengths, hd)
    positions = k_cache.shape[1]
    first = lax.axis_index("ctx")
    where_pos = first * positions + jnp.arange(positions)
    live = (where_pos[None, :] < lengths[:, None]).astype(f32)
    owns = jnp.broadcast_to((first == 0).astype(f32), (seqs, 128))

    flat_ids = routes.reshape(-1)
    onehot = (flat_ids[:, None] == jnp.arange(experts_all)[None, :]).astype(jnp.int32)
    rank = jnp.sum((jnp.cumsum(onehot, 0) - onehot) * onehot, -1)
    slot_index = flat_ids * capacity + rank
    select = (slot_index[:, None] == jnp.arange(experts_all * capacity)[None, :]).astype(f32)
    token_map = (jnp.arange(seqs * top_k)[:, None] // top_k == jnp.arange(seqs)[None, :]).astype(f32)
    placing = jnp.dot(select.T, token_map, precision=lax.Precision.HIGHEST).astype(bf16)
    placing = jnp.pad(placing, ((0, 0), (0, 128 - seqs)))
    weighting = jnp.dot(
        token_map.T, select * gates.reshape(-1)[:, None], precision=lax.Precision.HIGHEST
    )

    part = call(
        functools.partial(attend_kernel, seqs),
        "attend",
        shape(((seqs + 1) * QUERY_HEADS, hd)),
        (*shares, cosine, sine, live, owns, keys, values),
        [VM] * 10,
        [pltpu.VMEM((cols // hd * seqs, hd), f32)],
    )
    part = call(
        functools.partial(merge_kernel, seqs),
        "merge",
        shape(part.shape),
        [part] + exchange(part, 0, n_ctx, n_exp),
        [VM] * 4,
    )
    context, resid, outgoing = call(
        functools.partial(finish_kernel, seqs),
        "finish",
        (
            shape((seqs, QUERY_HEADS * hd)),
            shape(tokens.shape),
            shape((placing.shape[0], slice_width)),
        ),
        [part] + exchange(part, 1, n_ctx, n_exp) + [tokens, placing, w_near],
        [VM] * 7,
        [pltpu.VMEM((QUERY_HEADS * seqs, hd), f32)],
    )

    n_rows = n_exp * per_source
    rows = lax.all_to_all(
        outgoing.reshape(n_exp, per_source, slice_width), "exp", split_axis=0, concat_axis=0, tiled=True
    )
    message = call(
        functools.partial(gate_up_kernel, capacity),
        "gate_up",
        shape((n_rows, 2 * hidden + 128)),
        (rows.reshape(n_rows, slice_width), moe_gain[None], w_in),
        [VM] * 3,
    )
    sums = lax.all_to_all(
        message.reshape(n_ctx, n_rows // n_ctx, 2 * hidden + 128),
        "ctx",
        split_axis=0,
        concat_axis=0,
        tiled=True,
    )
    act = call(
        activate_kernel, "activate", shape((n_ctx, n_rows // n_ctx, hidden)), (sums,), [VM]
    )
    act = lax.all_to_all(act, "ctx", split_axis=0, concat_axis=0, tiled=True)
    expert_out = call(
        functools.partial(down_kernel, capacity),
        "down",
        shape((n_rows, slice_width)),
        (act.reshape(n_rows, hidden), w_down),
        [VM] * 2,
    )
    returned = lax.all_to_all(
        expert_out.reshape(n_exp, per_source, slice_width), "exp", split_axis=0, concat_axis=0, tiled=True
    )
    layer_out = call(
        combine_kernel,
        "combine",
        shape(tokens.shape),
        (resid, weighting, returned.reshape(n_rows, slice_width)),
        [VM] * 3,
    )
    return (context, layer_out)


def solution(mesh):
    placed = (
        P("exp", "ctx"),
        P("ctx"),
        P("ctx", None),
        P(None, "ctx"),
        P("exp", "ctx", None),
        P("exp", "ctx", None),
        P("exp"),
        P("ctx"),
        P("exp", None),
        P("exp", None),
        P("exp", "ctx", None),
        P("exp", None, "ctx"),
    )
    return jax.shard_map(
        local,
        mesh=mesh,
        in_specs=placed,
        out_specs=(P("exp", None), P("exp", "ctx")),
        check_vma=False,
    )
```

time: 448 us -> 106 us (0.24)
  waiting for transfers between devices: 202 us -> 25.8 us
  blocking collectives: 203 us -> 34.8 us
  starting transfers between devices: 9.15 us -> 24.7 us
  matrix products: 14.7 us -> 0.51 us
  between operations: 13.9 us -> 0.81 us
  Pallas kernels: 0 us -> 12.3 us
  local copies, waits for them, and re-layouts: 1 us -> 6.27 us
    psum x3 -> x0, waiting for transfers between devices: 194 us -> none  [the longest x1 86.1 us: local(): summed = lax.psum(gate_up, 'ctx')]
    psum x3 -> x0, blocking collectives: 122 us -> none  [the longest x1 56 us: local(): lax.psum((local_total * factor, local_acc * factor[..., None]), 'ctx')]
    pmax x1 -> x0, blocking collectives: 58 us -> none  [local(): whole_top = lax.pmax(local_top, 'ctx')]
    ppermute x0 -> x12, starting transfers between devices: none -> 15.4 us  [exchange(): got.append(lax.ppermute(value, AXES, pairs))]
    dot_general x10 -> x1, matrix products: 14.4 us -> 0.25 us  [local(): jnp.dot(select.T, token_map, precision=lax.Precision.HIGHEST).astype(bf16)]
    pallas_call x0 -> x10, Pallas kernels: none -> 12.3 us  [call(): pl.pallas_call(kernel, out_shape=out, in_specs=specs, out_specs=jax.tree....]
    all_to_all x1 -> x2, blocking collectives: 23.5 us -> 34.8 us  [the longest x1 22.2 us: local(): lax.all_to_all(outgoing.reshape(n_exp, per_source, slice_width), 'exp', s...]
    ppermute x0 -> x12, waiting for transfers between devices: none -> 11.1 us  [exchange(): got.append(lax.ppermute(value, AXES, pairs))]
  transfers between devices with their start and end apart: 4 -> 14, of which waited for: 4 -> 8; matrix products, arithmetic and copies ran while one was open for 0% -> 1% of each run, Pallas kernels for 0% -> 0%
where the time goes in v1:
time: 106 us
  blocking collectives  34.8 us (33%)
  waiting for transfers between devices  25.8 us (24%)
  starting transfers between devices  24.7 us (23%)
  Pallas kernels  12.3 us (12%)
  local copies, waits for them, and re-layouts  6.27 us (6%)
    all_to_all x1, blocking collectives, local(): lax.all_to_all(outgoing.reshape(n_exp, per_source, slice_width), 'exp', s...  22.2 us
    ppermute x12, starting transfers between devices, exchange(): got.append(lax.ppermute(value, AXES, pairs))  15.4 us
    all_to_all x1, blocking collectives, local(): lax.all_to_all(message.reshape(n_ctx, n_rows // n_ctx, 2 * hidden + 128),...  12.7 us
    pallas_call x10, Pallas kernels, call(): pl.pallas_call(kernel, out_shape=out, in_specs=specs, out_specs=jax.tree....  12.3 us
    ppermute x12, waiting for transfers between devices, exchange(): got.append(lax.ppermute(value, AXES, pairs))  11.1 us
    all_to_all x1, waiting for transfers between devices, local(): lax.all_to_all(expert_out.reshape(n_exp, per_source, slice_width), 'exp',...  7.58 us
    all_to_all x1, waiting for transfers between devices, local(): act = lax.all_to_all(act, 'ctx', split_axis=0, concat_axis=0, tiled=True)  7.06 us
    unnamed x24, local copies, waits for them, and re-layouts  5.97 us
  transfers between devices with their start and end apart: 14, of which 8 were waited for; matrix products, arithmetic and copies ran while one was open for 1% of the time, Pallas kernels for 0%

profile of v1, /device:TPU:1, one launch (start us, length us, event | category | flops | bytes accessed | tf_op | source)
XLA Modules:
  0.0 105.8 jit_solution(5855285759059687856)
XLA Ops:
  0.6 0.0 copy-start.11
  0.6 0.0 copy-start.9
  0.7 0.0 copy-start.3
  0.7 3.8 %project.1.after.m0 = bf16[8,5248]{1,0:T(8,128)(2,1)} custom-call(bf16[8,256]{1,0:T(8,128)(2,1)} %tokens.1, f32[1,256]{1,0:T(1,128)} %bitcast.14, bf16[256,5120]{1,0:T(8,128)(2,1)} %w_hbm.2), custom_call_target="tpu_custom_call" | custom-call | tf_op jit(solution)/shard_map/project/pallas_call | solution.py:310
  4.5 2.2 %collective-permute-start = (bf16[8,5248]{1,0:T(8,128)(2,1)}, bf16[8,5248]{1,0:T(8,128)(2,1)S(1)}, u32[]{:S(2)}, u32[]{:S(2)}) collective-permute-start(bf16[8,5248]{1,0:T(8,128)(2,1)} %project.1.after.m0), channel_id=1, source_target_pairs={{0,16},{1,65},{2,18},{3,67},{4,20},{5,69},{6,22},{7,71},{8,24},{9,... | collective-permute-start | bytes 251912 | tf_op jit(solution)/shard_map/ppermute | solution.py:26
  6.7 2.6 %collective-permute-start.1 = (bf16[8,5248]{1,0:T(8,128)(2,1)}, bf16[8,5248]{1,0:T(8,128)(2,1)S(1)}, u32[]{:S(2)}, u32[]{:S(2)}) collective-permute-start(bf16[8,5248]{1,0:T(8,128)(2,1)} %project.1.after.m0), channel_id=1, source_target_pairs={{0,32},{1,129},{2,34},{3,131},{4,36},{5,133},{6,38},{7,135},{8,40}... | collective-permute-start | bytes 251912 | tf_op jit(solution)/shard_map/ppermute | solution.py:26
  9.3 0.0 collective-permute-start.2
  9.3 0.0 copy-done.11
  9.4 0.1 compare_convert_fusion.live_ref
  9.5 0.1 reshape.84
  9.5 0.1 fusion.2
  9.6 0.1 reduce_window_sum.11
  9.7 0.1 fusion.9
  9.8 0.0 copy-done.3
  9.8 0.0 copy-start.1
  9.8 1.6 %copy-done.1 = bf16[4096,256]{1,0:T(8,128)(2,1)S(1)} copy-done((bf16[4096,256]{1,0:T(8,128)(2,1)S(1)}, bf16[4096,256]{1,0:T(8,128)(2,1)}, u32[]{:S(2)}) %copy-start.1) | copy-done | bytes 2097176
  11.4 1.2 %copy-done.4 = bf16[8,128,512]{2,1,0:T(8,128)(2,1)S(1)} copy-done((bf16[8,128,512]{2,1,0:T(8,128)(2,1)S(1)}, bf16[8,128,512]{2,1,0:T(8,128)(2,1)}, u32[]{:S(2)}) %copy-start.4) | copy-done | bytes 1048600
  12.7 0.9 copy-done.5
  13.5 0.3 load.1
  13.9 0.2 select_reduce_fusion
  14.0 0.0 collective-permute-done.m1
  14.0 0.0 collective-permute-done.1.m2
  14.1 0.0 collective-permute-done.2.m3
  14.1 0.4 copy-done.6
  14.4 0.2 add.32.m0
  14.6 1.3 %collective-permute-start.3 = (bf16[8,5248]{1,0:T(8,128)(2,1)S(1)}, bf16[8,5248]{1,0:T(8,128)(2,1)S(1)}, u32[]{:S(2)}, u32[]{:S(2)}) collective-permute-start(bf16[8,5248]{1,0:T(8,128)(2,1)S(1)} %add.32.m0), channel_id=1, source_target_pairs={{0,64},{1,17},{2,66},{3,19},{4,68},{5,21},{6,70},{7,23},{8,72},{9,... | collective-permute-start | bytes 251912 | tf_op jit(solution)/shard_map/ppermute | solution.py:26
  15.9 2.5 %collective-permute-start.4 = (bf16[8,5248]{1,0:T(8,128)(2,1)S(1)}, bf16[8,5248]{1,0:T(8,128)(2,1)S(1)}, u32[]{:S(2)}, u32[]{:S(2)}) collective-permute-start(bf16[8,5248]{1,0:T(8,128)(2,1)S(1)} %add.32.m0), channel_id=1, source_target_pairs={{0,128},{1,33},{2,130},{3,35},{4,132},{5,37},{6,134},{7,39},{8,136... | collective-permute-start | bytes 251912 | tf_op jit(solution)/shard_map/ppermute | solution.py:26
  18.3 0.2 collective-permute-start.5
  18.5 0.1 pad_maximum_fusion
  18.6 0.0 collective-permute-done.3.m1
  18.6 2.5 %collective-permute-done.4.m2 = bf16[8,5248]{1,0:T(8,128)(2,1)S(1)} collective-permute-done((bf16[8,5248]{1,0:T(8,128)(2,1)S(1)}, bf16[8,5248]{1,0:T(8,128)(2,1)S(1)}, u32[]{:S(2)}, u32[]{:S(2)}) %collective-permute-start.4) | collective-permute-done | bytes 84000 | tf_op jit(solution)/shard_map/ppermute | solution.py:26
  21.1 2.1 %collective-permute-done.5.m3 = bf16[8,5248]{1,0:T(8,128)(2,1)S(1)} collective-permute-done((bf16[8,5248]{1,0:T(8,128)(2,1)S(1)}, bf16[8,5248]{1,0:T(8,128)(2,1)S(1)}, u32[]{:S(2)}, u32[]{:S(2)}) %collective-permute-start.5) | collective-permute-done | bytes 84000 | tf_op jit(solution)/shard_map/ppermute | solution.py:26
  23.1 3.2 %attend.1.p0 = bf16[288,128]{1,0:T(8,128)(2,1)S(1)} custom-call(bf16[8,5248]{1,0:T(8,128)(2,1)S(1)} %add.32.m0, bf16[8,5248]{1,0:T(8,128)(2,1)S(1)} %collective-permute-done.3.m1, bf16[8,5248]{1,0:T(8,128)(2,1)S(1)} %collective-permute-done.4.m2, bf16[8,5248]{1,0:T(8,128)(2,1)S(1)} %collective-permute-done.5.m3, f32[8,128]{1,0:T(8,128)S(1)} %get-tuple-element.17.cosine, ...), custom_call_target="tpu_custom_call" | custom-call | tf_op jit(solution)/shard_map/attend/pallas_call | solution.py:310
  26.4 0.1 collective-permute-start.6
  26.5 3.5 %collective-permute-start.7 = (bf16[288,128]{1,0:T(8,128)(2,1)S(1)}, bf16[288,128]{1,0:T(8,128)(2,1)S(1)}, u32[]{:S(2)}, u32[]{:S(2)}) collective-permute-start(bf16[288,128]{1,0:T(8,128)(2,1)S(1)} %attend.1.p0), channel_id=1, source_target_pairs={{0,32},{1,129},{2,34},{3,131},{4,36},{5,133},{6,38},{7,135},{8,40}... | collective-permute-start | bytes 221192 | tf_op jit(solution)/shard_map/ppermute | solution.py:26
  30.0 0.3 collective-permute-start.8
  30.3 0.0 collective-permute-done.6.p1
  30.3 2.2 %collective-permute-done.7.p2 = bf16[288,128]{1,0:T(8,128)(2,1)S(1)} collective-permute-done((bf16[288,128]{1,0:T(8,128)(2,1)S(1)}, bf16[288,128]{1,0:T(8,128)(2,1)S(1)}, u32[]{:S(2)}, u32[]{:S(2)}) %collective-permute-start.7) | collective-permute-done | bytes 73760 | tf_op jit(solution)/shard_map/ppermute | solution.py:26
  32.5 1.9 %collective-permute-done.8.p3 = bf16[288,128]{1,0:T(8,128)(2,1)S(1)} collective-permute-done((bf16[288,128]{1,0:T(8,128)(2,1)S(1)}, bf16[288,128]{1,0:T(8,128)(2,1)S(1)}, u32[]{:S(2)}, u32[]{:S(2)}) %collective-permute-start.8) | collective-permute-done | bytes 73760 | tf_op jit(solution)/shard_map/ppermute | solution.py:26
  34.4 0.3 merge.1.p0
  34.8 0.7 collective-permute-start.10
  35.4 1.2 %collective-permute-start.11 = (bf16[288,128]{1,0:T(8,128)(2,1)S(1)}, bf16[288,128]{1,0:T(8,128)(2,1)S(1)}, u32[]{:S(2)}, u32[]{:S(2)}) collective-permute-start(bf16[288,128]{1,0:T(8,128)(2,1)S(1)} %merge.1.p0), channel_id=1, source_target_pairs={{0,192},{1,49},{2,194},{3,51},{4,196},{5,53},{6,198},{7,55},{8,200... | collective-permute-start | bytes 221192 | tf_op jit(solution)/shard_map/ppermute | solution.py:26
  36.6 0.9 collective-permute-start.9
  37.5 0.2 convolution_convert_fusion
  37.7 0.1 copy.15
  37.9 1.7 %collective-permute-done.10.p2 = bf16[288,128]{1,0:T(8,128)(2,1)S(1)} collective-permute-done((bf16[288,128]{1,0:T(8,128)(2,1)S(1)}, bf16[288,128]{1,0:T(8,128)(2,1)S(1)}, u32[]{:S(2)}, u32[]{:S(2)}) %collective-permute-start.10) | collective-permute-done | bytes 73760 | tf_op jit(solution)/shard_map/ppermute | solution.py:26
  39.6 0.7 collective-permute-done.11.p3
  40.3 0.0 collective-permute-done.9.p1
  40.3 0.0 copy-done.7
  40.3 1.3 %finish.1 = (bf16[8,4096]{1,0:T(8,128)(2,1)}, bf16[8,256]{1,0:T(8,128)(2,1)S(1)}, bf16[128,256]{1,0:T(8,128)(2,1)S(1)}) custom-call(bf16[288,128]{1,0:T(8,128)(2,1)S(1)} %merge.1.p0, bf16[288,128]{1,0:T(8,128)(2,1)S(1)} %collective-permute-done.9.p1, bf16[288,128]{1,0:T(8,128)(2,1)S(1)} %collective-permute-done.10.p2, ...), custom_call_target="tpu_custom_call" | custom-call | tf_op jit(solution)/shard_map/finish/pallas_call | solution.py:310
  41.6 22.2 %all_to_all.20 = bf16[16,8,256]{2,1,0:T(8,128)(2,1)S(1)} all-to-all(bf16[16,8,256]{2,1,0:T(8,128)(2,1)S(1)} %bitcast.12), channel_id=1, replica_groups=mesh['ctx'=16,'exp'=16] {'exp'}, dimensions={0} | all-to-all | bytes 131072 | tf_op jit(solution)/shard_map/all_to_all | solution.py:427
  63.8 0.0 copy-done.8
  63.8 1.9 %copy-done = bf16[4,256,1536]{2,1,0:T(8,128)(2,1)S(1)} copy-done((bf16[4,256,1536]{2,1,0:T(8,128)(2,1)S(1)}, bf16[4,256,1536]{2,1,0:T(8,128)(2,1)}, u32[]{:S(2)}) %copy-start) | copy-done | bytes 3145752
  65.7 0.6 gate_up.1
  66.3 12.7 %all_to_all.21.shares = bf16[16,8,1664]{2,1,0:T(8,128)(2,1)S(1)} all-to-all(bf16[16,8,1664]{2,1,0:T(8,128)(2,1)S(1)} %bitcast.8), channel_id=1, replica_groups=mesh['ctx'=16,'exp'=16] {'ctx'}, dimensions={0} | all-to-all | bytes 851968 | tf_op jit(solution)/shard_map/all_to_all | solution.py:437
  79.0 0.9 activate.1
  79.8 3.5 %all-to-all-start.2 = ((bf16[16,8,768]{2,1,0:T(8,128)(2,1)}), bf16[16,8,768]{2,1,0:T(8,128)(2,1)S(1)}, u32[]{:S(2)}, u32[]{:S(2)}) async-start(bf16[16,8,768]{2,1,0:T(8,128)(2,1)} %activate.1), calls=%async_computation.2 | async-start | bytes 393216 | tf_op jit(solution)/shard_map/all_to_all | solution.py:447
  83.4 0.1 mul.49
  83.4 7.1 %all-to-all-done.2 = bf16[16,8,768]{2,1,0:T(8,128)(2,1)S(1)} async-done(((bf16[16,8,768]{2,1,0:T(8,128)(2,1)}), bf16[16,8,768]{2,1,0:T(8,128)(2,1)S(1)}, u32[]{:S(2)}, u32[]{:S(2)}) %all-to-all-start.2) | async-done | bytes 196640 | tf_op jit(solution)/shard_map/all_to_all | solution.py:447
  90.5 1.0 down.1
  91.5 5.8 %all-to-all-start.3 = ((bf16[16,8,256]{2,1,0:T(8,128)(2,1)}), bf16[16,8,256]{2,1,0:T(8,128)(2,1)S(1)}, u32[]{:S(2)}, u32[]{:S(2)}) async-start(bf16[16,8,256]{2,1,0:T(8,128)(2,1)} %bitcast.6), calls=%async_computation.3 | async-start | bytes 131072 | tf_op jit(solution)/shard_map/all_to_all | solution.py:455
  97.3 0.3 fusion.weighting
  97.5 7.6 %all-to-all-done.3 = bf16[16,8,256]{2,1,0:T(8,128)(2,1)S(1)} async-done(((bf16[16,8,256]{2,1,0:T(8,128)(2,1)}), bf16[16,8,256]{2,1,0:T(8,128)(2,1)S(1)}, u32[]{:S(2)}, u32[]{:S(2)}) %all-to-all-start.3) | async-done | bytes 65568 | tf_op jit(solution)/shard_map/all_to_all | solution.py:455
  105.1 0.7 combine.1
  (17 shorter events, 0.1 us)
Async XLA Ops:
  0.6 8.7 %copy-start.11 = (s32[8]{0:T(128)S(1)}, s32[8]{0:T(128)}, u32[]{:S(2)}) copy-start(s32[8]{0:T(128)} %param.18) | copy-start | bytes 100
  0.6 8.8 %copy-start.9 = (s32[8,8]{1,0:T(8,128)S(1)}, s32[8,8]{1,0:T(8,128)}, u32[]{:S(2)}) copy-start(s32[8,8]{1,0:T(8,128)} %param.20) | copy-start | bytes 772
  0.7 9.2 %copy-start.3 = (bf16[8,128,512]{2,1,0:T(8,128)(2,1)S(1)}, bf16[8,128,512]{2,1,0:T(8,128)(2,1)}, u32[]{:S(2)}) copy-start(bf16[8,128,512]{2,1,0:T(8,128)(2,1)} %k_hbm.1) | copy-start | bytes 3145732
  4.5 9.5 %collective-permute-start = (bf16[8,5248]{1,0:T(8,128)(2,1)}, bf16[8,5248]{1,0:T(8,128)(2,1)S(1)}, u32[]{:S(2)}, u32[]{:S(2)}) collective-permute-start(bf16[8,5248]{1,0:T(8,128)(2,1)} %project.1.after.m0), channel_id=1, source_target_pairs={{0,16},{1,65},{2,18},{3,67},{4,20},{5,69},{6,22},{7,71},{8,24},{9,... | collective-permute-start | bytes 251912 | tf_op jit(solution)/shard_map/ppermute | solution.py:26
  6.7 7.3 %collective-permute-start.1 = (bf16[8,5248]{1,0:T(8,128)(2,1)}, bf16[8,5248]{1,0:T(8,128)(2,1)S(1)}, u32[]{:S(2)}, u32[]{:S(2)}) collective-permute-start(bf16[8,5248]{1,0:T(8,128)(2,1)} %project.1.after.m0), channel_id=1, source_target_pairs={{0,32},{1,129},{2,34},{3,131},{4,36},{5,133},{6,38},{7,135},{8,40}... | collective-permute-start | bytes 251912 | tf_op jit(solution)/shard_map/ppermute | solution.py:26
  9.3 4.7 %collective-permute-start.2 = (bf16[8,5248]{1,0:T(8,128)(2,1)}, bf16[8,5248]{1,0:T(8,128)(2,1)S(1)}, u32[]{:S(2)}, u32[]{:S(2)}) collective-permute-start(bf16[8,5248]{1,0:T(8,128)(2,1)} %project.1.after.m0), channel_id=1, source_target_pairs={{0,48},{1,193},{2,50},{3,195},{4,52},{5,197},{6,54},{7,199},{8,56}... | collective-permute-start | bytes 251912 | tf_op jit(solution)/shard_map/ppermute | solution.py:26
  9.8 1.6 %copy-start.1 = (bf16[4096,256]{1,0:T(8,128)(2,1)S(1)}, bf16[4096,256]{1,0:T(8,128)(2,1)}, u32[]{:S(2)}) copy-start(bf16[4096,256]{1,0:T(8,128)(2,1)} %w_hbm.3) | copy-start | bytes 6291460
  11.4 1.2 %copy-start.4 = (bf16[8,128,512]{2,1,0:T(8,128)(2,1)S(1)}, bf16[8,128,512]{2,1,0:T(8,128)(2,1)}, u32[]{:S(2)}) copy-start(bf16[8,128,512]{2,1,0:T(8,128)(2,1)} %v_hbm.1) | copy-start | bytes 3145732
  12.7 0.9 copy-start.5
  13.5 0.9 copy-start.6
  14.6 25.8 %copy-start.7 = (bf16[8,256]{1,0:T(8,128)(2,1)S(1)}, bf16[8,256]{1,0:T(8,128)(2,1)}, u32[]{:S(2)}) copy-start(bf16[8,256]{1,0:T(8,128)(2,1)} %tokens.1) | copy-start | bytes 12292
  14.6 4.0 %collective-permute-start.3 = (bf16[8,5248]{1,0:T(8,128)(2,1)S(1)}, bf16[8,5248]{1,0:T(8,128)(2,1)S(1)}, u32[]{:S(2)}, u32[]{:S(2)}) collective-permute-start(bf16[8,5248]{1,0:T(8,128)(2,1)S(1)} %add.32.m0), channel_id=1, source_target_pairs={{0,64},{1,17},{2,66},{3,19},{4,68},{5,21},{6,70},{7,23},{8,72},{9,... | collective-permute-start | bytes 251912 | tf_op jit(solution)/shard_map/ppermute | solution.py:26
  15.9 5.2 %collective-permute-start.4 = (bf16[8,5248]{1,0:T(8,128)(2,1)S(1)}, bf16[8,5248]{1,0:T(8,128)(2,1)S(1)}, u32[]{:S(2)}, u32[]{:S(2)}) collective-permute-start(bf16[8,5248]{1,0:T(8,128)(2,1)S(1)} %add.32.m0), channel_id=1, source_target_pairs={{0,128},{1,33},{2,130},{3,35},{4,132},{5,37},{6,134},{7,39},{8,136... | collective-permute-start | bytes 251912 | tf_op jit(solution)/shard_map/ppermute | solution.py:26
  18.3 4.8 %collective-permute-start.5 = (bf16[8,5248]{1,0:T(8,128)(2,1)S(1)}, bf16[8,5248]{1,0:T(8,128)(2,1)S(1)}, u32[]{:S(2)}, u32[]{:S(2)}) collective-permute-start(bf16[8,5248]{1,0:T(8,128)(2,1)S(1)} %add.32.m0), channel_id=1, source_target_pairs={{0,192},{1,49},{2,194},{3,51},{4,196},{5,53},{6,198},{7,55},{8,200... | collective-permute-start | bytes 251912 | tf_op jit(solution)/shard_map/ppermute | solution.py:26
  26.4 37.4 %copy-start.8 = (f32[256]{0:T(256)S(1)}, f32[256]{0:T(256)}, u32[]{:S(2)}) copy-start(f32[256]{0:T(256)} %param.19) | copy-start | bytes 3076
  26.4 3.9 %collective-permute-start.6 = (bf16[288,128]{1,0:T(8,128)(2,1)S(1)}, bf16[288,128]{1,0:T(8,128)(2,1)S(1)}, u32[]{:S(2)}, u32[]{:S(2)}) collective-permute-start(bf16[288,128]{1,0:T(8,128)(2,1)S(1)} %attend.1.p0), channel_id=1, source_target_pairs={{0,16},{1,65},{2,18},{3,67},{4,20},{5,69},{6,22},{7,71},{8,24},{9,... | collective-permute-start | bytes 221192 | tf_op jit(solution)/shard_map/ppermute | solution.py:26
  26.5 6.1 %collective-permute-start.7 = (bf16[288,128]{1,0:T(8,128)(2,1)S(1)}, bf16[288,128]{1,0:T(8,128)(2,1)S(1)}, u32[]{:S(2)}, u32[]{:S(2)}) collective-permute-start(bf16[288,128]{1,0:T(8,128)(2,1)S(1)} %attend.1.p0), channel_id=1, source_target_pairs={{0,32},{1,129},{2,34},{3,131},{4,36},{5,133},{6,38},{7,135},{8,40}... | collective-permute-start | bytes 221192 | tf_op jit(solution)/shard_map/ppermute | solution.py:26
  30.0 4.4 %collective-permute-start.8 = (bf16[288,128]{1,0:T(8,128)(2,1)S(1)}, bf16[288,128]{1,0:T(8,128)(2,1)S(1)}, u32[]{:S(2)}, u32[]{:S(2)}) collective-permute-start(bf16[288,128]{1,0:T(8,128)(2,1)S(1)} %attend.1.p0), channel_id=1, source_target_pairs={{0,48},{1,193},{2,50},{3,195},{4,52},{5,197},{6,54},{7,199},{8,56}... | collective-permute-start | bytes 221192 | tf_op jit(solution)/shard_map/ppermute | solution.py:26
  34.8 4.8 %collective-permute-start.10 = (bf16[288,128]{1,0:T(8,128)(2,1)S(1)}, bf16[288,128]{1,0:T(8,128)(2,1)S(1)}, u32[]{:S(2)}, u32[]{:S(2)}) collective-permute-start(bf16[288,128]{1,0:T(8,128)(2,1)S(1)} %merge.1.p0), channel_id=1, source_target_pairs={{0,128},{1,33},{2,130},{3,35},{4,132},{5,37},{6,134},{7,39},{8,136... | collective-permute-start | bytes 221192 | tf_op jit(solution)/shard_map/ppermute | solution.py:26
  35.4 4.9 %collective-permute-start.11 = (bf16[288,128]{1,0:T(8,128)(2,1)S(1)}, bf16[288,128]{1,0:T(8,128)(2,1)S(1)}, u32[]{:S(2)}, u32[]{:S(2)}) collective-permute-start(bf16[288,128]{1,0:T(8,128)(2,1)S(1)} %merge.1.p0), channel_id=1, source_target_pairs={{0,192},{1,49},{2,194},{3,51},{4,196},{5,53},{6,198},{7,55},{8,200... | collective-permute-start | bytes 221192 | tf_op jit(solution)/shard_map/ppermute | solution.py:26
  36.6 3.7 %collective-permute-start.9 = (bf16[288,128]{1,0:T(8,128)(2,1)S(1)}, bf16[288,128]{1,0:T(8,128)(2,1)S(1)}, u32[]{:S(2)}, u32[]{:S(2)}) collective-permute-start(bf16[288,128]{1,0:T(8,128)(2,1)S(1)} %merge.1.p0), channel_id=1, source_target_pairs={{0,64},{1,17},{2,66},{3,19},{4,68},{5,21},{6,70},{7,23},{8,72},{9,... | collective-permute-start | bytes 221192 | tf_op jit(solution)/shard_map/ppermute | solution.py:26
  63.8 1.9 %copy-start = (bf16[4,256,1536]{2,1,0:T(8,128)(2,1)S(1)}, bf16[4,256,1536]{2,1,0:T(8,128)(2,1)}, u32[]{:S(2)}) copy-start(bf16[4,256,1536]{2,1,0:T(8,128)(2,1)} %w_ref.2) | copy-start | bytes 9437188
  65.7 17.7 %copy-start.10 = (f32[8,8]{1,0:T(8,128)S(1)}, f32[8,8]{1,0:T(8,128)}, u32[]{:S(2)}) copy-start(f32[8,8]{1,0:T(8,128)} %param.21) | copy-start | bytes 772
  65.7 24.8 %copy-start.2 = (bf16[4,768,256]{2,1,0:T(8,128)(2,1)S(1)}, bf16[4,768,256]{2,1,0:T(8,128)(2,1)}, u32[]{:S(2)}) copy-start(bf16[4,768,256]{2,1,0:T(8,128)(2,1)} %w_ref.3) | copy-start | bytes 4718596
  79.8 10.7 %all-to-all-start.2 = ((bf16[16,8,768]{2,1,0:T(8,128)(2,1)}), bf16[16,8,768]{2,1,0:T(8,128)(2,1)S(1)}, u32[]{:S(2)}, u32[]{:S(2)}) async-start(bf16[16,8,768]{2,1,0:T(8,128)(2,1)} %activate.1), calls=%async_computation.2 | async-start | bytes 393216 | tf_op jit(solution)/shard_map/all_to_all | solution.py:447
  91.5 13.6 %all-to-all-start.3 = ((bf16[16,8,256]{2,1,0:T(8,128)(2,1)}), bf16[16,8,256]{2,1,0:T(8,128)(2,1)S(1)}, u32[]{:S(2)}, u32[]{:S(2)}) async-start(bf16[16,8,256]{2,1,0:T(8,128)(2,1)} %bitcast.6), calls=%async_computation.3 | async-start | bytes 131072 | tf_op jit(solution)/shard_map/all_to_all | solution.py:455

commit v2 on v1

--- a/solution.py
+++ b/solution.py
@@ -23,7 +23,8 @@
             for e in range(n_exp):
                 j = i ^ step if (e & 1) == stage else i ^ (side * step)
                 pairs.append((i * n_exp + e, j * n_exp + e))
-        got.append(lax.ppermute(value, AXES, pairs))
+        sent = value[step - 1] if isinstance(value, (list, tuple)) else value
+        got.append(lax.ppermute(sent, AXES, pairs))
     return got
 
 
@@ -88,10 +89,11 @@
         out[:, at] = jnp.dot(scaled, w_ref[:, at], preferred_element_type=f32).astype(bf16)
 
 
-def load_kernel(after, k_hbm, v_hbm, w_hbm, k_out, v_out, w_out, sems):
+def load_kernel(after, *refs):
+    count = len(refs) // 2
+    sems = refs[-1]
     copies = [
-        pltpu.make_async_copy(source, target, sems.at[i])
-        for i, (source, target) in enumerate(((k_hbm, k_out), (v_hbm, v_out), (w_hbm, w_out)))
+        pltpu.make_async_copy(refs[i], refs[count + i], sems.at[i]) for i in range(count)
     ]
     for copy in copies:
         copy.start()
@@ -99,8 +101,9 @@
         copy.wait()
 
 
-def add_kernel(m0, m1, m2, m3, after, out):
-    f32, bf16 = jnp.float32, jnp.bfloat16
+def add_kernel(m0, m1, m2, m3, *rest):
+    f32, bf16 = jnp.float32, jnp.bfloat16
+    out = rest[-1]
     cols = out.shape[1] - 128
 
     def total(at):
@@ -112,7 +115,9 @@
     out[:, cols:] = halves((squares + pltpu.roll(squares, 64, 1))[:, :1])
 
 
-def attend_kernel(seqs, m0, m1, m2, m3, cosine, sine, live_ref, owns, k_ref, v_ref, out, rows):
+def attend_kernel(
+    seqs, m0, m1, m2, m3, cosine, sine, live_ref, owns, k_ref, v_ref, after, out, rows
+):
     f32, bf16 = jnp.float32, jnp.bfloat16
     qh, kvh, hd = QUERY_HEADS, KEY_VALUE_HEADS, HEAD_DIMENSION
     group = qh // kvh
@@ -146,9 +151,10 @@
     zero = jnp.zeros((group, hd), f32)
     lanes = lane_ids()
     logs = jnp.zeros((qh, 128), f32)
+    scores, fresh = [], []
     for b in range(seqs):
         q = rows[pl.ds(b, qh, stride=seqs), :]
-        fresh = jnp.where(owns_new, jnp.sum(q * grouped(qh, b), 1, keepdims=True), -1e30)
+        fresh.append(jnp.where(owns_new, jnp.sum(q * grouped(qh, b), 1, keepdims=True), -1e30))
         wide = jnp.concatenate(
             [
                 jnp.concatenate(
@@ -166,20 +172,28 @@
             (((1,), (1,)), ((), ())),
             preferred_element_type=f32,
         )
+        scores.append(both[:qh] + both[qh:])
+    tops, weights, news, totals = [], [], [], []
+    for b in range(seqs):
         live = jnp.broadcast_to(live_ref[b : b + 1, :], (qh, positions)) > 0.5
-        s = jnp.where(live, both[:qh] + both[qh:], -1e30)
-        top = jnp.maximum(jnp.max(s, 1, keepdims=True), fresh)
+        s = jnp.where(live, scores[b], -1e30)
+        top = jnp.maximum(jnp.max(s, 1, keepdims=True), fresh[b])
         p = jnp.where(live, jnp.exp(s - top), 0.0)
-        p_new = jnp.where(owns_new, jnp.exp(fresh - top), 0.0)
-        total = jnp.sum(p, 1, keepdims=True) + p_new
-        acc = jnp.dot(p.astype(bf16), v_ref[b], preferred_element_type=f32)
+        p_new = jnp.where(owns_new, jnp.exp(fresh[b] - top), 0.0)
+        tops.append(top)
+        weights.append(p.astype(bf16))
+        news.append(p_new)
+        totals.append(jnp.sum(p, 1, keepdims=True) + p_new)
+    for b in range(seqs):
+        acc = jnp.dot(weights[b], v_ref[b], preferred_element_type=f32)
         acc = jnp.concatenate(
             [acc[g * group : (g + 1) * group, g * hd : (g + 1) * hd] for g in range(kvh)], 0
         )
-        some = total > 0
-        safe = jnp.where(some, total, 1.0)
-        out[b * qh : (b + 1) * qh, :] = ((acc + p_new * grouped(qh + kvh, b)) / safe).astype(bf16)
-        log = jnp.where(some, top + jnp.log(safe), -1e30)
+        some = totals[b] > 0
+        safe = jnp.where(some, totals[b], 1.0)
+        value = (acc + news[b] * grouped(qh + kvh, b)) / safe
+        out[b * qh : (b + 1) * qh, :] = value.astype(bf16)
+        log = jnp.where(some, tops[b] + jnp.log(safe), -1e30)
         logs = jnp.where(lanes == b, log, logs)
     out[seqs * qh : (seqs + 1) * qh, :] = spread(logs, seqs)
 
@@ -201,7 +215,7 @@
     return values, top + jnp.log(total)
 
 
-def merge_kernel(seqs, p0, p1, p2, p3, out):
+def merge_kernel(seqs, p0, p1, p2, p3, after, out):
     qh = QUERY_HEADS
     values, log = merged(seqs, (p0, p1, p2, p3))
     for b in range(seqs):
@@ -231,56 +245,67 @@
     return lax.rem(row, per_source) // capacity == j
 
 
-def gate_up_kernel(capacity, x_ref, gain, w_ref, out):
+def gate_up_kernel(capacity, place, x_ref, gain, w_ref, *outs):
     f32, bf16 = jnp.float32, jnp.bfloat16
     n_rows, width = x_ref.shape
     experts, _, cols = w_ref.shape
-    xf = x_ref[...].astype(f32)
-    out[:, cols:] = halves(jnp.sum(xf * xf, 1, keepdims=True))
+    part = n_rows // len(outs)
+    xf = jnp.concatenate(
+        [
+            x_ref[pl.ds(pl.multiple_of((place[0] ^ s) * part, part), part), :]
+            for s in range(len(outs))
+        ],
+        0,
+    ).astype(f32)
+    squares = halves(jnp.sum(xf * xf, 1, keepdims=True))
     gained = xf * gain[...]
     blocks = [
         jnp.where(own_rows(capacity, experts * capacity, n_rows, width, j), gained, 0.0).astype(bf16)
         for j in range(experts)
     ]
+    for s, out in enumerate(outs):
+        out[:, cols:] = squares[s * part : (s + 1) * part]
     step = 256
     for c in range(0, cols, step):
         total = jnp.dot(blocks[0], w_ref[0, :, c : c + step], preferred_element_type=f32)
         for j in range(1, experts):
             total += jnp.dot(blocks[j], w_ref[j, :, c : c + step], preferred_element_type=f32)
-        out[:, c : c + step] = total.astype(bf16)
-
-
-def activate_kernel(shares, out):
-    f32, bf16 = jnp.float32, jnp.bfloat16
-    hidden = out.shape[2]
+        total = total.astype(bf16)
+        for s, out in enumerate(outs):
+            out[:, c : c + step] = total[s * part : (s + 1) * part]
+
+
+def activate_kernel(m0, m1, m2, m3, out):
+    f32, bf16 = jnp.float32, jnp.bfloat16
+    hidden = out.shape[1]
 
     def total(at):
-        terms = [shares[i, :, at].astype(f32) for i in range(shares.shape[0])]
-        while len(terms) > 1:
-            terms = [p + q for p, q in zip(terms[::2], terms[1::2])]
-        return terms[0]
+        p, q, r, s = (m[:, at].astype(f32) for m in (m0, m1, m2, m3))
+        return (p + q) + (r + s)
 
     squares = total(slice(2 * hidden, 2 * hidden + 128))
     norm = lax.rsqrt((squares + pltpu.roll(squares, 64, 1)) / D + 1e-06)[:, :1]
     gate = total(slice(0, hidden)) * norm
     up = total(slice(hidden, 2 * hidden)) * norm
-    act = (gate / (1.0 + jnp.exp(-gate)) * up).astype(bf16)
-    for i in range(out.shape[0]):
-        out[i] = act
-
-
-def down_kernel(capacity, x_ref, w_ref, out):
+    out[...] = (gate / (1.0 + jnp.exp(-gate)) * up).astype(bf16)
+
+
+def down_kernel(capacity, place, x0, x1, x2, x3, w_ref, out):
     f32 = jnp.float32
-    n_rows, width = x_ref.shape
+    xf = jnp.concatenate([x[...].astype(f32) for x in (x0, x1, x2, x3)], 0)
+    n_rows, width = xf.shape
+    part = n_rows // 4
     experts = w_ref.shape[0]
-    xf = x_ref[...].astype(f32)
     total = None
     for j in range(experts):
         mine = own_rows(capacity, experts * capacity, n_rows, width, j)
         block = jnp.where(mine, xf, 0.0).astype(jnp.bfloat16)
-        part = jnp.dot(block, w_ref[j], preferred_element_type=f32)
-        total = part if total is None else total + part
-    out[...] = total.astype(jnp.bfloat16)
+        share = jnp.dot(block, w_ref[j], preferred_element_type=f32)
+        total = share if total is None else total + share
+    total = total.astype(jnp.bfloat16)
+    for s in range(4):
+        at = pl.ds(pl.multiple_of((place[0] ^ s) * part, part), part)
+        out[at, :] = total[s * part : (s + 1) * part]
 
 
 def combine_kernel(resid, weighting, returned, out):
@@ -300,6 +325,7 @@
 VM = pl.BlockSpec(memory_space=pltpu.VMEM)
 ANY = pl.BlockSpec(memory_space=pl.ANY)
 HBM = pl.BlockSpec(memory_space=pltpu.HBM)
+SM = pl.BlockSpec(memory_space=pltpu.SMEM)
 
 
 def shape(dims, dtype=jnp.bfloat16):
@@ -316,6 +342,18 @@
         compiler_params=pltpu.CompilerParams(vmem_limit_bytes=mib << 20),
         name=name,
     )(*inputs)
+
+
+def load(after, *arrays):
+    kept = [pltpu.with_memory_space_constraint(a, pltpu.HBM) for a in arrays]
+    return call(
+        load_kernel,
+        "load",
+        tuple(pltpu.VMEM(a.shape, a.dtype) for a in arrays),
+        (after, *kept),
+        [ANY] + [HBM] * len(arrays),
+        [pltpu.SemaphoreType.DMA((len(arrays),))],
+    )
 
 
 def local(
@@ -347,8 +385,11 @@
     message = call(
         project_kernel,
         "project",
-        shape((seqs, cols + 128)),
-        (tokens, attn_gain[None], w_qkv),
+        pltpu.VMEM((seqs, cols + 128), bf16),
+        [
+            pltpu.with_memory_space_constraint(a, pltpu.HBM)
+            for a in (tokens, attn_gain[None], w_qkv)
+        ],
         [HBM] * 3,
         [
             pltpu.VMEM(tokens.shape, bf16),
@@ -357,25 +398,14 @@
             pltpu.SemaphoreType.DMA((2,)),
             pltpu.SemaphoreType.DMA((10,)),
         ],
-        mib=62,
     )
     got = exchange(message, 0, n_ctx, n_exp)
-    keys, values, w_near = call(
-        load_kernel,
-        "load",
-        (shape(k_cache.shape), shape(value_cache.shape), shape(w_out.shape)),
-        (message, k_cache, value_cache, w_out),
-        [ANY] + [HBM] * 3,
-        [pltpu.SemaphoreType.DMA((3,))],
-    )
+    keys, values = load(message, k_cache, value_cache)
     message = call(
-        add_kernel,
-        "add",
-        shape(message.shape),
-        (message, *got, w_near),
-        [VM] * 4 + [ANY],
+        add_kernel, "add", shape(message.shape), (message, *got, keys), [VM] * 4 + [ANY]
     )
     shares = [message] + exchange(message, 1, n_ctx, n_exp)
+    (w_near,) = load(message, w_out)
     cosine, sine = rotation(lengths, hd)
     positions = k_cache.shape[1]
     first = lax.axis_index("ctx")
@@ -399,16 +429,18 @@
         functools.partial(attend_kernel, seqs),
         "attend",
         shape(((seqs + 1) * QUERY_HEADS, hd)),
-        (*shares, cosine, sine, live, owns, keys, values),
-        [VM] * 10,
+        (*shares, cosine, sine, live, owns, keys, values, w_near),
+        [VM] * 10 + [ANY],
         [pltpu.VMEM((cols // hd * seqs, hd), f32)],
     )
+    parts = [part] + exchange(part, 0, n_ctx, n_exp)
+    (w_in_near,) = load(part, w_in)
     part = call(
         functools.partial(merge_kernel, seqs),
         "merge",
         shape(part.shape),
-        [part] + exchange(part, 0, n_ctx, n_exp),
-        [VM] * 4,
+        parts + [w_in_near],
+        [VM] * 4 + [ANY],
     )
     context, resid, outgoing = call(
         functools.partial(finish_kernel, seqs),
@@ -427,30 +459,31 @@
     rows = lax.all_to_all(
         outgoing.reshape(n_exp, per_source, slice_width), "exp", split_axis=0, concat_axis=0, tiled=True
     )
-    message = call(
+    side = 4
+    place = jnp.where(lax.axis_index("exp") & 1, first >> 2, first & 3)[None]
+    wide = 2 * hidden + 128
+    sent = call(
         functools.partial(gate_up_kernel, capacity),
         "gate_up",
-        shape((n_rows, 2 * hidden + 128)),
-        (rows.reshape(n_rows, slice_width), moe_gain[None], w_in),
-        [VM] * 3,
-    )
-    sums = lax.all_to_all(
-        message.reshape(n_ctx, n_rows // n_ctx, 2 * hidden + 128),
-        "ctx",
-        split_axis=0,
-        concat_axis=0,
-        tiled=True,
-    )
+        (shape((n_rows // side, wide)),) * side,
+        (place, rows.reshape(n_rows, slice_width), moe_gain[None], w_in_near),
+        [SM] + [VM] * 3,
+    )
+    got = [sent[0]] + exchange(sent[1:], 0, n_ctx, n_exp)
+    total = call(add_kernel, "add_rows", shape(got[0].shape), got, [VM] * 4)
     act = call(
-        activate_kernel, "activate", shape((n_ctx, n_rows // n_ctx, hidden)), (sums,), [VM]
-    )
-    act = lax.all_to_all(act, "ctx", split_axis=0, concat_axis=0, tiled=True)
+        activate_kernel,
+        "activate",
+        shape((n_rows // side, hidden)),
+        [total] + exchange(total, 1, n_ctx, n_exp),
+        [VM] * 4,
+    )
     expert_out = call(
         functools.partial(down_kernel, capacity),
         "down",
         shape((n_rows, slice_width)),
-        (act.reshape(n_rows, hidden), w_down),
-        [VM] * 2,
+        [place, act] + exchange(act, 0, n_ctx, n_exp) + [w_down],
+        [SM] + [VM] * 5,
     )
     returned = lax.all_to_all(
         expert_out.reshape(n_exp, per_source, slice_width), "exp", split_axis=0, concat_axis=0, tiled=True

time: 106 us -> 104 us (0.981)
  blocking collectives: 34.8 us -> 0 us
  starting transfers between devices: 24.7 us -> 49.9 us
  waiting for transfers between devices: 25.8 us -> 34.4 us
  local copies, waits for them, and re-layouts: 6.27 us -> 3.32 us
  Pallas kernels: 12.3 us -> 14 us
    all_to_all x2 -> x0, blocking collectives: 34.8 us -> none  [the longest x1 22.2 us: local(): lax.all_to_all(outgoing.reshape(n_exp, per_source, slice_width), 'exp', s...]
    all_to_all x1, starting transfers between devices: 3.52 us -> 15.7 us  [local(): lax.all_to_all(outgoing.reshape(n_exp, per_source, slice_width), 'exp', s...]
    ppermute x12 -> x21, starting transfers between devices: 15.4 us -> 27.2 us  [exchange(): got.append(lax.ppermute(sent, AXES, pairs))]
    ppermute x12 -> x21, waiting for transfers between devices: 11.1 us -> 19 us  [exchange(): got.append(lax.ppermute(sent, AXES, pairs))]
    unnamed x24 -> x16, local copies, waits for them, and re-layouts: 5.97 us -> 3.03 us
    pallas_call x10 -> x13, Pallas kernels: 12.3 us -> 14 us  [call(): pl.pallas_call(kernel, out_shape=out, in_specs=specs, out_specs=jax.tree....]
    all_to_all x1, starting transfers between devices: 5.77 us -> 6.95 us  [local(): lax.all_to_all(expert_out.reshape(n_exp, per_source, slice_width), 'exp',...]
  transfers between devices with their start and end apart: 14 -> 23, of which waited for: 8 -> 14; matrix products, arithmetic and copies ran while one was open for 1% -> 1% of each run, Pallas kernels for 0% -> 5%
where the time goes in v2:
time: 104 us
  starting transfers between devices  49.9 us (48%)
  waiting for transfers between devices  34.4 us (33%)
  Pallas kernels  14 us (13%)
  local copies, waits for them, and re-layouts  3.32 us (3%)
    ppermute x21, starting transfers between devices, exchange(): got.append(lax.ppermute(sent, AXES, pairs))  27.2 us
    ppermute x21, waiting for transfers between devices, exchange(): got.append(lax.ppermute(sent, AXES, pairs))  19 us
    all_to_all x1, starting transfers between devices, local(): lax.all_to_all(outgoing.reshape(n_exp, per_source, slice_width), 'exp', s...  15.7 us
    pallas_call x13, Pallas kernels, call(): pl.pallas_call(kernel, out_shape=out, in_specs=specs, out_specs=jax.tree....  14 us
    all_to_all x1, waiting for transfers between devices, local(): lax.all_to_all(outgoing.reshape(n_exp, per_source, slice_width), 'exp', s...  7.81 us
    all_to_all x1, waiting for transfers between devices, local(): lax.all_to_all(expert_out.reshape(n_exp, per_source, slice_width), 'exp',...  7.58 us
    all_to_all x1, starting transfers between devices, local(): lax.all_to_all(expert_out.reshape(n_exp, per_source, slice_width), 'exp',...  6.95 us
    unnamed x16, local copies, waits for them, and re-layouts  3.03 us
  transfers between devices with their start and end apart: 23, of which 14 were waited for; matrix products, arithmetic and copies ran while one was open for 1% of the time, Pallas kernels for 5%

profile of v2, /device:TPU:1, one launch (start us, length us, event | category | flops | bytes accessed | tf_op | source)
XLA Modules:
  0.0 103.7 jit_solution(3474906802331947225)
XLA Ops:
  0.7 3.1 %project.1.after.m0 = bf16[8,5248]{1,0:T(8,128)(2,1)S(1)} custom-call(bf16[8,256]{1,0:T(8,128)(2,1)} %tokens.1, f32[1,256]{1,0:T(1,128)} %bitcast.10, bf16[256,5120]{1,0:T(8,128)(2,1)} %w_hbm.1), custom_call_target="tpu_custom_call" | custom-call | tf_op jit(solution)/shard_map/project/pallas_call | solution.py:336
  3.8 2.2 %collective-permute-start = (bf16[8,5248]{1,0:T(8,128)(2,1)S(1)}, bf16[8,5248]{1,0:T(8,128)(2,1)S(1)}, u32[]{:S(2)}, u32[]{:S(2)}) collective-permute-start(bf16[8,5248]{1,0:T(8,128)(2,1)S(1)} %project.1.after.m0), channel_id=1, source_target_pairs={{0,16},{1,65},{2,18},{3,67},{4,20},{5,69},{6,22},{7,71},{8,24},{9,... | collective-permute-start | bytes 251912 | tf_op jit(solution)/shard_map/ppermute | solution.py:27
  6.0 2.6 %collective-permute-start.1 = (bf16[8,5248]{1,0:T(8,128)(2,1)S(1)}, bf16[8,5248]{1,0:T(8,128)(2,1)S(1)}, u32[]{:S(2)}, u32[]{:S(2)}) collective-permute-start(bf16[8,5248]{1,0:T(8,128)(2,1)S(1)} %project.1.after.m0), channel_id=1, source_target_pairs={{0,32},{1,129},{2,34},{3,131},{4,36},{5,133},{6,38},{7,135},{8,40}... | collective-permute-start | bytes 251912 | tf_op jit(solution)/shard_map/ppermute | solution.py:27
  8.6 0.0 collective-permute-start.2
  8.7 0.1 compare_convert_fusion.live_ref
  8.7 0.1 reshape.78
  8.8 0.1 fusion.2
  8.9 0.1 reduce_window_sum.11
  9.0 1.6 %load.3 = (bf16[8,128,512]{2,1,0:T(8,128)(2,1)S(1)}, bf16[8,128,512]{2,1,0:T(8,128)(2,1)S(1)}) custom-call(bf16[8,5248]{1,0:T(8,128)(2,1)S(1)} %project.1.after.m0, bf16[8,128,512]{2,1,0:T(8,128)(2,1)} %refs_0_.3, bf16[8,128,512]{2,1,0:T(8,128)(2,1)} %refs_1_.1), custom_call_target="tpu_custom_call" | custom-call | tf_op jit(solution)/shard_map/load/pallas_call | solution.py:336
  10.6 0.1 fusion.9
  10.7 0.2 select_reduce_fusion
  10.9 0.5 collective-permute-done.1.m2
  11.4 1.8 %collective-permute-done.2.m3 = bf16[8,5248]{1,0:T(8,128)(2,1)S(1)} collective-permute-done((bf16[8,5248]{1,0:T(8,128)(2,1)S(1)}, bf16[8,5248]{1,0:T(8,128)(2,1)S(1)}, u32[]{:S(2)}, u32[]{:S(2)}) %collective-permute-start.2) | collective-permute-done | bytes 84000 | tf_op jit(solution)/shard_map/ppermute | solution.py:27
  13.1 0.1 add.32.after.m0
  13.3 1.3 %collective-permute-start.3 = (bf16[8,5248]{1,0:T(8,128)(2,1)S(1)}, bf16[8,5248]{1,0:T(8,128)(2,1)S(1)}, u32[]{:S(2)}, u32[]{:S(2)}) collective-permute-start(bf16[8,5248]{1,0:T(8,128)(2,1)S(1)} %add.32.after.m0), channel_id=1, source_target_pairs={{0,64},{1,17},{2,66},{3,19},{4,68},{5,21},{6,70},{7,23},{8,72},{9,... | collective-permute-start | bytes 251912 | tf_op jit(solution)/shard_map/ppermute | solution.py:27
  14.6 2.7 %collective-permute-start.4 = (bf16[8,5248]{1,0:T(8,128)(2,1)S(1)}, bf16[8,5248]{1,0:T(8,128)(2,1)S(1)}, u32[]{:S(2)}, u32[]{:S(2)}) collective-permute-start(bf16[8,5248]{1,0:T(8,128)(2,1)S(1)} %add.32.after.m0), channel_id=1, source_target_pairs={{0,128},{1,33},{2,130},{3,35},{4,132},{5,37},{6,134},{7,39},{8,136... | collective-permute-start | bytes 251912 | tf_op jit(solution)/shard_map/ppermute | solution.py:27
  17.3 0.1 pad_maximum_fusion
  17.4 1.6 %load.4.after.w_ref = bf16[4096,256]{1,0:T(8,128)(2,1)S(1)} custom-call(bf16[8,5248]{1,0:T(8,128)(2,1)S(1)} %add.32.after.m0, bf16[4096,256]{1,0:T(8,128)(2,1)} %refs_0_.4), custom_call_target="tpu_custom_call" | custom-call | tf_op jit(solution)/shard_map/load/pallas_call | solution.py:336
  19.0 1.0 %collective-permute-done.4.m2 = bf16[8,5248]{1,0:T(8,128)(2,1)S(1)} collective-permute-done((bf16[8,5248]{1,0:T(8,128)(2,1)S(1)}, bf16[8,5248]{1,0:T(8,128)(2,1)S(1)}, u32[]{:S(2)}, u32[]{:S(2)}) %collective-permute-start.4) | collective-permute-done | bytes 84000 | tf_op jit(solution)/shard_map/ppermute | solution.py:27
  20.1 2.1 %collective-permute-done.5.m3 = bf16[8,5248]{1,0:T(8,128)(2,1)S(1)} collective-permute-done((bf16[8,5248]{1,0:T(8,128)(2,1)S(1)}, bf16[8,5248]{1,0:T(8,128)(2,1)S(1)}, u32[]{:S(2)}, u32[]{:S(2)}) %collective-permute-start.5) | collective-permute-done | bytes 84000 | tf_op jit(solution)/shard_map/ppermute | solution.py:27
  22.1 1.1 %attend.1.after.p0 = bf16[288,128]{1,0:T(8,128)(2,1)S(1)} custom-call(bf16[8,5248]{1,0:T(8,128)(2,1)S(1)} %add.32.after.m0, bf16[8,5248]{1,0:T(8,128)(2,1)S(1)} %collective-permute-done.3.m1, bf16[8,5248]{1,0:T(8,128)(2,1)S(1)} %collective-permute-done.4.m2, bf16[8,5248]{1,0:T(8,128)(2,1)S(1)} %collective-permute-done.5.m3, ...), custom_call_target="tpu_custom_call" | custom-call | tf_op jit(solution)/shard_map/attend/pallas_call | solution.py:336
  23.2 0.1 collective-permute-start.6
  23.3 1.3 %collective-permute-start.7 = (bf16[288,128]{1,0:T(8,128)(2,1)S(1)}, bf16[288,128]{1,0:T(8,128)(2,1)S(1)}, u32[]{:S(2)}, u32[]{:S(2)}) collective-permute-start(bf16[288,128]{1,0:T(8,128)(2,1)S(1)} %attend.1.after.p0), channel_id=1, source_target_pairs={{0,32},{1,129},{2,34},{3,131},{4,36},{5,133},{6,38},{7,135},{8,40}... | collective-permute-start | bytes 221192 | tf_op jit(solution)/shard_map/ppermute | solution.py:27
  24.7 2.5 %collective-permute-start.8 = (bf16[288,128]{1,0:T(8,128)(2,1)S(1)}, bf16[288,128]{1,0:T(8,128)(2,1)S(1)}, u32[]{:S(2)}, u32[]{:S(2)}) collective-permute-start(bf16[288,128]{1,0:T(8,128)(2,1)S(1)} %attend.1.after.p0), channel_id=1, source_target_pairs={{0,48},{1,193},{2,50},{3,195},{4,52},{5,197},{6,54},{7,199},{8,56}... | collective-permute-start | bytes 221192 | tf_op jit(solution)/shard_map/ppermute | solution.py:27
  27.2 1.9 %load.5.after.w_ref = bf16[4,256,1536]{2,1,0:T(8,128)(2,1)S(1)} custom-call(bf16[288,128]{1,0:T(8,128)(2,1)S(1)} %attend.1.after.p0, bf16[4,256,1536]{2,1,0:T(8,128)(2,1)} %refs_0_.5), custom_call_target="tpu_custom_call" | custom-call | tf_op jit(solution)/shard_map/load/pallas_call | solution.py:336
  29.1 0.0 copy-start.3
  29.1 0.0 copy-start.4
  29.1 0.3 merge.1.p0
  29.5 0.4 collective-permute-start.10
  29.8 0.9 collective-permute-start.11
  30.7 1.5 %collective-permute-start.9 = (bf16[288,128]{1,0:T(8,128)(2,1)S(1)}, bf16[288,128]{1,0:T(8,128)(2,1)S(1)}, u32[]{:S(2)}, u32[]{:S(2)}) collective-permute-start(bf16[288,128]{1,0:T(8,128)(2,1)S(1)} %merge.1.p0), channel_id=1, source_target_pairs={{0,64},{1,17},{2,66},{3,19},{4,68},{5,21},{6,70},{7,23},{8,72},{9,... | collective-permute-start | bytes 221192 | tf_op jit(solution)/shard_map/ppermute | solution.py:27
  32.2 0.2 convolution_convert_fusion
  32.4 0.1 copy.15
  32.6 1.8 %collective-permute-done.10.p2 = bf16[288,128]{1,0:T(8,128)(2,1)S(1)} collective-permute-done((bf16[288,128]{1,0:T(8,128)(2,1)S(1)}, bf16[288,128]{1,0:T(8,128)(2,1)S(1)}, u32[]{:S(2)}, u32[]{:S(2)}) %collective-permute-start.10) | collective-permute-done | bytes 73760 | tf_op jit(solution)/shard_map/ppermute | solution.py:27
  34.4 0.9 collective-permute-done.11.p3
  35.3 1.6 %copy-done.1 = bf16[4096,256]{1,0:T(8,128)(2,1)S(1)} copy-done((bf16[4096,256]{1,0:T(8,128)(2,1)S(1)}, bf16[4096,256]{1,0:T(8,128)(2,1)}, u32[]{:S(2)}) %copy-start.1) | copy-done | bytes 2097176
  36.9 1.6 %finish.1 = (bf16[8,4096]{1,0:T(8,128)(2,1)}, bf16[8,256]{1,0:T(8,128)(2,1)S(1)}, bf16[128,256]{1,0:T(8,128)(2,1)}) custom-call(bf16[288,128]{1,0:T(8,128)(2,1)S(1)} %merge.1.p0, bf16[288,128]{1,0:T(8,128)(2,1)S(1)} %collective-permute-done.9.p1, bf16[288,128]{1,0:T(8,128)(2,1)S(1)} %collective-permute-done.10.p2, ...), custom_call_target="tpu_custom_call" | custom-call | tf_op jit(solution)/shard_map/finish/pallas_call | solution.py:336
  38.4 15.7 %all-to-all-start = ((bf16[16,8,256]{2,1,0:T(8,128)(2,1)}), bf16[16,8,256]{2,1,0:T(8,128)(2,1)S(1)}, u32[]{:S(2)}, u32[]{:S(2)}) async-start(bf16[16,8,256]{2,1,0:T(8,128)(2,1)} %bitcast.2), calls=%async_computation | async-start | bytes 131072 | tf_op jit(solution)/shard_map/all_to_all | solution.py:459
  54.2 7.8 %all-to-all-done = bf16[16,8,256]{2,1,0:T(8,128)(2,1)S(1)} async-done(((bf16[16,8,256]{2,1,0:T(8,128)(2,1)}), bf16[16,8,256]{2,1,0:T(8,128)(2,1)S(1)}, u32[]{:S(2)}, u32[]{:S(2)}) %all-to-all-start) | async-done | bytes 65568 | tf_op jit(solution)/shard_map/all_to_all | solution.py:459
  62.0 0.6 gate_up.1
  62.6 1.2 %collective-permute-start.12 = (bf16[32,1664]{1,0:T(8,128)(2,1)S(1)}, bf16[32,1664]{1,0:T(8,128)(2,1)S(1)}, u32[]{:S(2)}, u32[]{:S(2)}) collective-permute-start(bf16[32,1664]{1,0:T(8,128)(2,1)S(1)} %get-tuple-element.17), channel_id=1, source_target_pairs={{0,16},{1,65},{2,18},{3,67},{4,20},{5,69},{6,22},{7,71},{8,24},{9,... | collective-permute-start | bytes 319496 | tf_op jit(solution)/shard_map/ppermute | solution.py:27
  63.8 1.0 collective-permute-start.13
  64.8 1.7 %collective-permute-start.14 = (bf16[32,1664]{1,0:T(8,128)(2,1)S(1)}, bf16[32,1664]{1,0:T(8,128)(2,1)S(1)}, u32[]{:S(2)}, u32[]{:S(2)}) collective-permute-start(bf16[32,1664]{1,0:T(8,128)(2,1)S(1)} %get-tuple-element.19), channel_id=1, source_target_pairs={{0,48},{1,193},{2,50},{3,195},{4,52},{5,197},{6,54},{7,199},{8,56}... | collective-permute-start | bytes 319496 | tf_op jit(solution)/shard_map/ppermute | solution.py:27
  66.5 2.6 %collective-permute-done.13.m2 = bf16[32,1664]{1,0:T(8,128)(2,1)S(1)} collective-permute-done((bf16[32,1664]{1,0:T(8,128)(2,1)S(1)}, bf16[32,1664]{1,0:T(8,128)(2,1)S(1)}, u32[]{:S(2)}, u32[]{:S(2)}) %collective-permute-start.13) | collective-permute-done | bytes 106528 | tf_op jit(solution)/shard_map/ppermute | solution.py:27
  69.1 1.0 collective-permute-done.14.m3
  70.1 0.2 add_rows.1.m0
  70.3 0.0 collective-permute-start.15
  70.3 3.7 %collective-permute-start.16 = (bf16[32,1664]{1,0:T(8,128)(2,1)S(1)}, bf16[32,1664]{1,0:T(8,128)(2,1)S(1)}, u32[]{:S(2)}, u32[]{:S(2)}) collective-permute-start(bf16[32,1664]{1,0:T(8,128)(2,1)S(1)} %add_rows.1.m0), channel_id=1, source_target_pairs={{0,128},{1,33},{2,130},{3,35},{4,132},{5,37},{6,134},{7,39},{8,136... | collective-permute-start | bytes 319496 | tf_op jit(solution)/shard_map/ppermute | solution.py:27
  74.0 0.2 collective-permute-start.17
  74.2 3.1 %collective-permute-done.16.m2 = bf16[32,1664]{1,0:T(8,128)(2,1)S(1)} collective-permute-done((bf16[32,1664]{1,0:T(8,128)(2,1)S(1)}, bf16[32,1664]{1,0:T(8,128)(2,1)S(1)}, u32[]{:S(2)}, u32[]{:S(2)}) %collective-permute-start.16) | collective-permute-done | bytes 106528 | tf_op jit(solution)/shard_map/ppermute | solution.py:27
  77.3 1.8 %collective-permute-done.17.m3 = bf16[32,1664]{1,0:T(8,128)(2,1)S(1)} collective-permute-done((bf16[32,1664]{1,0:T(8,128)(2,1)S(1)}, bf16[32,1664]{1,0:T(8,128)(2,1)S(1)}, u32[]{:S(2)}, u32[]{:S(2)}) %collective-permute-start.17) | collective-permute-done | bytes 106528 | tf_op jit(solution)/shard_map/ppermute | solution.py:27
  79.1 0.2 activate.1.x0
  79.3 0.1 collective-permute-start.18
  79.4 2.2 %collective-permute-start.19 = (bf16[32,768]{1,0:T(8,128)(2,1)S(1)}, bf16[32,768]{1,0:T(8,128)(2,1)S(1)}, u32[]{:S(2)}, u32[]{:S(2)}) collective-permute-start(bf16[32,768]{1,0:T(8,128)(2,1)S(1)} %activate.1.x0), channel_id=1, source_target_pairs={{0,32},{1,129},{2,34},{3,131},{4,36},{5,133},{6,38},{7,135},{8,40}... | collective-permute-start | bytes 147464 | tf_op jit(solution)/shard_map/ppermute | solution.py:27
  81.6 1.6 %collective-permute-start.20 = (bf16[32,768]{1,0:T(8,128)(2,1)S(1)}, bf16[32,768]{1,0:T(8,128)(2,1)S(1)}, u32[]{:S(2)}, u32[]{:S(2)}) collective-permute-start(bf16[32,768]{1,0:T(8,128)(2,1)S(1)} %activate.1.x0), channel_id=1, source_target_pairs={{0,48},{1,193},{2,50},{3,195},{4,52},{5,197},{6,54},{7,199},{8,56}... | collective-permute-start | bytes 147464 | tf_op jit(solution)/shard_map/ppermute | solution.py:27
  83.2 0.1 mul.49
  83.3 0.6 collective-permute-done.19.x2
  83.9 1.9 %collective-permute-done.20.x3 = bf16[32,768]{1,0:T(8,128)(2,1)S(1)} collective-permute-done((bf16[32,768]{1,0:T(8,128)(2,1)S(1)}, bf16[32,768]{1,0:T(8,128)(2,1)S(1)}, u32[]{:S(2)}, u32[]{:S(2)}) %collective-permute-start.20) | collective-permute-done | bytes 49184 | tf_op jit(solution)/shard_map/ppermute | solution.py:27
  85.8 1.4 %copy-done.2 = bf16[4,768,256]{2,1,0:T(8,128)(2,1)S(1)} copy-done((bf16[4,768,256]{2,1,0:T(8,128)(2,1)S(1)}, bf16[4,768,256]{2,1,0:T(8,128)(2,1)}, u32[]{:S(2)}) %copy-start.2) | copy-done | bytes 1572888
  87.2 1.0 down.1
  88.2 6.9 %all-to-all-start.1 = ((bf16[16,8,256]{2,1,0:T(8,128)(2,1)}), bf16[16,8,256]{2,1,0:T(8,128)(2,1)S(1)}, u32[]{:S(2)}, u32[]{:S(2)}) async-start(bf16[16,8,256]{2,1,0:T(8,128)(2,1)} %bitcast.5), calls=%async_computation.1 | async-start | bytes 131072 | tf_op jit(solution)/shard_map/all_to_all | solution.py:488
  95.1 0.3 fusion.weighting
  95.4 7.6 %all-to-all-done.1 = bf16[16,8,256]{2,1,0:T(8,128)(2,1)S(1)} async-done(((bf16[16,8,256]{2,1,0:T(8,128)(2,1)}), bf16[16,8,256]{2,1,0:T(8,128)(2,1)S(1)}, u32[]{:S(2)}, u32[]{:S(2)}) %all-to-all-start.1) | async-done | bytes 65568 | tf_op jit(solution)/shard_map/all_to_all | solution.py:488
  103.0 0.7 combine.1
  (28 shorter events, 0.1 us)
Async XLA Ops:
  0.6 8.0 %copy-start.7 = (s32[8]{0:T(128)S(1)}, s32[8]{0:T(128)}, u32[]{:S(2)}) copy-start(s32[8]{0:T(128)} %param.18) | copy-start | bytes 100
  0.6 8.1 %copy-start.5 = (s32[8,8]{1,0:T(8,128)S(1)}, s32[8,8]{1,0:T(8,128)}, u32[]{:S(2)}) copy-start(s32[8,8]{1,0:T(8,128)} %param.20) | copy-start | bytes 772
  3.8 7.1 %collective-permute-start = (bf16[8,5248]{1,0:T(8,128)(2,1)S(1)}, bf16[8,5248]{1,0:T(8,128)(2,1)S(1)}, u32[]{:S(2)}, u32[]{:S(2)}) collective-permute-start(bf16[8,5248]{1,0:T(8,128)(2,1)S(1)} %project.1.after.m0), channel_id=1, source_target_pairs={{0,16},{1,65},{2,18},{3,67},{4,20},{5,69},{6,22},{7,71},{8,24},{9,... | collective-permute-start | bytes 251912 | tf_op jit(solution)/shard_map/ppermute | solution.py:27
  6.0 5.4 %collective-permute-start.1 = (bf16[8,5248]{1,0:T(8,128)(2,1)S(1)}, bf16[8,5248]{1,0:T(8,128)(2,1)S(1)}, u32[]{:S(2)}, u32[]{:S(2)}) collective-permute-start(bf16[8,5248]{1,0:T(8,128)(2,1)S(1)} %project.1.after.m0), channel_id=1, source_target_pairs={{0,32},{1,129},{2,34},{3,131},{4,36},{5,133},{6,38},{7,135},{8,40}... | collective-permute-start | bytes 251912 | tf_op jit(solution)/shard_map/ppermute | solution.py:27
  8.6 4.5 %collective-permute-start.2 = (bf16[8,5248]{1,0:T(8,128)(2,1)S(1)}, bf16[8,5248]{1,0:T(8,128)(2,1)S(1)}, u32[]{:S(2)}, u32[]{:S(2)}) collective-permute-start(bf16[8,5248]{1,0:T(8,128)(2,1)S(1)} %project.1.after.m0), channel_id=1, source_target_pairs={{0,48},{1,193},{2,50},{3,195},{4,52},{5,197},{6,54},{7,199},{8,56}... | collective-permute-start | bytes 251912 | tf_op jit(solution)/shard_map/ppermute | solution.py:27
  13.3 5.7 %collective-permute-start.3 = (bf16[8,5248]{1,0:T(8,128)(2,1)S(1)}, bf16[8,5248]{1,0:T(8,128)(2,1)S(1)}, u32[]{:S(2)}, u32[]{:S(2)}) collective-permute-start(bf16[8,5248]{1,0:T(8,128)(2,1)S(1)} %add.32.after.m0), channel_id=1, source_target_pairs={{0,64},{1,17},{2,66},{3,19},{4,68},{5,21},{6,70},{7,23},{8,72},{9,... | collective-permute-start | bytes 251912 | tf_op jit(solution)/shard_map/ppermute | solution.py:27
  14.6 5.4 %collective-permute-start.4 = (bf16[8,5248]{1,0:T(8,128)(2,1)S(1)}, bf16[8,5248]{1,0:T(8,128)(2,1)S(1)}, u32[]{:S(2)}, u32[]{:S(2)}) collective-permute-start(bf16[8,5248]{1,0:T(8,128)(2,1)S(1)} %add.32.after.m0), channel_id=1, source_target_pairs={{0,128},{1,33},{2,130},{3,35},{4,132},{5,37},{6,134},{7,39},{8,136... | collective-permute-start | bytes 251912 | tf_op jit(solution)/shard_map/ppermute | solution.py:27
  17.3 4.8 %collective-permute-start.5 = (bf16[8,5248]{1,0:T(8,128)(2,1)S(1)}, bf16[8,5248]{1,0:T(8,128)(2,1)S(1)}, u32[]{:S(2)}, u32[]{:S(2)}) collective-permute-start(bf16[8,5248]{1,0:T(8,128)(2,1)S(1)} %add.32.after.m0), channel_id=1, source_target_pairs={{0,192},{1,49},{2,194},{3,51},{4,196},{5,53},{6,198},{7,55},{8,200... | collective-permute-start | bytes 251912 | tf_op jit(solution)/shard_map/ppermute | solution.py:27
  19.0 10.1 %copy-start = (bf16[4096,256]{1,0:T(8,128)(2,1)}, bf16[4096,256]{1,0:T(8,128)(2,1)S(1)}, u32[]{:S(2)}) copy-start(bf16[4096,256]{1,0:T(8,128)(2,1)S(1)} %load.4.after.w_ref) | copy-start | bytes 6291460
  23.2 5.9 %collective-permute-start.6 = (bf16[288,128]{1,0:T(8,128)(2,1)S(1)}, bf16[288,128]{1,0:T(8,128)(2,1)S(1)}, u32[]{:S(2)}, u32[]{:S(2)}) collective-permute-start(bf16[288,128]{1,0:T(8,128)(2,1)S(1)} %attend.1.after.p0), channel_id=1, source_target_pairs={{0,16},{1,65},{2,18},{3,67},{4,20},{5,69},{6,22},{7,71},{8,24},{9,... | collective-permute-start | bytes 221192 | tf_op jit(solution)/shard_map/ppermute | solution.py:27
  23.3 5.8 %collective-permute-start.7 = (bf16[288,128]{1,0:T(8,128)(2,1)S(1)}, bf16[288,128]{1,0:T(8,128)(2,1)S(1)}, u32[]{:S(2)}, u32[]{:S(2)}) collective-permute-start(bf16[288,128]{1,0:T(8,128)(2,1)S(1)} %attend.1.after.p0), channel_id=1, source_target_pairs={{0,32},{1,129},{2,34},{3,131},{4,36},{5,133},{6,38},{7,135},{8,40}... | collective-permute-start | bytes 221192 | tf_op jit(solution)/shard_map/ppermute | solution.py:27
  24.7 4.5 %collective-permute-start.8 = (bf16[288,128]{1,0:T(8,128)(2,1)S(1)}, bf16[288,128]{1,0:T(8,128)(2,1)S(1)}, u32[]{:S(2)}, u32[]{:S(2)}) collective-permute-start(bf16[288,128]{1,0:T(8,128)(2,1)S(1)} %attend.1.after.p0), channel_id=1, source_target_pairs={{0,48},{1,193},{2,50},{3,195},{4,52},{5,197},{6,54},{7,199},{8,56}... | collective-permute-start | bytes 221192 | tf_op jit(solution)/shard_map/ppermute | solution.py:27
  29.1 6.2 %copy-start.3 = (bf16[8,256]{1,0:T(8,128)(2,1)S(1)}, bf16[8,256]{1,0:T(8,128)(2,1)}, u32[]{:S(2)}) copy-start(bf16[8,256]{1,0:T(8,128)(2,1)} %tokens.1) | copy-start | bytes 12292
  29.1 32.9 %copy-start.4 = (f32[256]{0:T(256)S(1)}, f32[256]{0:T(256)}, u32[]{:S(2)}) copy-start(f32[256]{0:T(256)} %param.19) | copy-start | bytes 3076
  29.5 4.9 %collective-permute-start.10 = (bf16[288,128]{1,0:T(8,128)(2,1)S(1)}, bf16[288,128]{1,0:T(8,128)(2,1)S(1)}, u32[]{:S(2)}, u32[]{:S(2)}) collective-permute-start(bf16[288,128]{1,0:T(8,128)(2,1)S(1)} %merge.1.p0), channel_id=1, source_target_pairs={{0,128},{1,33},{2,130},{3,35},{4,132},{5,37},{6,134},{7,39},{8,136... | collective-permute-start | bytes 221192 | tf_op jit(solution)/shard_map/ppermute | solution.py:27
  29.8 5.4 %collective-permute-start.11 = (bf16[288,128]{1,0:T(8,128)(2,1)S(1)}, bf16[288,128]{1,0:T(8,128)(2,1)S(1)}, u32[]{:S(2)}, u32[]{:S(2)}) collective-permute-start(bf16[288,128]{1,0:T(8,128)(2,1)S(1)} %merge.1.p0), channel_id=1, source_target_pairs={{0,192},{1,49},{2,194},{3,51},{4,196},{5,53},{6,198},{7,55},{8,200... | collective-permute-start | bytes 221192 | tf_op jit(solution)/shard_map/ppermute | solution.py:27
  30.7 4.6 %collective-permute-start.9 = (bf16[288,128]{1,0:T(8,128)(2,1)S(1)}, bf16[288,128]{1,0:T(8,128)(2,1)S(1)}, u32[]{:S(2)}, u32[]{:S(2)}) collective-permute-start(bf16[288,128]{1,0:T(8,128)(2,1)S(1)} %merge.1.p0), channel_id=1, source_target_pairs={{0,64},{1,17},{2,66},{3,19},{4,68},{5,21},{6,70},{7,23},{8,72},{9,... | collective-permute-start | bytes 221192 | tf_op jit(solution)/shard_map/ppermute | solution.py:27
  35.3 1.6 %copy-start.1 = (bf16[4096,256]{1,0:T(8,128)(2,1)S(1)}, bf16[4096,256]{1,0:T(8,128)(2,1)}, u32[]{:S(2)}) copy-start(bf16[4096,256]{1,0:T(8,128)(2,1)} %copy-done) | copy-start | bytes 6291460
  38.4 44.8 %copy-start.6 = (f32[8,8]{1,0:T(8,128)S(1)}, f32[8,8]{1,0:T(8,128)}, u32[]{:S(2)}) copy-start(f32[8,8]{1,0:T(8,128)} %param.21) | copy-start | bytes 772
  38.4 23.5 %all-to-all-start = ((bf16[16,8,256]{2,1,0:T(8,128)(2,1)}), bf16[16,8,256]{2,1,0:T(8,128)(2,1)S(1)}, u32[]{:S(2)}, u32[]{:S(2)}) async-start(bf16[16,8,256]{2,1,0:T(8,128)(2,1)} %bitcast.2), calls=%async_computation | async-start | bytes 131072 | tf_op jit(solution)/shard_map/all_to_all | solution.py:459
  62.6 3.9 %collective-permute-start.12 = (bf16[32,1664]{1,0:T(8,128)(2,1)S(1)}, bf16[32,1664]{1,0:T(8,128)(2,1)S(1)}, u32[]{:S(2)}, u32[]{:S(2)}) collective-permute-start(bf16[32,1664]{1,0:T(8,128)(2,1)S(1)} %get-tuple-element.17), channel_id=1, source_target_pairs={{0,16},{1,65},{2,18},{3,67},{4,20},{5,69},{6,22},{7,71},{8,24},{9,... | collective-permute-start | bytes 319496 | tf_op jit(solution)/shard_map/ppermute | solution.py:27
  63.8 5.4 %collective-permute-start.13 = (bf16[32,1664]{1,0:T(8,128)(2,1)S(1)}, bf16[32,1664]{1,0:T(8,128)(2,1)S(1)}, u32[]{:S(2)}, u32[]{:S(2)}) collective-permute-start(bf16[32,1664]{1,0:T(8,128)(2,1)S(1)} %get-tuple-element.18), channel_id=1, source_target_pairs={{0,32},{1,129},{2,34},{3,131},{4,36},{5,133},{6,38},{7,135},{8,40}... | collective-permute-start | bytes 319496 | tf_op jit(solution)/shard_map/ppermute | solution.py:27
  64.8 5.3 %collective-permute-start.14 = (bf16[32,1664]{1,0:T(8,128)(2,1)S(1)}, bf16[32,1664]{1,0:T(8,128)(2,1)S(1)}, u32[]{:S(2)}, u32[]{:S(2)}) collective-permute-start(bf16[32,1664]{1,0:T(8,128)(2,1)S(1)} %get-tuple-element.19), channel_id=1, source_target_pairs={{0,48},{1,193},{2,50},{3,195},{4,52},{5,197},{6,54},{7,199},{8,56}... | collective-permute-start | bytes 319496 | tf_op jit(solution)/shard_map/ppermute | solution.py:27
  70.3 3.9 %collective-permute-start.15 = (bf16[32,1664]{1,0:T(8,128)(2,1)S(1)}, bf16[32,1664]{1,0:T(8,128)(2,1)S(1)}, u32[]{:S(2)}, u32[]{:S(2)}) collective-permute-start(bf16[32,1664]{1,0:T(8,128)(2,1)S(1)} %add_rows.1.m0), channel_id=1, source_target_pairs={{0,64},{1,17},{2,66},{3,19},{4,68},{5,21},{6,70},{7,23},{8,72},{9,... | collective-permute-start | bytes 319496 | tf_op jit(solution)/shard_map/ppermute | solution.py:27
  70.3 6.9 %collective-permute-start.16 = (bf16[32,1664]{1,0:T(8,128)(2,1)S(1)}, bf16[32,1664]{1,0:T(8,128)(2,1)S(1)}, u32[]{:S(2)}, u32[]{:S(2)}) collective-permute-start(bf16[32,1664]{1,0:T(8,128)(2,1)S(1)} %add_rows.1.m0), channel_id=1, source_target_pairs={{0,128},{1,33},{2,130},{3,35},{4,132},{5,37},{6,134},{7,39},{8,136... | collective-permute-start | bytes 319496 | tf_op jit(solution)/shard_map/ppermute | solution.py:27
  74.0 5.1 %collective-permute-start.17 = (bf16[32,1664]{1,0:T(8,128)(2,1)S(1)}, bf16[32,1664]{1,0:T(8,128)(2,1)S(1)}, u32[]{:S(2)}, u32[]{:S(2)}) collective-permute-start(bf16[32,1664]{1,0:T(8,128)(2,1)S(1)} %add_rows.1.m0), channel_id=1, source_target_pairs={{0,192},{1,49},{2,194},{3,51},{4,196},{5,53},{6,198},{7,55},{8,200... | collective-permute-start | bytes 319496 | tf_op jit(solution)/shard_map/ppermute | solution.py:27
  79.3 4.0 %collective-permute-start.18 = (bf16[32,768]{1,0:T(8,128)(2,1)S(1)}, bf16[32,768]{1,0:T(8,128)(2,1)S(1)}, u32[]{:S(2)}, u32[]{:S(2)}) collective-permute-start(bf16[32,768]{1,0:T(8,128)(2,1)S(1)} %activate.1.x0), channel_id=1, source_target_pairs={{0,16},{1,65},{2,18},{3,67},{4,20},{5,69},{6,22},{7,71},{8,24},{9,... | collective-permute-start | bytes 147464 | tf_op jit(solution)/shard_map/ppermute | solution.py:27
  79.4 4.5 %collective-permute-start.19 = (bf16[32,768]{1,0:T(8,128)(2,1)S(1)}, bf16[32,768]{1,0:T(8,128)(2,1)S(1)}, u32[]{:S(2)}, u32[]{:S(2)}) collective-permute-start(bf16[32,768]{1,0:T(8,128)(2,1)S(1)} %activate.1.x0), channel_id=1, source_target_pairs={{0,32},{1,129},{2,34},{3,131},{4,36},{5,133},{6,38},{7,135},{8,40}... | collective-permute-start | bytes 147464 | tf_op jit(solution)/shard_map/ppermute | solution.py:27
  81.6 4.2 %collective-permute-start.20 = (bf16[32,768]{1,0:T(8,128)(2,1)S(1)}, bf16[32,768]{1,0:T(8,128)(2,1)S(1)}, u32[]{:S(2)}, u32[]{:S(2)}) collective-permute-start(bf16[32,768]{1,0:T(8,128)(2,1)S(1)} %activate.1.x0), channel_id=1, source_target_pairs={{0,48},{1,193},{2,50},{3,195},{4,52},{5,197},{6,54},{7,199},{8,56}... | collective-permute-start | bytes 147464 | tf_op jit(solution)/shard_map/ppermute | solution.py:27
  85.8 1.4 %copy-start.2 = (bf16[4,768,256]{2,1,0:T(8,128)(2,1)S(1)}, bf16[4,768,256]{2,1,0:T(8,128)(2,1)}, u32[]{:S(2)}) copy-start(bf16[4,768,256]{2,1,0:T(8,128)(2,1)} %w_ref.1) | copy-start | bytes 4718596
  88.2 14.8 %all-to-all-start.1 = ((bf16[16,8,256]{2,1,0:T(8,128)(2,1)}), bf16[16,8,256]{2,1,0:T(8,128)(2,1)S(1)}, u32[]{:S(2)}, u32[]{:S(2)}) async-start(bf16[16,8,256]{2,1,0:T(8,128)(2,1)} %bitcast.5), calls=%async_computation.1 | async-start | bytes 131072 | tf_op jit(solution)/shard_map/all_to_all | solution.py:488

commit v3 on v2

--- a/solution.py
+++ b/solution.py
@@ -59,6 +59,42 @@
     high = value.astype(jnp.bfloat16).astype(jnp.float32)
     lane = lax.broadcasted_iota(jnp.int32, (value.shape[0], 128), 1)
     return jnp.where(lane < 64, high, value - high).astype(jnp.bfloat16)
+
+
+def prepare_kernel(lengths, routes, gates, after, live, owns, placing, weighting):
+    f32 = jnp.float32
+    seqs, top_k = routes.shape
+    lane = lax.broadcasted_iota(jnp.int32, (seqs, 128), 1)
+    row = lax.broadcasted_iota(jnp.int32, (seqs, 128), 0)
+    first = lax.axis_index("ctx")
+    limits = jnp.zeros((seqs, 128), jnp.int32)
+    for b in range(seqs):
+        limits = jnp.where(row == b, lengths[b], limits)
+    live[...] = jnp.where(lane + first * 128 < limits, 1.0, 0.0)
+    owns[...] = jnp.where(lane * 0 + first == 0, 1.0, 0.0)
+    named = jnp.zeros((seqs, 128), f32)
+    weights = jnp.zeros((seqs, 128), f32)
+    for k in range(top_k):
+        hit = jnp.broadcast_to(routes[:, k : k + 1], (seqs, 128)) == lane // 2
+        named += jnp.where(hit, 1.0, 0.0)
+        weights += jnp.where(hit, jnp.broadcast_to(gates[:, k : k + 1], (seqs, 128)), 0.0)
+    earlier = jnp.zeros((1, 128), f32)
+    ranks = []
+    for b in range(seqs):
+        ranks.append(earlier)
+        earlier = earlier + named[b : b + 1]
+    rank = jnp.concatenate(ranks, 0)
+    chosen = (named > 0.5) & (jnp.abs(rank - (lane % 2).astype(f32)) < 0.5)
+    weighting[...] = jnp.where(chosen, weights, 0.0)
+    square = jnp.concatenate(
+        [jnp.where(chosen, 1.0, 0.0), jnp.zeros((128 - seqs, 128), f32)], 0
+    )
+    placing[...] = square.T.astype(jnp.bfloat16)
+
+
+def line_place():
+    first = lax.axis_index("ctx")
+    return jnp.where(lax.axis_index("exp") % 2 == 1, first // 4, first % 4)
 
 
 def project_kernel(tokens_hbm, gain_hbm, w_hbm, out, tokens, gain, w_ref, small, sems):
@@ -245,14 +281,15 @@
     return lax.rem(row, per_source) // capacity == j
 
 
-def gate_up_kernel(capacity, place, x_ref, gain, w_ref, *outs):
+def gate_up_kernel(capacity, x_ref, gain, w_ref, *outs):
     f32, bf16 = jnp.float32, jnp.bfloat16
     n_rows, width = x_ref.shape
     experts, _, cols = w_ref.shape
     part = n_rows // len(outs)
+    place = line_place()
     xf = jnp.concatenate(
         [
-            x_ref[pl.ds(pl.multiple_of((place[0] ^ s) * part, part), part), :]
+            x_ref[pl.ds(pl.multiple_of((place ^ s) * part, part), part), :]
             for s in range(len(outs))
         ],
         0,
@@ -290,7 +327,7 @@
     out[...] = (gate / (1.0 + jnp.exp(-gate)) * up).astype(bf16)
 
 
-def down_kernel(capacity, place, x0, x1, x2, x3, w_ref, out):
+def down_kernel(capacity, x0, x1, x2, x3, w_ref, out):
     f32 = jnp.float32
     xf = jnp.concatenate([x[...].astype(f32) for x in (x0, x1, x2, x3)], 0)
     n_rows, width = xf.shape
@@ -303,8 +340,9 @@
         share = jnp.dot(block, w_ref[j], preferred_element_type=f32)
         total = share if total is None else total + share
     total = total.astype(jnp.bfloat16)
+    place = line_place()
     for s in range(4):
-        at = pl.ds(pl.multiple_of((place[0] ^ s) * part, part), part)
+        at = pl.ds(pl.multiple_of((place ^ s) * part, part), part)
         out[at, :] = total[s * part : (s + 1) * part]
 
 
@@ -344,14 +382,18 @@
     )(*inputs)
 
 
+def near(array):
+    return pltpu.with_memory_space_constraint(array, pltpu.VMEM)
+
+
 def load(after, *arrays):
     kept = [pltpu.with_memory_space_constraint(a, pltpu.HBM) for a in arrays]
     return call(
         load_kernel,
         "load",
         tuple(pltpu.VMEM(a.shape, a.dtype) for a in arrays),
-        (after, *kept),
-        [ANY] + [HBM] * len(arrays),
+        (near(after), *kept),
+        [VM] + [HBM] * len(arrays),
         [pltpu.SemaphoreType.DMA((len(arrays),))],
     )
 
@@ -396,41 +438,40 @@
             pltpu.VMEM((1, slice_width), f32),
             pltpu.VMEM(w_qkv.shape, bf16),
             pltpu.SemaphoreType.DMA((2,)),
-            pltpu.SemaphoreType.DMA((10,)),
+            pltpu.SemaphoreType.DMA((2,)),
         ],
     )
     got = exchange(message, 0, n_ctx, n_exp)
     keys, values = load(message, k_cache, value_cache)
+    live, owns, placing, weighting = call(
+        prepare_kernel,
+        "prepare",
+        (
+            pltpu.VMEM((seqs, 128), f32),
+            pltpu.VMEM((seqs, 128), f32),
+            pltpu.VMEM((128, 128), bf16),
+            pltpu.VMEM((seqs, 128), f32),
+        ),
+        (lengths, routes, gates, near(message)),
+        [SM] + [VM] * 3,
+    )
+    cosine, sine = rotation(lengths, hd)
     message = call(
-        add_kernel, "add", shape(message.shape), (message, *got, keys), [VM] * 4 + [ANY]
+        add_kernel,
+        "add",
+        shape(message.shape),
+        (message, *got, near(keys), near(placing), cosine),
+        [VM] * 7,
     )
     shares = [message] + exchange(message, 1, n_ctx, n_exp)
     (w_near,) = load(message, w_out)
-    cosine, sine = rotation(lengths, hd)
-    positions = k_cache.shape[1]
-    first = lax.axis_index("ctx")
-    where_pos = first * positions + jnp.arange(positions)
-    live = (where_pos[None, :] < lengths[:, None]).astype(f32)
-    owns = jnp.broadcast_to((first == 0).astype(f32), (seqs, 128))
-
-    flat_ids = routes.reshape(-1)
-    onehot = (flat_ids[:, None] == jnp.arange(experts_all)[None, :]).astype(jnp.int32)
-    rank = jnp.sum((jnp.cumsum(onehot, 0) - onehot) * onehot, -1)
-    slot_index = flat_ids * capacity + rank
-    select = (slot_index[:, None] == jnp.arange(experts_all * capacity)[None, :]).astype(f32)
-    token_map = (jnp.arange(seqs * top_k)[:, None] // top_k == jnp.arange(seqs)[None, :]).astype(f32)
-    placing = jnp.dot(select.T, token_map, precision=lax.Precision.HIGHEST).astype(bf16)
-    placing = jnp.pad(placing, ((0, 0), (0, 128 - seqs)))
-    weighting = jnp.dot(
-        token_map.T, select * gates.reshape(-1)[:, None], precision=lax.Precision.HIGHEST
-    )
 
     part = call(
         functools.partial(attend_kernel, seqs),
         "attend",
         shape(((seqs + 1) * QUERY_HEADS, hd)),
-        (*shares, cosine, sine, live, owns, keys, values, w_near),
-        [VM] * 10 + [ANY],
+        (*shares, cosine, sine, near(live), near(owns), near(keys), near(values), near(w_near)),
+        [VM] * 11,
         [pltpu.VMEM((cols // hd * seqs, hd), f32)],
     )
     parts = [part] + exchange(part, 0, n_ctx, n_exp)
@@ -439,18 +480,18 @@
         functools.partial(merge_kernel, seqs),
         "merge",
         shape(part.shape),
-        parts + [w_in_near],
-        [VM] * 4 + [ANY],
+        parts + [near(w_in_near)],
+        [VM] * 5,
     )
     context, resid, outgoing = call(
         functools.partial(finish_kernel, seqs),
         "finish",
         (
-            shape((seqs, QUERY_HEADS * hd)),
+            pltpu.VMEM((seqs, QUERY_HEADS * hd), bf16),
             shape(tokens.shape),
             shape((placing.shape[0], slice_width)),
         ),
-        [part] + exchange(part, 1, n_ctx, n_exp) + [tokens, placing, w_near],
+        [part] + exchange(part, 1, n_ctx, n_exp) + [tokens, near(placing), near(w_near)],
         [VM] * 7,
         [pltpu.VMEM((QUERY_HEADS * seqs, hd), f32)],
     )
@@ -460,17 +501,27 @@
         outgoing.reshape(n_exp, per_source, slice_width), "exp", split_axis=0, concat_axis=0, tiled=True
     )
     side = 4
-    place = jnp.where(lax.axis_index("exp") & 1, first >> 2, first & 3)[None]
     wide = 2 * hidden + 128
     sent = call(
         functools.partial(gate_up_kernel, capacity),
         "gate_up",
         (shape((n_rows // side, wide)),) * side,
-        (place, rows.reshape(n_rows, slice_width), moe_gain[None], w_in_near),
-        [SM] + [VM] * 3,
+        (rows.reshape(n_rows, slice_width), moe_gain[None], near(w_in_near)),
+        [VM] * 3,
     )
     got = [sent[0]] + exchange(sent[1:], 0, n_ctx, n_exp)
-    total = call(add_kernel, "add_rows", shape(got[0].shape), got, [VM] * 4)
+    w_down_near, context = pl.pallas_call(
+        load_kernel,
+        out_shape=(pltpu.VMEM(w_down.shape, bf16), shape(context.shape)),
+        in_specs=[VM, HBM, VM],
+        out_specs=(VM, HBM),
+        scratch_shapes=[pltpu.SemaphoreType.DMA((2,))],
+        compiler_params=pltpu.CompilerParams(vmem_limit_bytes=8 << 20),
+        name="settle",
+    )(near(sent[0]), pltpu.with_memory_space_constraint(w_down, pltpu.HBM), near(context))
+    total = call(
+        add_kernel, "add_rows", shape(got[0].shape), got + [near(w_down_near)], [VM] * 5
+    )
     act = call(
         activate_kernel,
         "activate",
@@ -482,8 +533,8 @@
         functools.partial(down_kernel, capacity),
         "down",
         shape((n_rows, slice_width)),
-        [place, act] + exchange(act, 0, n_ctx, n_exp) + [w_down],
-        [SM] + [VM] * 5,
+        [act] + exchange(act, 0, n_ctx, n_exp) + [near(w_down_near)],
+        [VM] * 5,
     )
     returned = lax.all_to_all(
         expert_out.reshape(n_exp, per_source, slice_width), "exp", split_axis=0, concat_axis=0, tiled=True
@@ -492,7 +543,7 @@
         combine_kernel,
         "combine",
         shape(tokens.shape),
-        (resid, weighting, returned.reshape(n_rows, slice_width)),
+        (resid, near(weighting), returned.reshape(n_rows, slice_width)),
         [VM] * 3,
     )
     return (context, layer_out)

time: 104 us -> 92.7 us (0.89)
  blocking collectives: 0 us -> 36.5 us
  starting transfers between devices: 49.9 us -> 25 us
  waiting for transfers between devices: 34.4 us -> 15.9 us
  local copies, waits for them, and re-layouts: 3.32 us -> 0.03 us
    all_to_all x0 -> x2, blocking collectives: none -> 36.5 us  [the longest x1 21.9 us: local(): lax.all_to_all(outgoing.reshape(n_exp, per_source, slice_width), 'exp', s...]
    all_to_all x2 -> x0, starting transfers between devices: 22.7 us -> none  [the longest x1 15.7 us: local(): lax.all_to_all(outgoing.reshape(n_exp, per_source, slice_width), 'exp', s...]
    all_to_all x2 -> x0, waiting for transfers between devices: 15.4 us -> none  [the longest x1 7.81 us: local(): lax.all_to_all(outgoing.reshape(n_exp, per_source, slice_width), 'exp', s...]
    ppermute x21, waiting for transfers between devices: 19 us -> 15.9 us  [exchange(): got.append(lax.ppermute(sent, AXES, pairs))]
    unnamed x16 -> x10, local copies, waits for them, and re-layouts: 3.03 us -> 0.03 us
    ppermute x21, starting transfers between devices: 27.2 us -> 25 us  [exchange(): got.append(lax.ppermute(sent, AXES, pairs))]
    pallas_call x13 -> x14, Pallas kernels: 14 us -> 12.5 us  [call(): pl.pallas_call(kernel, out_shape=out, in_specs=specs, out_specs=jax.tree....]
    pallas_call x0 -> x1, Pallas kernels: none -> 1.45 us  [local(): pl.pallas_call(load_kernel, out_shape=(pltpu.VMEM(w_down.shape, bf16), sh...]
  transfers between devices with their start and end apart: 23 -> 21, of which waited for: 14 -> 11; matrix products, arithmetic and copies ran while one was open for 1% -> 0% of each run, Pallas kernels for 5% -> 8%
where the time goes in v3:
time: 92.7 us; the launch traced here: 92.4 us
  blocking collectives  36.5 us (39%)
  starting transfers between devices  25 us (27%)
  waiting for transfers between devices  15.9 us (17%)
  Pallas kernels  13.9 us (15%)
    ppermute x21, starting transfers between devices, exchange(): got.append(lax.ppermute(sent, AXES, pairs))  25 us
    all_to_all x1, blocking collectives, local(): lax.all_to_all(outgoing.reshape(n_exp, per_source, slice_width), 'exp', s...  21.9 us
    ppermute x21, waiting for transfers between devices, exchange(): got.append(lax.ppermute(sent, AXES, pairs))  15.9 us
    all_to_all x1, blocking collectives, local(): lax.all_to_all(expert_out.reshape(n_exp, per_source, slice_width), 'exp',...  14.6 us
    pallas_call x14, Pallas kernels, call(): pl.pallas_call(kernel, out_shape=out, in_specs=specs, out_specs=jax.tree....  12.5 us
  transfers between devices with their start and end apart: 21, of which 11 were waited for; matrix products, arithmetic and copies ran while one was open for 0% of the time, Pallas kernels for 8%

profile of v3, /device:TPU:1, one launch (start us, length us, event | category | flops | bytes accessed | tf_op | source)
XLA Modules:
  0.0 92.4 jit_solution(13252265530540817832)
XLA Ops:
  0.7 2.1 %project.1.after.m0 = bf16[8,5248]{1,0:T(8,128)(2,1)S(1)} custom-call(bf16[8,256]{1,0:T(8,128)(2,1)} %tokens.1, f32[1,256]{1,0:T(1,128)} %bitcast.11, bf16[256,5120]{1,0:T(8,128)(2,1)} %w_hbm.1), custom_call_target="tpu_custom_call" | custom-call | tf_op jit(solution)/shard_map/project/pallas_call | solution.py:374
  2.8 3.7 %collective-permute-start.2 = (bf16[8,5248]{1,0:T(8,128)(2,1)S(1)}, bf16[8,5248]{1,0:T(8,128)(2,1)S(1)}, u32[]{:S(2)}, u32[]{:S(2)}) collective-permute-start(bf16[8,5248]{1,0:T(8,128)(2,1)S(1)} %project.1.after.m0), channel_id=1, source_target_pairs={{0,48},{1,193},{2,50},{3,195},{4,52},{5,197},{6,54},{7,199},{8,56}... | collective-permute-start | bytes 251912 | tf_op jit(solution)/shard_map/ppermute | solution.py:27
  6.4 0.3 collective-permute-start.1
  6.8 0.3 collective-permute-start
  7.1 0.1 fusion
  7.2 0.7 prepare.1
  8.0 1.6 %load.3 = (bf16[8,128,512]{2,1,0:T(8,128)(2,1)S(1)}, bf16[8,128,512]{2,1,0:T(8,128)(2,1)S(1)}) custom-call(bf16[8,5248]{1,0:T(8,128)(2,1)S(1)} %project.1.after.m0, bf16[8,128,512]{2,1,0:T(8,128)(2,1)} %refs_0_.4, bf16[8,128,512]{2,1,0:T(8,128)(2,1)} %refs_1_.1), custom_call_target="tpu_custom_call" | custom-call | tf_op jit(solution)/shard_map/load/pallas_call | solution.py:374
  9.5 0.1 pad_maximum_fusion.rest_2_.cosine
  9.6 0.0 collective-permute-done.2.m3
  9.6 1.6 %collective-permute-done.1.m2 = bf16[8,5248]{1,0:T(8,128)(2,1)S(1)} collective-permute-done((bf16[8,5248]{1,0:T(8,128)(2,1)S(1)}, bf16[8,5248]{1,0:T(8,128)(2,1)S(1)}, u32[]{:S(2)}, u32[]{:S(2)}) %collective-permute-start.1) | collective-permute-done | bytes 84000 | tf_op jit(solution)/shard_map/ppermute | solution.py:27
  11.2 0.0 collective-permute-done.m1
  11.2 0.1 add.1.after.m0
  11.4 2.8 %collective-permute-start.5 = (bf16[8,5248]{1,0:T(8,128)(2,1)S(1)}, bf16[8,5248]{1,0:T(8,128)(2,1)S(1)}, u32[]{:S(2)}, u32[]{:S(2)}) collective-permute-start(bf16[8,5248]{1,0:T(8,128)(2,1)S(1)} %add.1.after.m0), channel_id=1, source_target_pairs={{0,192},{1,49},{2,194},{3,51},{4,196},{5,53},{6,198},{7,55},{8,200... | collective-permute-start | bytes 251912 | tf_op jit(solution)/shard_map/ppermute | solution.py:27
  14.2 0.2 collective-permute-start.4
  14.4 0.5 collective-permute-start.3
  14.9 0.1 pad_maximum_fusion.1.sine
  15.0 1.6 %load.4.after.w_ref = bf16[4096,256]{1,0:T(8,128)(2,1)S(1)} custom-call(bf16[8,5248]{1,0:T(8,128)(2,1)S(1)} %add.1.after.m0, bf16[4096,256]{1,0:T(8,128)(2,1)} %refs_0_.5), custom_call_target="tpu_custom_call" | custom-call | tf_op jit(solution)/shard_map/load/pallas_call | solution.py:374
  16.6 0.0 collective-permute-done.5.m3
  16.6 2.4 %collective-permute-done.4.m2 = bf16[8,5248]{1,0:T(8,128)(2,1)S(1)} collective-permute-done((bf16[8,5248]{1,0:T(8,128)(2,1)S(1)}, bf16[8,5248]{1,0:T(8,128)(2,1)S(1)}, u32[]{:S(2)}, u32[]{:S(2)}) %collective-permute-start.4) | collective-permute-done | bytes 84000 | tf_op jit(solution)/shard_map/ppermute | solution.py:27
  19.0 0.0 collective-permute-done.3.m1
  19.0 1.1 %attend.1.after.p0 = bf16[288,128]{1,0:T(8,128)(2,1)S(1)} custom-call(bf16[8,5248]{1,0:T(8,128)(2,1)S(1)} %add.1.after.m0, bf16[8,5248]{1,0:T(8,128)(2,1)S(1)} %collective-permute-done.3.m1, bf16[8,5248]{1,0:T(8,128)(2,1)S(1)} %collective-permute-done.4.m2, bf16[8,5248]{1,0:T(8,128)(2,1)S(1)} %collective-permute-done.5.m3, ...), custom_call_target="tpu_custom_call" | custom-call | tf_op jit(solution)/shard_map/attend/pallas_call | solution.py:374
  20.1 1.2 %collective-permute-start.8 = (bf16[288,128]{1,0:T(8,128)(2,1)S(1)}, bf16[288,128]{1,0:T(8,128)(2,1)S(1)}, u32[]{:S(2)}, u32[]{:S(2)}) collective-permute-start(bf16[288,128]{1,0:T(8,128)(2,1)S(1)} %attend.1.after.p0), channel_id=1, source_target_pairs={{0,48},{1,193},{2,50},{3,195},{4,52},{5,197},{6,54},{7,199},{8,56}... | collective-permute-start | bytes 221192 | tf_op jit(solution)/shard_map/ppermute | solution.py:27
  21.4 0.5 collective-permute-start.7
  21.8 1.6 %collective-permute-start.6 = (bf16[288,128]{1,0:T(8,128)(2,1)S(1)}, bf16[288,128]{1,0:T(8,128)(2,1)S(1)}, u32[]{:S(2)}, u32[]{:S(2)}) collective-permute-start(bf16[288,128]{1,0:T(8,128)(2,1)S(1)} %attend.1.after.p0), channel_id=1, source_target_pairs={{0,16},{1,65},{2,18},{3,67},{4,20},{5,69},{6,22},{7,71},{8,24},{9,... | collective-permute-start | bytes 221192 | tf_op jit(solution)/shard_map/ppermute | solution.py:27
  23.4 1.9 %load.5.after.w_ref = bf16[4,256,1536]{2,1,0:T(8,128)(2,1)S(1)} custom-call(bf16[288,128]{1,0:T(8,128)(2,1)S(1)} %attend.1.after.p0, bf16[4,256,1536]{2,1,0:T(8,128)(2,1)} %refs_0_.6), custom_call_target="tpu_custom_call" | custom-call | tf_op jit(solution)/shard_map/load/pallas_call | solution.py:374
  25.3 0.0 copy-start
  25.4 0.0 collective-permute-done.8.p3
  25.4 0.7 collective-permute-done.7.p2
  26.1 0.0 collective-permute-done.6.p1
  26.1 0.3 merge.1.p0
  26.4 0.0 copy-start.3
  26.4 1.6 %collective-permute-start.11 = (bf16[288,128]{1,0:T(8,128)(2,1)S(1)}, bf16[288,128]{1,0:T(8,128)(2,1)S(1)}, u32[]{:S(2)}, u32[]{:S(2)}) collective-permute-start(bf16[288,128]{1,0:T(8,128)(2,1)S(1)} %merge.1.p0), channel_id=1, source_target_pairs={{0,192},{1,49},{2,194},{3,51},{4,196},{5,53},{6,198},{7,55},{8,200... | collective-permute-start | bytes 221192 | tf_op jit(solution)/shard_map/ppermute | solution.py:27
  28.0 0.6 collective-permute-start.10
  28.5 1.2 %collective-permute-start.9 = (bf16[288,128]{1,0:T(8,128)(2,1)S(1)}, bf16[288,128]{1,0:T(8,128)(2,1)S(1)}, u32[]{:S(2)}, u32[]{:S(2)}) collective-permute-start(bf16[288,128]{1,0:T(8,128)(2,1)S(1)} %merge.1.p0), channel_id=1, source_target_pairs={{0,64},{1,17},{2,66},{3,19},{4,68},{5,21},{6,70},{7,23},{8,72},{9,... | collective-permute-start | bytes 221192 | tf_op jit(solution)/shard_map/ppermute | solution.py:27
  29.8 1.2 %collective-permute-done.11.p3 = bf16[288,128]{1,0:T(8,128)(2,1)S(1)} collective-permute-done((bf16[288,128]{1,0:T(8,128)(2,1)S(1)}, bf16[288,128]{1,0:T(8,128)(2,1)S(1)}, u32[]{:S(2)}, u32[]{:S(2)}) %collective-permute-start.11) | collective-permute-done | bytes 73760 | tf_op jit(solution)/shard_map/ppermute | solution.py:27
  30.9 1.8 %collective-permute-done.10.p2 = bf16[288,128]{1,0:T(8,128)(2,1)S(1)} collective-permute-done((bf16[288,128]{1,0:T(8,128)(2,1)S(1)}, bf16[288,128]{1,0:T(8,128)(2,1)S(1)}, u32[]{:S(2)}, u32[]{:S(2)}) %collective-permute-start.10) | collective-permute-done | bytes 73760 | tf_op jit(solution)/shard_map/ppermute | solution.py:27
  32.7 0.0 collective-permute-done.9.p1
  32.7 0.9 finish.1
  33.6 21.9 %all_to_all.10 = bf16[16,8,256]{2,1,0:T(8,128)(2,1)S(1)} all-to-all(bf16[16,8,256]{2,1,0:T(8,128)(2,1)S(1)} %bitcast.9), channel_id=1, replica_groups=mesh['ctx'=16,'exp'=16] {'exp'}, dimensions={0} | all-to-all | bytes 131072 | tf_op jit(solution)/shard_map/all_to_all | solution.py:500
  55.5 0.6 gate_up.1
  56.1 0.9 %collective-permute-start.12 = (bf16[32,1664]{1,0:T(8,128)(2,1)S(1)}, bf16[32,1664]{1,0:T(8,128)(2,1)S(1)}, u32[]{:S(2)}, u32[]{:S(2)}) collective-permute-start(bf16[32,1664]{1,0:T(8,128)(2,1)S(1)} %get-tuple-element.28), channel_id=1, source_target_pairs={{0,16},{1,65},{2,18},{3,67},{4,20},{5,69},{6,22},{7,71},{8,24},{9,... | collective-permute-start | bytes 319496 | tf_op jit(solution)/shard_map/ppermute | solution.py:27
  57.0 1.8 %collective-permute-start.13 = (bf16[32,1664]{1,0:T(8,128)(2,1)S(1)}, bf16[32,1664]{1,0:T(8,128)(2,1)S(1)}, u32[]{:S(2)}, u32[]{:S(2)}) collective-permute-start(bf16[32,1664]{1,0:T(8,128)(2,1)S(1)} %get-tuple-element.29), channel_id=1, source_target_pairs={{0,32},{1,129},{2,34},{3,131},{4,36},{5,133},{6,38},{7,135},{8,40}... | collective-permute-start | bytes 319496 | tf_op jit(solution)/shard_map/ppermute | solution.py:27
  58.9 1.2 %collective-permute-start.14 = (bf16[32,1664]{1,0:T(8,128)(2,1)S(1)}, bf16[32,1664]{1,0:T(8,128)(2,1)S(1)}, u32[]{:S(2)}, u32[]{:S(2)}) collective-permute-start(bf16[32,1664]{1,0:T(8,128)(2,1)S(1)} %get-tuple-element.30), channel_id=1, source_target_pairs={{0,48},{1,193},{2,50},{3,195},{4,52},{5,197},{6,54},{7,199},{8,56}... | collective-permute-start | bytes 319496 | tf_op jit(solution)/shard_map/ppermute | solution.py:27
  60.1 1.4 %settle.1 = (bf16[4,768,256]{2,1,0:T(8,128)(2,1)S(1)}, bf16[8,4096]{1,0:T(8,128)(2,1)}) custom-call(bf16[32,1664]{1,0:T(8,128)(2,1)S(1)} %get-tuple-element.23.after.m0, bf16[4,768,256]{2,1,0:T(8,128)(2,1)} %refs_0_.7, bf16[8,4096]{1,0:T(8,128)(2,1)S(1)} %get-tuple-element.24.refs_1_), custom_call_target="tpu_custom_call" | custom-call | tf_op jit(solution)/shard_map/settle/pallas_call | solution.py:513
  61.5 0.0 collective-permute-done.12.m1
  61.5 0.9 collective-permute-done.13.m2
  62.4 1.2 %collective-permute-done.14.m3 = bf16[32,1664]{1,0:T(8,128)(2,1)S(1)} collective-permute-done((bf16[32,1664]{1,0:T(8,128)(2,1)S(1)}, bf16[32,1664]{1,0:T(8,128)(2,1)S(1)}, u32[]{:S(2)}, u32[]{:S(2)}) %collective-permute-start.14) | collective-permute-done | bytes 106528 | tf_op jit(solution)/shard_map/ppermute | solution.py:27
  63.6 0.2 add_rows.1.m0
  63.9 1.8 %collective-permute-start.17 = (bf16[32,1664]{1,0:T(8,128)(2,1)S(1)}, bf16[32,1664]{1,0:T(8,128)(2,1)S(1)}, u32[]{:S(2)}, u32[]{:S(2)}) collective-permute-start(bf16[32,1664]{1,0:T(8,128)(2,1)S(1)} %add_rows.1.m0), channel_id=1, source_target_pairs={{0,192},{1,49},{2,194},{3,51},{4,196},{5,53},{6,198},{7,55},{8,200... | collective-permute-start | bytes 319496 | tf_op jit(solution)/shard_map/ppermute | solution.py:27
  65.7 1.1 %collective-permute-start.16 = (bf16[32,1664]{1,0:T(8,128)(2,1)S(1)}, bf16[32,1664]{1,0:T(8,128)(2,1)S(1)}, u32[]{:S(2)}, u32[]{:S(2)}) collective-permute-start(bf16[32,1664]{1,0:T(8,128)(2,1)S(1)} %add_rows.1.m0), channel_id=1, source_target_pairs={{0,128},{1,33},{2,130},{3,35},{4,132},{5,37},{6,134},{7,39},{8,136... | collective-permute-start | bytes 319496 | tf_op jit(solution)/shard_map/ppermute | solution.py:27
  66.7 0.4 collective-permute-start.15
  67.1 1.5 %collective-permute-done.17.m3 = bf16[32,1664]{1,0:T(8,128)(2,1)S(1)} collective-permute-done((bf16[32,1664]{1,0:T(8,128)(2,1)S(1)}, bf16[32,1664]{1,0:T(8,128)(2,1)S(1)}, u32[]{:S(2)}, u32[]{:S(2)}) %collective-permute-start.17) | collective-permute-done | bytes 106528 | tf_op jit(solution)/shard_map/ppermute | solution.py:27
  68.6 2.1 %collective-permute-done.16.m2 = bf16[32,1664]{1,0:T(8,128)(2,1)S(1)} collective-permute-done((bf16[32,1664]{1,0:T(8,128)(2,1)S(1)}, bf16[32,1664]{1,0:T(8,128)(2,1)S(1)}, u32[]{:S(2)}, u32[]{:S(2)}) %collective-permute-start.16) | collective-permute-done | bytes 106528 | tf_op jit(solution)/shard_map/ppermute | solution.py:27
  70.7 0.0 collective-permute-done.15.m1
  70.7 0.2 activate.1.x0
  70.9 1.4 %collective-permute-start.20 = (bf16[32,768]{1,0:T(8,128)(2,1)S(1)}, bf16[32,768]{1,0:T(8,128)(2,1)S(1)}, u32[]{:S(2)}, u32[]{:S(2)}) collective-permute-start(bf16[32,768]{1,0:T(8,128)(2,1)S(1)} %activate.1.x0), channel_id=1, source_target_pairs={{0,48},{1,193},{2,50},{3,195},{4,52},{5,197},{6,54},{7,199},{8,56}... | collective-permute-start | bytes 147464 | tf_op jit(solution)/shard_map/ppermute | solution.py:27
  72.3 0.6 collective-permute-start.19
  72.9 1.4 %collective-permute-start.18 = (bf16[32,768]{1,0:T(8,128)(2,1)S(1)}, bf16[32,768]{1,0:T(8,128)(2,1)S(1)}, u32[]{:S(2)}, u32[]{:S(2)}) collective-permute-start(bf16[32,768]{1,0:T(8,128)(2,1)S(1)} %activate.1.x0), channel_id=1, source_target_pairs={{0,16},{1,65},{2,18},{3,67},{4,20},{5,69},{6,22},{7,71},{8,24},{9,... | collective-permute-start | bytes 147464 | tf_op jit(solution)/shard_map/ppermute | solution.py:27
  74.3 0.9 collective-permute-done.20.x3
  75.2 1.6 %collective-permute-done.19.x2 = bf16[32,768]{1,0:T(8,128)(2,1)S(1)} collective-permute-done((bf16[32,768]{1,0:T(8,128)(2,1)S(1)}, bf16[32,768]{1,0:T(8,128)(2,1)S(1)}, u32[]{:S(2)}, u32[]{:S(2)}) %collective-permute-start.19) | collective-permute-done | bytes 49184 | tf_op jit(solution)/shard_map/ppermute | solution.py:27
  76.7 0.0 collective-permute-done.18.x1
  76.7 0.4 down.1
  77.1 14.6 %all_to_all.11 = bf16[16,8,256]{2,1,0:T(8,128)(2,1)S(1)} all-to-all(bf16[16,8,256]{2,1,0:T(8,128)(2,1)S(1)} %bitcast.7), channel_id=1, replica_groups=mesh['ctx'=16,'exp'=16] {'exp'}, dimensions={0} | all-to-all | bytes 131072 | tf_op jit(solution)/shard_map/all_to_all | solution.py:539
  91.7 0.7 combine.1
  (10 shorter events, 0.0 us)
Async XLA Ops:
  0.6 6.5 %copy-start.4 = (s32[8]{0:T(128)S(1)}, s32[8]{0:T(128)}, u32[]{:S(2)}) copy-start(s32[8]{0:T(128)} %lengths.1) | copy-start | bytes 100
  0.6 6.6 %copy-start.2 = (f32[8,8]{1,0:T(8,128)S(1)}, f32[8,8]{1,0:T(8,128)}, u32[]{:S(2)}) copy-start(f32[8,8]{1,0:T(8,128)} %gates.1) | copy-start | bytes 772
  0.7 6.6 %copy-start.1 = (s32[8,8]{1,0:T(8,128)S(1)}, s32[8,8]{1,0:T(8,128)}, u32[]{:S(2)}) copy-start(s32[8,8]{1,0:T(8,128)} %routes.1) | copy-start | bytes 772
  2.8 6.9 %collective-permute-start.2 = (bf16[8,5248]{1,0:T(8,128)(2,1)S(1)}, bf16[8,5248]{1,0:T(8,128)(2,1)S(1)}, u32[]{:S(2)}, u32[]{:S(2)}) collective-permute-start(bf16[8,5248]{1,0:T(8,128)(2,1)S(1)} %project.1.after.m0), channel_id=1, source_target_pairs={{0,48},{1,193},{2,50},{3,195},{4,52},{5,197},{6,54},{7,199},{8,56}... | collective-permute-start | bytes 251912 | tf_op jit(solution)/shard_map/ppermute | solution.py:27
  6.4 4.8 %collective-permute-start.1 = (bf16[8,5248]{1,0:T(8,128)(2,1)S(1)}, bf16[8,5248]{1,0:T(8,128)(2,1)S(1)}, u32[]{:S(2)}, u32[]{:S(2)}) collective-permute-start(bf16[8,5248]{1,0:T(8,128)(2,1)S(1)} %project.1.after.m0), channel_id=1, source_target_pairs={{0,32},{1,129},{2,34},{3,131},{4,36},{5,133},{6,38},{7,135},{8,40}... | collective-permute-start | bytes 251912 | tf_op jit(solution)/shard_map/ppermute | solution.py:27
  6.8 4.5 %collective-permute-start = (bf16[8,5248]{1,0:T(8,128)(2,1)S(1)}, bf16[8,5248]{1,0:T(8,128)(2,1)S(1)}, u32[]{:S(2)}, u32[]{:S(2)}) collective-permute-start(bf16[8,5248]{1,0:T(8,128)(2,1)S(1)} %project.1.after.m0), channel_id=1, source_target_pairs={{0,16},{1,65},{2,18},{3,67},{4,20},{5,69},{6,22},{7,71},{8,24},{9,... | collective-permute-start | bytes 251912 | tf_op jit(solution)/shard_map/ppermute | solution.py:27
  11.4 5.2 %collective-permute-start.5 = (bf16[8,5248]{1,0:T(8,128)(2,1)S(1)}, bf16[8,5248]{1,0:T(8,128)(2,1)S(1)}, u32[]{:S(2)}, u32[]{:S(2)}) collective-permute-start(bf16[8,5248]{1,0:T(8,128)(2,1)S(1)} %add.1.after.m0), channel_id=1, source_target_pairs={{0,192},{1,49},{2,194},{3,51},{4,196},{5,53},{6,198},{7,55},{8,200... | collective-permute-start | bytes 251912 | tf_op jit(solution)/shard_map/ppermute | solution.py:27
  14.2 4.8 %collective-permute-start.4 = (bf16[8,5248]{1,0:T(8,128)(2,1)S(1)}, bf16[8,5248]{1,0:T(8,128)(2,1)S(1)}, u32[]{:S(2)}, u32[]{:S(2)}) collective-permute-start(bf16[8,5248]{1,0:T(8,128)(2,1)S(1)} %add.1.after.m0), channel_id=1, source_target_pairs={{0,128},{1,33},{2,130},{3,35},{4,132},{5,37},{6,134},{7,39},{8,136... | collective-permute-start | bytes 251912 | tf_op jit(solution)/shard_map/ppermute | solution.py:27
  14.4 4.6 %collective-permute-start.3 = (bf16[8,5248]{1,0:T(8,128)(2,1)S(1)}, bf16[8,5248]{1,0:T(8,128)(2,1)S(1)}, u32[]{:S(2)}, u32[]{:S(2)}) collective-permute-start(bf16[8,5248]{1,0:T(8,128)(2,1)S(1)} %add.1.after.m0), channel_id=1, source_target_pairs={{0,64},{1,17},{2,66},{3,19},{4,68},{5,21},{6,70},{7,23},{8,72},{9,... | collective-permute-start | bytes 251912 | tf_op jit(solution)/shard_map/ppermute | solution.py:27
  20.1 5.2 %collective-permute-start.8 = (bf16[288,128]{1,0:T(8,128)(2,1)S(1)}, bf16[288,128]{1,0:T(8,128)(2,1)S(1)}, u32[]{:S(2)}, u32[]{:S(2)}) collective-permute-start(bf16[288,128]{1,0:T(8,128)(2,1)S(1)} %attend.1.after.p0), channel_id=1, source_target_pairs={{0,48},{1,193},{2,50},{3,195},{4,52},{5,197},{6,54},{7,199},{8,56}... | collective-permute-start | bytes 221192 | tf_op jit(solution)/shard_map/ppermute | solution.py:27
  21.4 4.7 %collective-permute-start.7 = (bf16[288,128]{1,0:T(8,128)(2,1)S(1)}, bf16[288,128]{1,0:T(8,128)(2,1)S(1)}, u32[]{:S(2)}, u32[]{:S(2)}) collective-permute-start(bf16[288,128]{1,0:T(8,128)(2,1)S(1)} %attend.1.after.p0), channel_id=1, source_target_pairs={{0,32},{1,129},{2,34},{3,131},{4,36},{5,133},{6,38},{7,135},{8,40}... | collective-permute-start | bytes 221192 | tf_op jit(solution)/shard_map/ppermute | solution.py:27
  21.8 4.2 %collective-permute-start.6 = (bf16[288,128]{1,0:T(8,128)(2,1)S(1)}, bf16[288,128]{1,0:T(8,128)(2,1)S(1)}, u32[]{:S(2)}, u32[]{:S(2)}) collective-permute-start(bf16[288,128]{1,0:T(8,128)(2,1)S(1)} %attend.1.after.p0), channel_id=1, source_target_pairs={{0,16},{1,65},{2,18},{3,67},{4,20},{5,69},{6,22},{7,71},{8,24},{9,... | collective-permute-start | bytes 221192 | tf_op jit(solution)/shard_map/ppermute | solution.py:27
  25.3 7.4 %copy-start = (bf16[8,256]{1,0:T(8,128)(2,1)S(1)}, bf16[8,256]{1,0:T(8,128)(2,1)}, u32[]{:S(2)}) copy-start(bf16[8,256]{1,0:T(8,128)(2,1)} %tokens.1) | copy-start | bytes 12292
  26.4 29.1 %copy-start.3 = (f32[256]{0:T(256)S(1)}, f32[256]{0:T(256)}, u32[]{:S(2)}) copy-start(f32[256]{0:T(256)} %param.19) | copy-start | bytes 3076
  26.4 4.5 %collective-permute-start.11 = (bf16[288,128]{1,0:T(8,128)(2,1)S(1)}, bf16[288,128]{1,0:T(8,128)(2,1)S(1)}, u32[]{:S(2)}, u32[]{:S(2)}) collective-permute-start(bf16[288,128]{1,0:T(8,128)(2,1)S(1)} %merge.1.p0), channel_id=1, source_target_pairs={{0,192},{1,49},{2,194},{3,51},{4,196},{5,53},{6,198},{7,55},{8,200... | collective-permute-start | bytes 221192 | tf_op jit(solution)/shard_map/ppermute | solution.py:27
  28.0 4.7 %collective-permute-start.10 = (bf16[288,128]{1,0:T(8,128)(2,1)S(1)}, bf16[288,128]{1,0:T(8,128)(2,1)S(1)}, u32[]{:S(2)}, u32[]{:S(2)}) collective-permute-start(bf16[288,128]{1,0:T(8,128)(2,1)S(1)} %merge.1.p0), channel_id=1, source_target_pairs={{0,128},{1,33},{2,130},{3,35},{4,132},{5,37},{6,134},{7,39},{8,136... | collective-permute-start | bytes 221192 | tf_op jit(solution)/shard_map/ppermute | solution.py:27
  28.5 4.2 %collective-permute-start.9 = (bf16[288,128]{1,0:T(8,128)(2,1)S(1)}, bf16[288,128]{1,0:T(8,128)(2,1)S(1)}, u32[]{:S(2)}, u32[]{:S(2)}) collective-permute-start(bf16[288,128]{1,0:T(8,128)(2,1)S(1)} %merge.1.p0), channel_id=1, source_target_pairs={{0,64},{1,17},{2,66},{3,19},{4,68},{5,21},{6,70},{7,23},{8,72},{9,... | collective-permute-start | bytes 221192 | tf_op jit(solution)/shard_map/ppermute | solution.py:27
  56.1 5.4 %collective-permute-start.12 = (bf16[32,1664]{1,0:T(8,128)(2,1)S(1)}, bf16[32,1664]{1,0:T(8,128)(2,1)S(1)}, u32[]{:S(2)}, u32[]{:S(2)}) collective-permute-start(bf16[32,1664]{1,0:T(8,128)(2,1)S(1)} %get-tuple-element.28), channel_id=1, source_target_pairs={{0,16},{1,65},{2,18},{3,67},{4,20},{5,69},{6,22},{7,71},{8,24},{9,... | collective-permute-start | bytes 319496 | tf_op jit(solution)/shard_map/ppermute | solution.py:27
  57.0 5.4 %collective-permute-start.13 = (bf16[32,1664]{1,0:T(8,128)(2,1)S(1)}, bf16[32,1664]{1,0:T(8,128)(2,1)S(1)}, u32[]{:S(2)}, u32[]{:S(2)}) collective-permute-start(bf16[32,1664]{1,0:T(8,128)(2,1)S(1)} %get-tuple-element.29), channel_id=1, source_target_pairs={{0,32},{1,129},{2,34},{3,131},{4,36},{5,133},{6,38},{7,135},{8,40}... | collective-permute-start | bytes 319496 | tf_op jit(solution)/shard_map/ppermute | solution.py:27
  58.9 4.8 %collective-permute-start.14 = (bf16[32,1664]{1,0:T(8,128)(2,1)S(1)}, bf16[32,1664]{1,0:T(8,128)(2,1)S(1)}, u32[]{:S(2)}, u32[]{:S(2)}) collective-permute-start(bf16[32,1664]{1,0:T(8,128)(2,1)S(1)} %get-tuple-element.30), channel_id=1, source_target_pairs={{0,48},{1,193},{2,50},{3,195},{4,52},{5,197},{6,54},{7,199},{8,56}... | collective-permute-start | bytes 319496 | tf_op jit(solution)/shard_map/ppermute | solution.py:27
  63.9 4.8 %collective-permute-start.17 = (bf16[32,1664]{1,0:T(8,128)(2,1)S(1)}, bf16[32,1664]{1,0:T(8,128)(2,1)S(1)}, u32[]{:S(2)}, u32[]{:S(2)}) collective-permute-start(bf16[32,1664]{1,0:T(8,128)(2,1)S(1)} %add_rows.1.m0), channel_id=1, source_target_pairs={{0,192},{1,49},{2,194},{3,51},{4,196},{5,53},{6,198},{7,55},{8,200... | collective-permute-start | bytes 319496 | tf_op jit(solution)/shard_map/ppermute | solution.py:27
  65.7 5.1 %collective-permute-start.16 = (bf16[32,1664]{1,0:T(8,128)(2,1)S(1)}, bf16[32,1664]{1,0:T(8,128)(2,1)S(1)}, u32[]{:S(2)}, u32[]{:S(2)}) collective-permute-start(bf16[32,1664]{1,0:T(8,128)(2,1)S(1)} %add_rows.1.m0), channel_id=1, source_target_pairs={{0,128},{1,33},{2,130},{3,35},{4,132},{5,37},{6,134},{7,39},{8,136... | collective-permute-start | bytes 319496 | tf_op jit(solution)/shard_map/ppermute | solution.py:27
  66.7 4.0 %collective-permute-start.15 = (bf16[32,1664]{1,0:T(8,128)(2,1)S(1)}, bf16[32,1664]{1,0:T(8,128)(2,1)S(1)}, u32[]{:S(2)}, u32[]{:S(2)}) collective-permute-start(bf16[32,1664]{1,0:T(8,128)(2,1)S(1)} %add_rows.1.m0), channel_id=1, source_target_pairs={{0,64},{1,17},{2,66},{3,19},{4,68},{5,21},{6,70},{7,23},{8,72},{9,... | collective-permute-start | bytes 319496 | tf_op jit(solution)/shard_map/ppermute | solution.py:27
  70.9 4.2 %collective-permute-start.20 = (bf16[32,768]{1,0:T(8,128)(2,1)S(1)}, bf16[32,768]{1,0:T(8,128)(2,1)S(1)}, u32[]{:S(2)}, u32[]{:S(2)}) collective-permute-start(bf16[32,768]{1,0:T(8,128)(2,1)S(1)} %activate.1.x0), channel_id=1, source_target_pairs={{0,48},{1,193},{2,50},{3,195},{4,52},{5,197},{6,54},{7,199},{8,56}... | collective-permute-start | bytes 147464 | tf_op jit(solution)/shard_map/ppermute | solution.py:27
  72.3 4.4 %collective-permute-start.19 = (bf16[32,768]{1,0:T(8,128)(2,1)S(1)}, bf16[32,768]{1,0:T(8,128)(2,1)S(1)}, u32[]{:S(2)}, u32[]{:S(2)}) collective-permute-start(bf16[32,768]{1,0:T(8,128)(2,1)S(1)} %activate.1.x0), channel_id=1, source_target_pairs={{0,32},{1,129},{2,34},{3,131},{4,36},{5,133},{6,38},{7,135},{8,40}... | collective-permute-start | bytes 147464 | tf_op jit(solution)/shard_map/ppermute | solution.py:27
  72.9 3.9 %collective-permute-start.18 = (bf16[32,768]{1,0:T(8,128)(2,1)S(1)}, bf16[32,768]{1,0:T(8,128)(2,1)S(1)}, u32[]{:S(2)}, u32[]{:S(2)}) collective-permute-start(bf16[32,768]{1,0:T(8,128)(2,1)S(1)} %activate.1.x0), channel_id=1, source_target_pairs={{0,16},{1,65},{2,18},{3,67},{4,20},{5,69},{6,22},{7,71},{8,24},{9,... | collective-permute-start | bytes 147464 | tf_op jit(solution)/shard_map/ppermute | solution.py:27

commit v4 on v3

--- a/solution.py
+++ b/solution.py
@@ -16,16 +16,16 @@
 
 def exchange(value, stage, n_ctx, n_exp):
     side = 4
-    got = []
-    for step in range(1, side):
+    got = {}
+    for step in (2, 3, 1) if isinstance(value, (list, tuple)) else (1, 3, 2):
         pairs = []
         for i in range(n_ctx):
             for e in range(n_exp):
                 j = i ^ step if (e & 1) == stage else i ^ (side * step)
                 pairs.append((i * n_exp + e, j * n_exp + e))
         sent = value[step - 1] if isinstance(value, (list, tuple)) else value
-        got.append(lax.ppermute(sent, AXES, pairs))
-    return got
+        got[step] = lax.ppermute(sent, AXES, pairs)
+    return [got[step] for step in range(1, side)]
 
 
 def rotation(pos, size):

time: 92.7 us -> 92.7 us (level)
  no operation moved by 1% of the time
where the time goes in v4:
time: 92.7 us; the launch traced here: 92.4 us
  blocking collectives  36.5 us (39%)
  starting transfers between devices  25 us (27%)
  waiting for transfers between devices  15.9 us (17%)
  Pallas kernels  13.9 us (15%)
    ppermute x21, starting transfers between devices, exchange(): got[step] = lax.ppermute(sent, AXES, pairs)  25 us
    all_to_all x1, blocking collectives, local(): lax.all_to_all(outgoing.reshape(n_exp, per_source, slice_width), 'exp', s...  21.9 us
    ppermute x21, waiting for transfers between devices, exchange(): got[step] = lax.ppermute(sent, AXES, pairs)  15.9 us
    all_to_all x1, blocking collectives, local(): lax.all_to_all(expert_out.reshape(n_exp, per_source, slice_width), 'exp',...  14.6 us
    pallas_call x14, Pallas kernels, call(): pl.pallas_call(kernel, out_shape=out, in_specs=specs, out_specs=jax.tree....  12.5 us
  transfers between devices with their start and end apart: 21, of which 11 were waited for; matrix products, arithmetic and copies ran while one was open for 0% of the time, Pallas kernels for 8%

profile of v4, /device:TPU:1, one launch (start us, length us, event | category | flops | bytes accessed | tf_op | source)
XLA Modules:
  0.0 92.4 jit_solution(13252265530540817832)
XLA Ops:
  0.7 2.1 %project.1.after.m0 = bf16[8,5248]{1,0:T(8,128)(2,1)S(1)} custom-call(bf16[8,256]{1,0:T(8,128)(2,1)} %tokens.1, f32[1,256]{1,0:T(1,128)} %bitcast.11, bf16[256,5120]{1,0:T(8,128)(2,1)} %w_hbm.1), custom_call_target="tpu_custom_call" | custom-call | tf_op jit(solution)/shard_map/project/pallas_call | solution.py:374
  2.8 3.7 %collective-permute-start.2 = (bf16[8,5248]{1,0:T(8,128)(2,1)S(1)}, bf16[8,5248]{1,0:T(8,128)(2,1)S(1)}, u32[]{:S(2)}, u32[]{:S(2)}) collective-permute-start(bf16[8,5248]{1,0:T(8,128)(2,1)S(1)} %project.1.after.m0), channel_id=1, source_target_pairs={{0,48},{1,193},{2,50},{3,195},{4,52},{5,197},{6,54},{7,199},{8,56}... | collective-permute-start | bytes 251912 | tf_op jit(solution)/shard_map/ppermute | solution.py:27
  6.4 0.3 collective-permute-start.1
  6.8 0.3 collective-permute-start
  7.1 0.1 fusion
  7.2 0.7 prepare.1
  8.0 1.6 %load.3 = (bf16[8,128,512]{2,1,0:T(8,128)(2,1)S(1)}, bf16[8,128,512]{2,1,0:T(8,128)(2,1)S(1)}) custom-call(bf16[8,5248]{1,0:T(8,128)(2,1)S(1)} %project.1.after.m0, bf16[8,128,512]{2,1,0:T(8,128)(2,1)} %refs_0_.4, bf16[8,128,512]{2,1,0:T(8,128)(2,1)} %refs_1_.1), custom_call_target="tpu_custom_call" | custom-call | tf_op jit(solution)/shard_map/load/pallas_call | solution.py:374
  9.5 0.1 pad_maximum_fusion.rest_2_.cosine
  9.6 0.0 collective-permute-done.2.m3
  9.6 1.6 %collective-permute-done.1.m2 = bf16[8,5248]{1,0:T(8,128)(2,1)S(1)} collective-permute-done((bf16[8,5248]{1,0:T(8,128)(2,1)S(1)}, bf16[8,5248]{1,0:T(8,128)(2,1)S(1)}, u32[]{:S(2)}, u32[]{:S(2)}) %collective-permute-start.1) | collective-permute-done | bytes 84000 | tf_op jit(solution)/shard_map/ppermute | solution.py:27
  11.2 0.0 collective-permute-done.m1
  11.2 0.1 add.1.after.m0
  11.4 2.8 %collective-permute-start.5 = (bf16[8,5248]{1,0:T(8,128)(2,1)S(1)}, bf16[8,5248]{1,0:T(8,128)(2,1)S(1)}, u32[]{:S(2)}, u32[]{:S(2)}) collective-permute-start(bf16[8,5248]{1,0:T(8,128)(2,1)S(1)} %add.1.after.m0), channel_id=1, source_target_pairs={{0,192},{1,49},{2,194},{3,51},{4,196},{5,53},{6,198},{7,55},{8,200... | collective-permute-start | bytes 251912 | tf_op jit(solution)/shard_map/ppermute | solution.py:27
  14.2 0.2 collective-permute-start.4
  14.4 0.5 collective-permute-start.3
  14.9 0.1 pad_maximum_fusion.1.sine
  15.0 1.6 %load.4.after.w_ref = bf16[4096,256]{1,0:T(8,128)(2,1)S(1)} custom-call(bf16[8,5248]{1,0:T(8,128)(2,1)S(1)} %add.1.after.m0, bf16[4096,256]{1,0:T(8,128)(2,1)} %refs_0_.5), custom_call_target="tpu_custom_call" | custom-call | tf_op jit(solution)/shard_map/load/pallas_call | solution.py:374
  16.6 0.0 collective-permute-done.5.m3
  16.6 2.4 %collective-permute-done.4.m2 = bf16[8,5248]{1,0:T(8,128)(2,1)S(1)} collective-permute-done((bf16[8,5248]{1,0:T(8,128)(2,1)S(1)}, bf16[8,5248]{1,0:T(8,128)(2,1)S(1)}, u32[]{:S(2)}, u32[]{:S(2)}) %collective-permute-start.4) | collective-permute-done | bytes 84000 | tf_op jit(solution)/shard_map/ppermute | solution.py:27
  19.0 0.0 collective-permute-done.3.m1
  19.0 1.1 %attend.1.after.p0 = bf16[288,128]{1,0:T(8,128)(2,1)S(1)} custom-call(bf16[8,5248]{1,0:T(8,128)(2,1)S(1)} %add.1.after.m0, bf16[8,5248]{1,0:T(8,128)(2,1)S(1)} %collective-permute-done.3.m1, bf16[8,5248]{1,0:T(8,128)(2,1)S(1)} %collective-permute-done.4.m2, bf16[8,5248]{1,0:T(8,128)(2,1)S(1)} %collective-permute-done.5.m3, ...), custom_call_target="tpu_custom_call" | custom-call | tf_op jit(solution)/shard_map/attend/pallas_call | solution.py:374
  20.1 1.2 %collective-permute-start.8 = (bf16[288,128]{1,0:T(8,128)(2,1)S(1)}, bf16[288,128]{1,0:T(8,128)(2,1)S(1)}, u32[]{:S(2)}, u32[]{:S(2)}) collective-permute-start(bf16[288,128]{1,0:T(8,128)(2,1)S(1)} %attend.1.after.p0), channel_id=1, source_target_pairs={{0,48},{1,193},{2,50},{3,195},{4,52},{5,197},{6,54},{7,199},{8,56}... | collective-permute-start | bytes 221192 | tf_op jit(solution)/shard_map/ppermute | solution.py:27
  21.4 0.5 collective-permute-start.7
  21.8 1.6 %collective-permute-start.6 = (bf16[288,128]{1,0:T(8,128)(2,1)S(1)}, bf16[288,128]{1,0:T(8,128)(2,1)S(1)}, u32[]{:S(2)}, u32[]{:S(2)}) collective-permute-start(bf16[288,128]{1,0:T(8,128)(2,1)S(1)} %attend.1.after.p0), channel_id=1, source_target_pairs={{0,16},{1,65},{2,18},{3,67},{4,20},{5,69},{6,22},{7,71},{8,24},{9,... | collective-permute-start | bytes 221192 | tf_op jit(solution)/shard_map/ppermute | solution.py:27
  23.4 1.9 %load.5.after.w_ref = bf16[4,256,1536]{2,1,0:T(8,128)(2,1)S(1)} custom-call(bf16[288,128]{1,0:T(8,128)(2,1)S(1)} %attend.1.after.p0, bf16[4,256,1536]{2,1,0:T(8,128)(2,1)} %refs_0_.6), custom_call_target="tpu_custom_call" | custom-call | tf_op jit(solution)/shard_map/load/pallas_call | solution.py:374
  25.3 0.0 copy-start
  25.4 0.0 collective-permute-done.8.p3
  25.4 0.7 collective-permute-done.7.p2
  26.1 0.0 collective-permute-done.6.p1
  26.1 0.3 merge.1.p0
  26.4 0.0 copy-start.3
  26.4 1.6 %collective-permute-start.11 = (bf16[288,128]{1,0:T(8,128)(2,1)S(1)}, bf16[288,128]{1,0:T(8,128)(2,1)S(1)}, u32[]{:S(2)}, u32[]{:S(2)}) collective-permute-start(bf16[288,128]{1,0:T(8,128)(2,1)S(1)} %merge.1.p0), channel_id=1, source_target_pairs={{0,192},{1,49},{2,194},{3,51},{4,196},{5,53},{6,198},{7,55},{8,200... | collective-permute-start | bytes 221192 | tf_op jit(solution)/shard_map/ppermute | solution.py:27
  28.0 0.6 collective-permute-start.10
  28.5 1.2 %collective-permute-start.9 = (bf16[288,128]{1,0:T(8,128)(2,1)S(1)}, bf16[288,128]{1,0:T(8,128)(2,1)S(1)}, u32[]{:S(2)}, u32[]{:S(2)}) collective-permute-start(bf16[288,128]{1,0:T(8,128)(2,1)S(1)} %merge.1.p0), channel_id=1, source_target_pairs={{0,64},{1,17},{2,66},{3,19},{4,68},{5,21},{6,70},{7,23},{8,72},{9,... | collective-permute-start | bytes 221192 | tf_op jit(solution)/shard_map/ppermute | solution.py:27
  29.8 1.2 %collective-permute-done.11.p3 = bf16[288,128]{1,0:T(8,128)(2,1)S(1)} collective-permute-done((bf16[288,128]{1,0:T(8,128)(2,1)S(1)}, bf16[288,128]{1,0:T(8,128)(2,1)S(1)}, u32[]{:S(2)}, u32[]{:S(2)}) %collective-permute-start.11) | collective-permute-done | bytes 73760 | tf_op jit(solution)/shard_map/ppermute | solution.py:27
  30.9 1.8 %collective-permute-done.10.p2 = bf16[288,128]{1,0:T(8,128)(2,1)S(1)} collective-permute-done((bf16[288,128]{1,0:T(8,128)(2,1)S(1)}, bf16[288,128]{1,0:T(8,128)(2,1)S(1)}, u32[]{:S(2)}, u32[]{:S(2)}) %collective-permute-start.10) | collective-permute-done | bytes 73760 | tf_op jit(solution)/shard_map/ppermute | solution.py:27
  32.7 0.0 collective-permute-done.9.p1
  32.7 0.9 finish.1
  33.6 21.9 %all_to_all.10 = bf16[16,8,256]{2,1,0:T(8,128)(2,1)S(1)} all-to-all(bf16[16,8,256]{2,1,0:T(8,128)(2,1)S(1)} %bitcast.9), channel_id=1, replica_groups=mesh['ctx'=16,'exp'=16] {'exp'}, dimensions={0} | all-to-all | bytes 131072 | tf_op jit(solution)/shard_map/all_to_all | solution.py:500
  55.5 0.6 gate_up.1
  56.1 0.9 %collective-permute-start.12 = (bf16[32,1664]{1,0:T(8,128)(2,1)S(1)}, bf16[32,1664]{1,0:T(8,128)(2,1)S(1)}, u32[]{:S(2)}, u32[]{:S(2)}) collective-permute-start(bf16[32,1664]{1,0:T(8,128)(2,1)S(1)} %get-tuple-element.28), channel_id=1, source_target_pairs={{0,16},{1,65},{2,18},{3,67},{4,20},{5,69},{6,22},{7,71},{8,24},{9,... | collective-permute-start | bytes 319496 | tf_op jit(solution)/shard_map/ppermute | solution.py:27
  57.0 1.8 %collective-permute-start.13 = (bf16[32,1664]{1,0:T(8,128)(2,1)S(1)}, bf16[32,1664]{1,0:T(8,128)(2,1)S(1)}, u32[]{:S(2)}, u32[]{:S(2)}) collective-permute-start(bf16[32,1664]{1,0:T(8,128)(2,1)S(1)} %get-tuple-element.29), channel_id=1, source_target_pairs={{0,32},{1,129},{2,34},{3,131},{4,36},{5,133},{6,38},{7,135},{8,40}... | collective-permute-start | bytes 319496 | tf_op jit(solution)/shard_map/ppermute | solution.py:27
  58.9 1.2 %collective-permute-start.14 = (bf16[32,1664]{1,0:T(8,128)(2,1)S(1)}, bf16[32,1664]{1,0:T(8,128)(2,1)S(1)}, u32[]{:S(2)}, u32[]{:S(2)}) collective-permute-start(bf16[32,1664]{1,0:T(8,128)(2,1)S(1)} %get-tuple-element.30), channel_id=1, source_target_pairs={{0,48},{1,193},{2,50},{3,195},{4,52},{5,197},{6,54},{7,199},{8,56}... | collective-permute-start | bytes 319496 | tf_op jit(solution)/shard_map/ppermute | solution.py:27
  60.1 1.4 %settle.1 = (bf16[4,768,256]{2,1,0:T(8,128)(2,1)S(1)}, bf16[8,4096]{1,0:T(8,128)(2,1)}) custom-call(bf16[32,1664]{1,0:T(8,128)(2,1)S(1)} %get-tuple-element.23.after.m0, bf16[4,768,256]{2,1,0:T(8,128)(2,1)} %refs_0_.7, bf16[8,4096]{1,0:T(8,128)(2,1)S(1)} %get-tuple-element.24.refs_1_), custom_call_target="tpu_custom_call" | custom-call | tf_op jit(solution)/shard_map/settle/pallas_call | solution.py:513
  61.5 0.0 collective-permute-done.12.m1
  61.5 0.9 collective-permute-done.13.m2
  62.4 1.2 %collective-permute-done.14.m3 = bf16[32,1664]{1,0:T(8,128)(2,1)S(1)} collective-permute-done((bf16[32,1664]{1,0:T(8,128)(2,1)S(1)}, bf16[32,1664]{1,0:T(8,128)(2,1)S(1)}, u32[]{:S(2)}, u32[]{:S(2)}) %collective-permute-start.14) | collective-permute-done | bytes 106528 | tf_op jit(solution)/shard_map/ppermute | solution.py:27
  63.6 0.2 add_rows.1.m0
  63.9 1.8 %collective-permute-start.17 = (bf16[32,1664]{1,0:T(8,128)(2,1)S(1)}, bf16[32,1664]{1,0:T(8,128)(2,1)S(1)}, u32[]{:S(2)}, u32[]{:S(2)}) collective-permute-start(bf16[32,1664]{1,0:T(8,128)(2,1)S(1)} %add_rows.1.m0), channel_id=1, source_target_pairs={{0,192},{1,49},{2,194},{3,51},{4,196},{5,53},{6,198},{7,55},{8,200... | collective-permute-start | bytes 319496 | tf_op jit(solution)/shard_map/ppermute | solution.py:27
  65.7 1.1 %collective-permute-start.16 = (bf16[32,1664]{1,0:T(8,128)(2,1)S(1)}, bf16[32,1664]{1,0:T(8,128)(2,1)S(1)}, u32[]{:S(2)}, u32[]{:S(2)}) collective-permute-start(bf16[32,1664]{1,0:T(8,128)(2,1)S(1)} %add_rows.1.m0), channel_id=1, source_target_pairs={{0,128},{1,33},{2,130},{3,35},{4,132},{5,37},{6,134},{7,39},{8,136... | collective-permute-start | bytes 319496 | tf_op jit(solution)/shard_map/ppermute | solution.py:27
  66.7 0.4 collective-permute-start.15
  67.1 1.5 %collective-permute-done.17.m3 = bf16[32,1664]{1,0:T(8,128)(2,1)S(1)} collective-permute-done((bf16[32,1664]{1,0:T(8,128)(2,1)S(1)}, bf16[32,1664]{1,0:T(8,128)(2,1)S(1)}, u32[]{:S(2)}, u32[]{:S(2)}) %collective-permute-start.17) | collective-permute-done | bytes 106528 | tf_op jit(solution)/shard_map/ppermute | solution.py:27
  68.6 2.1 %collective-permute-done.16.m2 = bf16[32,1664]{1,0:T(8,128)(2,1)S(1)} collective-permute-done((bf16[32,1664]{1,0:T(8,128)(2,1)S(1)}, bf16[32,1664]{1,0:T(8,128)(2,1)S(1)}, u32[]{:S(2)}, u32[]{:S(2)}) %collective-permute-start.16) | collective-permute-done | bytes 106528 | tf_op jit(solution)/shard_map/ppermute | solution.py:27
  70.7 0.0 collective-permute-done.15.m1
  70.7 0.2 activate.1.x0
  70.9 1.4 %collective-permute-start.20 = (bf16[32,768]{1,0:T(8,128)(2,1)S(1)}, bf16[32,768]{1,0:T(8,128)(2,1)S(1)}, u32[]{:S(2)}, u32[]{:S(2)}) collective-permute-start(bf16[32,768]{1,0:T(8,128)(2,1)S(1)} %activate.1.x0), channel_id=1, source_target_pairs={{0,48},{1,193},{2,50},{3,195},{4,52},{5,197},{6,54},{7,199},{8,56}... | collective-permute-start | bytes 147464 | tf_op jit(solution)/shard_map/ppermute | solution.py:27
  72.3 0.6 collective-permute-start.19
  72.9 1.4 %collective-permute-start.18 = (bf16[32,768]{1,0:T(8,128)(2,1)S(1)}, bf16[32,768]{1,0:T(8,128)(2,1)S(1)}, u32[]{:S(2)}, u32[]{:S(2)}) collective-permute-start(bf16[32,768]{1,0:T(8,128)(2,1)S(1)} %activate.1.x0), channel_id=1, source_target_pairs={{0,16},{1,65},{2,18},{3,67},{4,20},{5,69},{6,22},{7,71},{8,24},{9,... | collective-permute-start | bytes 147464 | tf_op jit(solution)/shard_map/ppermute | solution.py:27
  74.3 0.9 collective-permute-done.20.x3
  75.2 1.6 %collective-permute-done.19.x2 = bf16[32,768]{1,0:T(8,128)(2,1)S(1)} collective-permute-done((bf16[32,768]{1,0:T(8,128)(2,1)S(1)}, bf16[32,768]{1,0:T(8,128)(2,1)S(1)}, u32[]{:S(2)}, u32[]{:S(2)}) %collective-permute-start.19) | collective-permute-done | bytes 49184 | tf_op jit(solution)/shard_map/ppermute | solution.py:27
  76.7 0.0 collective-permute-done.18.x1
  76.7 0.4 down.1
  77.1 14.6 %all_to_all.11 = bf16[16,8,256]{2,1,0:T(8,128)(2,1)S(1)} all-to-all(bf16[16,8,256]{2,1,0:T(8,128)(2,1)S(1)} %bitcast.7), channel_id=1, replica_groups=mesh['ctx'=16,'exp'=16] {'exp'}, dimensions={0} | all-to-all | bytes 131072 | tf_op jit(solution)/shard_map/all_to_all | solution.py:539
  91.7 0.7 combine.1
  (10 shorter events, 0.0 us)
Async XLA Ops:
  0.6 6.5 %copy-start.4 = (s32[8]{0:T(128)S(1)}, s32[8]{0:T(128)}, u32[]{:S(2)}) copy-start(s32[8]{0:T(128)} %lengths.1) | copy-start | bytes 100
  0.6 6.6 %copy-start.2 = (f32[8,8]{1,0:T(8,128)S(1)}, f32[8,8]{1,0:T(8,128)}, u32[]{:S(2)}) copy-start(f32[8,8]{1,0:T(8,128)} %gates.1) | copy-start | bytes 772
  0.7 6.6 %copy-start.1 = (s32[8,8]{1,0:T(8,128)S(1)}, s32[8,8]{1,0:T(8,128)}, u32[]{:S(2)}) copy-start(s32[8,8]{1,0:T(8,128)} %routes.1) | copy-start | bytes 772
  2.8 6.9 %collective-permute-start.2 = (bf16[8,5248]{1,0:T(8,128)(2,1)S(1)}, bf16[8,5248]{1,0:T(8,128)(2,1)S(1)}, u32[]{:S(2)}, u32[]{:S(2)}) collective-permute-start(bf16[8,5248]{1,0:T(8,128)(2,1)S(1)} %project.1.after.m0), channel_id=1, source_target_pairs={{0,48},{1,193},{2,50},{3,195},{4,52},{5,197},{6,54},{7,199},{8,56}... | collective-permute-start | bytes 251912 | tf_op jit(solution)/shard_map/ppermute | solution.py:27
  6.4 4.8 %collective-permute-start.1 = (bf16[8,5248]{1,0:T(8,128)(2,1)S(1)}, bf16[8,5248]{1,0:T(8,128)(2,1)S(1)}, u32[]{:S(2)}, u32[]{:S(2)}) collective-permute-start(bf16[8,5248]{1,0:T(8,128)(2,1)S(1)} %project.1.after.m0), channel_id=1, source_target_pairs={{0,32},{1,129},{2,34},{3,131},{4,36},{5,133},{6,38},{7,135},{8,40}... | collective-permute-start | bytes 251912 | tf_op jit(solution)/shard_map/ppermute | solution.py:27
  6.8 4.5 %collective-permute-start = (bf16[8,5248]{1,0:T(8,128)(2,1)S(1)}, bf16[8,5248]{1,0:T(8,128)(2,1)S(1)}, u32[]{:S(2)}, u32[]{:S(2)}) collective-permute-start(bf16[8,5248]{1,0:T(8,128)(2,1)S(1)} %project.1.after.m0), channel_id=1, source_target_pairs={{0,16},{1,65},{2,18},{3,67},{4,20},{5,69},{6,22},{7,71},{8,24},{9,... | collective-permute-start | bytes 251912 | tf_op jit(solution)/shard_map/ppermute | solution.py:27
  11.4 5.2 %collective-permute-start.5 = (bf16[8,5248]{1,0:T(8,128)(2,1)S(1)}, bf16[8,5248]{1,0:T(8,128)(2,1)S(1)}, u32[]{:S(2)}, u32[]{:S(2)}) collective-permute-start(bf16[8,5248]{1,0:T(8,128)(2,1)S(1)} %add.1.after.m0), channel_id=1, source_target_pairs={{0,192},{1,49},{2,194},{3,51},{4,196},{5,53},{6,198},{7,55},{8,200... | collective-permute-start | bytes 251912 | tf_op jit(solution)/shard_map/ppermute | solution.py:27
  14.2 4.8 %collective-permute-start.4 = (bf16[8,5248]{1,0:T(8,128)(2,1)S(1)}, bf16[8,5248]{1,0:T(8,128)(2,1)S(1)}, u32[]{:S(2)}, u32[]{:S(2)}) collective-permute-start(bf16[8,5248]{1,0:T(8,128)(2,1)S(1)} %add.1.after.m0), channel_id=1, source_target_pairs={{0,128},{1,33},{2,130},{3,35},{4,132},{5,37},{6,134},{7,39},{8,136... | collective-permute-start | bytes 251912 | tf_op jit(solution)/shard_map/ppermute | solution.py:27
  14.4 4.6 %collective-permute-start.3 = (bf16[8,5248]{1,0:T(8,128)(2,1)S(1)}, bf16[8,5248]{1,0:T(8,128)(2,1)S(1)}, u32[]{:S(2)}, u32[]{:S(2)}) collective-permute-start(bf16[8,5248]{1,0:T(8,128)(2,1)S(1)} %add.1.after.m0), channel_id=1, source_target_pairs={{0,64},{1,17},{2,66},{3,19},{4,68},{5,21},{6,70},{7,23},{8,72},{9,... | collective-permute-start | bytes 251912 | tf_op jit(solution)/shard_map/ppermute | solution.py:27
  20.1 5.2 %collective-permute-start.8 = (bf16[288,128]{1,0:T(8,128)(2,1)S(1)}, bf16[288,128]{1,0:T(8,128)(2,1)S(1)}, u32[]{:S(2)}, u32[]{:S(2)}) collective-permute-start(bf16[288,128]{1,0:T(8,128)(2,1)S(1)} %attend.1.after.p0), channel_id=1, source_target_pairs={{0,48},{1,193},{2,50},{3,195},{4,52},{5,197},{6,54},{7,199},{8,56}... | collective-permute-start | bytes 221192 | tf_op jit(solution)/shard_map/ppermute | solution.py:27
  21.4 4.7 %collective-permute-start.7 = (bf16[288,128]{1,0:T(8,128)(2,1)S(1)}, bf16[288,128]{1,0:T(8,128)(2,1)S(1)}, u32[]{:S(2)}, u32[]{:S(2)}) collective-permute-start(bf16[288,128]{1,0:T(8,128)(2,1)S(1)} %attend.1.after.p0), channel_id=1, source_target_pairs={{0,32},{1,129},{2,34},{3,131},{4,36},{5,133},{6,38},{7,135},{8,40}... | collective-permute-start | bytes 221192 | tf_op jit(solution)/shard_map/ppermute | solution.py:27
  21.8 4.2 %collective-permute-start.6 = (bf16[288,128]{1,0:T(8,128)(2,1)S(1)}, bf16[288,128]{1,0:T(8,128)(2,1)S(1)}, u32[]{:S(2)}, u32[]{:S(2)}) collective-permute-start(bf16[288,128]{1,0:T(8,128)(2,1)S(1)} %attend.1.after.p0), channel_id=1, source_target_pairs={{0,16},{1,65},{2,18},{3,67},{4,20},{5,69},{6,22},{7,71},{8,24},{9,... | collective-permute-start | bytes 221192 | tf_op jit(solution)/shard_map/ppermute | solution.py:27
  25.3 7.4 %copy-start = (bf16[8,256]{1,0:T(8,128)(2,1)S(1)}, bf16[8,256]{1,0:T(8,128)(2,1)}, u32[]{:S(2)}) copy-start(bf16[8,256]{1,0:T(8,128)(2,1)} %tokens.1) | copy-start | bytes 12292
  26.4 29.1 %copy-start.3 = (f32[256]{0:T(256)S(1)}, f32[256]{0:T(256)}, u32[]{:S(2)}) copy-start(f32[256]{0:T(256)} %param.19) | copy-start | bytes 3076
  26.4 4.5 %collective-permute-start.11 = (bf16[288,128]{1,0:T(8,128)(2,1)S(1)}, bf16[288,128]{1,0:T(8,128)(2,1)S(1)}, u32[]{:S(2)}, u32[]{:S(2)}) collective-permute-start(bf16[288,128]{1,0:T(8,128)(2,1)S(1)} %merge.1.p0), channel_id=1, source_target_pairs={{0,192},{1,49},{2,194},{3,51},{4,196},{5,53},{6,198},{7,55},{8,200... | collective-permute-start | bytes 221192 | tf_op jit(solution)/shard_map/ppermute | solution.py:27
  28.0 4.7 %collective-permute-start.10 = (bf16[288,128]{1,0:T(8,128)(2,1)S(1)}, bf16[288,128]{1,0:T(8,128)(2,1)S(1)}, u32[]{:S(2)}, u32[]{:S(2)}) collective-permute-start(bf16[288,128]{1,0:T(8,128)(2,1)S(1)} %merge.1.p0), channel_id=1, source_target_pairs={{0,128},{1,33},{2,130},{3,35},{4,132},{5,37},{6,134},{7,39},{8,136... | collective-permute-start | bytes 221192 | tf_op jit(solution)/shard_map/ppermute | solution.py:27
  28.5 4.2 %collective-permute-start.9 = (bf16[288,128]{1,0:T(8,128)(2,1)S(1)}, bf16[288,128]{1,0:T(8,128)(2,1)S(1)}, u32[]{:S(2)}, u32[]{:S(2)}) collective-permute-start(bf16[288,128]{1,0:T(8,128)(2,1)S(1)} %merge.1.p0), channel_id=1, source_target_pairs={{0,64},{1,17},{2,66},{3,19},{4,68},{5,21},{6,70},{7,23},{8,72},{9,... | collective-permute-start | bytes 221192 | tf_op jit(solution)/shard_map/ppermute | solution.py:27
  56.1 5.4 %collective-permute-start.12 = (bf16[32,1664]{1,0:T(8,128)(2,1)S(1)}, bf16[32,1664]{1,0:T(8,128)(2,1)S(1)}, u32[]{:S(2)}, u32[]{:S(2)}) collective-permute-start(bf16[32,1664]{1,0:T(8,128)(2,1)S(1)} %get-tuple-element.28), channel_id=1, source_target_pairs={{0,16},{1,65},{2,18},{3,67},{4,20},{5,69},{6,22},{7,71},{8,24},{9,... | collective-permute-start | bytes 319496 | tf_op jit(solution)/shard_map/ppermute | solution.py:27
  57.0 5.4 %collective-permute-start.13 = (bf16[32,1664]{1,0:T(8,128)(2,1)S(1)}, bf16[32,1664]{1,0:T(8,128)(2,1)S(1)}, u32[]{:S(2)}, u32[]{:S(2)}) collective-permute-start(bf16[32,1664]{1,0:T(8,128)(2,1)S(1)} %get-tuple-element.29), channel_id=1, source_target_pairs={{0,32},{1,129},{2,34},{3,131},{4,36},{5,133},{6,38},{7,135},{8,40}... | collective-permute-start | bytes 319496 | tf_op jit(solution)/shard_map/ppermute | solution.py:27
  58.9 4.8 %collective-permute-start.14 = (bf16[32,1664]{1,0:T(8,128)(2,1)S(1)}, bf16[32,1664]{1,0:T(8,128)(2,1)S(1)}, u32[]{:S(2)}, u32[]{:S(2)}) collective-permute-start(bf16[32,1664]{1,0:T(8,128)(2,1)S(1)} %get-tuple-element.30), channel_id=1, source_target_pairs={{0,48},{1,193},{2,50},{3,195},{4,52},{5,197},{6,54},{7,199},{8,56}... | collective-permute-start | bytes 319496 | tf_op jit(solution)/shard_map/ppermute | solution.py:27
  63.9 4.8 %collective-permute-start.17 = (bf16[32,1664]{1,0:T(8,128)(2,1)S(1)}, bf16[32,1664]{1,0:T(8,128)(2,1)S(1)}, u32[]{:S(2)}, u32[]{:S(2)}) collective-permute-start(bf16[32,1664]{1,0:T(8,128)(2,1)S(1)} %add_rows.1.m0), channel_id=1, source_target_pairs={{0,192},{1,49},{2,194},{3,51},{4,196},{5,53},{6,198},{7,55},{8,200... | collective-permute-start | bytes 319496 | tf_op jit(solution)/shard_map/ppermute | solution.py:27
  65.7 5.1 %collective-permute-start.16 = (bf16[32,1664]{1,0:T(8,128)(2,1)S(1)}, bf16[32,1664]{1,0:T(8,128)(2,1)S(1)}, u32[]{:S(2)}, u32[]{:S(2)}) collective-permute-start(bf16[32,1664]{1,0:T(8,128)(2,1)S(1)} %add_rows.1.m0), channel_id=1, source_target_pairs={{0,128},{1,33},{2,130},{3,35},{4,132},{5,37},{6,134},{7,39},{8,136... | collective-permute-start | bytes 319496 | tf_op jit(solution)/shard_map/ppermute | solution.py:27
  66.7 4.0 %collective-permute-start.15 = (bf16[32,1664]{1,0:T(8,128)(2,1)S(1)}, bf16[32,1664]{1,0:T(8,128)(2,1)S(1)}, u32[]{:S(2)}, u32[]{:S(2)}) collective-permute-start(bf16[32,1664]{1,0:T(8,128)(2,1)S(1)} %add_rows.1.m0), channel_id=1, source_target_pairs={{0,64},{1,17},{2,66},{3,19},{4,68},{5,21},{6,70},{7,23},{8,72},{9,... | collective-permute-start | bytes 319496 | tf_op jit(solution)/shard_map/ppermute | solution.py:27
  70.9 4.2 %collective-permute-start.20 = (bf16[32,768]{1,0:T(8,128)(2,1)S(1)}, bf16[32,768]{1,0:T(8,128)(2,1)S(1)}, u32[]{:S(2)}, u32[]{:S(2)}) collective-permute-start(bf16[32,768]{1,0:T(8,128)(2,1)S(1)} %activate.1.x0), channel_id=1, source_target_pairs={{0,48},{1,193},{2,50},{3,195},{4,52},{5,197},{6,54},{7,199},{8,56}... | collective-permute-start | bytes 147464 | tf_op jit(solution)/shard_map/ppermute | solution.py:27
  72.3 4.4 %collective-permute-start.19 = (bf16[32,768]{1,0:T(8,128)(2,1)S(1)}, bf16[32,768]{1,0:T(8,128)(2,1)S(1)}, u32[]{:S(2)}, u32[]{:S(2)}) collective-permute-start(bf16[32,768]{1,0:T(8,128)(2,1)S(1)} %activate.1.x0), channel_id=1, source_target_pairs={{0,32},{1,129},{2,34},{3,131},{4,36},{5,133},{6,38},{7,135},{8,40}... | collective-permute-start | bytes 147464 | tf_op jit(solution)/shard_map/ppermute | solution.py:27
  72.9 3.9 %collective-permute-start.18 = (bf16[32,768]{1,0:T(8,128)(2,1)S(1)}, bf16[32,768]{1,0:T(8,128)(2,1)S(1)}, u32[]{:S(2)}, u32[]{:S(2)}) collective-permute-start(bf16[32,768]{1,0:T(8,128)(2,1)S(1)} %activate.1.x0), channel_id=1, source_target_pairs={{0,16},{1,65},{2,18},{3,67},{4,20},{5,69},{6,22},{7,71},{8,24},{9,... | collective-permute-start | bytes 147464 | tf_op jit(solution)/shard_map/ppermute | solution.py:27

commit v5 on v4

--- a/solution.py
+++ b/solution.py
@@ -25,7 +25,7 @@
                 pairs.append((i * n_exp + e, j * n_exp + e))
         sent = value[step - 1] if isinstance(value, (list, tuple)) else value
         got[step] = lax.ppermute(sent, AXES, pairs)
-    return [got[step] for step in range(1, side)]
+    return [got[step] for step in (1, 3, 2)]
 
 
 def rotation(pos, size):
@@ -137,7 +137,7 @@
         copy.wait()
 
 
-def add_kernel(m0, m1, m2, m3, *rest):
+def add_kernel(m0, m1, m3, m2, *rest):
     f32, bf16 = jnp.float32, jnp.bfloat16
     out = rest[-1]
     cols = out.shape[1] - 128
@@ -152,7 +152,7 @@
 
 
 def attend_kernel(
-    seqs, m0, m1, m2, m3, cosine, sine, live_ref, owns, k_ref, v_ref, after, out, rows
+    seqs, m0, m1, m3, m2, cosine, sine, live_ref, owns, k_ref, v_ref, after, out, rows
 ):
     f32, bf16 = jnp.float32, jnp.bfloat16
     qh, kvh, hd = QUERY_HEADS, KEY_VALUE_HEADS, HEAD_DIMENSION
@@ -251,7 +251,7 @@
     return values, top + jnp.log(total)
 
 
-def merge_kernel(seqs, p0, p1, p2, p3, after, out):
+def merge_kernel(seqs, p0, p1, p3, p2, after, out):
     qh = QUERY_HEADS
     values, log = merged(seqs, (p0, p1, p2, p3))
     for b in range(seqs):
@@ -259,7 +259,7 @@
     out[seqs * qh : (seqs + 1) * qh, :] = spread(log, seqs)
 
 
-def finish_kernel(seqs, p0, p1, p2, p3, tokens, placing, w_ref, context, resid, outgoing, rows):
+def finish_kernel(seqs, p0, p1, p3, p2, tokens, placing, w_ref, context, resid, outgoing, rows):
     f32, bf16 = jnp.float32, jnp.bfloat16
     qh = QUERY_HEADS
     values, _ = merged(seqs, (p0, p1, p2, p3))
@@ -312,7 +312,7 @@
             out[:, c : c + step] = total[s * part : (s + 1) * part]
 
 
-def activate_kernel(m0, m1, m2, m3, out):
+def activate_kernel(m0, m1, m3, m2, out):
     f32, bf16 = jnp.float32, jnp.bfloat16
     hidden = out.shape[1]
 
@@ -327,7 +327,7 @@
     out[...] = (gate / (1.0 + jnp.exp(-gate)) * up).astype(bf16)
 
 
-def down_kernel(capacity, x0, x1, x2, x3, w_ref, out):
+def down_kernel(capacity, x0, x1, x3, x2, w_ref, out):
     f32 = jnp.float32
     xf = jnp.concatenate([x[...].astype(f32) for x in (x0, x1, x2, x3)], 0)
     n_rows, width = xf.shape
@@ -509,7 +509,7 @@
         (rows.reshape(n_rows, slice_width), moe_gain[None], near(w_in_near)),
         [VM] * 3,
     )
-    got = [sent[0]] + exchange(sent[1:], 0, n_ctx, n_exp)
+    got = [sent[0]] + exchange(sent[1:], 0, n_ctx, n_exp)[::-1]
     w_down_near, context = pl.pallas_call(
         load_kernel,
         out_shape=(pltpu.VMEM(w_down.shape, bf16), shape(context.shape)),

time: 92.7 us -> 91.9 us (level)
  starting transfers between devices: 25 us -> 22.1 us
  waiting for transfers between devices: 15.9 us -> 18.5 us
    ppermute x21, starting transfers between devices: 25 us -> 22.1 us  [exchange(): got[step] = lax.ppermute(sent, AXES, pairs)]
    ppermute x21, waiting for transfers between devices: 15.9 us -> 18.5 us  [exchange(): got[step] = lax.ppermute(sent, AXES, pairs)]
  transfers between devices with their start and end apart: 21 -> 21, of which waited for: 11 -> 12; matrix products, arithmetic and copies ran while one was open for 0% -> 0% of each run, Pallas kernels for 8% -> 8%
where the time goes in v5:
time: 91.9 us; the launch traced here: 91.5 us
  blocking collectives  35.9 us (39%)
  starting transfers between devices  22.1 us (24%)
  waiting for transfers between devices  18.5 us (20%)
  Pallas kernels  13.9 us (15%)
    ppermute x21, starting transfers between devices, exchange(): got[step] = lax.ppermute(sent, AXES, pairs)  22.1 us
    all_to_all x1, blocking collectives, local(): lax.all_to_all(outgoing.reshape(n_exp, per_source, slice_width), 'exp', s...  21.5 us
    ppermute x21, waiting for transfers between devices, exchange(): got[step] = lax.ppermute(sent, AXES, pairs)  18.5 us
    all_to_all x1, blocking collectives, local(): lax.all_to_all(expert_out.reshape(n_exp, per_source, slice_width), 'exp',...  14.5 us
    pallas_call x14, Pallas kernels, call(): pl.pallas_call(kernel, out_shape=out, in_specs=specs, out_specs=jax.tree....  12.5 us
  transfers between devices with their start and end apart: 21, of which 12 were waited for; matrix products, arithmetic and copies ran while one was open for 0% of the time, Pallas kernels for 8%

profile of v5, /device:TPU:1, one launch (start us, length us, event | category | flops | bytes accessed | tf_op | source)
XLA Modules:
  0.0 91.5 jit_solution(14352238965691260111)
XLA Ops:
  0.7 2.1 %project.1.after.m0 = bf16[8,5248]{1,0:T(8,128)(2,1)S(1)} custom-call(bf16[8,256]{1,0:T(8,128)(2,1)} %tokens.1, f32[1,256]{1,0:T(1,128)} %bitcast.11, bf16[256,5120]{1,0:T(8,128)(2,1)} %w_hbm.1), custom_call_target="tpu_custom_call" | custom-call | tf_op jit(solution)/shard_map/project/pallas_call | solution.py:374
  2.8 3.8 %collective-permute-start.2 = (bf16[8,5248]{1,0:T(8,128)(2,1)S(1)}, bf16[8,5248]{1,0:T(8,128)(2,1)S(1)}, u32[]{:S(2)}, u32[]{:S(2)}) collective-permute-start(bf16[8,5248]{1,0:T(8,128)(2,1)S(1)} %project.1.after.m0), channel_id=1, source_target_pairs={{0,32},{1,129},{2,34},{3,131},{4,36},{5,133},{6,38},{7,135},{8,40}... | collective-permute-start | bytes 251912 | tf_op jit(solution)/shard_map/ppermute | solution.py:27
  6.6 0.8 collective-permute-start.1
  7.4 0.0 collective-permute-start
  7.4 0.1 fusion
  7.5 0.7 prepare.1
  8.2 1.6 %load.3 = (bf16[8,128,512]{2,1,0:T(8,128)(2,1)S(1)}, bf16[8,128,512]{2,1,0:T(8,128)(2,1)S(1)}) custom-call(bf16[8,5248]{1,0:T(8,128)(2,1)S(1)} %project.1.after.m0, bf16[8,128,512]{2,1,0:T(8,128)(2,1)} %refs_0_.4, bf16[8,128,512]{2,1,0:T(8,128)(2,1)} %refs_1_.1), custom_call_target="tpu_custom_call" | custom-call | tf_op jit(solution)/shard_map/load/pallas_call | solution.py:374
  9.8 0.1 pad_maximum_fusion.rest_2_.cosine
  9.9 0.0 collective-permute-done.2.m2
  9.9 1.5 %collective-permute-done.1.m3 = bf16[8,5248]{1,0:T(8,128)(2,1)S(1)} collective-permute-done((bf16[8,5248]{1,0:T(8,128)(2,1)S(1)}, bf16[8,5248]{1,0:T(8,128)(2,1)S(1)}, u32[]{:S(2)}, u32[]{:S(2)}) %collective-permute-start.1) | collective-permute-done | bytes 84000 | tf_op jit(solution)/shard_map/ppermute | solution.py:27
  11.4 0.0 collective-permute-done.m1
  11.4 0.2 add.1.after.m0
  11.6 2.5 %collective-permute-start.5 = (bf16[8,5248]{1,0:T(8,128)(2,1)S(1)}, bf16[8,5248]{1,0:T(8,128)(2,1)S(1)}, u32[]{:S(2)}, u32[]{:S(2)}) collective-permute-start(bf16[8,5248]{1,0:T(8,128)(2,1)S(1)} %add.1.after.m0), channel_id=1, source_target_pairs={{0,128},{1,33},{2,130},{3,35},{4,132},{5,37},{6,134},{7,39},{8,136... | collective-permute-start | bytes 251912 | tf_op jit(solution)/shard_map/ppermute | solution.py:27
  14.1 0.9 collective-permute-start.4
  14.9 0.0 collective-permute-start.3
  14.9 0.1 pad_maximum_fusion.1.sine
  15.0 1.6 %load.4.after.w_ref = bf16[4096,256]{1,0:T(8,128)(2,1)S(1)} custom-call(bf16[8,5248]{1,0:T(8,128)(2,1)S(1)} %add.1.after.m0, bf16[4096,256]{1,0:T(8,128)(2,1)} %refs_0_.5), custom_call_target="tpu_custom_call" | custom-call | tf_op jit(solution)/shard_map/load/pallas_call | solution.py:374
  16.6 0.0 collective-permute-done.5.m2
  16.6 2.2 %collective-permute-done.4.m3 = bf16[8,5248]{1,0:T(8,128)(2,1)S(1)} collective-permute-done((bf16[8,5248]{1,0:T(8,128)(2,1)S(1)}, bf16[8,5248]{1,0:T(8,128)(2,1)S(1)}, u32[]{:S(2)}, u32[]{:S(2)}) %collective-permute-start.4) | collective-permute-done | bytes 84000 | tf_op jit(solution)/shard_map/ppermute | solution.py:27
  18.8 0.0 collective-permute-done.3.m1
  18.8 1.1 %attend.1.after.p0 = bf16[288,128]{1,0:T(8,128)(2,1)S(1)} custom-call(bf16[8,5248]{1,0:T(8,128)(2,1)S(1)} %add.1.after.m0, bf16[8,5248]{1,0:T(8,128)(2,1)S(1)} %collective-permute-done.3.m1, bf16[8,5248]{1,0:T(8,128)(2,1)S(1)} %collective-permute-done.4.m3, bf16[8,5248]{1,0:T(8,128)(2,1)S(1)} %collective-permute-done.5.m2, ...), custom_call_target="tpu_custom_call" | custom-call | tf_op jit(solution)/shard_map/attend/pallas_call | solution.py:374
  19.9 1.7 %collective-permute-start.8 = (bf16[288,128]{1,0:T(8,128)(2,1)S(1)}, bf16[288,128]{1,0:T(8,128)(2,1)S(1)}, u32[]{:S(2)}, u32[]{:S(2)}) collective-permute-start(bf16[288,128]{1,0:T(8,128)(2,1)S(1)} %attend.1.after.p0), channel_id=1, source_target_pairs={{0,32},{1,129},{2,34},{3,131},{4,36},{5,133},{6,38},{7,135},{8,40}... | collective-permute-start | bytes 221192 | tf_op jit(solution)/shard_map/ppermute | solution.py:27
  21.6 0.8 collective-permute-start.7
  22.4 0.2 collective-permute-start.6
  22.6 1.9 %load.5.after.w_ref = bf16[4,256,1536]{2,1,0:T(8,128)(2,1)S(1)} custom-call(bf16[288,128]{1,0:T(8,128)(2,1)S(1)} %attend.1.after.p0, bf16[4,256,1536]{2,1,0:T(8,128)(2,1)} %refs_0_.6), custom_call_target="tpu_custom_call" | custom-call | tf_op jit(solution)/shard_map/load/pallas_call | solution.py:374
  24.5 0.0 copy-start
  24.6 0.1 collective-permute-done.8.p2
  24.7 1.3 %collective-permute-done.7.p3 = bf16[288,128]{1,0:T(8,128)(2,1)S(1)} collective-permute-done((bf16[288,128]{1,0:T(8,128)(2,1)S(1)}, bf16[288,128]{1,0:T(8,128)(2,1)S(1)}, u32[]{:S(2)}, u32[]{:S(2)}) %collective-permute-start.7) | collective-permute-done | bytes 73760 | tf_op jit(solution)/shard_map/ppermute | solution.py:27
  26.0 0.0 collective-permute-done.6.p1
  26.0 0.3 merge.1.p0
  26.4 0.0 copy-start.3
  26.4 1.6 %collective-permute-start.11 = (bf16[288,128]{1,0:T(8,128)(2,1)S(1)}, bf16[288,128]{1,0:T(8,128)(2,1)S(1)}, u32[]{:S(2)}, u32[]{:S(2)}) collective-permute-start(bf16[288,128]{1,0:T(8,128)(2,1)S(1)} %merge.1.p0), channel_id=1, source_target_pairs={{0,128},{1,33},{2,130},{3,35},{4,132},{5,37},{6,134},{7,39},{8,136... | collective-permute-start | bytes 221192 | tf_op jit(solution)/shard_map/ppermute | solution.py:27
  27.9 0.9 collective-permute-start.10
  28.8 0.3 collective-permute-start.9
  29.1 2.8 %collective-permute-done.11.p2 = bf16[288,128]{1,0:T(8,128)(2,1)S(1)} collective-permute-done((bf16[288,128]{1,0:T(8,128)(2,1)S(1)}, bf16[288,128]{1,0:T(8,128)(2,1)S(1)}, u32[]{:S(2)}, u32[]{:S(2)}) %collective-permute-start.11) | collective-permute-done | bytes 73760 | tf_op jit(solution)/shard_map/ppermute | solution.py:27
  32.0 0.6 collective-permute-done.10.p3
  32.6 0.0 collective-permute-done.9.p1
  32.6 0.9 %finish.1 = (bf16[8,4096]{1,0:T(8,128)(2,1)S(1)}, bf16[8,256]{1,0:T(8,128)(2,1)S(1)}, bf16[128,256]{1,0:T(8,128)(2,1)S(1)}) custom-call(bf16[288,128]{1,0:T(8,128)(2,1)S(1)} %merge.1.p0, bf16[288,128]{1,0:T(8,128)(2,1)S(1)} %collective-permute-done.9.p1, bf16[288,128]{1,0:T(8,128)(2,1)S(1)} %collective-permute-done.10.p3, ...), custom_call_target="tpu_custom_call" | custom-call | tf_op jit(solution)/shard_map/finish/pallas_call | solution.py:374
  33.5 21.5 %all_to_all.10 = bf16[16,8,256]{2,1,0:T(8,128)(2,1)S(1)} all-to-all(bf16[16,8,256]{2,1,0:T(8,128)(2,1)S(1)} %bitcast.9), channel_id=1, replica_groups=mesh['ctx'=16,'exp'=16] {'exp'}, dimensions={0} | all-to-all | bytes 131072 | tf_op jit(solution)/shard_map/all_to_all | solution.py:500
  55.0 0.6 gate_up.1
  55.5 2.2 %collective-permute-start.12 = (bf16[32,1664]{1,0:T(8,128)(2,1)S(1)}, bf16[32,1664]{1,0:T(8,128)(2,1)S(1)}, u32[]{:S(2)}, u32[]{:S(2)}) collective-permute-start(bf16[32,1664]{1,0:T(8,128)(2,1)S(1)} %get-tuple-element.28), channel_id=1, source_target_pairs={{0,32},{1,129},{2,34},{3,131},{4,36},{5,133},{6,38},{7,135},{8,40}... | collective-permute-start | bytes 319496 | tf_op jit(solution)/shard_map/ppermute | solution.py:27
  57.7 0.8 collective-permute-start.13
  58.5 0.0 collective-permute-start.14
  58.5 1.4 %settle.1 = (bf16[4,768,256]{2,1,0:T(8,128)(2,1)S(1)}, bf16[8,4096]{1,0:T(8,128)(2,1)}) custom-call(bf16[32,1664]{1,0:T(8,128)(2,1)S(1)} %get-tuple-element.23.after.m0, bf16[4,768,256]{2,1,0:T(8,128)(2,1)} %refs_0_.7, bf16[8,4096]{1,0:T(8,128)(2,1)S(1)} %get-tuple-element.24.refs_1_), custom_call_target="tpu_custom_call" | custom-call | tf_op jit(solution)/shard_map/settle/pallas_call | solution.py:513
  60.0 1.0 %collective-permute-done.12.m1 = bf16[32,1664]{1,0:T(8,128)(2,1)S(1)} collective-permute-done((bf16[32,1664]{1,0:T(8,128)(2,1)S(1)}, bf16[32,1664]{1,0:T(8,128)(2,1)S(1)}, u32[]{:S(2)}, u32[]{:S(2)}) %collective-permute-start.12) | collective-permute-done | bytes 106528 | tf_op jit(solution)/shard_map/ppermute | solution.py:27
  61.0 1.5 %collective-permute-done.13.m3 = bf16[32,1664]{1,0:T(8,128)(2,1)S(1)} collective-permute-done((bf16[32,1664]{1,0:T(8,128)(2,1)S(1)}, bf16[32,1664]{1,0:T(8,128)(2,1)S(1)}, u32[]{:S(2)}, u32[]{:S(2)}) %collective-permute-start.13) | collective-permute-done | bytes 106528 | tf_op jit(solution)/shard_map/ppermute | solution.py:27
  62.5 0.0 collective-permute-done.14.m2
  62.5 0.2 add_rows.1.m0
  62.7 2.4 %collective-permute-start.17 = (bf16[32,1664]{1,0:T(8,128)(2,1)S(1)}, bf16[32,1664]{1,0:T(8,128)(2,1)S(1)}, u32[]{:S(2)}, u32[]{:S(2)}) collective-permute-start(bf16[32,1664]{1,0:T(8,128)(2,1)S(1)} %add_rows.1.m0), channel_id=1, source_target_pairs={{0,128},{1,33},{2,130},{3,35},{4,132},{5,37},{6,134},{7,39},{8,136... | collective-permute-start | bytes 319496 | tf_op jit(solution)/shard_map/ppermute | solution.py:27
  65.1 0.4 collective-permute-start.16
  65.5 0.2 collective-permute-start.15
  65.7 2.1 %collective-permute-done.17.m2 = bf16[32,1664]{1,0:T(8,128)(2,1)S(1)} collective-permute-done((bf16[32,1664]{1,0:T(8,128)(2,1)S(1)}, bf16[32,1664]{1,0:T(8,128)(2,1)S(1)}, u32[]{:S(2)}, u32[]{:S(2)}) %collective-permute-start.17) | collective-permute-done | bytes 106528 | tf_op jit(solution)/shard_map/ppermute | solution.py:27
  67.8 2.4 %collective-permute-done.16.m3 = bf16[32,1664]{1,0:T(8,128)(2,1)S(1)} collective-permute-done((bf16[32,1664]{1,0:T(8,128)(2,1)S(1)}, bf16[32,1664]{1,0:T(8,128)(2,1)S(1)}, u32[]{:S(2)}, u32[]{:S(2)}) %collective-permute-start.16) | collective-permute-done | bytes 106528 | tf_op jit(solution)/shard_map/ppermute | solution.py:27
  70.2 0.0 collective-permute-done.15.m1
  70.2 0.2 activate.1.x0
  70.4 1.4 %collective-permute-start.20 = (bf16[32,768]{1,0:T(8,128)(2,1)S(1)}, bf16[32,768]{1,0:T(8,128)(2,1)S(1)}, u32[]{:S(2)}, u32[]{:S(2)}) collective-permute-start(bf16[32,768]{1,0:T(8,128)(2,1)S(1)} %activate.1.x0), channel_id=1, source_target_pairs={{0,32},{1,129},{2,34},{3,131},{4,36},{5,133},{6,38},{7,135},{8,40}... | collective-permute-start | bytes 147464 | tf_op jit(solution)/shard_map/ppermute | solution.py:27
  71.8 1.2 %collective-permute-start.19 = (bf16[32,768]{1,0:T(8,128)(2,1)S(1)}, bf16[32,768]{1,0:T(8,128)(2,1)S(1)}, u32[]{:S(2)}, u32[]{:S(2)}) collective-permute-start(bf16[32,768]{1,0:T(8,128)(2,1)S(1)} %activate.1.x0), channel_id=1, source_target_pairs={{0,48},{1,193},{2,50},{3,195},{4,52},{5,197},{6,54},{7,199},{8,56}... | collective-permute-start | bytes 147464 | tf_op jit(solution)/shard_map/ppermute | solution.py:27
  73.0 0.1 collective-permute-start.18
  73.1 1.8 %collective-permute-done.20.x2 = bf16[32,768]{1,0:T(8,128)(2,1)S(1)} collective-permute-done((bf16[32,768]{1,0:T(8,128)(2,1)S(1)}, bf16[32,768]{1,0:T(8,128)(2,1)S(1)}, u32[]{:S(2)}, u32[]{:S(2)}) %collective-permute-start.20) | collective-permute-done | bytes 49184 | tf_op jit(solution)/shard_map/ppermute | solution.py:27
  74.9 1.0 %collective-permute-done.19.x3 = bf16[32,768]{1,0:T(8,128)(2,1)S(1)} collective-permute-done((bf16[32,768]{1,0:T(8,128)(2,1)S(1)}, bf16[32,768]{1,0:T(8,128)(2,1)S(1)}, u32[]{:S(2)}, u32[]{:S(2)}) %collective-permute-start.19) | collective-permute-done | bytes 49184 | tf_op jit(solution)/shard_map/ppermute | solution.py:27
  75.9 0.0 collective-permute-done.18.x1
  75.9 0.4 down.1
  76.3 14.5 %all_to_all.11 = bf16[16,8,256]{2,1,0:T(8,128)(2,1)S(1)} all-to-all(bf16[16,8,256]{2,1,0:T(8,128)(2,1)S(1)} %bitcast.7), channel_id=1, replica_groups=mesh['ctx'=16,'exp'=16] {'exp'}, dimensions={0} | all-to-all | bytes 131072 | tf_op jit(solution)/shard_map/all_to_all | solution.py:539
  90.8 0.7 combine.1
  (10 shorter events, 0.0 us)
Async XLA Ops:
  0.6 6.7 %copy-start.4 = (s32[8]{0:T(128)S(1)}, s32[8]{0:T(128)}, u32[]{:S(2)}) copy-start(s32[8]{0:T(128)} %lengths.1) | copy-start | bytes 100
  0.6 6.9 %copy-start.2 = (f32[8,8]{1,0:T(8,128)S(1)}, f32[8,8]{1,0:T(8,128)}, u32[]{:S(2)}) copy-start(f32[8,8]{1,0:T(8,128)} %gates.1) | copy-start | bytes 772
  0.7 6.9 %copy-start.1 = (s32[8,8]{1,0:T(8,128)S(1)}, s32[8,8]{1,0:T(8,128)}, u32[]{:S(2)}) copy-start(s32[8,8]{1,0:T(8,128)} %routes.1) | copy-start | bytes 772
  2.8 7.1 %collective-permute-start.2 = (bf16[8,5248]{1,0:T(8,128)(2,1)S(1)}, bf16[8,5248]{1,0:T(8,128)(2,1)S(1)}, u32[]{:S(2)}, u32[]{:S(2)}) collective-permute-start(bf16[8,5248]{1,0:T(8,128)(2,1)S(1)} %project.1.after.m0), channel_id=1, source_target_pairs={{0,32},{1,129},{2,34},{3,131},{4,36},{5,133},{6,38},{7,135},{8,40}... | collective-permute-start | bytes 251912 | tf_op jit(solution)/shard_map/ppermute | solution.py:27
  6.6 4.8 %collective-permute-start.1 = (bf16[8,5248]{1,0:T(8,128)(2,1)S(1)}, bf16[8,5248]{1,0:T(8,128)(2,1)S(1)}, u32[]{:S(2)}, u32[]{:S(2)}) collective-permute-start(bf16[8,5248]{1,0:T(8,128)(2,1)S(1)} %project.1.after.m0), channel_id=1, source_target_pairs={{0,48},{1,193},{2,50},{3,195},{4,52},{5,197},{6,54},{7,199},{8,56}... | collective-permute-start | bytes 251912 | tf_op jit(solution)/shard_map/ppermute | solution.py:27
  7.4 4.0 %collective-permute-start = (bf16[8,5248]{1,0:T(8,128)(2,1)S(1)}, bf16[8,5248]{1,0:T(8,128)(2,1)S(1)}, u32[]{:S(2)}, u32[]{:S(2)}) collective-permute-start(bf16[8,5248]{1,0:T(8,128)(2,1)S(1)} %project.1.after.m0), channel_id=1, source_target_pairs={{0,16},{1,65},{2,18},{3,67},{4,20},{5,69},{6,22},{7,71},{8,24},{9,... | collective-permute-start | bytes 251912 | tf_op jit(solution)/shard_map/ppermute | solution.py:27
  11.6 5.1 %collective-permute-start.5 = (bf16[8,5248]{1,0:T(8,128)(2,1)S(1)}, bf16[8,5248]{1,0:T(8,128)(2,1)S(1)}, u32[]{:S(2)}, u32[]{:S(2)}) collective-permute-start(bf16[8,5248]{1,0:T(8,128)(2,1)S(1)} %add.1.after.m0), channel_id=1, source_target_pairs={{0,128},{1,33},{2,130},{3,35},{4,132},{5,37},{6,134},{7,39},{8,136... | collective-permute-start | bytes 251912 | tf_op jit(solution)/shard_map/ppermute | solution.py:27
  14.1 4.8 %collective-permute-start.4 = (bf16[8,5248]{1,0:T(8,128)(2,1)S(1)}, bf16[8,5248]{1,0:T(8,128)(2,1)S(1)}, u32[]{:S(2)}, u32[]{:S(2)}) collective-permute-start(bf16[8,5248]{1,0:T(8,128)(2,1)S(1)} %add.1.after.m0), channel_id=1, source_target_pairs={{0,192},{1,49},{2,194},{3,51},{4,196},{5,53},{6,198},{7,55},{8,200... | collective-permute-start | bytes 251912 | tf_op jit(solution)/shard_map/ppermute | solution.py:27
  14.9 3.9 %collective-permute-start.3 = (bf16[8,5248]{1,0:T(8,128)(2,1)S(1)}, bf16[8,5248]{1,0:T(8,128)(2,1)S(1)}, u32[]{:S(2)}, u32[]{:S(2)}) collective-permute-start(bf16[8,5248]{1,0:T(8,128)(2,1)S(1)} %add.1.after.m0), channel_id=1, source_target_pairs={{0,64},{1,17},{2,66},{3,19},{4,68},{5,21},{6,70},{7,23},{8,72},{9,... | collective-permute-start | bytes 251912 | tf_op jit(solution)/shard_map/ppermute | solution.py:27
  19.9 4.8 %collective-permute-start.8 = (bf16[288,128]{1,0:T(8,128)(2,1)S(1)}, bf16[288,128]{1,0:T(8,128)(2,1)S(1)}, u32[]{:S(2)}, u32[]{:S(2)}) collective-permute-start(bf16[288,128]{1,0:T(8,128)(2,1)S(1)} %attend.1.after.p0), channel_id=1, source_target_pairs={{0,32},{1,129},{2,34},{3,131},{4,36},{5,133},{6,38},{7,135},{8,40}... | collective-permute-start | bytes 221192 | tf_op jit(solution)/shard_map/ppermute | solution.py:27
  21.6 4.4 %collective-permute-start.7 = (bf16[288,128]{1,0:T(8,128)(2,1)S(1)}, bf16[288,128]{1,0:T(8,128)(2,1)S(1)}, u32[]{:S(2)}, u32[]{:S(2)}) collective-permute-start(bf16[288,128]{1,0:T(8,128)(2,1)S(1)} %attend.1.after.p0), channel_id=1, source_target_pairs={{0,48},{1,193},{2,50},{3,195},{4,52},{5,197},{6,54},{7,199},{8,56}... | collective-permute-start | bytes 221192 | tf_op jit(solution)/shard_map/ppermute | solution.py:27
  22.4 3.6 %collective-permute-start.6 = (bf16[288,128]{1,0:T(8,128)(2,1)S(1)}, bf16[288,128]{1,0:T(8,128)(2,1)S(1)}, u32[]{:S(2)}, u32[]{:S(2)}) collective-permute-start(bf16[288,128]{1,0:T(8,128)(2,1)S(1)} %attend.1.after.p0), channel_id=1, source_target_pairs={{0,16},{1,65},{2,18},{3,67},{4,20},{5,69},{6,22},{7,71},{8,24},{9,... | collective-permute-start | bytes 221192 | tf_op jit(solution)/shard_map/ppermute | solution.py:27
  24.5 8.0 %copy-start = (bf16[8,256]{1,0:T(8,128)(2,1)S(1)}, bf16[8,256]{1,0:T(8,128)(2,1)}, u32[]{:S(2)}) copy-start(bf16[8,256]{1,0:T(8,128)(2,1)} %tokens.1) | copy-start | bytes 12292
  26.4 28.6 %copy-start.3 = (f32[256]{0:T(256)S(1)}, f32[256]{0:T(256)}, u32[]{:S(2)}) copy-start(f32[256]{0:T(256)} %param.19) | copy-start | bytes 3076
  26.4 5.6 %collective-permute-start.11 = (bf16[288,128]{1,0:T(8,128)(2,1)S(1)}, bf16[288,128]{1,0:T(8,128)(2,1)S(1)}, u32[]{:S(2)}, u32[]{:S(2)}) collective-permute-start(bf16[288,128]{1,0:T(8,128)(2,1)S(1)} %merge.1.p0), channel_id=1, source_target_pairs={{0,128},{1,33},{2,130},{3,35},{4,132},{5,37},{6,134},{7,39},{8,136... | collective-permute-start | bytes 221192 | tf_op jit(solution)/shard_map/ppermute | solution.py:27
  27.9 4.6 %collective-permute-start.10 = (bf16[288,128]{1,0:T(8,128)(2,1)S(1)}, bf16[288,128]{1,0:T(8,128)(2,1)S(1)}, u32[]{:S(2)}, u32[]{:S(2)}) collective-permute-start(bf16[288,128]{1,0:T(8,128)(2,1)S(1)} %merge.1.p0), channel_id=1, source_target_pairs={{0,192},{1,49},{2,194},{3,51},{4,196},{5,53},{6,198},{7,55},{8,200... | collective-permute-start | bytes 221192 | tf_op jit(solution)/shard_map/ppermute | solution.py:27
  28.8 3.7 %collective-permute-start.9 = (bf16[288,128]{1,0:T(8,128)(2,1)S(1)}, bf16[288,128]{1,0:T(8,128)(2,1)S(1)}, u32[]{:S(2)}, u32[]{:S(2)}) collective-permute-start(bf16[288,128]{1,0:T(8,128)(2,1)S(1)} %merge.1.p0), channel_id=1, source_target_pairs={{0,64},{1,17},{2,66},{3,19},{4,68},{5,21},{6,70},{7,23},{8,72},{9,... | collective-permute-start | bytes 221192 | tf_op jit(solution)/shard_map/ppermute | solution.py:27
  55.5 5.4 %collective-permute-start.12 = (bf16[32,1664]{1,0:T(8,128)(2,1)S(1)}, bf16[32,1664]{1,0:T(8,128)(2,1)S(1)}, u32[]{:S(2)}, u32[]{:S(2)}) collective-permute-start(bf16[32,1664]{1,0:T(8,128)(2,1)S(1)} %get-tuple-element.28), channel_id=1, source_target_pairs={{0,32},{1,129},{2,34},{3,131},{4,36},{5,133},{6,38},{7,135},{8,40}... | collective-permute-start | bytes 319496 | tf_op jit(solution)/shard_map/ppermute | solution.py:27
  57.7 4.8 %collective-permute-start.13 = (bf16[32,1664]{1,0:T(8,128)(2,1)S(1)}, bf16[32,1664]{1,0:T(8,128)(2,1)S(1)}, u32[]{:S(2)}, u32[]{:S(2)}) collective-permute-start(bf16[32,1664]{1,0:T(8,128)(2,1)S(1)} %get-tuple-element.29), channel_id=1, source_target_pairs={{0,48},{1,193},{2,50},{3,195},{4,52},{5,197},{6,54},{7,199},{8,56}... | collective-permute-start | bytes 319496 | tf_op jit(solution)/shard_map/ppermute | solution.py:27
  58.5 4.0 %collective-permute-start.14 = (bf16[32,1664]{1,0:T(8,128)(2,1)S(1)}, bf16[32,1664]{1,0:T(8,128)(2,1)S(1)}, u32[]{:S(2)}, u32[]{:S(2)}) collective-permute-start(bf16[32,1664]{1,0:T(8,128)(2,1)S(1)} %get-tuple-element.30), channel_id=1, source_target_pairs={{0,16},{1,65},{2,18},{3,67},{4,20},{5,69},{6,22},{7,71},{8,24},{9,... | collective-permute-start | bytes 319496 | tf_op jit(solution)/shard_map/ppermute | solution.py:27
  62.7 5.1 %collective-permute-start.17 = (bf16[32,1664]{1,0:T(8,128)(2,1)S(1)}, bf16[32,1664]{1,0:T(8,128)(2,1)S(1)}, u32[]{:S(2)}, u32[]{:S(2)}) collective-permute-start(bf16[32,1664]{1,0:T(8,128)(2,1)S(1)} %add_rows.1.m0), channel_id=1, source_target_pairs={{0,128},{1,33},{2,130},{3,35},{4,132},{5,37},{6,134},{7,39},{8,136... | collective-permute-start | bytes 319496 | tf_op jit(solution)/shard_map/ppermute | solution.py:27
  65.1 5.1 %collective-permute-start.16 = (bf16[32,1664]{1,0:T(8,128)(2,1)S(1)}, bf16[32,1664]{1,0:T(8,128)(2,1)S(1)}, u32[]{:S(2)}, u32[]{:S(2)}) collective-permute-start(bf16[32,1664]{1,0:T(8,128)(2,1)S(1)} %add_rows.1.m0), channel_id=1, source_target_pairs={{0,192},{1,49},{2,194},{3,51},{4,196},{5,53},{6,198},{7,55},{8,200... | collective-permute-start | bytes 319496 | tf_op jit(solution)/shard_map/ppermute | solution.py:27
  65.5 4.7 %collective-permute-start.15 = (bf16[32,1664]{1,0:T(8,128)(2,1)S(1)}, bf16[32,1664]{1,0:T(8,128)(2,1)S(1)}, u32[]{:S(2)}, u32[]{:S(2)}) collective-permute-start(bf16[32,1664]{1,0:T(8,128)(2,1)S(1)} %add_rows.1.m0), channel_id=1, source_target_pairs={{0,64},{1,17},{2,66},{3,19},{4,68},{5,21},{6,70},{7,23},{8,72},{9,... | collective-permute-start | bytes 319496 | tf_op jit(solution)/shard_map/ppermute | solution.py:27
  70.4 4.5 %collective-permute-start.20 = (bf16[32,768]{1,0:T(8,128)(2,1)S(1)}, bf16[32,768]{1,0:T(8,128)(2,1)S(1)}, u32[]{:S(2)}, u32[]{:S(2)}) collective-permute-start(bf16[32,768]{1,0:T(8,128)(2,1)S(1)} %activate.1.x0), channel_id=1, source_target_pairs={{0,32},{1,129},{2,34},{3,131},{4,36},{5,133},{6,38},{7,135},{8,40}... | collective-permute-start | bytes 147464 | tf_op jit(solution)/shard_map/ppermute | solution.py:27
  71.8 4.2 %collective-permute-start.19 = (bf16[32,768]{1,0:T(8,128)(2,1)S(1)}, bf16[32,768]{1,0:T(8,128)(2,1)S(1)}, u32[]{:S(2)}, u32[]{:S(2)}) collective-permute-start(bf16[32,768]{1,0:T(8,128)(2,1)S(1)} %activate.1.x0), channel_id=1, source_target_pairs={{0,48},{1,193},{2,50},{3,195},{4,52},{5,197},{6,54},{7,199},{8,56}... | collective-permute-start | bytes 147464 | tf_op jit(solution)/shard_map/ppermute | solution.py:27
  73.0 3.0 %collective-permute-start.18 = (bf16[32,768]{1,0:T(8,128)(2,1)S(1)}, bf16[32,768]{1,0:T(8,128)(2,1)S(1)}, u32[]{:S(2)}, u32[]{:S(2)}) collective-permute-start(bf16[32,768]{1,0:T(8,128)(2,1)S(1)} %activate.1.x0), channel_id=1, source_target_pairs={{0,16},{1,65},{2,18},{3,67},{4,20},{5,69},{6,22},{7,71},{8,24},{9,... | collective-permute-start | bytes 147464 | tf_op jit(solution)/shard_map/ppermute | solution.py:27

commit v6 on v5

--- a/solution.py
+++ b/solution.py
@@ -12,6 +12,8 @@
 KEY_VALUE_HEADS = 4
 HEAD_DIMENSION = 128
 AXES = ("ctx", "exp")
+SQUARES = 1024.0
+SHARES = 16.0
 
 
 def exchange(value, stage, n_ctx, n_exp):
@@ -59,6 +61,11 @@
     high = value.astype(jnp.bfloat16).astype(jnp.float32)
     lane = lax.broadcasted_iota(jnp.int32, (value.shape[0], 128), 1)
     return jnp.where(lane < 64, high, value - high).astype(jnp.bfloat16)
+
+
+def added(arrays):
+    own, one, three, two = (a.astype(jnp.float32) for a in arrays)
+    return (own + one) + (two + three)
 
 
 def prepare_kernel(lengths, routes, gates, after, live, owns, placing, weighting):
@@ -118,11 +125,12 @@
         copy.wait()
     xf = tokens[...].astype(f32)
     scaled = (xf * gain[...]).astype(bf16)
-    out[:, cols:] = halves(jnp.sum(xf * xf, 1, keepdims=True))
+    squares = jnp.sum(xf * xf, 1, keepdims=True) * (SQUARES / D)
+    out[:, cols:] = halves(squares).astype(f32)
     for c, copy in enumerate(copies):
         copy.wait()
         at = slice(c * width, (c + 1) * width)
-        out[:, at] = jnp.dot(scaled, w_ref[:, at], preferred_element_type=f32).astype(bf16)
+        out[:, at] = jnp.dot(scaled, w_ref[:, at], preferred_element_type=f32) * SHARES
 
 
 def load_kernel(after, *refs):
@@ -152,7 +160,7 @@
 
 
 def attend_kernel(
-    seqs, m0, m1, m3, m2, cosine, sine, live_ref, owns, k_ref, v_ref, after, out, rows
+    seqs, shares, cosine, sine, live_ref, owns, k_ref, v_ref, after, out, rows
 ):
     f32, bf16 = jnp.float32, jnp.bfloat16
     qh, kvh, hd = QUERY_HEADS, KEY_VALUE_HEADS, HEAD_DIMENSION
@@ -160,11 +168,10 @@
     positions = k_ref.shape[1]
 
     def share(h):
-        p, q, r, s = (m[:, h * hd : (h + 1) * hd].astype(f32) for m in (m0, m1, m2, m3))
-        return (p + q) + (r + s)
+        return shares[:, h * hd : (h + 1) * hd]
 
     squares = share(qh + 2 * kvh)
-    norm = lax.rsqrt((squares + pltpu.roll(squares, 64, 1)) / D + 1e-06)
+    norm = lax.rsqrt((squares + pltpu.roll(squares, 64, 1)) / SQUARES + 1e-06) / SHARES
     cos, sin = cosine[...] * norm, sine[...] * norm
     scale = hd**-0.5
     cos_q, sin_q = cos * scale, sin * scale
@@ -427,7 +434,7 @@
     message = call(
         project_kernel,
         "project",
-        pltpu.VMEM((seqs, cols + 128), bf16),
+        pltpu.VMEM((seqs, cols + 128), f32),
         [
             pltpu.with_memory_space_constraint(a, pltpu.HBM)
             for a in (tokens, attn_gain[None], w_qkv)
@@ -441,8 +448,9 @@
             pltpu.SemaphoreType.DMA((2,)),
         ],
     )
+    whole, message = message, lax.optimization_barrier(message.astype(jnp.float16))
     got = exchange(message, 0, n_ctx, n_exp)
-    keys, values = load(message, k_cache, value_cache)
+    keys, values = load(whole, k_cache, value_cache)
     live, owns, placing, weighting = call(
         prepare_kernel,
         "prepare",
@@ -452,26 +460,21 @@
             pltpu.VMEM((128, 128), bf16),
             pltpu.VMEM((seqs, 128), f32),
         ),
-        (lengths, routes, gates, near(message)),
+        (lengths, routes, gates, near(whole)),
         [SM] + [VM] * 3,
     )
     cosine, sine = rotation(lengths, hd)
-    message = call(
-        add_kernel,
-        "add",
-        shape(message.shape),
-        (message, *got, near(keys), near(placing), cosine),
-        [VM] * 7,
-    )
-    shares = [message] + exchange(message, 1, n_ctx, n_exp)
-    (w_near,) = load(message, w_out)
+    total = added([message] + got)
+    message = lax.optimization_barrier(total.astype(jnp.float16))
+    shares = added([message] + exchange(message, 1, n_ctx, n_exp))
+    (w_near,) = load(total, w_out)
 
     part = call(
         functools.partial(attend_kernel, seqs),
         "attend",
         shape(((seqs + 1) * QUERY_HEADS, hd)),
-        (*shares, cosine, sine, near(live), near(owns), near(keys), near(values), near(w_near)),
-        [VM] * 11,
+        (shares, cosine, sine, near(live), near(owns), near(keys), near(values), near(w_near)),
+        [VM] * 8,
         [pltpu.VMEM((cols // hd * seqs, hd), f32)],
     )
     parts = [part] + exchange(part, 0, n_ctx, n_exp)

time: 91.9 us -> 92.2 us (level)
  blocking collectives: 35.9 us -> 37.8 us
    all_to_all x1, blocking collectives: 21.5 us -> 23.5 us  [local(): lax.all_to_all(outgoing.reshape(n_exp, per_source, slice_width), 'exp', s...]
    pallas_call x14 -> x13, Pallas kernels: 12.5 us -> 12.3 us  [call(): pl.pallas_call(kernel, out_shape=out, in_specs=specs, out_specs=jax.tree....]
where the time goes in v6:
time: 92.2 us; the launch traced here: 91.9 us
  blocking collectives  37.8 us (41%)
  starting transfers between devices  21.4 us (23%)
  waiting for transfers between devices  17.8 us (19%)
  Pallas kernels  13.8 us (15%)
    all_to_all x1, blocking collectives, local(): lax.all_to_all(outgoing.reshape(n_exp, per_source, slice_width), 'exp', s...  23.5 us
    ppermute x21, starting transfers between devices, exchange(): got[step] = lax.ppermute(sent, AXES, pairs)  21.4 us
    ppermute x21, waiting for transfers between devices, exchange(): got[step] = lax.ppermute(sent, AXES, pairs)  17.8 us
    all_to_all x1, blocking collectives, local(): lax.all_to_all(expert_out.reshape(n_exp, per_source, slice_width), 'exp',...  14.3 us
    pallas_call x13, Pallas kernels, call(): pl.pallas_call(kernel, out_shape=out, in_specs=specs, out_specs=jax.tree....  12.3 us
  transfers between devices with their start and end apart: 21, of which 12 were waited for; matrix products, arithmetic and copies ran while one was open for 0% of the time, Pallas kernels for 8%

profile of v6, /device:TPU:1, one launch (start us, length us, event | category | flops | bytes accessed | tf_op | source)
XLA Modules:
  0.0 91.9 jit_solution(9297502539431995620)
XLA Ops:
  0.6 0.0 copy-start.4
  0.7 2.1 %project.1.after = f32[8,5248]{1,0:T(8,128)S(1)} custom-call(bf16[8,256]{1,0:T(8,128)(2,1)} %tokens.1, f32[1,256]{1,0:T(1,128)} %bitcast.11, bf16[256,5120]{1,0:T(8,128)(2,1)} %w_hbm.1), custom_call_target="tpu_custom_call" | custom-call | tf_op jit(solution)/shard_map/project/pallas_call | solution.py:381
  2.8 3.7 %collective-permute-start.2 = (f16[8,5248]{1,0:T(8,128)(2,1)S(1)}, f16[8,5248]{1,0:T(8,128)(2,1)S(1)}, u32[]{:S(2)}, u32[]{:S(2)}) collective-permute-start(f16[8,5248]{1,0:T(8,128)(2,1)S(1)} %convert_element_type.40), channel_id=1, source_target_pairs={{0,48},{1,193},{2,50},{3,195},{4,52},{5,197},{6,54},{7,199},{8,56}... | collective-permute-start | bytes 251912 | tf_op jit(solution)/shard_map/ppermute | solution.py:29
  6.4 0.3 collective-permute-start.1
  6.8 0.3 collective-permute-start
  7.1 0.1 fusion
  7.2 0.7 prepare.1
  8.0 1.6 %load.3 = (bf16[8,128,512]{2,1,0:T(8,128)(2,1)S(1)}, bf16[8,128,512]{2,1,0:T(8,128)(2,1)S(1)}) custom-call(f32[8,5248]{1,0:T(8,128)S(1)} %project.1.after, bf16[8,128,512]{2,1,0:T(8,128)(2,1)} %refs_0_.4, bf16[8,128,512]{2,1,0:T(8,128)(2,1)} %refs_1_.1), custom_call_target="tpu_custom_call" | custom-call | tf_op jit(solution)/shard_map/load/pallas_call | solution.py:381
  9.6 0.0 collective-permute-done.2
  9.6 1.7 %collective-permute-done.1 = f16[8,5248]{1,0:T(8,128)(2,1)S(1)} collective-permute-done((f16[8,5248]{1,0:T(8,128)(2,1)S(1)}, f16[8,5248]{1,0:T(8,128)(2,1)S(1)}, u32[]{:S(2)}, u32[]{:S(2)}) %collective-permute-start.1) | collective-permute-done | bytes 84000 | tf_op jit(solution)/shard_map/ppermute | solution.py:29
  11.2 0.0 collective-permute-done
  11.2 0.1 fusion.1
  11.3 2.9 %collective-permute-start.5 = (f16[8,5248]{1,0:T(8,128)(2,1)S(1)}, f16[8,5248]{1,0:T(8,128)(2,1)S(1)}, u32[]{:S(2)}, u32[]{:S(2)}) collective-permute-start(f16[8,5248]{1,0:T(8,128)(2,1)S(1)} %get-tuple-element.32), channel_id=1, source_target_pairs={{0,192},{1,49},{2,194},{3,51},{4,196},{5,53},{6,198},{7,55},{8,200... | collective-permute-start | bytes 251912 | tf_op jit(solution)/shard_map/ppermute | solution.py:29
  14.2 0.2 collective-permute-start.4
  14.4 0.5 collective-permute-start.3
  14.8 0.1 pad_maximum_fusion
  14.9 1.6 %load.4.after.w_ref = bf16[4096,256]{1,0:T(8,128)(2,1)S(1)} custom-call(f32[8,5248]{1,0:T(8,128)S(1)} %get-tuple-element.33.after, bf16[4096,256]{1,0:T(8,128)(2,1)} %refs_0_.5), custom_call_target="tpu_custom_call" | custom-call | tf_op jit(solution)/shard_map/load/pallas_call | solution.py:381
  16.5 0.0 collective-permute-done.5
  16.5 2.4 %collective-permute-done.4 = f16[8,5248]{1,0:T(8,128)(2,1)S(1)} collective-permute-done((f16[8,5248]{1,0:T(8,128)(2,1)S(1)}, f16[8,5248]{1,0:T(8,128)(2,1)S(1)}, u32[]{:S(2)}, u32[]{:S(2)}) %collective-permute-start.4) | collective-permute-done | bytes 84000 | tf_op jit(solution)/shard_map/ppermute | solution.py:29
  19.0 0.0 collective-permute-done.3
  19.0 1.1 %attend.1.after.p0 = bf16[288,128]{1,0:T(8,128)(2,1)S(1)} custom-call(f32[8,5248]{1,0:T(8,128)S(1)} %add_add_fusion.shares, f32[8,128]{1,0:T(8,128)S(1)} %get-tuple-element.37.cosine, f32[8,128]{1,0:T(8,128)S(1)} %get-tuple-element.38.sine, f32[8,128]{1,0:T(8,128)S(1)} %get-tuple-element.17.live_ref, f32[8,128]{1,0:T(8,128)S(1)} %get-tuple-element.18.owns, ...), custom_call_target="tpu_custom_call" | custom-call | tf_op jit(solution)/shard_map/attend/pallas_call | solution.py:381
  20.1 1.5 %collective-permute-start.8 = (bf16[288,128]{1,0:T(8,128)(2,1)S(1)}, bf16[288,128]{1,0:T(8,128)(2,1)S(1)}, u32[]{:S(2)}, u32[]{:S(2)}) collective-permute-start(bf16[288,128]{1,0:T(8,128)(2,1)S(1)} %attend.1.after.p0), channel_id=1, source_target_pairs={{0,32},{1,129},{2,34},{3,131},{4,36},{5,133},{6,38},{7,135},{8,40}... | collective-permute-start | bytes 221192 | tf_op jit(solution)/shard_map/ppermute | solution.py:29
  21.6 0.8 collective-permute-start.7
  22.4 0.4 collective-permute-start.6
  22.8 1.9 %load.5.after.w_ref = bf16[4,256,1536]{2,1,0:T(8,128)(2,1)S(1)} custom-call(bf16[288,128]{1,0:T(8,128)(2,1)S(1)} %attend.1.after.p0, bf16[4,256,1536]{2,1,0:T(8,128)(2,1)} %refs_0_.6), custom_call_target="tpu_custom_call" | custom-call | tf_op jit(solution)/shard_map/load/pallas_call | solution.py:381
  24.7 0.0 copy-start
  24.7 0.1 collective-permute-done.8.p2
  24.9 1.2 %collective-permute-done.7.p3 = bf16[288,128]{1,0:T(8,128)(2,1)S(1)} collective-permute-done((bf16[288,128]{1,0:T(8,128)(2,1)S(1)}, bf16[288,128]{1,0:T(8,128)(2,1)S(1)}, u32[]{:S(2)}, u32[]{:S(2)}) %collective-permute-start.7) | collective-permute-done | bytes 73760 | tf_op jit(solution)/shard_map/ppermute | solution.py:29
  26.1 0.0 collective-permute-done.6.p1
  26.1 0.3 merge.1.p0
  26.4 0.0 copy-start.3
  26.4 1.6 %collective-permute-start.11 = (bf16[288,128]{1,0:T(8,128)(2,1)S(1)}, bf16[288,128]{1,0:T(8,128)(2,1)S(1)}, u32[]{:S(2)}, u32[]{:S(2)}) collective-permute-start(bf16[288,128]{1,0:T(8,128)(2,1)S(1)} %merge.1.p0), channel_id=1, source_target_pairs={{0,128},{1,33},{2,130},{3,35},{4,132},{5,37},{6,134},{7,39},{8,136... | collective-permute-start | bytes 221192 | tf_op jit(solution)/shard_map/ppermute | solution.py:29
  28.0 0.8 collective-permute-start.10
  28.8 0.3 collective-permute-start.9
  29.1 2.3 %collective-permute-done.11.p2 = bf16[288,128]{1,0:T(8,128)(2,1)S(1)} collective-permute-done((bf16[288,128]{1,0:T(8,128)(2,1)S(1)}, bf16[288,128]{1,0:T(8,128)(2,1)S(1)}, u32[]{:S(2)}, u32[]{:S(2)}) %collective-permute-start.11) | collective-permute-done | bytes 73760 | tf_op jit(solution)/shard_map/ppermute | solution.py:29
  31.5 1.0 %collective-permute-done.10.p3 = bf16[288,128]{1,0:T(8,128)(2,1)S(1)} collective-permute-done((bf16[288,128]{1,0:T(8,128)(2,1)S(1)}, bf16[288,128]{1,0:T(8,128)(2,1)S(1)}, u32[]{:S(2)}, u32[]{:S(2)}) %collective-permute-start.10) | collective-permute-done | bytes 73760 | tf_op jit(solution)/shard_map/ppermute | solution.py:29
  32.4 0.0 collective-permute-done.9.p1
  32.4 0.9 %finish.1 = (bf16[8,4096]{1,0:T(8,128)(2,1)S(1)}, bf16[8,256]{1,0:T(8,128)(2,1)S(1)}, bf16[128,256]{1,0:T(8,128)(2,1)S(1)}) custom-call(bf16[288,128]{1,0:T(8,128)(2,1)S(1)} %merge.1.p0, bf16[288,128]{1,0:T(8,128)(2,1)S(1)} %collective-permute-done.9.p1, bf16[288,128]{1,0:T(8,128)(2,1)S(1)} %collective-permute-done.10.p3, ...), custom_call_target="tpu_custom_call" | custom-call | tf_op jit(solution)/shard_map/finish/pallas_call | solution.py:381
  33.4 23.5 %all_to_all.10 = bf16[16,8,256]{2,1,0:T(8,128)(2,1)S(1)} all-to-all(bf16[16,8,256]{2,1,0:T(8,128)(2,1)S(1)} %bitcast.9), channel_id=1, replica_groups=mesh['ctx'=16,'exp'=16] {'exp'}, dimensions={0} | all-to-all | bytes 131072 | tf_op jit(solution)/shard_map/all_to_all | solution.py:503
  56.8 0.6 gate_up.1
  57.4 1.3 %collective-permute-start.12 = (bf16[32,1664]{1,0:T(8,128)(2,1)S(1)}, bf16[32,1664]{1,0:T(8,128)(2,1)S(1)}, u32[]{:S(2)}, u32[]{:S(2)}) collective-permute-start(bf16[32,1664]{1,0:T(8,128)(2,1)S(1)} %get-tuple-element.28), channel_id=1, source_target_pairs={{0,32},{1,129},{2,34},{3,131},{4,36},{5,133},{6,38},{7,135},{8,40}... | collective-permute-start | bytes 319496 | tf_op jit(solution)/shard_map/ppermute | solution.py:29
  58.7 0.8 collective-permute-start.13
  59.5 0.6 collective-permute-start.14
  60.2 1.4 %settle.1 = (bf16[4,768,256]{2,1,0:T(8,128)(2,1)S(1)}, bf16[8,4096]{1,0:T(8,128)(2,1)}) custom-call(bf16[32,1664]{1,0:T(8,128)(2,1)S(1)} %get-tuple-element.23.after.m0, bf16[4,768,256]{2,1,0:T(8,128)(2,1)} %refs_0_.7, bf16[8,4096]{1,0:T(8,128)(2,1)S(1)} %get-tuple-element.24.refs_1_), custom_call_target="tpu_custom_call" | custom-call | tf_op jit(solution)/shard_map/settle/pallas_call | solution.py:516
  61.6 1.2 %collective-permute-done.12.m1 = bf16[32,1664]{1,0:T(8,128)(2,1)S(1)} collective-permute-done((bf16[32,1664]{1,0:T(8,128)(2,1)S(1)}, bf16[32,1664]{1,0:T(8,128)(2,1)S(1)}, u32[]{:S(2)}, u32[]{:S(2)}) %collective-permute-start.12) | collective-permute-done | bytes 106528 | tf_op jit(solution)/shard_map/ppermute | solution.py:29
  62.9 1.1 %collective-permute-done.13.m3 = bf16[32,1664]{1,0:T(8,128)(2,1)S(1)} collective-permute-done((bf16[32,1664]{1,0:T(8,128)(2,1)S(1)}, bf16[32,1664]{1,0:T(8,128)(2,1)S(1)}, u32[]{:S(2)}, u32[]{:S(2)}) %collective-permute-start.13) | collective-permute-done | bytes 106528 | tf_op jit(solution)/shard_map/ppermute | solution.py:29
  64.0 0.0 collective-permute-done.14.m2
  64.0 0.2 add_rows.1.m0
  64.2 0.8 collective-permute-start.17
  65.0 0.8 collective-permute-start.16
  65.8 1.1 %collective-permute-start.15 = (bf16[32,1664]{1,0:T(8,128)(2,1)S(1)}, bf16[32,1664]{1,0:T(8,128)(2,1)S(1)}, u32[]{:S(2)}, u32[]{:S(2)}) collective-permute-start(bf16[32,1664]{1,0:T(8,128)(2,1)S(1)} %add_rows.1.m0), channel_id=1, source_target_pairs={{0,64},{1,17},{2,66},{3,19},{4,68},{5,21},{6,70},{7,23},{8,72},{9,... | collective-permute-start | bytes 319496 | tf_op jit(solution)/shard_map/ppermute | solution.py:29
  66.9 2.5 %collective-permute-done.17.m2 = bf16[32,1664]{1,0:T(8,128)(2,1)S(1)} collective-permute-done((bf16[32,1664]{1,0:T(8,128)(2,1)S(1)}, bf16[32,1664]{1,0:T(8,128)(2,1)S(1)}, u32[]{:S(2)}, u32[]{:S(2)}) %collective-permute-start.17) | collective-permute-done | bytes 106528 | tf_op jit(solution)/shard_map/ppermute | solution.py:29
  69.4 1.4 %collective-permute-done.16.m3 = bf16[32,1664]{1,0:T(8,128)(2,1)S(1)} collective-permute-done((bf16[32,1664]{1,0:T(8,128)(2,1)S(1)}, bf16[32,1664]{1,0:T(8,128)(2,1)S(1)}, u32[]{:S(2)}, u32[]{:S(2)}) %collective-permute-start.16) | collective-permute-done | bytes 106528 | tf_op jit(solution)/shard_map/ppermute | solution.py:29
  70.7 0.0 collective-permute-done.15.m1
  70.7 0.2 activate.1.x0
  70.9 1.4 %collective-permute-start.20 = (bf16[32,768]{1,0:T(8,128)(2,1)S(1)}, bf16[32,768]{1,0:T(8,128)(2,1)S(1)}, u32[]{:S(2)}, u32[]{:S(2)}) collective-permute-start(bf16[32,768]{1,0:T(8,128)(2,1)S(1)} %activate.1.x0), channel_id=1, source_target_pairs={{0,32},{1,129},{2,34},{3,131},{4,36},{5,133},{6,38},{7,135},{8,40}... | collective-permute-start | bytes 147464 | tf_op jit(solution)/shard_map/ppermute | solution.py:29
  72.3 0.9 %collective-permute-start.19 = (bf16[32,768]{1,0:T(8,128)(2,1)S(1)}, bf16[32,768]{1,0:T(8,128)(2,1)S(1)}, u32[]{:S(2)}, u32[]{:S(2)}) collective-permute-start(bf16[32,768]{1,0:T(8,128)(2,1)S(1)} %activate.1.x0), channel_id=1, source_target_pairs={{0,48},{1,193},{2,50},{3,195},{4,52},{5,197},{6,54},{7,199},{8,56}... | collective-permute-start | bytes 147464 | tf_op jit(solution)/shard_map/ppermute | solution.py:29
  73.3 0.4 collective-permute-start.18
  73.7 1.8 %collective-permute-done.20.x2 = bf16[32,768]{1,0:T(8,128)(2,1)S(1)} collective-permute-done((bf16[32,768]{1,0:T(8,128)(2,1)S(1)}, bf16[32,768]{1,0:T(8,128)(2,1)S(1)}, u32[]{:S(2)}, u32[]{:S(2)}) %collective-permute-start.20) | collective-permute-done | bytes 49184 | tf_op jit(solution)/shard_map/ppermute | solution.py:29
  75.5 1.0 %collective-permute-done.19.x3 = bf16[32,768]{1,0:T(8,128)(2,1)S(1)} collective-permute-done((bf16[32,768]{1,0:T(8,128)(2,1)S(1)}, bf16[32,768]{1,0:T(8,128)(2,1)S(1)}, u32[]{:S(2)}, u32[]{:S(2)}) %collective-permute-start.19) | collective-permute-done | bytes 49184 | tf_op jit(solution)/shard_map/ppermute | solution.py:29
  76.5 0.0 collective-permute-done.18.x1
  76.5 0.4 down.1
  76.9 14.3 %all_to_all.11 = bf16[16,8,256]{2,1,0:T(8,128)(2,1)S(1)} all-to-all(bf16[16,8,256]{2,1,0:T(8,128)(2,1)S(1)} %bitcast.7), channel_id=1, replica_groups=mesh['ctx'=16,'exp'=16] {'exp'}, dimensions={0} | all-to-all | bytes 131072 | tf_op jit(solution)/shard_map/all_to_all | solution.py:542
  91.2 0.7 combine.1
  (11 shorter events, 0.1 us)
Async XLA Ops:
  0.6 6.5 %copy-start.4 = (s32[8]{0:T(128)S(1)}, s32[8]{0:T(128)}, u32[]{:S(2)}) copy-start(s32[8]{0:T(128)} %lengths.1) | copy-start | bytes 100
  0.6 6.6 %copy-start.2 = (f32[8,8]{1,0:T(8,128)S(1)}, f32[8,8]{1,0:T(8,128)}, u32[]{:S(2)}) copy-start(f32[8,8]{1,0:T(8,128)} %gates.1) | copy-start | bytes 772
  0.7 6.6 %copy-start.1 = (s32[8,8]{1,0:T(8,128)S(1)}, s32[8,8]{1,0:T(8,128)}, u32[]{:S(2)}) copy-start(s32[8,8]{1,0:T(8,128)} %routes.1) | copy-start | bytes 772
  2.8 6.8 %collective-permute-start.2 = (f16[8,5248]{1,0:T(8,128)(2,1)S(1)}, f16[8,5248]{1,0:T(8,128)(2,1)S(1)}, u32[]{:S(2)}, u32[]{:S(2)}) collective-permute-start(f16[8,5248]{1,0:T(8,128)(2,1)S(1)} %convert_element_type.40), channel_id=1, source_target_pairs={{0,48},{1,193},{2,50},{3,195},{4,52},{5,197},{6,54},{7,199},{8,56}... | collective-permute-start | bytes 251912 | tf_op jit(solution)/shard_map/ppermute | solution.py:29
  6.4 4.8 %collective-permute-start.1 = (f16[8,5248]{1,0:T(8,128)(2,1)S(1)}, f16[8,5248]{1,0:T(8,128)(2,1)S(1)}, u32[]{:S(2)}, u32[]{:S(2)}) collective-permute-start(f16[8,5248]{1,0:T(8,128)(2,1)S(1)} %convert_element_type.40), channel_id=1, source_target_pairs={{0,32},{1,129},{2,34},{3,131},{4,36},{5,133},{6,38},{7,135},{8,40}... | collective-permute-start | bytes 251912 | tf_op jit(solution)/shard_map/ppermute | solution.py:29
  6.8 4.5 %collective-permute-start = (f16[8,5248]{1,0:T(8,128)(2,1)S(1)}, f16[8,5248]{1,0:T(8,128)(2,1)S(1)}, u32[]{:S(2)}, u32[]{:S(2)}) collective-permute-start(f16[8,5248]{1,0:T(8,128)(2,1)S(1)} %convert_element_type.40), channel_id=1, source_target_pairs={{0,16},{1,65},{2,18},{3,67},{4,20},{5,69},{6,22},{7,71},{8,24},{9,... | collective-permute-start | bytes 251912 | tf_op jit(solution)/shard_map/ppermute | solution.py:29
  11.3 5.2 %collective-permute-start.5 = (f16[8,5248]{1,0:T(8,128)(2,1)S(1)}, f16[8,5248]{1,0:T(8,128)(2,1)S(1)}, u32[]{:S(2)}, u32[]{:S(2)}) collective-permute-start(f16[8,5248]{1,0:T(8,128)(2,1)S(1)} %get-tuple-element.32), channel_id=1, source_target_pairs={{0,192},{1,49},{2,194},{3,51},{4,196},{5,53},{6,198},{7,55},{8,200... | collective-permute-start | bytes 251912 | tf_op jit(solution)/shard_map/ppermute | solution.py:29
  14.2 4.8 %collective-permute-start.4 = (f16[8,5248]{1,0:T(8,128)(2,1)S(1)}, f16[8,5248]{1,0:T(8,128)(2,1)S(1)}, u32[]{:S(2)}, u32[]{:S(2)}) collective-permute-start(f16[8,5248]{1,0:T(8,128)(2,1)S(1)} %get-tuple-element.32), channel_id=1, source_target_pairs={{0,128},{1,33},{2,130},{3,35},{4,132},{5,37},{6,134},{7,39},{8,136... | collective-permute-start | bytes 251912 | tf_op jit(solution)/shard_map/ppermute | solution.py:29
  14.4 4.6 %collective-permute-start.3 = (f16[8,5248]{1,0:T(8,128)(2,1)S(1)}, f16[8,5248]{1,0:T(8,128)(2,1)S(1)}, u32[]{:S(2)}, u32[]{:S(2)}) collective-permute-start(f16[8,5248]{1,0:T(8,128)(2,1)S(1)} %get-tuple-element.32), channel_id=1, source_target_pairs={{0,64},{1,17},{2,66},{3,19},{4,68},{5,21},{6,70},{7,23},{8,72},{9,... | collective-permute-start | bytes 251912 | tf_op jit(solution)/shard_map/ppermute | solution.py:29
  20.1 4.8 %collective-permute-start.8 = (bf16[288,128]{1,0:T(8,128)(2,1)S(1)}, bf16[288,128]{1,0:T(8,128)(2,1)S(1)}, u32[]{:S(2)}, u32[]{:S(2)}) collective-permute-start(bf16[288,128]{1,0:T(8,128)(2,1)S(1)} %attend.1.after.p0), channel_id=1, source_target_pairs={{0,32},{1,129},{2,34},{3,131},{4,36},{5,133},{6,38},{7,135},{8,40}... | collective-permute-start | bytes 221192 | tf_op jit(solution)/shard_map/ppermute | solution.py:29
  21.6 4.4 %collective-permute-start.7 = (bf16[288,128]{1,0:T(8,128)(2,1)S(1)}, bf16[288,128]{1,0:T(8,128)(2,1)S(1)}, u32[]{:S(2)}, u32[]{:S(2)}) collective-permute-start(bf16[288,128]{1,0:T(8,128)(2,1)S(1)} %attend.1.after.p0), channel_id=1, source_target_pairs={{0,48},{1,193},{2,50},{3,195},{4,52},{5,197},{6,54},{7,199},{8,56}... | collective-permute-start | bytes 221192 | tf_op jit(solution)/shard_map/ppermute | solution.py:29
  22.4 3.6 %collective-permute-start.6 = (bf16[288,128]{1,0:T(8,128)(2,1)S(1)}, bf16[288,128]{1,0:T(8,128)(2,1)S(1)}, u32[]{:S(2)}, u32[]{:S(2)}) collective-permute-start(bf16[288,128]{1,0:T(8,128)(2,1)S(1)} %attend.1.after.p0), channel_id=1, source_target_pairs={{0,16},{1,65},{2,18},{3,67},{4,20},{5,69},{6,22},{7,71},{8,24},{9,... | collective-permute-start | bytes 221192 | tf_op jit(solution)/shard_map/ppermute | solution.py:29
  24.7 7.7 %copy-start = (bf16[8,256]{1,0:T(8,128)(2,1)S(1)}, bf16[8,256]{1,0:T(8,128)(2,1)}, u32[]{:S(2)}) copy-start(bf16[8,256]{1,0:T(8,128)(2,1)} %tokens.1) | copy-start | bytes 12292
  26.4 30.4 %copy-start.3 = (f32[256]{0:T(256)S(1)}, f32[256]{0:T(256)}, u32[]{:S(2)}) copy-start(f32[256]{0:T(256)} %param.19) | copy-start | bytes 3076
  26.4 5.1 %collective-permute-start.11 = (bf16[288,128]{1,0:T(8,128)(2,1)S(1)}, bf16[288,128]{1,0:T(8,128)(2,1)S(1)}, u32[]{:S(2)}, u32[]{:S(2)}) collective-permute-start(bf16[288,128]{1,0:T(8,128)(2,1)S(1)} %merge.1.p0), channel_id=1, source_target_pairs={{0,128},{1,33},{2,130},{3,35},{4,132},{5,37},{6,134},{7,39},{8,136... | collective-permute-start | bytes 221192 | tf_op jit(solution)/shard_map/ppermute | solution.py:29
  28.0 4.4 %collective-permute-start.10 = (bf16[288,128]{1,0:T(8,128)(2,1)S(1)}, bf16[288,128]{1,0:T(8,128)(2,1)S(1)}, u32[]{:S(2)}, u32[]{:S(2)}) collective-permute-start(bf16[288,128]{1,0:T(8,128)(2,1)S(1)} %merge.1.p0), channel_id=1, source_target_pairs={{0,192},{1,49},{2,194},{3,51},{4,196},{5,53},{6,198},{7,55},{8,200... | collective-permute-start | bytes 221192 | tf_op jit(solution)/shard_map/ppermute | solution.py:29
  28.8 3.6 %collective-permute-start.9 = (bf16[288,128]{1,0:T(8,128)(2,1)S(1)}, bf16[288,128]{1,0:T(8,128)(2,1)S(1)}, u32[]{:S(2)}, u32[]{:S(2)}) collective-permute-start(bf16[288,128]{1,0:T(8,128)(2,1)S(1)} %merge.1.p0), channel_id=1, source_target_pairs={{0,64},{1,17},{2,66},{3,19},{4,68},{5,21},{6,70},{7,23},{8,72},{9,... | collective-permute-start | bytes 221192 | tf_op jit(solution)/shard_map/ppermute | solution.py:29
  57.4 5.4 %collective-permute-start.12 = (bf16[32,1664]{1,0:T(8,128)(2,1)S(1)}, bf16[32,1664]{1,0:T(8,128)(2,1)S(1)}, u32[]{:S(2)}, u32[]{:S(2)}) collective-permute-start(bf16[32,1664]{1,0:T(8,128)(2,1)S(1)} %get-tuple-element.28), channel_id=1, source_target_pairs={{0,32},{1,129},{2,34},{3,131},{4,36},{5,133},{6,38},{7,135},{8,40}... | collective-permute-start | bytes 319496 | tf_op jit(solution)/shard_map/ppermute | solution.py:29
  58.7 5.3 %collective-permute-start.13 = (bf16[32,1664]{1,0:T(8,128)(2,1)S(1)}, bf16[32,1664]{1,0:T(8,128)(2,1)S(1)}, u32[]{:S(2)}, u32[]{:S(2)}) collective-permute-start(bf16[32,1664]{1,0:T(8,128)(2,1)S(1)} %get-tuple-element.29), channel_id=1, source_target_pairs={{0,48},{1,193},{2,50},{3,195},{4,52},{5,197},{6,54},{7,199},{8,56}... | collective-permute-start | bytes 319496 | tf_op jit(solution)/shard_map/ppermute | solution.py:29
  59.5 4.5 %collective-permute-start.14 = (bf16[32,1664]{1,0:T(8,128)(2,1)S(1)}, bf16[32,1664]{1,0:T(8,128)(2,1)S(1)}, u32[]{:S(2)}, u32[]{:S(2)}) collective-permute-start(bf16[32,1664]{1,0:T(8,128)(2,1)S(1)} %get-tuple-element.30), channel_id=1, source_target_pairs={{0,16},{1,65},{2,18},{3,67},{4,20},{5,69},{6,22},{7,71},{8,24},{9,... | collective-permute-start | bytes 319496 | tf_op jit(solution)/shard_map/ppermute | solution.py:29
  64.2 5.2 %collective-permute-start.17 = (bf16[32,1664]{1,0:T(8,128)(2,1)S(1)}, bf16[32,1664]{1,0:T(8,128)(2,1)S(1)}, u32[]{:S(2)}, u32[]{:S(2)}) collective-permute-start(bf16[32,1664]{1,0:T(8,128)(2,1)S(1)} %add_rows.1.m0), channel_id=1, source_target_pairs={{0,128},{1,33},{2,130},{3,35},{4,132},{5,37},{6,134},{7,39},{8,136... | collective-permute-start | bytes 319496 | tf_op jit(solution)/shard_map/ppermute | solution.py:29
  65.0 5.7 %collective-permute-start.16 = (bf16[32,1664]{1,0:T(8,128)(2,1)S(1)}, bf16[32,1664]{1,0:T(8,128)(2,1)S(1)}, u32[]{:S(2)}, u32[]{:S(2)}) collective-permute-start(bf16[32,1664]{1,0:T(8,128)(2,1)S(1)} %add_rows.1.m0), channel_id=1, source_target_pairs={{0,192},{1,49},{2,194},{3,51},{4,196},{5,53},{6,198},{7,55},{8,200... | collective-permute-start | bytes 319496 | tf_op jit(solution)/shard_map/ppermute | solution.py:29
  65.8 4.9 %collective-permute-start.15 = (bf16[32,1664]{1,0:T(8,128)(2,1)S(1)}, bf16[32,1664]{1,0:T(8,128)(2,1)S(1)}, u32[]{:S(2)}, u32[]{:S(2)}) collective-permute-start(bf16[32,1664]{1,0:T(8,128)(2,1)S(1)} %add_rows.1.m0), channel_id=1, source_target_pairs={{0,64},{1,17},{2,66},{3,19},{4,68},{5,21},{6,70},{7,23},{8,72},{9,... | collective-permute-start | bytes 319496 | tf_op jit(solution)/shard_map/ppermute | solution.py:29
  70.9 4.5 %collective-permute-start.20 = (bf16[32,768]{1,0:T(8,128)(2,1)S(1)}, bf16[32,768]{1,0:T(8,128)(2,1)S(1)}, u32[]{:S(2)}, u32[]{:S(2)}) collective-permute-start(bf16[32,768]{1,0:T(8,128)(2,1)S(1)} %activate.1.x0), channel_id=1, source_target_pairs={{0,32},{1,129},{2,34},{3,131},{4,36},{5,133},{6,38},{7,135},{8,40}... | collective-permute-start | bytes 147464 | tf_op jit(solution)/shard_map/ppermute | solution.py:29
  72.3 4.2 %collective-permute-start.19 = (bf16[32,768]{1,0:T(8,128)(2,1)S(1)}, bf16[32,768]{1,0:T(8,128)(2,1)S(1)}, u32[]{:S(2)}, u32[]{:S(2)}) collective-permute-start(bf16[32,768]{1,0:T(8,128)(2,1)S(1)} %activate.1.x0), channel_id=1, source_target_pairs={{0,48},{1,193},{2,50},{3,195},{4,52},{5,197},{6,54},{7,199},{8,56}... | collective-permute-start | bytes 147464 | tf_op jit(solution)/shard_map/ppermute | solution.py:29
  73.3 3.2 %collective-permute-start.18 = (bf16[32,768]{1,0:T(8,128)(2,1)S(1)}, bf16[32,768]{1,0:T(8,128)(2,1)S(1)}, u32[]{:S(2)}, u32[]{:S(2)}) collective-permute-start(bf16[32,768]{1,0:T(8,128)(2,1)S(1)} %activate.1.x0), channel_id=1, source_target_pairs={{0,16},{1,65},{2,18},{3,67},{4,20},{5,69},{6,22},{7,71},{8,24},{9,... | collective-permute-start | bytes 147464 | tf_op jit(solution)/shard_map/ppermute | solution.py:29

commit v7 on v6

--- a/solution.py
+++ b/solution.py
@@ -65,7 +65,7 @@
 
 def added(arrays):
     own, one, three, two = (a.astype(jnp.float32) for a in arrays)
-    return (own + one) + (two + three)
+    return (own + one) + (three + two)
 
 
 def prepare_kernel(lengths, routes, gates, after, live, owns, placing, weighting):

time: 92.2 us -> 91.8 us (level)
  blocking collectives: 37.8 us -> 35.9 us
    all_to_all x1, blocking collectives: 23.5 us -> 21.5 us  [local(): lax.all_to_all(outgoing.reshape(n_exp, per_source, slice_width), 'exp', s...]
  transfers between devices with their start and end apart: 21 -> 21, of which waited for: 12 -> 13; matrix products, arithmetic and copies ran while one was open for 0% -> 0% of each run, Pallas kernels for 8% -> 8%
where the time goes in v7:
time: 91.8 us; the launch traced here: 91.5 us
  blocking collectives  35.9 us (39%)
  starting transfers between devices  22.1 us (24%)
  waiting for transfers between devices  18.6 us (20%)
  Pallas kernels  13.8 us (15%)
    ppermute x21, starting transfers between devices, exchange(): got[step] = lax.ppermute(sent, AXES, pairs)  22.1 us
    all_to_all x1, blocking collectives, local(): lax.all_to_all(outgoing.reshape(n_exp, per_source, slice_width), 'exp', s...  21.5 us
    ppermute x21, waiting for transfers between devices, exchange(): got[step] = lax.ppermute(sent, AXES, pairs)  18.6 us
    all_to_all x1, blocking collectives, local(): lax.all_to_all(expert_out.reshape(n_exp, per_source, slice_width), 'exp',...  14.4 us
    pallas_call x13, Pallas kernels, call(): pl.pallas_call(kernel, out_shape=out, in_specs=specs, out_specs=jax.tree....  12.3 us
  transfers between devices with their start and end apart: 21, of which 13 were waited for; matrix products, arithmetic and copies ran while one was open for 0% of the time, Pallas kernels for 8%

profile of v7, /device:TPU:1, one launch (start us, length us, event | category | flops | bytes accessed | tf_op | source)
XLA Modules:
  0.0 91.5 jit_solution(14556979025431707501)
XLA Ops:
  0.6 0.0 copy-start.4
  0.7 2.1 %project.1.after = f32[8,5248]{1,0:T(8,128)S(1)} custom-call(bf16[8,256]{1,0:T(8,128)(2,1)} %tokens.1, f32[1,256]{1,0:T(1,128)} %bitcast.11, bf16[256,5120]{1,0:T(8,128)(2,1)} %w_hbm.1), custom_call_target="tpu_custom_call" | custom-call | tf_op jit(solution)/shard_map/project/pallas_call | solution.py:381
  2.8 3.8 %collective-permute-start.2 = (f16[8,5248]{1,0:T(8,128)(2,1)S(1)}, f16[8,5248]{1,0:T(8,128)(2,1)S(1)}, u32[]{:S(2)}, u32[]{:S(2)}) collective-permute-start(f16[8,5248]{1,0:T(8,128)(2,1)S(1)} %convert_element_type.40), channel_id=1, source_target_pairs={{0,32},{1,129},{2,34},{3,131},{4,36},{5,133},{6,38},{7,135},{8,40}... | collective-permute-start | bytes 251912 | tf_op jit(solution)/shard_map/ppermute | solution.py:29
  6.6 0.8 collective-permute-start.1
  7.4 0.0 collective-permute-start
  7.4 0.1 fusion
  7.5 0.7 prepare.1
  8.3 1.6 %load.3 = (bf16[8,128,512]{2,1,0:T(8,128)(2,1)S(1)}, bf16[8,128,512]{2,1,0:T(8,128)(2,1)S(1)}) custom-call(f32[8,5248]{1,0:T(8,128)S(1)} %project.1.after, bf16[8,128,512]{2,1,0:T(8,128)(2,1)} %refs_0_.4, bf16[8,128,512]{2,1,0:T(8,128)(2,1)} %refs_1_.1), custom_call_target="tpu_custom_call" | custom-call | tf_op jit(solution)/shard_map/load/pallas_call | solution.py:381
  9.8 0.0 collective-permute-done.2
  9.8 1.6 %collective-permute-done.1 = f16[8,5248]{1,0:T(8,128)(2,1)S(1)} collective-permute-done((f16[8,5248]{1,0:T(8,128)(2,1)S(1)}, f16[8,5248]{1,0:T(8,128)(2,1)S(1)}, u32[]{:S(2)}, u32[]{:S(2)}) %collective-permute-start.1) | collective-permute-done | bytes 84000 | tf_op jit(solution)/shard_map/ppermute | solution.py:29
  11.4 0.0 collective-permute-done
  11.4 0.1 fusion.1
  11.5 2.5 %collective-permute-start.5 = (f16[8,5248]{1,0:T(8,128)(2,1)S(1)}, f16[8,5248]{1,0:T(8,128)(2,1)S(1)}, u32[]{:S(2)}, u32[]{:S(2)}) collective-permute-start(f16[8,5248]{1,0:T(8,128)(2,1)S(1)} %get-tuple-element.32), channel_id=1, source_target_pairs={{0,128},{1,33},{2,130},{3,35},{4,132},{5,37},{6,134},{7,39},{8,136... | collective-permute-start | bytes 251912 | tf_op jit(solution)/shard_map/ppermute | solution.py:29
  14.0 0.9 collective-permute-start.4
  14.9 0.0 collective-permute-start.3
  14.9 0.1 pad_maximum_fusion
  15.0 1.6 %load.4.after.w_ref = bf16[4096,256]{1,0:T(8,128)(2,1)S(1)} custom-call(f32[8,5248]{1,0:T(8,128)S(1)} %get-tuple-element.33.after, bf16[4096,256]{1,0:T(8,128)(2,1)} %refs_0_.5), custom_call_target="tpu_custom_call" | custom-call | tf_op jit(solution)/shard_map/load/pallas_call | solution.py:381
  16.6 0.0 collective-permute-done.5
  16.6 2.2 %collective-permute-done.4 = f16[8,5248]{1,0:T(8,128)(2,1)S(1)} collective-permute-done((f16[8,5248]{1,0:T(8,128)(2,1)S(1)}, f16[8,5248]{1,0:T(8,128)(2,1)S(1)}, u32[]{:S(2)}, u32[]{:S(2)}) %collective-permute-start.4) | collective-permute-done | bytes 84000 | tf_op jit(solution)/shard_map/ppermute | solution.py:29
  18.8 0.0 collective-permute-done.3
  18.8 1.1 %attend.1.after.p0 = bf16[288,128]{1,0:T(8,128)(2,1)S(1)} custom-call(f32[8,5248]{1,0:T(8,128)S(1)} %add_add_fusion.shares, f32[8,128]{1,0:T(8,128)S(1)} %get-tuple-element.37.cosine, f32[8,128]{1,0:T(8,128)S(1)} %get-tuple-element.38.sine, f32[8,128]{1,0:T(8,128)S(1)} %get-tuple-element.17.live_ref, f32[8,128]{1,0:T(8,128)S(1)} %get-tuple-element.18.owns, ...), custom_call_target="tpu_custom_call" | custom-call | tf_op jit(solution)/shard_map/attend/pallas_call | solution.py:381
  19.9 1.6 %collective-permute-start.8 = (bf16[288,128]{1,0:T(8,128)(2,1)S(1)}, bf16[288,128]{1,0:T(8,128)(2,1)S(1)}, u32[]{:S(2)}, u32[]{:S(2)}) collective-permute-start(bf16[288,128]{1,0:T(8,128)(2,1)S(1)} %attend.1.after.p0), channel_id=1, source_target_pairs={{0,32},{1,129},{2,34},{3,131},{4,36},{5,133},{6,38},{7,135},{8,40}... | collective-permute-start | bytes 221192 | tf_op jit(solution)/shard_map/ppermute | solution.py:29
  21.6 0.8 collective-permute-start.7
  22.3 0.3 collective-permute-start.6
  22.6 1.9 %load.5.after.w_ref = bf16[4,256,1536]{2,1,0:T(8,128)(2,1)S(1)} custom-call(bf16[288,128]{1,0:T(8,128)(2,1)S(1)} %attend.1.after.p0, bf16[4,256,1536]{2,1,0:T(8,128)(2,1)} %refs_0_.6), custom_call_target="tpu_custom_call" | custom-call | tf_op jit(solution)/shard_map/load/pallas_call | solution.py:381
  24.5 0.0 copy-start
  24.5 0.1 collective-permute-done.8.p2
  24.7 1.3 %collective-permute-done.7.p3 = bf16[288,128]{1,0:T(8,128)(2,1)S(1)} collective-permute-done((bf16[288,128]{1,0:T(8,128)(2,1)S(1)}, bf16[288,128]{1,0:T(8,128)(2,1)S(1)}, u32[]{:S(2)}, u32[]{:S(2)}) %collective-permute-start.7) | collective-permute-done | bytes 73760 | tf_op jit(solution)/shard_map/ppermute | solution.py:29
  26.0 0.0 collective-permute-done.6.p1
  26.0 0.3 merge.1.p0
  26.3 0.0 copy-start.3
  26.3 1.6 %collective-permute-start.11 = (bf16[288,128]{1,0:T(8,128)(2,1)S(1)}, bf16[288,128]{1,0:T(8,128)(2,1)S(1)}, u32[]{:S(2)}, u32[]{:S(2)}) collective-permute-start(bf16[288,128]{1,0:T(8,128)(2,1)S(1)} %merge.1.p0), channel_id=1, source_target_pairs={{0,128},{1,33},{2,130},{3,35},{4,132},{5,37},{6,134},{7,39},{8,136... | collective-permute-start | bytes 221192 | tf_op jit(solution)/shard_map/ppermute | solution.py:29
  27.9 0.9 collective-permute-start.10
  28.8 0.3 collective-permute-start.9
  29.1 2.8 %collective-permute-done.11.p2 = bf16[288,128]{1,0:T(8,128)(2,1)S(1)} collective-permute-done((bf16[288,128]{1,0:T(8,128)(2,1)S(1)}, bf16[288,128]{1,0:T(8,128)(2,1)S(1)}, u32[]{:S(2)}, u32[]{:S(2)}) %collective-permute-start.11) | collective-permute-done | bytes 73760 | tf_op jit(solution)/shard_map/ppermute | solution.py:29
  31.9 0.6 collective-permute-done.10.p3
  32.5 0.0 collective-permute-done.9.p1
  32.5 0.9 %finish.1 = (bf16[8,4096]{1,0:T(8,128)(2,1)S(1)}, bf16[8,256]{1,0:T(8,128)(2,1)S(1)}, bf16[128,256]{1,0:T(8,128)(2,1)S(1)}) custom-call(bf16[288,128]{1,0:T(8,128)(2,1)S(1)} %merge.1.p0, bf16[288,128]{1,0:T(8,128)(2,1)S(1)} %collective-permute-done.9.p1, bf16[288,128]{1,0:T(8,128)(2,1)S(1)} %collective-permute-done.10.p3, ...), custom_call_target="tpu_custom_call" | custom-call | tf_op jit(solution)/shard_map/finish/pallas_call | solution.py:381
  33.4 21.5 %all_to_all.10 = bf16[16,8,256]{2,1,0:T(8,128)(2,1)S(1)} all-to-all(bf16[16,8,256]{2,1,0:T(8,128)(2,1)S(1)} %bitcast.9), channel_id=1, replica_groups=mesh['ctx'=16,'exp'=16] {'exp'}, dimensions={0} | all-to-all | bytes 131072 | tf_op jit(solution)/shard_map/all_to_all | solution.py:503
  54.9 0.6 gate_up.1
  55.5 2.2 %collective-permute-start.12 = (bf16[32,1664]{1,0:T(8,128)(2,1)S(1)}, bf16[32,1664]{1,0:T(8,128)(2,1)S(1)}, u32[]{:S(2)}, u32[]{:S(2)}) collective-permute-start(bf16[32,1664]{1,0:T(8,128)(2,1)S(1)} %get-tuple-element.28), channel_id=1, source_target_pairs={{0,32},{1,129},{2,34},{3,131},{4,36},{5,133},{6,38},{7,135},{8,40}... | collective-permute-start | bytes 319496 | tf_op jit(solution)/shard_map/ppermute | solution.py:29
  57.6 0.8 collective-permute-start.13
  58.4 0.0 collective-permute-start.14
  58.4 1.4 %settle.1 = (bf16[4,768,256]{2,1,0:T(8,128)(2,1)S(1)}, bf16[8,4096]{1,0:T(8,128)(2,1)}) custom-call(bf16[32,1664]{1,0:T(8,128)(2,1)S(1)} %get-tuple-element.23.after.m0, bf16[4,768,256]{2,1,0:T(8,128)(2,1)} %refs_0_.7, bf16[8,4096]{1,0:T(8,128)(2,1)S(1)} %get-tuple-element.24.refs_1_), custom_call_target="tpu_custom_call" | custom-call | tf_op jit(solution)/shard_map/settle/pallas_call | solution.py:516
  59.9 1.0 %collective-permute-done.12.m1 = bf16[32,1664]{1,0:T(8,128)(2,1)S(1)} collective-permute-done((bf16[32,1664]{1,0:T(8,128)(2,1)S(1)}, bf16[32,1664]{1,0:T(8,128)(2,1)S(1)}, u32[]{:S(2)}, u32[]{:S(2)}) %collective-permute-start.12) | collective-permute-done | bytes 106528 | tf_op jit(solution)/shard_map/ppermute | solution.py:29
  60.9 1.5 %collective-permute-done.13.m3 = bf16[32,1664]{1,0:T(8,128)(2,1)S(1)} collective-permute-done((bf16[32,1664]{1,0:T(8,128)(2,1)S(1)}, bf16[32,1664]{1,0:T(8,128)(2,1)S(1)}, u32[]{:S(2)}, u32[]{:S(2)}) %collective-permute-start.13) | collective-permute-done | bytes 106528 | tf_op jit(solution)/shard_map/ppermute | solution.py:29
  62.4 0.0 collective-permute-done.14.m2
  62.4 0.2 add_rows.1.m0
  62.6 2.5 %collective-permute-start.17 = (bf16[32,1664]{1,0:T(8,128)(2,1)S(1)}, bf16[32,1664]{1,0:T(8,128)(2,1)S(1)}, u32[]{:S(2)}, u32[]{:S(2)}) collective-permute-start(bf16[32,1664]{1,0:T(8,128)(2,1)S(1)} %add_rows.1.m0), channel_id=1, source_target_pairs={{0,128},{1,33},{2,130},{3,35},{4,132},{5,37},{6,134},{7,39},{8,136... | collective-permute-start | bytes 319496 | tf_op jit(solution)/shard_map/ppermute | solution.py:29
  65.1 0.4 collective-permute-start.16
  65.6 0.1 collective-permute-start.15
  65.6 2.1 %collective-permute-done.17.m2 = bf16[32,1664]{1,0:T(8,128)(2,1)S(1)} collective-permute-done((bf16[32,1664]{1,0:T(8,128)(2,1)S(1)}, bf16[32,1664]{1,0:T(8,128)(2,1)S(1)}, u32[]{:S(2)}, u32[]{:S(2)}) %collective-permute-start.17) | collective-permute-done | bytes 106528 | tf_op jit(solution)/shard_map/ppermute | solution.py:29
  67.7 2.5 %collective-permute-done.16.m3 = bf16[32,1664]{1,0:T(8,128)(2,1)S(1)} collective-permute-done((bf16[32,1664]{1,0:T(8,128)(2,1)S(1)}, bf16[32,1664]{1,0:T(8,128)(2,1)S(1)}, u32[]{:S(2)}, u32[]{:S(2)}) %collective-permute-start.16) | collective-permute-done | bytes 106528 | tf_op jit(solution)/shard_map/ppermute | solution.py:29
  70.2 0.0 collective-permute-done.15.m1
  70.2 0.2 activate.1.x0
  70.4 1.3 %collective-permute-start.20 = (bf16[32,768]{1,0:T(8,128)(2,1)S(1)}, bf16[32,768]{1,0:T(8,128)(2,1)S(1)}, u32[]{:S(2)}, u32[]{:S(2)}) collective-permute-start(bf16[32,768]{1,0:T(8,128)(2,1)S(1)} %activate.1.x0), channel_id=1, source_target_pairs={{0,32},{1,129},{2,34},{3,131},{4,36},{5,133},{6,38},{7,135},{8,40}... | collective-permute-start | bytes 147464 | tf_op jit(solution)/shard_map/ppermute | solution.py:29
  71.7 1.3 %collective-permute-start.19 = (bf16[32,768]{1,0:T(8,128)(2,1)S(1)}, bf16[32,768]{1,0:T(8,128)(2,1)S(1)}, u32[]{:S(2)}, u32[]{:S(2)}) collective-permute-start(bf16[32,768]{1,0:T(8,128)(2,1)S(1)} %activate.1.x0), channel_id=1, source_target_pairs={{0,48},{1,193},{2,50},{3,195},{4,52},{5,197},{6,54},{7,199},{8,56}... | collective-permute-start | bytes 147464 | tf_op jit(solution)/shard_map/ppermute | solution.py:29
  73.0 0.2 collective-permute-start.18
  73.1 1.8 %collective-permute-done.20.x2 = bf16[32,768]{1,0:T(8,128)(2,1)S(1)} collective-permute-done((bf16[32,768]{1,0:T(8,128)(2,1)S(1)}, bf16[32,768]{1,0:T(8,128)(2,1)S(1)}, u32[]{:S(2)}, u32[]{:S(2)}) %collective-permute-start.20) | collective-permute-done | bytes 49184 | tf_op jit(solution)/shard_map/ppermute | solution.py:29
  74.9 0.9 %collective-permute-done.19.x3 = bf16[32,768]{1,0:T(8,128)(2,1)S(1)} collective-permute-done((bf16[32,768]{1,0:T(8,128)(2,1)S(1)}, bf16[32,768]{1,0:T(8,128)(2,1)S(1)}, u32[]{:S(2)}, u32[]{:S(2)}) %collective-permute-start.19) | collective-permute-done | bytes 49184 | tf_op jit(solution)/shard_map/ppermute | solution.py:29
  75.9 0.1 collective-permute-done.18.x1
  75.9 0.4 down.1
  76.3 14.4 %all_to_all.11 = bf16[16,8,256]{2,1,0:T(8,128)(2,1)S(1)} all-to-all(bf16[16,8,256]{2,1,0:T(8,128)(2,1)S(1)} %bitcast.7), channel_id=1, replica_groups=mesh['ctx'=16,'exp'=16] {'exp'}, dimensions={0} | all-to-all | bytes 131072 | tf_op jit(solution)/shard_map/all_to_all | solution.py:542
  90.8 0.7 combine.1
  (11 shorter events, 0.1 us)
Async XLA Ops:
  0.6 6.8 %copy-start.4 = (s32[8]{0:T(128)S(1)}, s32[8]{0:T(128)}, u32[]{:S(2)}) copy-start(s32[8]{0:T(128)} %lengths.1) | copy-start | bytes 100
  0.6 6.9 %copy-start.2 = (f32[8,8]{1,0:T(8,128)S(1)}, f32[8,8]{1,0:T(8,128)}, u32[]{:S(2)}) copy-start(f32[8,8]{1,0:T(8,128)} %gates.1) | copy-start | bytes 772
  0.7 6.9 %copy-start.1 = (s32[8,8]{1,0:T(8,128)S(1)}, s32[8,8]{1,0:T(8,128)}, u32[]{:S(2)}) copy-start(s32[8,8]{1,0:T(8,128)} %routes.1) | copy-start | bytes 772
  2.8 7.1 %collective-permute-start.2 = (f16[8,5248]{1,0:T(8,128)(2,1)S(1)}, f16[8,5248]{1,0:T(8,128)(2,1)S(1)}, u32[]{:S(2)}, u32[]{:S(2)}) collective-permute-start(f16[8,5248]{1,0:T(8,128)(2,1)S(1)} %convert_element_type.40), channel_id=1, source_target_pairs={{0,32},{1,129},{2,34},{3,131},{4,36},{5,133},{6,38},{7,135},{8,40}... | collective-permute-start | bytes 251912 | tf_op jit(solution)/shard_map/ppermute | solution.py:29
  6.6 4.8 %collective-permute-start.1 = (f16[8,5248]{1,0:T(8,128)(2,1)S(1)}, f16[8,5248]{1,0:T(8,128)(2,1)S(1)}, u32[]{:S(2)}, u32[]{:S(2)}) collective-permute-start(f16[8,5248]{1,0:T(8,128)(2,1)S(1)} %convert_element_type.40), channel_id=1, source_target_pairs={{0,48},{1,193},{2,50},{3,195},{4,52},{5,197},{6,54},{7,199},{8,56}... | collective-permute-start | bytes 251912 | tf_op jit(solution)/shard_map/ppermute | solution.py:29
  7.4 4.0 %collective-permute-start = (f16[8,5248]{1,0:T(8,128)(2,1)S(1)}, f16[8,5248]{1,0:T(8,128)(2,1)S(1)}, u32[]{:S(2)}, u32[]{:S(2)}) collective-permute-start(f16[8,5248]{1,0:T(8,128)(2,1)S(1)} %convert_element_type.40), channel_id=1, source_target_pairs={{0,16},{1,65},{2,18},{3,67},{4,20},{5,69},{6,22},{7,71},{8,24},{9,... | collective-permute-start | bytes 251912 | tf_op jit(solution)/shard_map/ppermute | solution.py:29
  11.5 5.1 %collective-permute-start.5 = (f16[8,5248]{1,0:T(8,128)(2,1)S(1)}, f16[8,5248]{1,0:T(8,128)(2,1)S(1)}, u32[]{:S(2)}, u32[]{:S(2)}) collective-permute-start(f16[8,5248]{1,0:T(8,128)(2,1)S(1)} %get-tuple-element.32), channel_id=1, source_target_pairs={{0,128},{1,33},{2,130},{3,35},{4,132},{5,37},{6,134},{7,39},{8,136... | collective-permute-start | bytes 251912 | tf_op jit(solution)/shard_map/ppermute | solution.py:29
  14.0 4.8 %collective-permute-start.4 = (f16[8,5248]{1,0:T(8,128)(2,1)S(1)}, f16[8,5248]{1,0:T(8,128)(2,1)S(1)}, u32[]{:S(2)}, u32[]{:S(2)}) collective-permute-start(f16[8,5248]{1,0:T(8,128)(2,1)S(1)} %get-tuple-element.32), channel_id=1, source_target_pairs={{0,192},{1,49},{2,194},{3,51},{4,196},{5,53},{6,198},{7,55},{8,200... | collective-permute-start | bytes 251912 | tf_op jit(solution)/shard_map/ppermute | solution.py:29
  14.9 3.9 %collective-permute-start.3 = (f16[8,5248]{1,0:T(8,128)(2,1)S(1)}, f16[8,5248]{1,0:T(8,128)(2,1)S(1)}, u32[]{:S(2)}, u32[]{:S(2)}) collective-permute-start(f16[8,5248]{1,0:T(8,128)(2,1)S(1)} %get-tuple-element.32), channel_id=1, source_target_pairs={{0,64},{1,17},{2,66},{3,19},{4,68},{5,21},{6,70},{7,23},{8,72},{9,... | collective-permute-start | bytes 251912 | tf_op jit(solution)/shard_map/ppermute | solution.py:29
  19.9 4.8 %collective-permute-start.8 = (bf16[288,128]{1,0:T(8,128)(2,1)S(1)}, bf16[288,128]{1,0:T(8,128)(2,1)S(1)}, u32[]{:S(2)}, u32[]{:S(2)}) collective-permute-start(bf16[288,128]{1,0:T(8,128)(2,1)S(1)} %attend.1.after.p0), channel_id=1, source_target_pairs={{0,32},{1,129},{2,34},{3,131},{4,36},{5,133},{6,38},{7,135},{8,40}... | collective-permute-start | bytes 221192 | tf_op jit(solution)/shard_map/ppermute | solution.py:29
  21.6 4.4 %collective-permute-start.7 = (bf16[288,128]{1,0:T(8,128)(2,1)S(1)}, bf16[288,128]{1,0:T(8,128)(2,1)S(1)}, u32[]{:S(2)}, u32[]{:S(2)}) collective-permute-start(bf16[288,128]{1,0:T(8,128)(2,1)S(1)} %attend.1.after.p0), channel_id=1, source_target_pairs={{0,48},{1,193},{2,50},{3,195},{4,52},{5,197},{6,54},{7,199},{8,56}... | collective-permute-start | bytes 221192 | tf_op jit(solution)/shard_map/ppermute | solution.py:29
  22.3 3.6 %collective-permute-start.6 = (bf16[288,128]{1,0:T(8,128)(2,1)S(1)}, bf16[288,128]{1,0:T(8,128)(2,1)S(1)}, u32[]{:S(2)}, u32[]{:S(2)}) collective-permute-start(bf16[288,128]{1,0:T(8,128)(2,1)S(1)} %attend.1.after.p0), channel_id=1, source_target_pairs={{0,16},{1,65},{2,18},{3,67},{4,20},{5,69},{6,22},{7,71},{8,24},{9,... | collective-permute-start | bytes 221192 | tf_op jit(solution)/shard_map/ppermute | solution.py:29
  24.5 8.0 %copy-start = (bf16[8,256]{1,0:T(8,128)(2,1)S(1)}, bf16[8,256]{1,0:T(8,128)(2,1)}, u32[]{:S(2)}) copy-start(bf16[8,256]{1,0:T(8,128)(2,1)} %tokens.1) | copy-start | bytes 12292
  26.3 28.6 %copy-start.3 = (f32[256]{0:T(256)S(1)}, f32[256]{0:T(256)}, u32[]{:S(2)}) copy-start(f32[256]{0:T(256)} %param.19) | copy-start | bytes 3076
  26.3 5.6 %collective-permute-start.11 = (bf16[288,128]{1,0:T(8,128)(2,1)S(1)}, bf16[288,128]{1,0:T(8,128)(2,1)S(1)}, u32[]{:S(2)}, u32[]{:S(2)}) collective-permute-start(bf16[288,128]{1,0:T(8,128)(2,1)S(1)} %merge.1.p0), channel_id=1, source_target_pairs={{0,128},{1,33},{2,130},{3,35},{4,132},{5,37},{6,134},{7,39},{8,136... | collective-permute-start | bytes 221192 | tf_op jit(solution)/shard_map/ppermute | solution.py:29
  27.9 4.6 %collective-permute-start.10 = (bf16[288,128]{1,0:T(8,128)(2,1)S(1)}, bf16[288,128]{1,0:T(8,128)(2,1)S(1)}, u32[]{:S(2)}, u32[]{:S(2)}) collective-permute-start(bf16[288,128]{1,0:T(8,128)(2,1)S(1)} %merge.1.p0), channel_id=1, source_target_pairs={{0,192},{1,49},{2,194},{3,51},{4,196},{5,53},{6,198},{7,55},{8,200... | collective-permute-start | bytes 221192 | tf_op jit(solution)/shard_map/ppermute | solution.py:29
  28.8 3.7 %collective-permute-start.9 = (bf16[288,128]{1,0:T(8,128)(2,1)S(1)}, bf16[288,128]{1,0:T(8,128)(2,1)S(1)}, u32[]{:S(2)}, u32[]{:S(2)}) collective-permute-start(bf16[288,128]{1,0:T(8,128)(2,1)S(1)} %merge.1.p0), channel_id=1, source_target_pairs={{0,64},{1,17},{2,66},{3,19},{4,68},{5,21},{6,70},{7,23},{8,72},{9,... | collective-permute-start | bytes 221192 | tf_op jit(solution)/shard_map/ppermute | solution.py:29
  55.5 5.4 %collective-permute-start.12 = (bf16[32,1664]{1,0:T(8,128)(2,1)S(1)}, bf16[32,1664]{1,0:T(8,128)(2,1)S(1)}, u32[]{:S(2)}, u32[]{:S(2)}) collective-permute-start(bf16[32,1664]{1,0:T(8,128)(2,1)S(1)} %get-tuple-element.28), channel_id=1, source_target_pairs={{0,32},{1,129},{2,34},{3,131},{4,36},{5,133},{6,38},{7,135},{8,40}... | collective-permute-start | bytes 319496 | tf_op jit(solution)/shard_map/ppermute | solution.py:29
  57.6 4.8 %collective-permute-start.13 = (bf16[32,1664]{1,0:T(8,128)(2,1)S(1)}, bf16[32,1664]{1,0:T(8,128)(2,1)S(1)}, u32[]{:S(2)}, u32[]{:S(2)}) collective-permute-start(bf16[32,1664]{1,0:T(8,128)(2,1)S(1)} %get-tuple-element.29), channel_id=1, source_target_pairs={{0,48},{1,193},{2,50},{3,195},{4,52},{5,197},{6,54},{7,199},{8,56}... | collective-permute-start | bytes 319496 | tf_op jit(solution)/shard_map/ppermute | solution.py:29
  58.4 4.0 %collective-permute-start.14 = (bf16[32,1664]{1,0:T(8,128)(2,1)S(1)}, bf16[32,1664]{1,0:T(8,128)(2,1)S(1)}, u32[]{:S(2)}, u32[]{:S(2)}) collective-permute-start(bf16[32,1664]{1,0:T(8,128)(2,1)S(1)} %get-tuple-element.30), channel_id=1, source_target_pairs={{0,16},{1,65},{2,18},{3,67},{4,20},{5,69},{6,22},{7,71},{8,24},{9,... | collective-permute-start | bytes 319496 | tf_op jit(solution)/shard_map/ppermute | solution.py:29
  62.6 5.1 %collective-permute-start.17 = (bf16[32,1664]{1,0:T(8,128)(2,1)S(1)}, bf16[32,1664]{1,0:T(8,128)(2,1)S(1)}, u32[]{:S(2)}, u32[]{:S(2)}) collective-permute-start(bf16[32,1664]{1,0:T(8,128)(2,1)S(1)} %add_rows.1.m0), channel_id=1, source_target_pairs={{0,128},{1,33},{2,130},{3,35},{4,132},{5,37},{6,134},{7,39},{8,136... | collective-permute-start | bytes 319496 | tf_op jit(solution)/shard_map/ppermute | solution.py:29
  65.1 5.1 %collective-permute-start.16 = (bf16[32,1664]{1,0:T(8,128)(2,1)S(1)}, bf16[32,1664]{1,0:T(8,128)(2,1)S(1)}, u32[]{:S(2)}, u32[]{:S(2)}) collective-permute-start(bf16[32,1664]{1,0:T(8,128)(2,1)S(1)} %add_rows.1.m0), channel_id=1, source_target_pairs={{0,192},{1,49},{2,194},{3,51},{4,196},{5,53},{6,198},{7,55},{8,200... | collective-permute-start | bytes 319496 | tf_op jit(solution)/shard_map/ppermute | solution.py:29
  65.6 4.6 %collective-permute-start.15 = (bf16[32,1664]{1,0:T(8,128)(2,1)S(1)}, bf16[32,1664]{1,0:T(8,128)(2,1)S(1)}, u32[]{:S(2)}, u32[]{:S(2)}) collective-permute-start(bf16[32,1664]{1,0:T(8,128)(2,1)S(1)} %add_rows.1.m0), channel_id=1, source_target_pairs={{0,64},{1,17},{2,66},{3,19},{4,68},{5,21},{6,70},{7,23},{8,72},{9,... | collective-permute-start | bytes 319496 | tf_op jit(solution)/shard_map/ppermute | solution.py:29
  70.4 4.5 %collective-permute-start.20 = (bf16[32,768]{1,0:T(8,128)(2,1)S(1)}, bf16[32,768]{1,0:T(8,128)(2,1)S(1)}, u32[]{:S(2)}, u32[]{:S(2)}) collective-permute-start(bf16[32,768]{1,0:T(8,128)(2,1)S(1)} %activate.1.x0), channel_id=1, source_target_pairs={{0,32},{1,129},{2,34},{3,131},{4,36},{5,133},{6,38},{7,135},{8,40}... | collective-permute-start | bytes 147464 | tf_op jit(solution)/shard_map/ppermute | solution.py:29
  71.7 4.2 %collective-permute-start.19 = (bf16[32,768]{1,0:T(8,128)(2,1)S(1)}, bf16[32,768]{1,0:T(8,128)(2,1)S(1)}, u32[]{:S(2)}, u32[]{:S(2)}) collective-permute-start(bf16[32,768]{1,0:T(8,128)(2,1)S(1)} %activate.1.x0), channel_id=1, source_target_pairs={{0,48},{1,193},{2,50},{3,195},{4,52},{5,197},{6,54},{7,199},{8,56}... | collective-permute-start | bytes 147464 | tf_op jit(solution)/shard_map/ppermute | solution.py:29
  73.0 2.9 %collective-permute-start.18 = (bf16[32,768]{1,0:T(8,128)(2,1)S(1)}, bf16[32,768]{1,0:T(8,128)(2,1)S(1)}, u32[]{:S(2)}, u32[]{:S(2)}) collective-permute-start(bf16[32,768]{1,0:T(8,128)(2,1)S(1)} %activate.1.x0), channel_id=1, source_target_pairs={{0,16},{1,65},{2,18},{3,67},{4,20},{5,69},{6,22},{7,71},{8,24},{9,... | collective-permute-start | bytes 147464 | tf_op jit(solution)/shard_map/ppermute | solution.py:29

commit v8 on v7

--- a/solution.py
+++ b/solution.py
@@ -16,14 +16,15 @@
 SHARES = 16.0
 
 
-def exchange(value, stage, n_ctx, n_exp):
+def exchange(value, stage, n_ctx, n_exp, turned=True):
     side = 4
     got = {}
     for step in (2, 3, 1) if isinstance(value, (list, tuple)) else (1, 3, 2):
         pairs = []
         for i in range(n_ctx):
             for e in range(n_exp):
-                j = i ^ step if (e & 1) == stage else i ^ (side * step)
+                along_x = (e & 1 if turned else 1) == stage
+                j = i ^ step if along_x else i ^ (side * step)
                 pairs.append((i * n_exp + e, j * n_exp + e))
         sent = value[step - 1] if isinstance(value, (list, tuple)) else value
         got[step] = lax.ppermute(sent, AXES, pairs)
@@ -100,8 +101,7 @@
 
 
 def line_place():
-    first = lax.axis_index("ctx")
-    return jnp.where(lax.axis_index("exp") % 2 == 1, first // 4, first % 4)
+    return lax.axis_index("ctx") // 4
 
 
 def project_kernel(tokens_hbm, gain_hbm, w_hbm, out, tokens, gain, w_ref, small, sems):
@@ -512,7 +512,7 @@
         (rows.reshape(n_rows, slice_width), moe_gain[None], near(w_in_near)),
         [VM] * 3,
     )
-    got = [sent[0]] + exchange(sent[1:], 0, n_ctx, n_exp)[::-1]
+    got = [sent[0]] + exchange(sent[1:], 0, n_ctx, n_exp, False)[::-1]
     w_down_near, context = pl.pallas_call(
         load_kernel,
         out_shape=(pltpu.VMEM(w_down.shape, bf16), shape(context.shape)),
@@ -529,14 +529,14 @@
         activate_kernel,
         "activate",
         shape((n_rows // side, hidden)),
-        [total] + exchange(total, 1, n_ctx, n_exp),
+        [total] + exchange(total, 1, n_ctx, n_exp, False),
         [VM] * 4,
     )
     expert_out = call(
         functools.partial(down_kernel, capacity),
         "down",
         shape((n_rows, slice_width)),
-        [act] + exchange(act, 0, n_ctx, n_exp) + [near(w_down_near)],
+        [act] + exchange(act, 0, n_ctx, n_exp, False) + [near(w_down_near)],
         [VM] * 5,
     )
     returned = lax.all_to_all(

time: 91.8 us -> 93.3 us (1.016)
  waiting for transfers between devices: 18.6 us -> 21 us
  blocking collectives: 35.9 us -> 34.3 us
    ppermute x21, waiting for transfers between devices: 18.6 us -> 21 us  [exchange(): got[step] = lax.ppermute(sent, AXES, pairs)]
    all_to_all x1, blocking collectives: 14.4 us -> 12.8 us  [local(): lax.all_to_all(expert_out.reshape(n_exp, per_source, slice_width), 'exp',...]
  transfers between devices with their start and end apart: 21 -> 21, of which waited for: 13 -> 14; matrix products, arithmetic and copies ran while one was open for 0% -> 0% of each run, Pallas kernels for 8% -> 8%
where the time goes in v8:
time: 93.3 us; the launch traced here: 93 us
  blocking collectives  34.3 us (37%)
  starting transfers between devices  22.8 us (24%)
  waiting for transfers between devices  21 us (23%)
  Pallas kernels  13.8 us (15%)
    ppermute x21, starting transfers between devices, exchange(): got[step] = lax.ppermute(sent, AXES, pairs)  22.8 us
    all_to_all x1, blocking collectives, local(): lax.all_to_all(outgoing.reshape(n_exp, per_source, slice_width), 'exp', s...  21.5 us
    ppermute x21, waiting for transfers between devices, exchange(): got[step] = lax.ppermute(sent, AXES, pairs)  21 us
    all_to_all x1, blocking collectives, local(): lax.all_to_all(expert_out.reshape(n_exp, per_source, slice_width), 'exp',...  12.8 us
    pallas_call x13, Pallas kernels, call(): pl.pallas_call(kernel, out_shape=out, in_specs=specs, out_specs=jax.tree....  12.3 us
  transfers between devices with their start and end apart: 21, of which 14 were waited for; matrix products, arithmetic and copies ran while one was open for 0% of the time, Pallas kernels for 8%

profile of v8, /device:TPU:1, one launch (start us, length us, event | category | flops | bytes accessed | tf_op | source)
XLA Modules:
  0.0 93.0 jit_solution(7376511930710631934)
XLA Ops:
  0.7 2.1 %project.1.after = f32[8,5248]{1,0:T(8,128)S(1)} custom-call(bf16[8,256]{1,0:T(8,128)(2,1)} %tokens.1, f32[1,256]{1,0:T(1,128)} %bitcast.11, bf16[256,5120]{1,0:T(8,128)(2,1)} %w_hbm.1), custom_call_target="tpu_custom_call" | custom-call | tf_op jit(solution)/shard_map/project/pallas_call | solution.py:381
  2.8 3.8 %collective-permute-start.2 = (f16[8,5248]{1,0:T(8,128)(2,1)S(1)}, f16[8,5248]{1,0:T(8,128)(2,1)S(1)}, u32[]{:S(2)}, u32[]{:S(2)}) collective-permute-start(f16[8,5248]{1,0:T(8,128)(2,1)S(1)} %convert_element_type.40), channel_id=1, source_target_pairs={{0,32},{1,129},{2,34},{3,131},{4,36},{5,133},{6,38},{7,135},{8,40}... | collective-permute-start | bytes 251912 | tf_op jit(solution)/shard_map/ppermute | solution.py:30
  6.6 0.8 collective-permute-start.1
  7.4 0.0 collective-permute-start
  7.4 0.1 fusion
  7.5 0.0 copy-done.2
  7.5 0.7 prepare.1
  8.3 1.6 %load.3 = (bf16[8,128,512]{2,1,0:T(8,128)(2,1)S(1)}, bf16[8,128,512]{2,1,0:T(8,128)(2,1)S(1)}) custom-call(f32[8,5248]{1,0:T(8,128)S(1)} %project.1.after, bf16[8,128,512]{2,1,0:T(8,128)(2,1)} %refs_0_.4, bf16[8,128,512]{2,1,0:T(8,128)(2,1)} %refs_1_.1), custom_call_target="tpu_custom_call" | custom-call | tf_op jit(solution)/shard_map/load/pallas_call | solution.py:381
  9.8 0.0 collective-permute-done.2
  9.8 1.6 %collective-permute-done.1 = f16[8,5248]{1,0:T(8,128)(2,1)S(1)} collective-permute-done((f16[8,5248]{1,0:T(8,128)(2,1)S(1)}, f16[8,5248]{1,0:T(8,128)(2,1)S(1)}, u32[]{:S(2)}, u32[]{:S(2)}) %collective-permute-start.1) | collective-permute-done | bytes 84000 | tf_op jit(solution)/shard_map/ppermute | solution.py:30
  11.4 0.0 collective-permute-done
  11.4 0.1 fusion.1
  11.5 2.5 %collective-permute-start.5 = (f16[8,5248]{1,0:T(8,128)(2,1)S(1)}, f16[8,5248]{1,0:T(8,128)(2,1)S(1)}, u32[]{:S(2)}, u32[]{:S(2)}) collective-permute-start(f16[8,5248]{1,0:T(8,128)(2,1)S(1)} %get-tuple-element.32), channel_id=1, source_target_pairs={{0,128},{1,33},{2,130},{3,35},{4,132},{5,37},{6,134},{7,39},{8,136... | collective-permute-start | bytes 251912 | tf_op jit(solution)/shard_map/ppermute | solution.py:30
  14.0 0.9 collective-permute-start.4
  14.9 0.0 collective-permute-start.3
  14.9 0.1 pad_maximum_fusion
  15.0 1.6 %load.4.after.w_ref = bf16[4096,256]{1,0:T(8,128)(2,1)S(1)} custom-call(f32[8,5248]{1,0:T(8,128)S(1)} %get-tuple-element.33.after, bf16[4096,256]{1,0:T(8,128)(2,1)} %refs_0_.5), custom_call_target="tpu_custom_call" | custom-call | tf_op jit(solution)/shard_map/load/pallas_call | solution.py:381
  16.6 0.0 collective-permute-done.5
  16.6 2.2 %collective-permute-done.4 = f16[8,5248]{1,0:T(8,128)(2,1)S(1)} collective-permute-done((f16[8,5248]{1,0:T(8,128)(2,1)S(1)}, f16[8,5248]{1,0:T(8,128)(2,1)S(1)}, u32[]{:S(2)}, u32[]{:S(2)}) %collective-permute-start.4) | collective-permute-done | bytes 84000 | tf_op jit(solution)/shard_map/ppermute | solution.py:30
  18.8 0.0 collective-permute-done.3
  18.8 1.1 %attend.1.after.p0 = bf16[288,128]{1,0:T(8,128)(2,1)S(1)} custom-call(f32[8,5248]{1,0:T(8,128)S(1)} %add_add_fusion.shares, f32[8,128]{1,0:T(8,128)S(1)} %get-tuple-element.37.cosine, f32[8,128]{1,0:T(8,128)S(1)} %get-tuple-element.38.sine, f32[8,128]{1,0:T(8,128)S(1)} %get-tuple-element.17.live_ref, f32[8,128]{1,0:T(8,128)S(1)} %get-tuple-element.18.owns, ...), custom_call_target="tpu_custom_call" | custom-call | tf_op jit(solution)/shard_map/attend/pallas_call | solution.py:381
  19.9 1.6 %collective-permute-start.8 = (bf16[288,128]{1,0:T(8,128)(2,1)S(1)}, bf16[288,128]{1,0:T(8,128)(2,1)S(1)}, u32[]{:S(2)}, u32[]{:S(2)}) collective-permute-start(bf16[288,128]{1,0:T(8,128)(2,1)S(1)} %attend.1.after.p0), channel_id=1, source_target_pairs={{0,32},{1,129},{2,34},{3,131},{4,36},{5,133},{6,38},{7,135},{8,40}... | collective-permute-start | bytes 221192 | tf_op jit(solution)/shard_map/ppermute | solution.py:30
  21.6 0.8 collective-permute-start.7
  22.3 0.3 collective-permute-start.6
  22.6 1.9 %load.5.after.w_ref = bf16[4,256,1536]{2,1,0:T(8,128)(2,1)S(1)} custom-call(bf16[288,128]{1,0:T(8,128)(2,1)S(1)} %attend.1.after.p0, bf16[4,256,1536]{2,1,0:T(8,128)(2,1)} %refs_0_.6), custom_call_target="tpu_custom_call" | custom-call | tf_op jit(solution)/shard_map/load/pallas_call | solution.py:381
  24.5 0.0 copy-start
  24.5 0.1 collective-permute-done.8.p2
  24.7 1.3 %collective-permute-done.7.p3 = bf16[288,128]{1,0:T(8,128)(2,1)S(1)} collective-permute-done((bf16[288,128]{1,0:T(8,128)(2,1)S(1)}, bf16[288,128]{1,0:T(8,128)(2,1)S(1)}, u32[]{:S(2)}, u32[]{:S(2)}) %collective-permute-start.7) | collective-permute-done | bytes 73760 | tf_op jit(solution)/shard_map/ppermute | solution.py:30
  26.0 0.0 collective-permute-done.6.p1
  26.0 0.3 merge.1.p0
  26.3 0.0 copy-start.3
  26.3 1.6 %collective-permute-start.11 = (bf16[288,128]{1,0:T(8,128)(2,1)S(1)}, bf16[288,128]{1,0:T(8,128)(2,1)S(1)}, u32[]{:S(2)}, u32[]{:S(2)}) collective-permute-start(bf16[288,128]{1,0:T(8,128)(2,1)S(1)} %merge.1.p0), channel_id=1, source_target_pairs={{0,128},{1,33},{2,130},{3,35},{4,132},{5,37},{6,134},{7,39},{8,136... | collective-permute-start | bytes 221192 | tf_op jit(solution)/shard_map/ppermute | solution.py:30
  27.9 0.9 collective-permute-start.10
  28.8 0.3 collective-permute-start.9
  29.1 2.8 %collective-permute-done.11.p2 = bf16[288,128]{1,0:T(8,128)(2,1)S(1)} collective-permute-done((bf16[288,128]{1,0:T(8,128)(2,1)S(1)}, bf16[288,128]{1,0:T(8,128)(2,1)S(1)}, u32[]{:S(2)}, u32[]{:S(2)}) %collective-permute-start.11) | collective-permute-done | bytes 73760 | tf_op jit(solution)/shard_map/ppermute | solution.py:30
  31.9 0.6 collective-permute-done.10.p3
  32.5 0.0 collective-permute-done.9.p1
  32.5 0.9 finish.1
  33.4 21.5 %all_to_all.10 = bf16[16,8,256]{2,1,0:T(8,128)(2,1)S(1)} all-to-all(bf16[16,8,256]{2,1,0:T(8,128)(2,1)S(1)} %bitcast.9), channel_id=1, replica_groups=mesh['ctx'=16,'exp'=16] {'exp'}, dimensions={0} | all-to-all | bytes 131072 | tf_op jit(solution)/shard_map/all_to_all | solution.py:503
  54.9 0.6 gate_up.1
  55.5 2.2 %collective-permute-start.12 = (bf16[32,1664]{1,0:T(8,128)(2,1)S(1)}, bf16[32,1664]{1,0:T(8,128)(2,1)S(1)}, u32[]{:S(2)}, u32[]{:S(2)}) collective-permute-start(bf16[32,1664]{1,0:T(8,128)(2,1)S(1)} %get-tuple-element.28), channel_id=1, source_target_pairs={{0,128},{1,129},{2,130},{3,131},{4,132},{5,133},{6,134},{7,135},{8... | collective-permute-start | bytes 319496 | tf_op jit(solution)/shard_map/ppermute | solution.py:30
  57.6 0.8 collective-permute-start.13
  58.4 0.0 collective-permute-start.14
  58.4 1.4 %settle.1 = (bf16[4,768,256]{2,1,0:T(8,128)(2,1)S(1)}, bf16[8,4096]{1,0:T(8,128)(2,1)}) custom-call(bf16[32,1664]{1,0:T(8,128)(2,1)S(1)} %get-tuple-element.23.after.m0, bf16[4,768,256]{2,1,0:T(8,128)(2,1)} %refs_0_.7, bf16[8,4096]{1,0:T(8,128)(2,1)S(1)} %get-tuple-element.24.refs_1_), custom_call_target="tpu_custom_call" | custom-call | tf_op jit(solution)/shard_map/settle/pallas_call | solution.py:516
  59.9 1.6 %collective-permute-done.12.m1 = bf16[32,1664]{1,0:T(8,128)(2,1)S(1)} collective-permute-done((bf16[32,1664]{1,0:T(8,128)(2,1)S(1)}, bf16[32,1664]{1,0:T(8,128)(2,1)S(1)}, u32[]{:S(2)}, u32[]{:S(2)}) %collective-permute-start.12) | collective-permute-done | bytes 106528 | tf_op jit(solution)/shard_map/ppermute | solution.py:30
  61.5 2.5 %collective-permute-done.13.m3 = bf16[32,1664]{1,0:T(8,128)(2,1)S(1)} collective-permute-done((bf16[32,1664]{1,0:T(8,128)(2,1)S(1)}, bf16[32,1664]{1,0:T(8,128)(2,1)S(1)}, u32[]{:S(2)}, u32[]{:S(2)}) %collective-permute-start.13) | collective-permute-done | bytes 106528 | tf_op jit(solution)/shard_map/ppermute | solution.py:30
  64.0 0.0 collective-permute-done.14.m2
  64.0 0.2 add_rows.1.m0
  64.2 2.6 %collective-permute-start.17 = (bf16[32,1664]{1,0:T(8,128)(2,1)S(1)}, bf16[32,1664]{1,0:T(8,128)(2,1)S(1)}, u32[]{:S(2)}, u32[]{:S(2)}) collective-permute-start(bf16[32,1664]{1,0:T(8,128)(2,1)S(1)} %add_rows.1.m0), channel_id=1, source_target_pairs={{0,32},{1,33},{2,34},{3,35},{4,36},{5,37},{6,38},{7,39},{8,40},{9,... | collective-permute-start | bytes 319496 | tf_op jit(solution)/shard_map/ppermute | solution.py:30
  66.8 0.4 collective-permute-start.16
  67.2 0.3 collective-permute-start.15
  67.5 1.8 %collective-permute-done.17.m2 = bf16[32,1664]{1,0:T(8,128)(2,1)S(1)} collective-permute-done((bf16[32,1664]{1,0:T(8,128)(2,1)S(1)}, bf16[32,1664]{1,0:T(8,128)(2,1)S(1)}, u32[]{:S(2)}, u32[]{:S(2)}) %collective-permute-start.17) | collective-permute-done | bytes 106528 | tf_op jit(solution)/shard_map/ppermute | solution.py:30
  69.3 2.7 %collective-permute-done.16.m3 = bf16[32,1664]{1,0:T(8,128)(2,1)S(1)} collective-permute-done((bf16[32,1664]{1,0:T(8,128)(2,1)S(1)}, bf16[32,1664]{1,0:T(8,128)(2,1)S(1)}, u32[]{:S(2)}, u32[]{:S(2)}) %collective-permute-start.16) | collective-permute-done | bytes 106528 | tf_op jit(solution)/shard_map/ppermute | solution.py:30
  72.0 0.4 collective-permute-done.15.m1
  72.4 0.2 activate.1.x0
  72.5 0.9 collective-permute-start.20
  73.4 2.2 %collective-permute-start.19 = (bf16[32,768]{1,0:T(8,128)(2,1)S(1)}, bf16[32,768]{1,0:T(8,128)(2,1)S(1)}, u32[]{:S(2)}, u32[]{:S(2)}) collective-permute-start(bf16[32,768]{1,0:T(8,128)(2,1)S(1)} %activate.1.x0), channel_id=1, source_target_pairs={{0,192},{1,193},{2,194},{3,195},{4,196},{5,197},{6,198},{7,199},{8... | collective-permute-start | bytes 147464 | tf_op jit(solution)/shard_map/ppermute | solution.py:30
  75.6 0.0 collective-permute-start.18
  75.6 1.4 %collective-permute-done.20.x2 = bf16[32,768]{1,0:T(8,128)(2,1)S(1)} collective-permute-done((bf16[32,768]{1,0:T(8,128)(2,1)S(1)}, bf16[32,768]{1,0:T(8,128)(2,1)S(1)}, u32[]{:S(2)}, u32[]{:S(2)}) %collective-permute-start.20) | collective-permute-done | bytes 49184 | tf_op jit(solution)/shard_map/ppermute | solution.py:30
  77.1 0.5 collective-permute-done.19.x3
  77.6 1.4 %collective-permute-done.18.x1 = bf16[32,768]{1,0:T(8,128)(2,1)S(1)} collective-permute-done((bf16[32,768]{1,0:T(8,128)(2,1)S(1)}, bf16[32,768]{1,0:T(8,128)(2,1)S(1)}, u32[]{:S(2)}, u32[]{:S(2)}) %collective-permute-start.18) | collective-permute-done | bytes 49184 | tf_op jit(solution)/shard_map/ppermute | solution.py:30
  79.0 0.4 down.1
  79.4 12.8 %all_to_all.11 = bf16[16,8,256]{2,1,0:T(8,128)(2,1)S(1)} all-to-all(bf16[16,8,256]{2,1,0:T(8,128)(2,1)S(1)} %bitcast.7), channel_id=1, replica_groups=mesh['ctx'=16,'exp'=16] {'exp'}, dimensions={0} | all-to-all | bytes 131072 | tf_op jit(solution)/shard_map/all_to_all | solution.py:542
  92.2 0.7 combine.1
  (11 shorter events, 0.1 us)
Async XLA Ops:
  0.6 6.8 %copy-start.4 = (s32[8]{0:T(128)S(1)}, s32[8]{0:T(128)}, u32[]{:S(2)}) copy-start(s32[8]{0:T(128)} %lengths.1) | copy-start | bytes 100
  0.6 6.9 %copy-start.2 = (f32[8,8]{1,0:T(8,128)S(1)}, f32[8,8]{1,0:T(8,128)}, u32[]{:S(2)}) copy-start(f32[8,8]{1,0:T(8,128)} %gates.1) | copy-start | bytes 772
  0.7 6.9 %copy-start.1 = (s32[8,8]{1,0:T(8,128)S(1)}, s32[8,8]{1,0:T(8,128)}, u32[]{:S(2)}) copy-start(s32[8,8]{1,0:T(8,128)} %routes.1) | copy-start | bytes 772
  2.8 7.1 %collective-permute-start.2 = (f16[8,5248]{1,0:T(8,128)(2,1)S(1)}, f16[8,5248]{1,0:T(8,128)(2,1)S(1)}, u32[]{:S(2)}, u32[]{:S(2)}) collective-permute-start(f16[8,5248]{1,0:T(8,128)(2,1)S(1)} %convert_element_type.40), channel_id=1, source_target_pairs={{0,32},{1,129},{2,34},{3,131},{4,36},{5,133},{6,38},{7,135},{8,40}... | collective-permute-start | bytes 251912 | tf_op jit(solution)/shard_map/ppermute | solution.py:30
  6.6 4.8 %collective-permute-start.1 = (f16[8,5248]{1,0:T(8,128)(2,1)S(1)}, f16[8,5248]{1,0:T(8,128)(2,1)S(1)}, u32[]{:S(2)}, u32[]{:S(2)}) collective-permute-start(f16[8,5248]{1,0:T(8,128)(2,1)S(1)} %convert_element_type.40), channel_id=1, source_target_pairs={{0,48},{1,193},{2,50},{3,195},{4,52},{5,197},{6,54},{7,199},{8,56}... | collective-permute-start | bytes 251912 | tf_op jit(solution)/shard_map/ppermute | solution.py:30
  7.4 4.0 %collective-permute-start = (f16[8,5248]{1,0:T(8,128)(2,1)S(1)}, f16[8,5248]{1,0:T(8,128)(2,1)S(1)}, u32[]{:S(2)}, u32[]{:S(2)}) collective-permute-start(f16[8,5248]{1,0:T(8,128)(2,1)S(1)} %convert_element_type.40), channel_id=1, source_target_pairs={{0,16},{1,65},{2,18},{3,67},{4,20},{5,69},{6,22},{7,71},{8,24},{9,... | collective-permute-start | bytes 251912 | tf_op jit(solution)/shard_map/ppermute | solution.py:30
  11.5 5.1 %collective-permute-start.5 = (f16[8,5248]{1,0:T(8,128)(2,1)S(1)}, f16[8,5248]{1,0:T(8,128)(2,1)S(1)}, u32[]{:S(2)}, u32[]{:S(2)}) collective-permute-start(f16[8,5248]{1,0:T(8,128)(2,1)S(1)} %get-tuple-element.32), channel_id=1, source_target_pairs={{0,128},{1,33},{2,130},{3,35},{4,132},{5,37},{6,134},{7,39},{8,136... | collective-permute-start | bytes 251912 | tf_op jit(solution)/shard_map/ppermute | solution.py:30
  14.0 4.8 %collective-permute-start.4 = (f16[8,5248]{1,0:T(8,128)(2,1)S(1)}, f16[8,5248]{1,0:T(8,128)(2,1)S(1)}, u32[]{:S(2)}, u32[]{:S(2)}) collective-permute-start(f16[8,5248]{1,0:T(8,128)(2,1)S(1)} %get-tuple-element.32), channel_id=1, source_target_pairs={{0,192},{1,49},{2,194},{3,51},{4,196},{5,53},{6,198},{7,55},{8,200... | collective-permute-start | bytes 251912 | tf_op jit(solution)/shard_map/ppermute | solution.py:30
  14.9 3.9 %collective-permute-start.3 = (f16[8,5248]{1,0:T(8,128)(2,1)S(1)}, f16[8,5248]{1,0:T(8,128)(2,1)S(1)}, u32[]{:S(2)}, u32[]{:S(2)}) collective-permute-start(f16[8,5248]{1,0:T(8,128)(2,1)S(1)} %get-tuple-element.32), channel_id=1, source_target_pairs={{0,64},{1,17},{2,66},{3,19},{4,68},{5,21},{6,70},{7,23},{8,72},{9,... | collective-permute-start | bytes 251912 | tf_op jit(solution)/shard_map/ppermute | solution.py:30
  19.9 4.8 %collective-permute-start.8 = (bf16[288,128]{1,0:T(8,128)(2,1)S(1)}, bf16[288,128]{1,0:T(8,128)(2,1)S(1)}, u32[]{:S(2)}, u32[]{:S(2)}) collective-permute-start(bf16[288,128]{1,0:T(8,128)(2,1)S(1)} %attend.1.after.p0), channel_id=1, source_target_pairs={{0,32},{1,129},{2,34},{3,131},{4,36},{5,133},{6,38},{7,135},{8,40}... | collective-permute-start | bytes 221192 | tf_op jit(solution)/shard_map/ppermute | solution.py:30
  21.6 4.4 %collective-permute-start.7 = (bf16[288,128]{1,0:T(8,128)(2,1)S(1)}, bf16[288,128]{1,0:T(8,128)(2,1)S(1)}, u32[]{:S(2)}, u32[]{:S(2)}) collective-permute-start(bf16[288,128]{1,0:T(8,128)(2,1)S(1)} %attend.1.after.p0), channel_id=1, source_target_pairs={{0,48},{1,193},{2,50},{3,195},{4,52},{5,197},{6,54},{7,199},{8,56}... | collective-permute-start | bytes 221192 | tf_op jit(solution)/shard_map/ppermute | solution.py:30
  22.3 3.6 %collective-permute-start.6 = (bf16[288,128]{1,0:T(8,128)(2,1)S(1)}, bf16[288,128]{1,0:T(8,128)(2,1)S(1)}, u32[]{:S(2)}, u32[]{:S(2)}) collective-permute-start(bf16[288,128]{1,0:T(8,128)(2,1)S(1)} %attend.1.after.p0), channel_id=1, source_target_pairs={{0,16},{1,65},{2,18},{3,67},{4,20},{5,69},{6,22},{7,71},{8,24},{9,... | collective-permute-start | bytes 221192 | tf_op jit(solution)/shard_map/ppermute | solution.py:30
  24.5 8.0 %copy-start = (bf16[8,256]{1,0:T(8,128)(2,1)S(1)}, bf16[8,256]{1,0:T(8,128)(2,1)}, u32[]{:S(2)}) copy-start(bf16[8,256]{1,0:T(8,128)(2,1)} %tokens.1) | copy-start | bytes 12292
  26.3 28.6 %copy-start.3 = (f32[256]{0:T(256)S(1)}, f32[256]{0:T(256)}, u32[]{:S(2)}) copy-start(f32[256]{0:T(256)} %param.19) | copy-start | bytes 3076
  26.3 5.6 %collective-permute-start.11 = (bf16[288,128]{1,0:T(8,128)(2,1)S(1)}, bf16[288,128]{1,0:T(8,128)(2,1)S(1)}, u32[]{:S(2)}, u32[]{:S(2)}) collective-permute-start(bf16[288,128]{1,0:T(8,128)(2,1)S(1)} %merge.1.p0), channel_id=1, source_target_pairs={{0,128},{1,33},{2,130},{3,35},{4,132},{5,37},{6,134},{7,39},{8,136... | collective-permute-start | bytes 221192 | tf_op jit(solution)/shard_map/ppermute | solution.py:30
  27.9 4.6 %collective-permute-start.10 = (bf16[288,128]{1,0:T(8,128)(2,1)S(1)}, bf16[288,128]{1,0:T(8,128)(2,1)S(1)}, u32[]{:S(2)}, u32[]{:S(2)}) collective-permute-start(bf16[288,128]{1,0:T(8,128)(2,1)S(1)} %merge.1.p0), channel_id=1, source_target_pairs={{0,192},{1,49},{2,194},{3,51},{4,196},{5,53},{6,198},{7,55},{8,200... | collective-permute-start | bytes 221192 | tf_op jit(solution)/shard_map/ppermute | solution.py:30
  28.8 3.7 %collective-permute-start.9 = (bf16[288,128]{1,0:T(8,128)(2,1)S(1)}, bf16[288,128]{1,0:T(8,128)(2,1)S(1)}, u32[]{:S(2)}, u32[]{:S(2)}) collective-permute-start(bf16[288,128]{1,0:T(8,128)(2,1)S(1)} %merge.1.p0), channel_id=1, source_target_pairs={{0,64},{1,17},{2,66},{3,19},{4,68},{5,21},{6,70},{7,23},{8,72},{9,... | collective-permute-start | bytes 221192 | tf_op jit(solution)/shard_map/ppermute | solution.py:30
  55.5 6.0 %collective-permute-start.12 = (bf16[32,1664]{1,0:T(8,128)(2,1)S(1)}, bf16[32,1664]{1,0:T(8,128)(2,1)S(1)}, u32[]{:S(2)}, u32[]{:S(2)}) collective-permute-start(bf16[32,1664]{1,0:T(8,128)(2,1)S(1)} %get-tuple-element.28), channel_id=1, source_target_pairs={{0,128},{1,129},{2,130},{3,131},{4,132},{5,133},{6,134},{7,135},{8... | collective-permute-start | bytes 319496 | tf_op jit(solution)/shard_map/ppermute | solution.py:30
  57.6 6.3 %collective-permute-start.13 = (bf16[32,1664]{1,0:T(8,128)(2,1)S(1)}, bf16[32,1664]{1,0:T(8,128)(2,1)S(1)}, u32[]{:S(2)}, u32[]{:S(2)}) collective-permute-start(bf16[32,1664]{1,0:T(8,128)(2,1)S(1)} %get-tuple-element.29), channel_id=1, source_target_pairs={{0,192},{1,193},{2,194},{3,195},{4,196},{5,197},{6,198},{7,199},{8... | collective-permute-start | bytes 319496 | tf_op jit(solution)/shard_map/ppermute | solution.py:30
  58.4 5.5 %collective-permute-start.14 = (bf16[32,1664]{1,0:T(8,128)(2,1)S(1)}, bf16[32,1664]{1,0:T(8,128)(2,1)S(1)}, u32[]{:S(2)}, u32[]{:S(2)}) collective-permute-start(bf16[32,1664]{1,0:T(8,128)(2,1)S(1)} %get-tuple-element.30), channel_id=1, source_target_pairs={{0,64},{1,65},{2,66},{3,67},{4,68},{5,69},{6,70},{7,71},{8,72},{9,... | collective-permute-start | bytes 319496 | tf_op jit(solution)/shard_map/ppermute | solution.py:30
  64.2 5.1 %collective-permute-start.17 = (bf16[32,1664]{1,0:T(8,128)(2,1)S(1)}, bf16[32,1664]{1,0:T(8,128)(2,1)S(1)}, u32[]{:S(2)}, u32[]{:S(2)}) collective-permute-start(bf16[32,1664]{1,0:T(8,128)(2,1)S(1)} %add_rows.1.m0), channel_id=1, source_target_pairs={{0,32},{1,33},{2,34},{3,35},{4,36},{5,37},{6,38},{7,39},{8,40},{9,... | collective-permute-start | bytes 319496 | tf_op jit(solution)/shard_map/ppermute | solution.py:30
  66.8 5.2 %collective-permute-start.16 = (bf16[32,1664]{1,0:T(8,128)(2,1)S(1)}, bf16[32,1664]{1,0:T(8,128)(2,1)S(1)}, u32[]{:S(2)}, u32[]{:S(2)}) collective-permute-start(bf16[32,1664]{1,0:T(8,128)(2,1)S(1)} %add_rows.1.m0), channel_id=1, source_target_pairs={{0,48},{1,49},{2,50},{3,51},{4,52},{5,53},{6,54},{7,55},{8,56},{9,... | collective-permute-start | bytes 319496 | tf_op jit(solution)/shard_map/ppermute | solution.py:30
  67.2 5.2 %collective-permute-start.15 = (bf16[32,1664]{1,0:T(8,128)(2,1)S(1)}, bf16[32,1664]{1,0:T(8,128)(2,1)S(1)}, u32[]{:S(2)}, u32[]{:S(2)}) collective-permute-start(bf16[32,1664]{1,0:T(8,128)(2,1)S(1)} %add_rows.1.m0), channel_id=1, source_target_pairs={{0,16},{1,17},{2,18},{3,19},{4,20},{5,21},{6,22},{7,23},{8,24},{9,... | collective-permute-start | bytes 319496 | tf_op jit(solution)/shard_map/ppermute | solution.py:30
  72.5 4.5 %collective-permute-start.20 = (bf16[32,768]{1,0:T(8,128)(2,1)S(1)}, bf16[32,768]{1,0:T(8,128)(2,1)S(1)}, u32[]{:S(2)}, u32[]{:S(2)}) collective-permute-start(bf16[32,768]{1,0:T(8,128)(2,1)S(1)} %activate.1.x0), channel_id=1, source_target_pairs={{0,128},{1,129},{2,130},{3,131},{4,132},{5,133},{6,134},{7,135},{8... | collective-permute-start | bytes 147464 | tf_op jit(solution)/shard_map/ppermute | solution.py:30
  73.4 4.2 %collective-permute-start.19 = (bf16[32,768]{1,0:T(8,128)(2,1)S(1)}, bf16[32,768]{1,0:T(8,128)(2,1)S(1)}, u32[]{:S(2)}, u32[]{:S(2)}) collective-permute-start(bf16[32,768]{1,0:T(8,128)(2,1)S(1)} %activate.1.x0), channel_id=1, source_target_pairs={{0,192},{1,193},{2,194},{3,195},{4,196},{5,197},{6,198},{7,199},{8... | collective-permute-start | bytes 147464 | tf_op jit(solution)/shard_map/ppermute | solution.py:30
  75.6 3.4 %collective-permute-start.18 = (bf16[32,768]{1,0:T(8,128)(2,1)S(1)}, bf16[32,768]{1,0:T(8,128)(2,1)S(1)}, u32[]{:S(2)}, u32[]{:S(2)}) collective-permute-start(bf16[32,768]{1,0:T(8,128)(2,1)S(1)} %activate.1.x0), channel_id=1, source_target_pairs={{0,64},{1,65},{2,66},{3,67},{4,68},{5,69},{6,70},{7,71},{8,72},{9,... | collective-permute-start | bytes 147464 | tf_op jit(solution)/shard_map/ppermute | solution.py:30

commit v9 on v7

--- a/solution.py
+++ b/solution.py
@@ -92,7 +92,13 @@
         earlier = earlier + named[b : b + 1]
     rank = jnp.concatenate(ranks, 0)
     chosen = (named > 0.5) & (jnp.abs(rank - (lane % 2).astype(f32)) < 0.5)
-    weighting[...] = jnp.where(chosen, weights, 0.0)
+    weights = jnp.where(chosen, weights, 0.0)
+    high = weights.astype(jnp.bfloat16).astype(f32)
+    rest = weights - high
+    middle = rest.astype(jnp.bfloat16).astype(f32)
+    low = rest - middle
+    terms = jnp.concatenate([high, middle, low, jnp.zeros_like(low)], 0)
+    weighting[...] = terms.astype(jnp.bfloat16)
     square = jnp.concatenate(
         [jnp.where(chosen, 1.0, 0.0), jnp.zeros((128 - seqs, 128), f32)], 0
     )
@@ -355,14 +361,8 @@
 
 def combine_kernel(resid, weighting, returned, out):
     f32, bf16 = jnp.float32, jnp.bfloat16
-    weights = weighting[...]
-    seqs = weights.shape[0]
-    high = weights.astype(bf16).astype(f32)
-    rest = weights - high
-    middle = rest.astype(bf16).astype(f32)
-    low = rest - middle
-    stack = jnp.concatenate([high, middle, low, jnp.zeros_like(low)], 0).astype(bf16)
-    sums = jnp.dot(stack, returned[...], preferred_element_type=f32)
+    seqs = resid.shape[0]
+    sums = jnp.dot(weighting[...], returned[...], preferred_element_type=f32)
     moe = (sums[:seqs] + sums[seqs : 2 * seqs]) + sums[2 * seqs : 3 * seqs]
     out[...] = (resid[...].astype(f32) + moe).astype(bf16)
 
@@ -458,7 +458,7 @@
             pltpu.VMEM((seqs, 128), f32),
             pltpu.VMEM((seqs, 128), f32),
             pltpu.VMEM((128, 128), bf16),
-            pltpu.VMEM((seqs, 128), f32),
+            pltpu.VMEM((4 * seqs, 128), bf16),
         ),
         (lengths, routes, gates, near(whole)),
         [SM] + [VM] * 3,
@@ -496,7 +496,7 @@
         ),
         [part] + exchange(part, 1, n_ctx, n_exp) + [tokens, near(placing), near(w_near)],
         [VM] * 7,
-        [pltpu.VMEM((QUERY_HEADS * seqs, hd), f32)],
+        [pltpu.VMEM(((QUERY_HEADS + 1) * seqs, hd), f32)],
     )
 
     n_rows = n_exp * per_source

time: 91.8 us -> 91.8 us (level)
  no operation moved by 1% of the time
where the time goes in v9:
time: 91.8 us; the launch traced here: 91.5 us
  blocking collectives  35.9 us (39%)
  starting transfers between devices  22.1 us (24%)
  waiting for transfers between devices  18.6 us (20%)
  Pallas kernels  13.8 us (15%)
    ppermute x21, starting transfers between devices, exchange(): got[step] = lax.ppermute(sent, AXES, pairs)  22.1 us
    all_to_all x1, blocking collectives, local(): lax.all_to_all(outgoing.reshape(n_exp, per_source, slice_width), 'exp', s...  21.5 us
    ppermute x21, waiting for transfers between devices, exchange(): got[step] = lax.ppermute(sent, AXES, pairs)  18.6 us
    all_to_all x1, blocking collectives, local(): lax.all_to_all(expert_out.reshape(n_exp, per_source, slice_width), 'exp',...  14.4 us
    pallas_call x13, Pallas kernels, call(): pl.pallas_call(kernel, out_shape=out, in_specs=specs, out_specs=jax.tree....  12.3 us
  transfers between devices with their start and end apart: 21, of which 13 were waited for; matrix products, arithmetic and copies ran while one was open for 0% of the time, Pallas kernels for 8%

profile of v9, /device:TPU:1, one launch (start us, length us, event | category | flops | bytes accessed | tf_op | source)
XLA Modules:
  0.0 91.5 jit_solution(14566439391713069658)
XLA Ops:
  0.6 0.0 copy-start.4
  0.7 2.1 %project.1.after = f32[8,5248]{1,0:T(8,128)S(1)} custom-call(bf16[8,256]{1,0:T(8,128)(2,1)} %tokens.1, f32[1,256]{1,0:T(1,128)} %bitcast.11, bf16[256,5120]{1,0:T(8,128)(2,1)} %w_hbm.1), custom_call_target="tpu_custom_call" | custom-call | tf_op jit(solution)/shard_map/project/pallas_call | solution.py:381
  2.8 3.8 %collective-permute-start.2 = (f16[8,5248]{1,0:T(8,128)(2,1)S(1)}, f16[8,5248]{1,0:T(8,128)(2,1)S(1)}, u32[]{:S(2)}, u32[]{:S(2)}) collective-permute-start(f16[8,5248]{1,0:T(8,128)(2,1)S(1)} %convert_element_type.40), channel_id=1, source_target_pairs={{0,32},{1,129},{2,34},{3,131},{4,36},{5,133},{6,38},{7,135},{8,40}... | collective-permute-start | bytes 251912 | tf_op jit(solution)/shard_map/ppermute | solution.py:29
  6.6 0.8 collective-permute-start.1
  7.4 0.0 collective-permute-start
  7.4 0.1 fusion
  7.5 0.7 prepare.1
  8.3 1.6 %load.3 = (bf16[8,128,512]{2,1,0:T(8,128)(2,1)S(1)}, bf16[8,128,512]{2,1,0:T(8,128)(2,1)S(1)}) custom-call(f32[8,5248]{1,0:T(8,128)S(1)} %project.1.after, bf16[8,128,512]{2,1,0:T(8,128)(2,1)} %refs_0_.4, bf16[8,128,512]{2,1,0:T(8,128)(2,1)} %refs_1_.1), custom_call_target="tpu_custom_call" | custom-call | tf_op jit(solution)/shard_map/load/pallas_call | solution.py:381
  9.8 0.0 collective-permute-done.2
  9.8 1.6 %collective-permute-done.1 = f16[8,5248]{1,0:T(8,128)(2,1)S(1)} collective-permute-done((f16[8,5248]{1,0:T(8,128)(2,1)S(1)}, f16[8,5248]{1,0:T(8,128)(2,1)S(1)}, u32[]{:S(2)}, u32[]{:S(2)}) %collective-permute-start.1) | collective-permute-done | bytes 84000 | tf_op jit(solution)/shard_map/ppermute | solution.py:29
  11.4 0.0 collective-permute-done
  11.4 0.1 fusion.1
  11.5 2.5 %collective-permute-start.5 = (f16[8,5248]{1,0:T(8,128)(2,1)S(1)}, f16[8,5248]{1,0:T(8,128)(2,1)S(1)}, u32[]{:S(2)}, u32[]{:S(2)}) collective-permute-start(f16[8,5248]{1,0:T(8,128)(2,1)S(1)} %get-tuple-element.32), channel_id=1, source_target_pairs={{0,128},{1,33},{2,130},{3,35},{4,132},{5,37},{6,134},{7,39},{8,136... | collective-permute-start | bytes 251912 | tf_op jit(solution)/shard_map/ppermute | solution.py:29
  14.0 0.9 collective-permute-start.4
  14.9 0.0 collective-permute-start.3
  14.9 0.1 pad_maximum_fusion
  15.0 1.6 %load.4.after.w_ref = bf16[4096,256]{1,0:T(8,128)(2,1)S(1)} custom-call(f32[8,5248]{1,0:T(8,128)S(1)} %get-tuple-element.33.after, bf16[4096,256]{1,0:T(8,128)(2,1)} %refs_0_.5), custom_call_target="tpu_custom_call" | custom-call | tf_op jit(solution)/shard_map/load/pallas_call | solution.py:381
  16.6 0.0 collective-permute-done.5
  16.6 2.2 %collective-permute-done.4 = f16[8,5248]{1,0:T(8,128)(2,1)S(1)} collective-permute-done((f16[8,5248]{1,0:T(8,128)(2,1)S(1)}, f16[8,5248]{1,0:T(8,128)(2,1)S(1)}, u32[]{:S(2)}, u32[]{:S(2)}) %collective-permute-start.4) | collective-permute-done | bytes 84000 | tf_op jit(solution)/shard_map/ppermute | solution.py:29
  18.8 0.0 collective-permute-done.3
  18.8 1.1 %attend.1.after.p0 = bf16[288,128]{1,0:T(8,128)(2,1)S(1)} custom-call(f32[8,5248]{1,0:T(8,128)S(1)} %add_add_fusion.shares, f32[8,128]{1,0:T(8,128)S(1)} %get-tuple-element.37.cosine, f32[8,128]{1,0:T(8,128)S(1)} %get-tuple-element.38.sine, f32[8,128]{1,0:T(8,128)S(1)} %get-tuple-element.17.live_ref, f32[8,128]{1,0:T(8,128)S(1)} %get-tuple-element.18.owns, ...), custom_call_target="tpu_custom_call" | custom-call | tf_op jit(solution)/shard_map/attend/pallas_call | solution.py:381
  19.9 1.6 %collective-permute-start.8 = (bf16[288,128]{1,0:T(8,128)(2,1)S(1)}, bf16[288,128]{1,0:T(8,128)(2,1)S(1)}, u32[]{:S(2)}, u32[]{:S(2)}) collective-permute-start(bf16[288,128]{1,0:T(8,128)(2,1)S(1)} %attend.1.after.p0), channel_id=1, source_target_pairs={{0,32},{1,129},{2,34},{3,131},{4,36},{5,133},{6,38},{7,135},{8,40}... | collective-permute-start | bytes 221192 | tf_op jit(solution)/shard_map/ppermute | solution.py:29
  21.6 0.8 collective-permute-start.7
  22.3 0.3 collective-permute-start.6
  22.6 1.9 %load.5.after.w_ref = bf16[4,256,1536]{2,1,0:T(8,128)(2,1)S(1)} custom-call(bf16[288,128]{1,0:T(8,128)(2,1)S(1)} %attend.1.after.p0, bf16[4,256,1536]{2,1,0:T(8,128)(2,1)} %refs_0_.6), custom_call_target="tpu_custom_call" | custom-call | tf_op jit(solution)/shard_map/load/pallas_call | solution.py:381
  24.5 0.0 copy-start
  24.5 0.1 collective-permute-done.8.p2
  24.7 1.3 %collective-permute-done.7.p3 = bf16[288,128]{1,0:T(8,128)(2,1)S(1)} collective-permute-done((bf16[288,128]{1,0:T(8,128)(2,1)S(1)}, bf16[288,128]{1,0:T(8,128)(2,1)S(1)}, u32[]{:S(2)}, u32[]{:S(2)}) %collective-permute-start.7) | collective-permute-done | bytes 73760 | tf_op jit(solution)/shard_map/ppermute | solution.py:29
  26.0 0.0 collective-permute-done.6.p1
  26.0 0.3 merge.1.p0
  26.3 0.0 copy-start.3
  26.3 1.6 %collective-permute-start.11 = (bf16[288,128]{1,0:T(8,128)(2,1)S(1)}, bf16[288,128]{1,0:T(8,128)(2,1)S(1)}, u32[]{:S(2)}, u32[]{:S(2)}) collective-permute-start(bf16[288,128]{1,0:T(8,128)(2,1)S(1)} %merge.1.p0), channel_id=1, source_target_pairs={{0,128},{1,33},{2,130},{3,35},{4,132},{5,37},{6,134},{7,39},{8,136... | collective-permute-start | bytes 221192 | tf_op jit(solution)/shard_map/ppermute | solution.py:29
  27.9 0.9 collective-permute-start.10
  28.8 0.3 collective-permute-start.9
  29.1 2.8 %collective-permute-done.11.p2 = bf16[288,128]{1,0:T(8,128)(2,1)S(1)} collective-permute-done((bf16[288,128]{1,0:T(8,128)(2,1)S(1)}, bf16[288,128]{1,0:T(8,128)(2,1)S(1)}, u32[]{:S(2)}, u32[]{:S(2)}) %collective-permute-start.11) | collective-permute-done | bytes 73760 | tf_op jit(solution)/shard_map/ppermute | solution.py:29
  31.9 0.6 collective-permute-done.10.p3
  32.5 0.0 collective-permute-done.9.p1
  32.5 0.9 %finish.1 = (bf16[8,4096]{1,0:T(8,128)(2,1)S(1)}, bf16[8,256]{1,0:T(8,128)(2,1)S(1)}, bf16[128,256]{1,0:T(8,128)(2,1)S(1)}) custom-call(bf16[288,128]{1,0:T(8,128)(2,1)S(1)} %merge.1.p0, bf16[288,128]{1,0:T(8,128)(2,1)S(1)} %collective-permute-done.9.p1, bf16[288,128]{1,0:T(8,128)(2,1)S(1)} %collective-permute-done.10.p3, ...), custom_call_target="tpu_custom_call" | custom-call | tf_op jit(solution)/shard_map/finish/pallas_call | solution.py:381
  33.4 21.5 %all_to_all.10 = bf16[16,8,256]{2,1,0:T(8,128)(2,1)S(1)} all-to-all(bf16[16,8,256]{2,1,0:T(8,128)(2,1)S(1)} %bitcast.9), channel_id=1, replica_groups=mesh['ctx'=16,'exp'=16] {'exp'}, dimensions={0} | all-to-all | bytes 131072 | tf_op jit(solution)/shard_map/all_to_all | solution.py:503
  54.9 0.6 gate_up.1
  55.5 2.2 %collective-permute-start.12 = (bf16[32,1664]{1,0:T(8,128)(2,1)S(1)}, bf16[32,1664]{1,0:T(8,128)(2,1)S(1)}, u32[]{:S(2)}, u32[]{:S(2)}) collective-permute-start(bf16[32,1664]{1,0:T(8,128)(2,1)S(1)} %get-tuple-element.28), channel_id=1, source_target_pairs={{0,32},{1,129},{2,34},{3,131},{4,36},{5,133},{6,38},{7,135},{8,40}... | collective-permute-start | bytes 319496 | tf_op jit(solution)/shard_map/ppermute | solution.py:29
  57.6 0.8 collective-permute-start.13
  58.4 0.0 collective-permute-start.14
  58.4 1.4 %settle.1 = (bf16[4,768,256]{2,1,0:T(8,128)(2,1)S(1)}, bf16[8,4096]{1,0:T(8,128)(2,1)}) custom-call(bf16[32,1664]{1,0:T(8,128)(2,1)S(1)} %get-tuple-element.23.after.m0, bf16[4,768,256]{2,1,0:T(8,128)(2,1)} %refs_0_.7, bf16[8,4096]{1,0:T(8,128)(2,1)S(1)} %get-tuple-element.24.refs_1_), custom_call_target="tpu_custom_call" | custom-call | tf_op jit(solution)/shard_map/settle/pallas_call | solution.py:516
  59.9 1.0 %collective-permute-done.12.m1 = bf16[32,1664]{1,0:T(8,128)(2,1)S(1)} collective-permute-done((bf16[32,1664]{1,0:T(8,128)(2,1)S(1)}, bf16[32,1664]{1,0:T(8,128)(2,1)S(1)}, u32[]{:S(2)}, u32[]{:S(2)}) %collective-permute-start.12) | collective-permute-done | bytes 106528 | tf_op jit(solution)/shard_map/ppermute | solution.py:29
  60.9 1.5 %collective-permute-done.13.m3 = bf16[32,1664]{1,0:T(8,128)(2,1)S(1)} collective-permute-done((bf16[32,1664]{1,0:T(8,128)(2,1)S(1)}, bf16[32,1664]{1,0:T(8,128)(2,1)S(1)}, u32[]{:S(2)}, u32[]{:S(2)}) %collective-permute-start.13) | collective-permute-done | bytes 106528 | tf_op jit(solution)/shard_map/ppermute | solution.py:29
  62.4 0.0 collective-permute-done.14.m2
  62.4 0.2 add_rows.1.m0
  62.6 2.5 %collective-permute-start.17 = (bf16[32,1664]{1,0:T(8,128)(2,1)S(1)}, bf16[32,1664]{1,0:T(8,128)(2,1)S(1)}, u32[]{:S(2)}, u32[]{:S(2)}) collective-permute-start(bf16[32,1664]{1,0:T(8,128)(2,1)S(1)} %add_rows.1.m0), channel_id=1, source_target_pairs={{0,128},{1,33},{2,130},{3,35},{4,132},{5,37},{6,134},{7,39},{8,136... | collective-permute-start | bytes 319496 | tf_op jit(solution)/shard_map/ppermute | solution.py:29
  65.1 0.4 collective-permute-start.16
  65.6 0.1 collective-permute-start.15
  65.6 2.1 %collective-permute-done.17.m2 = bf16[32,1664]{1,0:T(8,128)(2,1)S(1)} collective-permute-done((bf16[32,1664]{1,0:T(8,128)(2,1)S(1)}, bf16[32,1664]{1,0:T(8,128)(2,1)S(1)}, u32[]{:S(2)}, u32[]{:S(2)}) %collective-permute-start.17) | collective-permute-done | bytes 106528 | tf_op jit(solution)/shard_map/ppermute | solution.py:29
  67.7 2.5 %collective-permute-done.16.m3 = bf16[32,1664]{1,0:T(8,128)(2,1)S(1)} collective-permute-done((bf16[32,1664]{1,0:T(8,128)(2,1)S(1)}, bf16[32,1664]{1,0:T(8,128)(2,1)S(1)}, u32[]{:S(2)}, u32[]{:S(2)}) %collective-permute-start.16) | collective-permute-done | bytes 106528 | tf_op jit(solution)/shard_map/ppermute | solution.py:29
  70.2 0.0 collective-permute-done.15.m1
  70.2 0.2 activate.1.x0
  70.4 1.3 %collective-permute-start.20 = (bf16[32,768]{1,0:T(8,128)(2,1)S(1)}, bf16[32,768]{1,0:T(8,128)(2,1)S(1)}, u32[]{:S(2)}, u32[]{:S(2)}) collective-permute-start(bf16[32,768]{1,0:T(8,128)(2,1)S(1)} %activate.1.x0), channel_id=1, source_target_pairs={{0,32},{1,129},{2,34},{3,131},{4,36},{5,133},{6,38},{7,135},{8,40}... | collective-permute-start | bytes 147464 | tf_op jit(solution)/shard_map/ppermute | solution.py:29
  71.7 1.3 %collective-permute-start.19 = (bf16[32,768]{1,0:T(8,128)(2,1)S(1)}, bf16[32,768]{1,0:T(8,128)(2,1)S(1)}, u32[]{:S(2)}, u32[]{:S(2)}) collective-permute-start(bf16[32,768]{1,0:T(8,128)(2,1)S(1)} %activate.1.x0), channel_id=1, source_target_pairs={{0,48},{1,193},{2,50},{3,195},{4,52},{5,197},{6,54},{7,199},{8,56}... | collective-permute-start | bytes 147464 | tf_op jit(solution)/shard_map/ppermute | solution.py:29
  73.0 0.2 collective-permute-start.18
  73.1 1.8 %collective-permute-done.20.x2 = bf16[32,768]{1,0:T(8,128)(2,1)S(1)} collective-permute-done((bf16[32,768]{1,0:T(8,128)(2,1)S(1)}, bf16[32,768]{1,0:T(8,128)(2,1)S(1)}, u32[]{:S(2)}, u32[]{:S(2)}) %collective-permute-start.20) | collective-permute-done | bytes 49184 | tf_op jit(solution)/shard_map/ppermute | solution.py:29
  74.9 0.9 %collective-permute-done.19.x3 = bf16[32,768]{1,0:T(8,128)(2,1)S(1)} collective-permute-done((bf16[32,768]{1,0:T(8,128)(2,1)S(1)}, bf16[32,768]{1,0:T(8,128)(2,1)S(1)}, u32[]{:S(2)}, u32[]{:S(2)}) %collective-permute-start.19) | collective-permute-done | bytes 49184 | tf_op jit(solution)/shard_map/ppermute | solution.py:29
  75.9 0.1 collective-permute-done.18.x1
  75.9 0.4 down.1
  76.3 14.4 %all_to_all.11 = bf16[16,8,256]{2,1,0:T(8,128)(2,1)S(1)} all-to-all(bf16[16,8,256]{2,1,0:T(8,128)(2,1)S(1)} %bitcast.7), channel_id=1, replica_groups=mesh['ctx'=16,'exp'=16] {'exp'}, dimensions={0} | all-to-all | bytes 131072 | tf_op jit(solution)/shard_map/all_to_all | solution.py:542
  90.8 0.7 combine.1
  (11 shorter events, 0.1 us)
Async XLA Ops:
  0.6 6.8 %copy-start.4 = (s32[8]{0:T(128)S(1)}, s32[8]{0:T(128)}, u32[]{:S(2)}) copy-start(s32[8]{0:T(128)} %lengths.1) | copy-start | bytes 100
  0.6 6.9 %copy-start.2 = (f32[8,8]{1,0:T(8,128)S(1)}, f32[8,8]{1,0:T(8,128)}, u32[]{:S(2)}) copy-start(f32[8,8]{1,0:T(8,128)} %gates.1) | copy-start | bytes 772
  0.7 6.9 %copy-start.1 = (s32[8,8]{1,0:T(8,128)S(1)}, s32[8,8]{1,0:T(8,128)}, u32[]{:S(2)}) copy-start(s32[8,8]{1,0:T(8,128)} %routes.1) | copy-start | bytes 772
  2.8 7.1 %collective-permute-start.2 = (f16[8,5248]{1,0:T(8,128)(2,1)S(1)}, f16[8,5248]{1,0:T(8,128)(2,1)S(1)}, u32[]{:S(2)}, u32[]{:S(2)}) collective-permute-start(f16[8,5248]{1,0:T(8,128)(2,1)S(1)} %convert_element_type.40), channel_id=1, source_target_pairs={{0,32},{1,129},{2,34},{3,131},{4,36},{5,133},{6,38},{7,135},{8,40}... | collective-permute-start | bytes 251912 | tf_op jit(solution)/shard_map/ppermute | solution.py:29
  6.6 4.8 %collective-permute-start.1 = (f16[8,5248]{1,0:T(8,128)(2,1)S(1)}, f16[8,5248]{1,0:T(8,128)(2,1)S(1)}, u32[]{:S(2)}, u32[]{:S(2)}) collective-permute-start(f16[8,5248]{1,0:T(8,128)(2,1)S(1)} %convert_element_type.40), channel_id=1, source_target_pairs={{0,48},{1,193},{2,50},{3,195},{4,52},{5,197},{6,54},{7,199},{8,56}... | collective-permute-start | bytes 251912 | tf_op jit(solution)/shard_map/ppermute | solution.py:29
  7.4 4.0 %collective-permute-start = (f16[8,5248]{1,0:T(8,128)(2,1)S(1)}, f16[8,5248]{1,0:T(8,128)(2,1)S(1)}, u32[]{:S(2)}, u32[]{:S(2)}) collective-permute-start(f16[8,5248]{1,0:T(8,128)(2,1)S(1)} %convert_element_type.40), channel_id=1, source_target_pairs={{0,16},{1,65},{2,18},{3,67},{4,20},{5,69},{6,22},{7,71},{8,24},{9,... | collective-permute-start | bytes 251912 | tf_op jit(solution)/shard_map/ppermute | solution.py:29
  11.5 5.1 %collective-permute-start.5 = (f16[8,5248]{1,0:T(8,128)(2,1)S(1)}, f16[8,5248]{1,0:T(8,128)(2,1)S(1)}, u32[]{:S(2)}, u32[]{:S(2)}) collective-permute-start(f16[8,5248]{1,0:T(8,128)(2,1)S(1)} %get-tuple-element.32), channel_id=1, source_target_pairs={{0,128},{1,33},{2,130},{3,35},{4,132},{5,37},{6,134},{7,39},{8,136... | collective-permute-start | bytes 251912 | tf_op jit(solution)/shard_map/ppermute | solution.py:29
  14.0 4.8 %collective-permute-start.4 = (f16[8,5248]{1,0:T(8,128)(2,1)S(1)}, f16[8,5248]{1,0:T(8,128)(2,1)S(1)}, u32[]{:S(2)}, u32[]{:S(2)}) collective-permute-start(f16[8,5248]{1,0:T(8,128)(2,1)S(1)} %get-tuple-element.32), channel_id=1, source_target_pairs={{0,192},{1,49},{2,194},{3,51},{4,196},{5,53},{6,198},{7,55},{8,200... | collective-permute-start | bytes 251912 | tf_op jit(solution)/shard_map/ppermute | solution.py:29
  14.9 3.9 %collective-permute-start.3 = (f16[8,5248]{1,0:T(8,128)(2,1)S(1)}, f16[8,5248]{1,0:T(8,128)(2,1)S(1)}, u32[]{:S(2)}, u32[]{:S(2)}) collective-permute-start(f16[8,5248]{1,0:T(8,128)(2,1)S(1)} %get-tuple-element.32), channel_id=1, source_target_pairs={{0,64},{1,17},{2,66},{3,19},{4,68},{5,21},{6,70},{7,23},{8,72},{9,... | collective-permute-start | bytes 251912 | tf_op jit(solution)/shard_map/ppermute | solution.py:29
  19.9 4.8 %collective-permute-start.8 = (bf16[288,128]{1,0:T(8,128)(2,1)S(1)}, bf16[288,128]{1,0:T(8,128)(2,1)S(1)}, u32[]{:S(2)}, u32[]{:S(2)}) collective-permute-start(bf16[288,128]{1,0:T(8,128)(2,1)S(1)} %attend.1.after.p0), channel_id=1, source_target_pairs={{0,32},{1,129},{2,34},{3,131},{4,36},{5,133},{6,38},{7,135},{8,40}... | collective-permute-start | bytes 221192 | tf_op jit(solution)/shard_map/ppermute | solution.py:29
  21.6 4.4 %collective-permute-start.7 = (bf16[288,128]{1,0:T(8,128)(2,1)S(1)}, bf16[288,128]{1,0:T(8,128)(2,1)S(1)}, u32[]{:S(2)}, u32[]{:S(2)}) collective-permute-start(bf16[288,128]{1,0:T(8,128)(2,1)S(1)} %attend.1.after.p0), channel_id=1, source_target_pairs={{0,48},{1,193},{2,50},{3,195},{4,52},{5,197},{6,54},{7,199},{8,56}... | collective-permute-start | bytes 221192 | tf_op jit(solution)/shard_map/ppermute | solution.py:29
  22.3 3.6 %collective-permute-start.6 = (bf16[288,128]{1,0:T(8,128)(2,1)S(1)}, bf16[288,128]{1,0:T(8,128)(2,1)S(1)}, u32[]{:S(2)}, u32[]{:S(2)}) collective-permute-start(bf16[288,128]{1,0:T(8,128)(2,1)S(1)} %attend.1.after.p0), channel_id=1, source_target_pairs={{0,16},{1,65},{2,18},{3,67},{4,20},{5,69},{6,22},{7,71},{8,24},{9,... | collective-permute-start | bytes 221192 | tf_op jit(solution)/shard_map/ppermute | solution.py:29
  24.5 8.0 %copy-start = (bf16[8,256]{1,0:T(8,128)(2,1)S(1)}, bf16[8,256]{1,0:T(8,128)(2,1)}, u32[]{:S(2)}) copy-start(bf16[8,256]{1,0:T(8,128)(2,1)} %tokens.1) | copy-start | bytes 12292
  26.3 28.6 %copy-start.3 = (f32[256]{0:T(256)S(1)}, f32[256]{0:T(256)}, u32[]{:S(2)}) copy-start(f32[256]{0:T(256)} %param.19) | copy-start | bytes 3076
  26.3 5.6 %collective-permute-start.11 = (bf16[288,128]{1,0:T(8,128)(2,1)S(1)}, bf16[288,128]{1,0:T(8,128)(2,1)S(1)}, u32[]{:S(2)}, u32[]{:S(2)}) collective-permute-start(bf16[288,128]{1,0:T(8,128)(2,1)S(1)} %merge.1.p0), channel_id=1, source_target_pairs={{0,128},{1,33},{2,130},{3,35},{4,132},{5,37},{6,134},{7,39},{8,136... | collective-permute-start | bytes 221192 | tf_op jit(solution)/shard_map/ppermute | solution.py:29
  27.9 4.6 %collective-permute-start.10 = (bf16[288,128]{1,0:T(8,128)(2,1)S(1)}, bf16[288,128]{1,0:T(8,128)(2,1)S(1)}, u32[]{:S(2)}, u32[]{:S(2)}) collective-permute-start(bf16[288,128]{1,0:T(8,128)(2,1)S(1)} %merge.1.p0), channel_id=1, source_target_pairs={{0,192},{1,49},{2,194},{3,51},{4,196},{5,53},{6,198},{7,55},{8,200... | collective-permute-start | bytes 221192 | tf_op jit(solution)/shard_map/ppermute | solution.py:29
  28.8 3.7 %collective-permute-start.9 = (bf16[288,128]{1,0:T(8,128)(2,1)S(1)}, bf16[288,128]{1,0:T(8,128)(2,1)S(1)}, u32[]{:S(2)}, u32[]{:S(2)}) collective-permute-start(bf16[288,128]{1,0:T(8,128)(2,1)S(1)} %merge.1.p0), channel_id=1, source_target_pairs={{0,64},{1,17},{2,66},{3,19},{4,68},{5,21},{6,70},{7,23},{8,72},{9,... | collective-permute-start | bytes 221192 | tf_op jit(solution)/shard_map/ppermute | solution.py:29
  55.5 5.4 %collective-permute-start.12 = (bf16[32,1664]{1,0:T(8,128)(2,1)S(1)}, bf16[32,1664]{1,0:T(8,128)(2,1)S(1)}, u32[]{:S(2)}, u32[]{:S(2)}) collective-permute-start(bf16[32,1664]{1,0:T(8,128)(2,1)S(1)} %get-tuple-element.28), channel_id=1, source_target_pairs={{0,32},{1,129},{2,34},{3,131},{4,36},{5,133},{6,38},{7,135},{8,40}... | collective-permute-start | bytes 319496 | tf_op jit(solution)/shard_map/ppermute | solution.py:29
  57.6 4.8 %collective-permute-start.13 = (bf16[32,1664]{1,0:T(8,128)(2,1)S(1)}, bf16[32,1664]{1,0:T(8,128)(2,1)S(1)}, u32[]{:S(2)}, u32[]{:S(2)}) collective-permute-start(bf16[32,1664]{1,0:T(8,128)(2,1)S(1)} %get-tuple-element.29), channel_id=1, source_target_pairs={{0,48},{1,193},{2,50},{3,195},{4,52},{5,197},{6,54},{7,199},{8,56}... | collective-permute-start | bytes 319496 | tf_op jit(solution)/shard_map/ppermute | solution.py:29
  58.4 4.0 %collective-permute-start.14 = (bf16[32,1664]{1,0:T(8,128)(2,1)S(1)}, bf16[32,1664]{1,0:T(8,128)(2,1)S(1)}, u32[]{:S(2)}, u32[]{:S(2)}) collective-permute-start(bf16[32,1664]{1,0:T(8,128)(2,1)S(1)} %get-tuple-element.30), channel_id=1, source_target_pairs={{0,16},{1,65},{2,18},{3,67},{4,20},{5,69},{6,22},{7,71},{8,24},{9,... | collective-permute-start | bytes 319496 | tf_op jit(solution)/shard_map/ppermute | solution.py:29
  62.6 5.1 %collective-permute-start.17 = (bf16[32,1664]{1,0:T(8,128)(2,1)S(1)}, bf16[32,1664]{1,0:T(8,128)(2,1)S(1)}, u32[]{:S(2)}, u32[]{:S(2)}) collective-permute-start(bf16[32,1664]{1,0:T(8,128)(2,1)S(1)} %add_rows.1.m0), channel_id=1, source_target_pairs={{0,128},{1,33},{2,130},{3,35},{4,132},{5,37},{6,134},{7,39},{8,136... | collective-permute-start | bytes 319496 | tf_op jit(solution)/shard_map/ppermute | solution.py:29
  65.1 5.1 %collective-permute-start.16 = (bf16[32,1664]{1,0:T(8,128)(2,1)S(1)}, bf16[32,1664]{1,0:T(8,128)(2,1)S(1)}, u32[]{:S(2)}, u32[]{:S(2)}) collective-permute-start(bf16[32,1664]{1,0:T(8,128)(2,1)S(1)} %add_rows.1.m0), channel_id=1, source_target_pairs={{0,192},{1,49},{2,194},{3,51},{4,196},{5,53},{6,198},{7,55},{8,200... | collective-permute-start | bytes 319496 | tf_op jit(solution)/shard_map/ppermute | solution.py:29
  65.6 4.6 %collective-permute-start.15 = (bf16[32,1664]{1,0:T(8,128)(2,1)S(1)}, bf16[32,1664]{1,0:T(8,128)(2,1)S(1)}, u32[]{:S(2)}, u32[]{:S(2)}) collective-permute-start(bf16[32,1664]{1,0:T(8,128)(2,1)S(1)} %add_rows.1.m0), channel_id=1, source_target_pairs={{0,64},{1,17},{2,66},{3,19},{4,68},{5,21},{6,70},{7,23},{8,72},{9,... | collective-permute-start | bytes 319496 | tf_op jit(solution)/shard_map/ppermute | solution.py:29
  70.4 4.5 %collective-permute-start.20 = (bf16[32,768]{1,0:T(8,128)(2,1)S(1)}, bf16[32,768]{1,0:T(8,128)(2,1)S(1)}, u32[]{:S(2)}, u32[]{:S(2)}) collective-permute-start(bf16[32,768]{1,0:T(8,128)(2,1)S(1)} %activate.1.x0), channel_id=1, source_target_pairs={{0,32},{1,129},{2,34},{3,131},{4,36},{5,133},{6,38},{7,135},{8,40}... | collective-permute-start | bytes 147464 | tf_op jit(solution)/shard_map/ppermute | solution.py:29
  71.7 4.2 %collective-permute-start.19 = (bf16[32,768]{1,0:T(8,128)(2,1)S(1)}, bf16[32,768]{1,0:T(8,128)(2,1)S(1)}, u32[]{:S(2)}, u32[]{:S(2)}) collective-permute-start(bf16[32,768]{1,0:T(8,128)(2,1)S(1)} %activate.1.x0), channel_id=1, source_target_pairs={{0,48},{1,193},{2,50},{3,195},{4,52},{5,197},{6,54},{7,199},{8,56}... | collective-permute-start | bytes 147464 | tf_op jit(solution)/shard_map/ppermute | solution.py:29
  73.0 2.9 %collective-permute-start.18 = (bf16[32,768]{1,0:T(8,128)(2,1)S(1)}, bf16[32,768]{1,0:T(8,128)(2,1)S(1)}, u32[]{:S(2)}, u32[]{:S(2)}) collective-permute-start(bf16[32,768]{1,0:T(8,128)(2,1)S(1)} %activate.1.x0), channel_id=1, source_target_pairs={{0,16},{1,65},{2,18},{3,67},{4,20},{5,69},{6,22},{7,71},{8,24},{9,... | collective-permute-start | bytes 147464 | tf_op jit(solution)/shard_map/ppermute | solution.py:29

commit v10 on v9

--- a/solution.py
+++ b/solution.py
@@ -125,7 +125,7 @@
         pltpu.make_async_copy(tokens_hbm, tokens, small.at[0]),
         pltpu.make_async_copy(gain_hbm, gain, small.at[1]),
     ]
-    for copy in first + copies:
+    for copy in copies[:1] + first + copies[1:]:
         copy.start()
     for copy in first:
         copy.wait()

time: 91.8 us -> 91.8 us (level)
  no operation moved by 1% of the time
where the time goes in v10:
time: 91.8 us; the launch traced here: 91.5 us
  blocking collectives  35.9 us (39%)
  starting transfers between devices  22.1 us (24%)
  waiting for transfers between devices  18.6 us (20%)
  Pallas kernels  13.8 us (15%)
    ppermute x21, starting transfers between devices, exchange(): got[step] = lax.ppermute(sent, AXES, pairs)  22.1 us
    all_to_all x1, blocking collectives, local(): lax.all_to_all(outgoing.reshape(n_exp, per_source, slice_width), 'exp', s...  21.5 us
    ppermute x21, waiting for transfers between devices, exchange(): got[step] = lax.ppermute(sent, AXES, pairs)  18.6 us
    all_to_all x1, blocking collectives, local(): lax.all_to_all(expert_out.reshape(n_exp, per_source, slice_width), 'exp',...  14.4 us
    pallas_call x13, Pallas kernels, call(): pl.pallas_call(kernel, out_shape=out, in_specs=specs, out_specs=jax.tree....  12.3 us
  transfers between devices with their start and end apart: 21, of which 13 were waited for; matrix products, arithmetic and copies ran while one was open for 0% of the time, Pallas kernels for 8%

profile of v10, /device:TPU:1, one launch (start us, length us, event | category | flops | bytes accessed | tf_op | source)
XLA Modules:
  0.0 91.5 jit_solution(7235015719429773647)
XLA Ops:
  0.6 0.0 copy-start.4
  0.7 2.1 %project.1.after = f32[8,5248]{1,0:T(8,128)S(1)} custom-call(bf16[8,256]{1,0:T(8,128)(2,1)} %tokens.1, f32[1,256]{1,0:T(1,128)} %bitcast.11, bf16[256,5120]{1,0:T(8,128)(2,1)} %w_hbm.1), custom_call_target="tpu_custom_call" | custom-call | tf_op jit(solution)/shard_map/project/pallas_call | solution.py:381
  2.8 3.8 %collective-permute-start.2 = (f16[8,5248]{1,0:T(8,128)(2,1)S(1)}, f16[8,5248]{1,0:T(8,128)(2,1)S(1)}, u32[]{:S(2)}, u32[]{:S(2)}) collective-permute-start(f16[8,5248]{1,0:T(8,128)(2,1)S(1)} %convert_element_type.40), channel_id=1, source_target_pairs={{0,32},{1,129},{2,34},{3,131},{4,36},{5,133},{6,38},{7,135},{8,40}... | collective-permute-start | bytes 251912 | tf_op jit(solution)/shard_map/ppermute | solution.py:29
  6.6 0.8 collective-permute-start.1
  7.4 0.0 collective-permute-start
  7.4 0.1 fusion
  7.5 0.7 prepare.1
  8.3 1.6 %load.3 = (bf16[8,128,512]{2,1,0:T(8,128)(2,1)S(1)}, bf16[8,128,512]{2,1,0:T(8,128)(2,1)S(1)}) custom-call(f32[8,5248]{1,0:T(8,128)S(1)} %project.1.after, bf16[8,128,512]{2,1,0:T(8,128)(2,1)} %refs_0_.4, bf16[8,128,512]{2,1,0:T(8,128)(2,1)} %refs_1_.1), custom_call_target="tpu_custom_call" | custom-call | tf_op jit(solution)/shard_map/load/pallas_call | solution.py:381
  9.8 0.0 collective-permute-done.2
  9.8 1.6 %collective-permute-done.1 = f16[8,5248]{1,0:T(8,128)(2,1)S(1)} collective-permute-done((f16[8,5248]{1,0:T(8,128)(2,1)S(1)}, f16[8,5248]{1,0:T(8,128)(2,1)S(1)}, u32[]{:S(2)}, u32[]{:S(2)}) %collective-permute-start.1) | collective-permute-done | bytes 84000 | tf_op jit(solution)/shard_map/ppermute | solution.py:29
  11.4 0.0 collective-permute-done
  11.4 0.1 fusion.1
  11.5 2.5 %collective-permute-start.5 = (f16[8,5248]{1,0:T(8,128)(2,1)S(1)}, f16[8,5248]{1,0:T(8,128)(2,1)S(1)}, u32[]{:S(2)}, u32[]{:S(2)}) collective-permute-start(f16[8,5248]{1,0:T(8,128)(2,1)S(1)} %get-tuple-element.32), channel_id=1, source_target_pairs={{0,128},{1,33},{2,130},{3,35},{4,132},{5,37},{6,134},{7,39},{8,136... | collective-permute-start | bytes 251912 | tf_op jit(solution)/shard_map/ppermute | solution.py:29
  14.0 0.9 collective-permute-start.4
  14.9 0.0 collective-permute-start.3
  14.9 0.1 pad_maximum_fusion
  15.0 1.6 %load.4.after.w_ref = bf16[4096,256]{1,0:T(8,128)(2,1)S(1)} custom-call(f32[8,5248]{1,0:T(8,128)S(1)} %get-tuple-element.33.after, bf16[4096,256]{1,0:T(8,128)(2,1)} %refs_0_.5), custom_call_target="tpu_custom_call" | custom-call | tf_op jit(solution)/shard_map/load/pallas_call | solution.py:381
  16.6 0.0 collective-permute-done.5
  16.6 2.2 %collective-permute-done.4 = f16[8,5248]{1,0:T(8,128)(2,1)S(1)} collective-permute-done((f16[8,5248]{1,0:T(8,128)(2,1)S(1)}, f16[8,5248]{1,0:T(8,128)(2,1)S(1)}, u32[]{:S(2)}, u32[]{:S(2)}) %collective-permute-start.4) | collective-permute-done | bytes 84000 | tf_op jit(solution)/shard_map/ppermute | solution.py:29
  18.8 0.0 collective-permute-done.3
  18.8 1.1 %attend.1.after.p0 = bf16[288,128]{1,0:T(8,128)(2,1)S(1)} custom-call(f32[8,5248]{1,0:T(8,128)S(1)} %add_add_fusion.shares, f32[8,128]{1,0:T(8,128)S(1)} %get-tuple-element.37.cosine, f32[8,128]{1,0:T(8,128)S(1)} %get-tuple-element.38.sine, f32[8,128]{1,0:T(8,128)S(1)} %get-tuple-element.17.live_ref, f32[8,128]{1,0:T(8,128)S(1)} %get-tuple-element.18.owns, ...), custom_call_target="tpu_custom_call" | custom-call | tf_op jit(solution)/shard_map/attend/pallas_call | solution.py:381
  19.9 1.6 %collective-permute-start.8 = (bf16[288,128]{1,0:T(8,128)(2,1)S(1)}, bf16[288,128]{1,0:T(8,128)(2,1)S(1)}, u32[]{:S(2)}, u32[]{:S(2)}) collective-permute-start(bf16[288,128]{1,0:T(8,128)(2,1)S(1)} %attend.1.after.p0), channel_id=1, source_target_pairs={{0,32},{1,129},{2,34},{3,131},{4,36},{5,133},{6,38},{7,135},{8,40}... | collective-permute-start | bytes 221192 | tf_op jit(solution)/shard_map/ppermute | solution.py:29
  21.6 0.8 collective-permute-start.7
  22.3 0.3 collective-permute-start.6
  22.6 1.9 %load.5.after.w_ref = bf16[4,256,1536]{2,1,0:T(8,128)(2,1)S(1)} custom-call(bf16[288,128]{1,0:T(8,128)(2,1)S(1)} %attend.1.after.p0, bf16[4,256,1536]{2,1,0:T(8,128)(2,1)} %refs_0_.6), custom_call_target="tpu_custom_call" | custom-call | tf_op jit(solution)/shard_map/load/pallas_call | solution.py:381
  24.5 0.0 copy-start
  24.5 0.1 collective-permute-done.8.p2
  24.7 1.3 %collective-permute-done.7.p3 = bf16[288,128]{1,0:T(8,128)(2,1)S(1)} collective-permute-done((bf16[288,128]{1,0:T(8,128)(2,1)S(1)}, bf16[288,128]{1,0:T(8,128)(2,1)S(1)}, u32[]{:S(2)}, u32[]{:S(2)}) %collective-permute-start.7) | collective-permute-done | bytes 73760 | tf_op jit(solution)/shard_map/ppermute | solution.py:29
  26.0 0.0 collective-permute-done.6.p1
  26.0 0.3 merge.1.p0
  26.3 0.0 copy-start.3
  26.3 1.6 %collective-permute-start.11 = (bf16[288,128]{1,0:T(8,128)(2,1)S(1)}, bf16[288,128]{1,0:T(8,128)(2,1)S(1)}, u32[]{:S(2)}, u32[]{:S(2)}) collective-permute-start(bf16[288,128]{1,0:T(8,128)(2,1)S(1)} %merge.1.p0), channel_id=1, source_target_pairs={{0,128},{1,33},{2,130},{3,35},{4,132},{5,37},{6,134},{7,39},{8,136... | collective-permute-start | bytes 221192 | tf_op jit(solution)/shard_map/ppermute | solution.py:29
  27.9 0.9 collective-permute-start.10
  28.8 0.3 collective-permute-start.9
  29.1 2.8 %collective-permute-done.11.p2 = bf16[288,128]{1,0:T(8,128)(2,1)S(1)} collective-permute-done((bf16[288,128]{1,0:T(8,128)(2,1)S(1)}, bf16[288,128]{1,0:T(8,128)(2,1)S(1)}, u32[]{:S(2)}, u32[]{:S(2)}) %collective-permute-start.11) | collective-permute-done | bytes 73760 | tf_op jit(solution)/shard_map/ppermute | solution.py:29
  31.9 0.6 collective-permute-done.10.p3
  32.5 0.0 collective-permute-done.9.p1
  32.5 0.9 %finish.1 = (bf16[8,4096]{1,0:T(8,128)(2,1)S(1)}, bf16[8,256]{1,0:T(8,128)(2,1)S(1)}, bf16[128,256]{1,0:T(8,128)(2,1)S(1)}) custom-call(bf16[288,128]{1,0:T(8,128)(2,1)S(1)} %merge.1.p0, bf16[288,128]{1,0:T(8,128)(2,1)S(1)} %collective-permute-done.9.p1, bf16[288,128]{1,0:T(8,128)(2,1)S(1)} %collective-permute-done.10.p3, ...), custom_call_target="tpu_custom_call" | custom-call | tf_op jit(solution)/shard_map/finish/pallas_call | solution.py:381
  33.4 21.5 %all_to_all.10 = bf16[16,8,256]{2,1,0:T(8,128)(2,1)S(1)} all-to-all(bf16[16,8,256]{2,1,0:T(8,128)(2,1)S(1)} %bitcast.9), channel_id=1, replica_groups=mesh['ctx'=16,'exp'=16] {'exp'}, dimensions={0} | all-to-all | bytes 131072 | tf_op jit(solution)/shard_map/all_to_all | solution.py:503
  54.9 0.6 gate_up.1
  55.5 2.2 %collective-permute-start.12 = (bf16[32,1664]{1,0:T(8,128)(2,1)S(1)}, bf16[32,1664]{1,0:T(8,128)(2,1)S(1)}, u32[]{:S(2)}, u32[]{:S(2)}) collective-permute-start(bf16[32,1664]{1,0:T(8,128)(2,1)S(1)} %get-tuple-element.28), channel_id=1, source_target_pairs={{0,32},{1,129},{2,34},{3,131},{4,36},{5,133},{6,38},{7,135},{8,40}... | collective-permute-start | bytes 319496 | tf_op jit(solution)/shard_map/ppermute | solution.py:29
  57.6 0.8 collective-permute-start.13
  58.4 0.0 collective-permute-start.14
  58.4 1.4 %settle.1 = (bf16[4,768,256]{2,1,0:T(8,128)(2,1)S(1)}, bf16[8,4096]{1,0:T(8,128)(2,1)}) custom-call(bf16[32,1664]{1,0:T(8,128)(2,1)S(1)} %get-tuple-element.23.after.m0, bf16[4,768,256]{2,1,0:T(8,128)(2,1)} %refs_0_.7, bf16[8,4096]{1,0:T(8,128)(2,1)S(1)} %get-tuple-element.24.refs_1_), custom_call_target="tpu_custom_call" | custom-call | tf_op jit(solution)/shard_map/settle/pallas_call | solution.py:516
  59.9 1.0 %collective-permute-done.12.m1 = bf16[32,1664]{1,0:T(8,128)(2,1)S(1)} collective-permute-done((bf16[32,1664]{1,0:T(8,128)(2,1)S(1)}, bf16[32,1664]{1,0:T(8,128)(2,1)S(1)}, u32[]{:S(2)}, u32[]{:S(2)}) %collective-permute-start.12) | collective-permute-done | bytes 106528 | tf_op jit(solution)/shard_map/ppermute | solution.py:29
  60.9 1.5 %collective-permute-done.13.m3 = bf16[32,1664]{1,0:T(8,128)(2,1)S(1)} collective-permute-done((bf16[32,1664]{1,0:T(8,128)(2,1)S(1)}, bf16[32,1664]{1,0:T(8,128)(2,1)S(1)}, u32[]{:S(2)}, u32[]{:S(2)}) %collective-permute-start.13) | collective-permute-done | bytes 106528 | tf_op jit(solution)/shard_map/ppermute | solution.py:29
  62.4 0.0 collective-permute-done.14.m2
  62.4 0.2 add_rows.1.m0
  62.6 2.5 %collective-permute-start.17 = (bf16[32,1664]{1,0:T(8,128)(2,1)S(1)}, bf16[32,1664]{1,0:T(8,128)(2,1)S(1)}, u32[]{:S(2)}, u32[]{:S(2)}) collective-permute-start(bf16[32,1664]{1,0:T(8,128)(2,1)S(1)} %add_rows.1.m0), channel_id=1, source_target_pairs={{0,128},{1,33},{2,130},{3,35},{4,132},{5,37},{6,134},{7,39},{8,136... | collective-permute-start | bytes 319496 | tf_op jit(solution)/shard_map/ppermute | solution.py:29
  65.1 0.4 collective-permute-start.16
  65.6 0.1 collective-permute-start.15
  65.6 2.1 %collective-permute-done.17.m2 = bf16[32,1664]{1,0:T(8,128)(2,1)S(1)} collective-permute-done((bf16[32,1664]{1,0:T(8,128)(2,1)S(1)}, bf16[32,1664]{1,0:T(8,128)(2,1)S(1)}, u32[]{:S(2)}, u32[]{:S(2)}) %collective-permute-start.17) | collective-permute-done | bytes 106528 | tf_op jit(solution)/shard_map/ppermute | solution.py:29
  67.7 2.5 %collective-permute-done.16.m3 = bf16[32,1664]{1,0:T(8,128)(2,1)S(1)} collective-permute-done((bf16[32,1664]{1,0:T(8,128)(2,1)S(1)}, bf16[32,1664]{1,0:T(8,128)(2,1)S(1)}, u32[]{:S(2)}, u32[]{:S(2)}) %collective-permute-start.16) | collective-permute-done | bytes 106528 | tf_op jit(solution)/shard_map/ppermute | solution.py:29
  70.2 0.0 collective-permute-done.15.m1
  70.2 0.2 activate.1.x0
  70.4 1.3 %collective-permute-start.20 = (bf16[32,768]{1,0:T(8,128)(2,1)S(1)}, bf16[32,768]{1,0:T(8,128)(2,1)S(1)}, u32[]{:S(2)}, u32[]{:S(2)}) collective-permute-start(bf16[32,768]{1,0:T(8,128)(2,1)S(1)} %activate.1.x0), channel_id=1, source_target_pairs={{0,32},{1,129},{2,34},{3,131},{4,36},{5,133},{6,38},{7,135},{8,40}... | collective-permute-start | bytes 147464 | tf_op jit(solution)/shard_map/ppermute | solution.py:29
  71.7 1.3 %collective-permute-start.19 = (bf16[32,768]{1,0:T(8,128)(2,1)S(1)}, bf16[32,768]{1,0:T(8,128)(2,1)S(1)}, u32[]{:S(2)}, u32[]{:S(2)}) collective-permute-start(bf16[32,768]{1,0:T(8,128)(2,1)S(1)} %activate.1.x0), channel_id=1, source_target_pairs={{0,48},{1,193},{2,50},{3,195},{4,52},{5,197},{6,54},{7,199},{8,56}... | collective-permute-start | bytes 147464 | tf_op jit(solution)/shard_map/ppermute | solution.py:29
  73.0 0.2 collective-permute-start.18
  73.1 1.8 %collective-permute-done.20.x2 = bf16[32,768]{1,0:T(8,128)(2,1)S(1)} collective-permute-done((bf16[32,768]{1,0:T(8,128)(2,1)S(1)}, bf16[32,768]{1,0:T(8,128)(2,1)S(1)}, u32[]{:S(2)}, u32[]{:S(2)}) %collective-permute-start.20) | collective-permute-done | bytes 49184 | tf_op jit(solution)/shard_map/ppermute | solution.py:29
  74.9 0.9 %collective-permute-done.19.x3 = bf16[32,768]{1,0:T(8,128)(2,1)S(1)} collective-permute-done((bf16[32,768]{1,0:T(8,128)(2,1)S(1)}, bf16[32,768]{1,0:T(8,128)(2,1)S(1)}, u32[]{:S(2)}, u32[]{:S(2)}) %collective-permute-start.19) | collective-permute-done | bytes 49184 | tf_op jit(solution)/shard_map/ppermute | solution.py:29
  75.9 0.1 collective-permute-done.18.x1
  75.9 0.4 down.1
  76.3 14.4 %all_to_all.11 = bf16[16,8,256]{2,1,0:T(8,128)(2,1)S(1)} all-to-all(bf16[16,8,256]{2,1,0:T(8,128)(2,1)S(1)} %bitcast.7), channel_id=1, replica_groups=mesh['ctx'=16,'exp'=16] {'exp'}, dimensions={0} | all-to-all | bytes 131072 | tf_op jit(solution)/shard_map/all_to_all | solution.py:542
  90.8 0.7 combine.1
  (11 shorter events, 0.1 us)
Async XLA Ops:
  0.6 6.8 %copy-start.4 = (s32[8]{0:T(128)S(1)}, s32[8]{0:T(128)}, u32[]{:S(2)}) copy-start(s32[8]{0:T(128)} %lengths.1) | copy-start | bytes 100
  0.6 6.9 %copy-start.2 = (f32[8,8]{1,0:T(8,128)S(1)}, f32[8,8]{1,0:T(8,128)}, u32[]{:S(2)}) copy-start(f32[8,8]{1,0:T(8,128)} %gates.1) | copy-start | bytes 772
  0.7 6.9 %copy-start.1 = (s32[8,8]{1,0:T(8,128)S(1)}, s32[8,8]{1,0:T(8,128)}, u32[]{:S(2)}) copy-start(s32[8,8]{1,0:T(8,128)} %routes.1) | copy-start | bytes 772
  2.8 7.1 %collective-permute-start.2 = (f16[8,5248]{1,0:T(8,128)(2,1)S(1)}, f16[8,5248]{1,0:T(8,128)(2,1)S(1)}, u32[]{:S(2)}, u32[]{:S(2)}) collective-permute-start(f16[8,5248]{1,0:T(8,128)(2,1)S(1)} %convert_element_type.40), channel_id=1, source_target_pairs={{0,32},{1,129},{2,34},{3,131},{4,36},{5,133},{6,38},{7,135},{8,40}... | collective-permute-start | bytes 251912 | tf_op jit(solution)/shard_map/ppermute | solution.py:29
  6.6 4.8 %collective-permute-start.1 = (f16[8,5248]{1,0:T(8,128)(2,1)S(1)}, f16[8,5248]{1,0:T(8,128)(2,1)S(1)}, u32[]{:S(2)}, u32[]{:S(2)}) collective-permute-start(f16[8,5248]{1,0:T(8,128)(2,1)S(1)} %convert_element_type.40), channel_id=1, source_target_pairs={{0,48},{1,193},{2,50},{3,195},{4,52},{5,197},{6,54},{7,199},{8,56}... | collective-permute-start | bytes 251912 | tf_op jit(solution)/shard_map/ppermute | solution.py:29
  7.4 4.0 %collective-permute-start = (f16[8,5248]{1,0:T(8,128)(2,1)S(1)}, f16[8,5248]{1,0:T(8,128)(2,1)S(1)}, u32[]{:S(2)}, u32[]{:S(2)}) collective-permute-start(f16[8,5248]{1,0:T(8,128)(2,1)S(1)} %convert_element_type.40), channel_id=1, source_target_pairs={{0,16},{1,65},{2,18},{3,67},{4,20},{5,69},{6,22},{7,71},{8,24},{9,... | collective-permute-start | bytes 251912 | tf_op jit(solution)/shard_map/ppermute | solution.py:29
  11.5 5.1 %collective-permute-start.5 = (f16[8,5248]{1,0:T(8,128)(2,1)S(1)}, f16[8,5248]{1,0:T(8,128)(2,1)S(1)}, u32[]{:S(2)}, u32[]{:S(2)}) collective-permute-start(f16[8,5248]{1,0:T(8,128)(2,1)S(1)} %get-tuple-element.32), channel_id=1, source_target_pairs={{0,128},{1,33},{2,130},{3,35},{4,132},{5,37},{6,134},{7,39},{8,136... | collective-permute-start | bytes 251912 | tf_op jit(solution)/shard_map/ppermute | solution.py:29
  14.0 4.8 %collective-permute-start.4 = (f16[8,5248]{1,0:T(8,128)(2,1)S(1)}, f16[8,5248]{1,0:T(8,128)(2,1)S(1)}, u32[]{:S(2)}, u32[]{:S(2)}) collective-permute-start(f16[8,5248]{1,0:T(8,128)(2,1)S(1)} %get-tuple-element.32), channel_id=1, source_target_pairs={{0,192},{1,49},{2,194},{3,51},{4,196},{5,53},{6,198},{7,55},{8,200... | collective-permute-start | bytes 251912 | tf_op jit(solution)/shard_map/ppermute | solution.py:29
  14.9 3.9 %collective-permute-start.3 = (f16[8,5248]{1,0:T(8,128)(2,1)S(1)}, f16[8,5248]{1,0:T(8,128)(2,1)S(1)}, u32[]{:S(2)}, u32[]{:S(2)}) collective-permute-start(f16[8,5248]{1,0:T(8,128)(2,1)S(1)} %get-tuple-element.32), channel_id=1, source_target_pairs={{0,64},{1,17},{2,66},{3,19},{4,68},{5,21},{6,70},{7,23},{8,72},{9,... | collective-permute-start | bytes 251912 | tf_op jit(solution)/shard_map/ppermute | solution.py:29
  19.9 4.8 %collective-permute-start.8 = (bf16[288,128]{1,0:T(8,128)(2,1)S(1)}, bf16[288,128]{1,0:T(8,128)(2,1)S(1)}, u32[]{:S(2)}, u32[]{:S(2)}) collective-permute-start(bf16[288,128]{1,0:T(8,128)(2,1)S(1)} %attend.1.after.p0), channel_id=1, source_target_pairs={{0,32},{1,129},{2,34},{3,131},{4,36},{5,133},{6,38},{7,135},{8,40}... | collective-permute-start | bytes 221192 | tf_op jit(solution)/shard_map/ppermute | solution.py:29
  21.6 4.4 %collective-permute-start.7 = (bf16[288,128]{1,0:T(8,128)(2,1)S(1)}, bf16[288,128]{1,0:T(8,128)(2,1)S(1)}, u32[]{:S(2)}, u32[]{:S(2)}) collective-permute-start(bf16[288,128]{1,0:T(8,128)(2,1)S(1)} %attend.1.after.p0), channel_id=1, source_target_pairs={{0,48},{1,193},{2,50},{3,195},{4,52},{5,197},{6,54},{7,199},{8,56}... | collective-permute-start | bytes 221192 | tf_op jit(solution)/shard_map/ppermute | solution.py:29
  22.3 3.6 %collective-permute-start.6 = (bf16[288,128]{1,0:T(8,128)(2,1)S(1)}, bf16[288,128]{1,0:T(8,128)(2,1)S(1)}, u32[]{:S(2)}, u32[]{:S(2)}) collective-permute-start(bf16[288,128]{1,0:T(8,128)(2,1)S(1)} %attend.1.after.p0), channel_id=1, source_target_pairs={{0,16},{1,65},{2,18},{3,67},{4,20},{5,69},{6,22},{7,71},{8,24},{9,... | collective-permute-start | bytes 221192 | tf_op jit(solution)/shard_map/ppermute | solution.py:29
  24.5 8.0 %copy-start = (bf16[8,256]{1,0:T(8,128)(2,1)S(1)}, bf16[8,256]{1,0:T(8,128)(2,1)}, u32[]{:S(2)}) copy-start(bf16[8,256]{1,0:T(8,128)(2,1)} %tokens.1) | copy-start | bytes 12292
  26.3 28.6 %copy-start.3 = (f32[256]{0:T(256)S(1)}, f32[256]{0:T(256)}, u32[]{:S(2)}) copy-start(f32[256]{0:T(256)} %param.19) | copy-start | bytes 3076
  26.3 5.6 %collective-permute-start.11 = (bf16[288,128]{1,0:T(8,128)(2,1)S(1)}, bf16[288,128]{1,0:T(8,128)(2,1)S(1)}, u32[]{:S(2)}, u32[]{:S(2)}) collective-permute-start(bf16[288,128]{1,0:T(8,128)(2,1)S(1)} %merge.1.p0), channel_id=1, source_target_pairs={{0,128},{1,33},{2,130},{3,35},{4,132},{5,37},{6,134},{7,39},{8,136... | collective-permute-start | bytes 221192 | tf_op jit(solution)/shard_map/ppermute | solution.py:29
  27.9 4.6 %collective-permute-start.10 = (bf16[288,128]{1,0:T(8,128)(2,1)S(1)}, bf16[288,128]{1,0:T(8,128)(2,1)S(1)}, u32[]{:S(2)}, u32[]{:S(2)}) collective-permute-start(bf16[288,128]{1,0:T(8,128)(2,1)S(1)} %merge.1.p0), channel_id=1, source_target_pairs={{0,192},{1,49},{2,194},{3,51},{4,196},{5,53},{6,198},{7,55},{8,200... | collective-permute-start | bytes 221192 | tf_op jit(solution)/shard_map/ppermute | solution.py:29
  28.8 3.7 %collective-permute-start.9 = (bf16[288,128]{1,0:T(8,128)(2,1)S(1)}, bf16[288,128]{1,0:T(8,128)(2,1)S(1)}, u32[]{:S(2)}, u32[]{:S(2)}) collective-permute-start(bf16[288,128]{1,0:T(8,128)(2,1)S(1)} %merge.1.p0), channel_id=1, source_target_pairs={{0,64},{1,17},{2,66},{3,19},{4,68},{5,21},{6,70},{7,23},{8,72},{9,... | collective-permute-start | bytes 221192 | tf_op jit(solution)/shard_map/ppermute | solution.py:29
  55.5 5.4 %collective-permute-start.12 = (bf16[32,1664]{1,0:T(8,128)(2,1)S(1)}, bf16[32,1664]{1,0:T(8,128)(2,1)S(1)}, u32[]{:S(2)}, u32[]{:S(2)}) collective-permute-start(bf16[32,1664]{1,0:T(8,128)(2,1)S(1)} %get-tuple-element.28), channel_id=1, source_target_pairs={{0,32},{1,129},{2,34},{3,131},{4,36},{5,133},{6,38},{7,135},{8,40}... | collective-permute-start | bytes 319496 | tf_op jit(solution)/shard_map/ppermute | solution.py:29
  57.6 4.8 %collective-permute-start.13 = (bf16[32,1664]{1,0:T(8,128)(2,1)S(1)}, bf16[32,1664]{1,0:T(8,128)(2,1)S(1)}, u32[]{:S(2)}, u32[]{:S(2)}) collective-permute-start(bf16[32,1664]{1,0:T(8,128)(2,1)S(1)} %get-tuple-element.29), channel_id=1, source_target_pairs={{0,48},{1,193},{2,50},{3,195},{4,52},{5,197},{6,54},{7,199},{8,56}... | collective-permute-start | bytes 319496 | tf_op jit(solution)/shard_map/ppermute | solution.py:29
  58.4 4.0 %collective-permute-start.14 = (bf16[32,1664]{1,0:T(8,128)(2,1)S(1)}, bf16[32,1664]{1,0:T(8,128)(2,1)S(1)}, u32[]{:S(2)}, u32[]{:S(2)}) collective-permute-start(bf16[32,1664]{1,0:T(8,128)(2,1)S(1)} %get-tuple-element.30), channel_id=1, source_target_pairs={{0,16},{1,65},{2,18},{3,67},{4,20},{5,69},{6,22},{7,71},{8,24},{9,... | collective-permute-start | bytes 319496 | tf_op jit(solution)/shard_map/ppermute | solution.py:29
  62.6 5.1 %collective-permute-start.17 = (bf16[32,1664]{1,0:T(8,128)(2,1)S(1)}, bf16[32,1664]{1,0:T(8,128)(2,1)S(1)}, u32[]{:S(2)}, u32[]{:S(2)}) collective-permute-start(bf16[32,1664]{1,0:T(8,128)(2,1)S(1)} %add_rows.1.m0), channel_id=1, source_target_pairs={{0,128},{1,33},{2,130},{3,35},{4,132},{5,37},{6,134},{7,39},{8,136... | collective-permute-start | bytes 319496 | tf_op jit(solution)/shard_map/ppermute | solution.py:29
  65.1 5.1 %collective-permute-start.16 = (bf16[32,1664]{1,0:T(8,128)(2,1)S(1)}, bf16[32,1664]{1,0:T(8,128)(2,1)S(1)}, u32[]{:S(2)}, u32[]{:S(2)}) collective-permute-start(bf16[32,1664]{1,0:T(8,128)(2,1)S(1)} %add_rows.1.m0), channel_id=1, source_target_pairs={{0,192},{1,49},{2,194},{3,51},{4,196},{5,53},{6,198},{7,55},{8,200... | collective-permute-start | bytes 319496 | tf_op jit(solution)/shard_map/ppermute | solution.py:29
  65.6 4.6 %collective-permute-start.15 = (bf16[32,1664]{1,0:T(8,128)(2,1)S(1)}, bf16[32,1664]{1,0:T(8,128)(2,1)S(1)}, u32[]{:S(2)}, u32[]{:S(2)}) collective-permute-start(bf16[32,1664]{1,0:T(8,128)(2,1)S(1)} %add_rows.1.m0), channel_id=1, source_target_pairs={{0,64},{1,17},{2,66},{3,19},{4,68},{5,21},{6,70},{7,23},{8,72},{9,... | collective-permute-start | bytes 319496 | tf_op jit(solution)/shard_map/ppermute | solution.py:29
  70.4 4.5 %collective-permute-start.20 = (bf16[32,768]{1,0:T(8,128)(2,1)S(1)}, bf16[32,768]{1,0:T(8,128)(2,1)S(1)}, u32[]{:S(2)}, u32[]{:S(2)}) collective-permute-start(bf16[32,768]{1,0:T(8,128)(2,1)S(1)} %activate.1.x0), channel_id=1, source_target_pairs={{0,32},{1,129},{2,34},{3,131},{4,36},{5,133},{6,38},{7,135},{8,40}... | collective-permute-start | bytes 147464 | tf_op jit(solution)/shard_map/ppermute | solution.py:29
  71.7 4.2 %collective-permute-start.19 = (bf16[32,768]{1,0:T(8,128)(2,1)S(1)}, bf16[32,768]{1,0:T(8,128)(2,1)S(1)}, u32[]{:S(2)}, u32[]{:S(2)}) collective-permute-start(bf16[32,768]{1,0:T(8,128)(2,1)S(1)} %activate.1.x0), channel_id=1, source_target_pairs={{0,48},{1,193},{2,50},{3,195},{4,52},{5,197},{6,54},{7,199},{8,56}... | collective-permute-start | bytes 147464 | tf_op jit(solution)/shard_map/ppermute | solution.py:29
  73.0 2.9 %collective-permute-start.18 = (bf16[32,768]{1,0:T(8,128)(2,1)S(1)}, bf16[32,768]{1,0:T(8,128)(2,1)S(1)}, u32[]{:S(2)}, u32[]{:S(2)}) collective-permute-start(bf16[32,768]{1,0:T(8,128)(2,1)S(1)} %activate.1.x0), channel_id=1, source_target_pairs={{0,16},{1,65},{2,18},{3,67},{4,20},{5,69},{6,22},{7,71},{8,24},{9,... | collective-permute-start | bytes 147464 | tf_op jit(solution)/shard_map/ppermute | solution.py:29

commit v11 on v10

--- a/solution.py
+++ b/solution.py
@@ -16,14 +16,14 @@
 SHARES = 16.0
 
 
-def exchange(value, stage, n_ctx, n_exp):
+def exchange(value, stage, n_ctx, n_exp, first=0):
     side = 4
     got = {}
     for step in (2, 3, 1) if isinstance(value, (list, tuple)) else (1, 3, 2):
         pairs = []
         for i in range(n_ctx):
             for e in range(n_exp):
-                j = i ^ step if (e & 1) == stage else i ^ (side * step)
+                j = i ^ step if (e & 1) == stage ^ first else i ^ (side * step)
                 pairs.append((i * n_exp + e, j * n_exp + e))
         sent = value[step - 1] if isinstance(value, (list, tuple)) else value
         got[step] = lax.ppermute(sent, AXES, pairs)
@@ -107,7 +107,7 @@
 
 def line_place():
     first = lax.axis_index("ctx")
-    return jnp.where(lax.axis_index("exp") % 2 == 1, first // 4, first % 4)
+    return jnp.where(lax.axis_index("exp") % 2 == 1, first % 4, first // 4)
 
 
 def project_kernel(tokens_hbm, gain_hbm, w_hbm, out, tokens, gain, w_ref, small, sems):
@@ -512,7 +512,7 @@
         (rows.reshape(n_rows, slice_width), moe_gain[None], near(w_in_near)),
         [VM] * 3,
     )
-    got = [sent[0]] + exchange(sent[1:], 0, n_ctx, n_exp)[::-1]
+    got = [sent[0]] + exchange(sent[1:], 0, n_ctx, n_exp, 1)[::-1]
     w_down_near, context = pl.pallas_call(
         load_kernel,
         out_shape=(pltpu.VMEM(w_down.shape, bf16), shape(context.shape)),
@@ -529,14 +529,14 @@
         activate_kernel,
         "activate",
         shape((n_rows // side, hidden)),
-        [total] + exchange(total, 1, n_ctx, n_exp),
+        [total] + exchange(total, 1, n_ctx, n_exp, 1),
         [VM] * 4,
     )
     expert_out = call(
         functools.partial(down_kernel, capacity),
         "down",
         shape((n_rows, slice_width)),
-        [act] + exchange(act, 0, n_ctx, n_exp) + [near(w_down_near)],
+        [act] + exchange(act, 0, n_ctx, n_exp, 1) + [near(w_down_near)],
         [VM] * 5,
     )
     returned = lax.all_to_all(

time: 91.8 us -> 91.6 us (level)
  transfers between devices with their start and end apart: 21 -> 21, of which waited for: 13 -> 12; matrix products, arithmetic and copies ran while one was open for 0% -> 0% of each run, Pallas kernels for 8% -> 8%
where the time goes in v11:
time: 91.6 us; the launch traced here: 91.3 us
  blocking collectives  35.8 us (39%)
  starting transfers between devices  22 us (24%)
  waiting for transfers between devices  18.7 us (20%)
  Pallas kernels  13.8 us (15%)
    ppermute x21, starting transfers between devices, exchange(): got[step] = lax.ppermute(sent, AXES, pairs)  22 us
    all_to_all x1, blocking collectives, local(): lax.all_to_all(outgoing.reshape(n_exp, per_source, slice_width), 'exp', s...  21.5 us
    ppermute x21, waiting for transfers between devices, exchange(): got[step] = lax.ppermute(sent, AXES, pairs)  18.7 us
    all_to_all x1, blocking collectives, local(): lax.all_to_all(expert_out.reshape(n_exp, per_source, slice_width), 'exp',...  14.3 us
    pallas_call x13, Pallas kernels, call(): pl.pallas_call(kernel, out_shape=out, in_specs=specs, out_specs=jax.tree....  12.3 us
  transfers between devices with their start and end apart: 21, of which 12 were waited for; matrix products, arithmetic and copies ran while one was open for 0% of the time, Pallas kernels for 8%

profile of v11, /device:TPU:1, one launch (start us, length us, event | category | flops | bytes accessed | tf_op | source)
XLA Modules:
  0.0 91.3 jit_solution(5449140826973823161)
XLA Ops:
  0.6 0.0 copy-start.4
  0.7 2.1 %project.1.after = f32[8,5248]{1,0:T(8,128)S(1)} custom-call(bf16[8,256]{1,0:T(8,128)(2,1)} %tokens.1, f32[1,256]{1,0:T(1,128)} %bitcast.11, bf16[256,5120]{1,0:T(8,128)(2,1)} %w_hbm.1), custom_call_target="tpu_custom_call" | custom-call | tf_op jit(solution)/shard_map/project/pallas_call | solution.py:381
  2.8 3.8 %collective-permute-start.2 = (f16[8,5248]{1,0:T(8,128)(2,1)S(1)}, f16[8,5248]{1,0:T(8,128)(2,1)S(1)}, u32[]{:S(2)}, u32[]{:S(2)}) collective-permute-start(f16[8,5248]{1,0:T(8,128)(2,1)S(1)} %convert_element_type.40), channel_id=1, source_target_pairs={{0,32},{1,129},{2,34},{3,131},{4,36},{5,133},{6,38},{7,135},{8,40}... | collective-permute-start | bytes 251912 | tf_op jit(solution)/shard_map/ppermute | solution.py:29
  6.6 0.8 collective-permute-start.1
  7.4 0.0 collective-permute-start
  7.4 0.1 fusion
  7.5 0.7 prepare.1
  8.3 1.6 %load.3 = (bf16[8,128,512]{2,1,0:T(8,128)(2,1)S(1)}, bf16[8,128,512]{2,1,0:T(8,128)(2,1)S(1)}) custom-call(f32[8,5248]{1,0:T(8,128)S(1)} %project.1.after, bf16[8,128,512]{2,1,0:T(8,128)(2,1)} %refs_0_.4, bf16[8,128,512]{2,1,0:T(8,128)(2,1)} %refs_1_.1), custom_call_target="tpu_custom_call" | custom-call | tf_op jit(solution)/shard_map/load/pallas_call | solution.py:381
  9.8 0.0 collective-permute-done.2
  9.8 1.6 %collective-permute-done.1 = f16[8,5248]{1,0:T(8,128)(2,1)S(1)} collective-permute-done((f16[8,5248]{1,0:T(8,128)(2,1)S(1)}, f16[8,5248]{1,0:T(8,128)(2,1)S(1)}, u32[]{:S(2)}, u32[]{:S(2)}) %collective-permute-start.1) | collective-permute-done | bytes 84000 | tf_op jit(solution)/shard_map/ppermute | solution.py:29
  11.4 0.0 collective-permute-done
  11.4 0.1 fusion.1
  11.5 2.5 %collective-permute-start.5 = (f16[8,5248]{1,0:T(8,128)(2,1)S(1)}, f16[8,5248]{1,0:T(8,128)(2,1)S(1)}, u32[]{:S(2)}, u32[]{:S(2)}) collective-permute-start(f16[8,5248]{1,0:T(8,128)(2,1)S(1)} %get-tuple-element.32), channel_id=1, source_target_pairs={{0,128},{1,33},{2,130},{3,35},{4,132},{5,37},{6,134},{7,39},{8,136... | collective-permute-start | bytes 251912 | tf_op jit(solution)/shard_map/ppermute | solution.py:29
  14.0 0.9 collective-permute-start.4
  14.9 0.0 collective-permute-start.3
  14.9 0.1 pad_maximum_fusion
  15.0 1.6 %load.4.after.w_ref = bf16[4096,256]{1,0:T(8,128)(2,1)S(1)} custom-call(f32[8,5248]{1,0:T(8,128)S(1)} %get-tuple-element.33.after, bf16[4096,256]{1,0:T(8,128)(2,1)} %refs_0_.5), custom_call_target="tpu_custom_call" | custom-call | tf_op jit(solution)/shard_map/load/pallas_call | solution.py:381
  16.6 0.0 collective-permute-done.5
  16.6 2.2 %collective-permute-done.4 = f16[8,5248]{1,0:T(8,128)(2,1)S(1)} collective-permute-done((f16[8,5248]{1,0:T(8,128)(2,1)S(1)}, f16[8,5248]{1,0:T(8,128)(2,1)S(1)}, u32[]{:S(2)}, u32[]{:S(2)}) %collective-permute-start.4) | collective-permute-done | bytes 84000 | tf_op jit(solution)/shard_map/ppermute | solution.py:29
  18.8 0.0 collective-permute-done.3
  18.8 1.1 %attend.1.after.p0 = bf16[288,128]{1,0:T(8,128)(2,1)S(1)} custom-call(f32[8,5248]{1,0:T(8,128)S(1)} %add_add_fusion.shares, f32[8,128]{1,0:T(8,128)S(1)} %get-tuple-element.37.cosine, f32[8,128]{1,0:T(8,128)S(1)} %get-tuple-element.38.sine, f32[8,128]{1,0:T(8,128)S(1)} %get-tuple-element.17.live_ref, f32[8,128]{1,0:T(8,128)S(1)} %get-tuple-element.18.owns, ...), custom_call_target="tpu_custom_call" | custom-call | tf_op jit(solution)/shard_map/attend/pallas_call | solution.py:381
  19.9 1.6 %collective-permute-start.8 = (bf16[288,128]{1,0:T(8,128)(2,1)S(1)}, bf16[288,128]{1,0:T(8,128)(2,1)S(1)}, u32[]{:S(2)}, u32[]{:S(2)}) collective-permute-start(bf16[288,128]{1,0:T(8,128)(2,1)S(1)} %attend.1.after.p0), channel_id=1, source_target_pairs={{0,32},{1,129},{2,34},{3,131},{4,36},{5,133},{6,38},{7,135},{8,40}... | collective-permute-start | bytes 221192 | tf_op jit(solution)/shard_map/ppermute | solution.py:29
  21.6 0.8 collective-permute-start.7
  22.3 0.3 collective-permute-start.6
  22.6 1.9 %load.5.after.w_ref = bf16[4,256,1536]{2,1,0:T(8,128)(2,1)S(1)} custom-call(bf16[288,128]{1,0:T(8,128)(2,1)S(1)} %attend.1.after.p0, bf16[4,256,1536]{2,1,0:T(8,128)(2,1)} %refs_0_.6), custom_call_target="tpu_custom_call" | custom-call | tf_op jit(solution)/shard_map/load/pallas_call | solution.py:381
  24.5 0.0 copy-start
  24.5 0.1 collective-permute-done.8.p2
  24.7 1.3 %collective-permute-done.7.p3 = bf16[288,128]{1,0:T(8,128)(2,1)S(1)} collective-permute-done((bf16[288,128]{1,0:T(8,128)(2,1)S(1)}, bf16[288,128]{1,0:T(8,128)(2,1)S(1)}, u32[]{:S(2)}, u32[]{:S(2)}) %collective-permute-start.7) | collective-permute-done | bytes 73760 | tf_op jit(solution)/shard_map/ppermute | solution.py:29
  26.0 0.0 collective-permute-done.6.p1
  26.0 0.3 merge.1.p0
  26.3 0.0 copy-start.3
  26.3 1.6 %collective-permute-start.11 = (bf16[288,128]{1,0:T(8,128)(2,1)S(1)}, bf16[288,128]{1,0:T(8,128)(2,1)S(1)}, u32[]{:S(2)}, u32[]{:S(2)}) collective-permute-start(bf16[288,128]{1,0:T(8,128)(2,1)S(1)} %merge.1.p0), channel_id=1, source_target_pairs={{0,128},{1,33},{2,130},{3,35},{4,132},{5,37},{6,134},{7,39},{8,136... | collective-permute-start | bytes 221192 | tf_op jit(solution)/shard_map/ppermute | solution.py:29
  27.9 0.9 collective-permute-start.10
  28.8 0.3 collective-permute-start.9
  29.1 2.8 %collective-permute-done.11.p2 = bf16[288,128]{1,0:T(8,128)(2,1)S(1)} collective-permute-done((bf16[288,128]{1,0:T(8,128)(2,1)S(1)}, bf16[288,128]{1,0:T(8,128)(2,1)S(1)}, u32[]{:S(2)}, u32[]{:S(2)}) %collective-permute-start.11) | collective-permute-done | bytes 73760 | tf_op jit(solution)/shard_map/ppermute | solution.py:29
  31.9 0.6 collective-permute-done.10.p3
  32.5 0.0 collective-permute-done.9.p1
  32.5 0.9 %finish.1 = (bf16[8,4096]{1,0:T(8,128)(2,1)S(1)}, bf16[8,256]{1,0:T(8,128)(2,1)S(1)}, bf16[128,256]{1,0:T(8,128)(2,1)S(1)}) custom-call(bf16[288,128]{1,0:T(8,128)(2,1)S(1)} %merge.1.p0, bf16[288,128]{1,0:T(8,128)(2,1)S(1)} %collective-permute-done.9.p1, bf16[288,128]{1,0:T(8,128)(2,1)S(1)} %collective-permute-done.10.p3, ...), custom_call_target="tpu_custom_call" | custom-call | tf_op jit(solution)/shard_map/finish/pallas_call | solution.py:381
  33.4 21.5 %all_to_all.10 = bf16[16,8,256]{2,1,0:T(8,128)(2,1)S(1)} all-to-all(bf16[16,8,256]{2,1,0:T(8,128)(2,1)S(1)} %bitcast.9), channel_id=1, replica_groups=mesh['ctx'=16,'exp'=16] {'exp'}, dimensions={0} | all-to-all | bytes 131072 | tf_op jit(solution)/shard_map/all_to_all | solution.py:503
  54.9 0.6 gate_up.1
  55.5 2.6 %collective-permute-start.12 = (bf16[32,1664]{1,0:T(8,128)(2,1)S(1)}, bf16[32,1664]{1,0:T(8,128)(2,1)S(1)}, u32[]{:S(2)}, u32[]{:S(2)}) collective-permute-start(bf16[32,1664]{1,0:T(8,128)(2,1)S(1)} %get-tuple-element.28), channel_id=1, source_target_pairs={{0,128},{1,33},{2,130},{3,35},{4,132},{5,37},{6,134},{7,39},{8,136... | collective-permute-start | bytes 319496 | tf_op jit(solution)/shard_map/ppermute | solution.py:29
  58.1 0.4 collective-permute-start.13
  58.4 0.1 collective-permute-start.14
  58.6 1.4 %settle.1 = (bf16[4,768,256]{2,1,0:T(8,128)(2,1)S(1)}, bf16[8,4096]{1,0:T(8,128)(2,1)}) custom-call(bf16[32,1664]{1,0:T(8,128)(2,1)S(1)} %get-tuple-element.23.after.m0, bf16[4,768,256]{2,1,0:T(8,128)(2,1)} %refs_0_.7, bf16[8,4096]{1,0:T(8,128)(2,1)S(1)} %get-tuple-element.24.refs_1_), custom_call_target="tpu_custom_call" | custom-call | tf_op jit(solution)/shard_map/settle/pallas_call | solution.py:516
  60.0 0.9 %collective-permute-done.12.m1 = bf16[32,1664]{1,0:T(8,128)(2,1)S(1)} collective-permute-done((bf16[32,1664]{1,0:T(8,128)(2,1)S(1)}, bf16[32,1664]{1,0:T(8,128)(2,1)S(1)}, u32[]{:S(2)}, u32[]{:S(2)}) %collective-permute-start.12) | collective-permute-done | bytes 106528 | tf_op jit(solution)/shard_map/ppermute | solution.py:29
  60.9 2.2 %collective-permute-done.13.m3 = bf16[32,1664]{1,0:T(8,128)(2,1)S(1)} collective-permute-done((bf16[32,1664]{1,0:T(8,128)(2,1)S(1)}, bf16[32,1664]{1,0:T(8,128)(2,1)S(1)}, u32[]{:S(2)}, u32[]{:S(2)}) %collective-permute-start.13) | collective-permute-done | bytes 106528 | tf_op jit(solution)/shard_map/ppermute | solution.py:29
  63.1 0.0 collective-permute-done.14.m2
  63.1 0.2 add_rows.1.m0
  63.3 1.7 %collective-permute-start.17 = (bf16[32,1664]{1,0:T(8,128)(2,1)S(1)}, bf16[32,1664]{1,0:T(8,128)(2,1)S(1)}, u32[]{:S(2)}, u32[]{:S(2)}) collective-permute-start(bf16[32,1664]{1,0:T(8,128)(2,1)S(1)} %add_rows.1.m0), channel_id=1, source_target_pairs={{0,32},{1,129},{2,34},{3,131},{4,36},{5,133},{6,38},{7,135},{8,40}... | collective-permute-start | bytes 319496 | tf_op jit(solution)/shard_map/ppermute | solution.py:29
  65.1 1.0 %collective-permute-start.16 = (bf16[32,1664]{1,0:T(8,128)(2,1)S(1)}, bf16[32,1664]{1,0:T(8,128)(2,1)S(1)}, u32[]{:S(2)}, u32[]{:S(2)}) collective-permute-start(bf16[32,1664]{1,0:T(8,128)(2,1)S(1)} %add_rows.1.m0), channel_id=1, source_target_pairs={{0,48},{1,193},{2,50},{3,195},{4,52},{5,197},{6,54},{7,199},{8,56}... | collective-permute-start | bytes 319496 | tf_op jit(solution)/shard_map/ppermute | solution.py:29
  66.1 0.0 collective-permute-start.15
  66.1 2.4 %collective-permute-done.17.m2 = bf16[32,1664]{1,0:T(8,128)(2,1)S(1)} collective-permute-done((bf16[32,1664]{1,0:T(8,128)(2,1)S(1)}, bf16[32,1664]{1,0:T(8,128)(2,1)S(1)}, u32[]{:S(2)}, u32[]{:S(2)}) %collective-permute-start.17) | collective-permute-done | bytes 106528 | tf_op jit(solution)/shard_map/ppermute | solution.py:29
  68.4 1.6 %collective-permute-done.16.m3 = bf16[32,1664]{1,0:T(8,128)(2,1)S(1)} collective-permute-done((bf16[32,1664]{1,0:T(8,128)(2,1)S(1)}, bf16[32,1664]{1,0:T(8,128)(2,1)S(1)}, u32[]{:S(2)}, u32[]{:S(2)}) %collective-permute-start.16) | collective-permute-done | bytes 106528 | tf_op jit(solution)/shard_map/ppermute | solution.py:29
  70.1 0.0 collective-permute-done.15.m1
  70.1 0.2 activate.1.x0
  70.3 1.5 %collective-permute-start.20 = (bf16[32,768]{1,0:T(8,128)(2,1)S(1)}, bf16[32,768]{1,0:T(8,128)(2,1)S(1)}, u32[]{:S(2)}, u32[]{:S(2)}) collective-permute-start(bf16[32,768]{1,0:T(8,128)(2,1)S(1)} %activate.1.x0), channel_id=1, source_target_pairs={{0,128},{1,33},{2,130},{3,35},{4,132},{5,37},{6,134},{7,39},{8,136... | collective-permute-start | bytes 147464 | tf_op jit(solution)/shard_map/ppermute | solution.py:29
  71.7 1.2 %collective-permute-start.19 = (bf16[32,768]{1,0:T(8,128)(2,1)S(1)}, bf16[32,768]{1,0:T(8,128)(2,1)S(1)}, u32[]{:S(2)}, u32[]{:S(2)}) collective-permute-start(bf16[32,768]{1,0:T(8,128)(2,1)S(1)} %activate.1.x0), channel_id=1, source_target_pairs={{0,192},{1,49},{2,194},{3,51},{4,196},{5,53},{6,198},{7,55},{8,200... | collective-permute-start | bytes 147464 | tf_op jit(solution)/shard_map/ppermute | solution.py:29
  72.9 0.1 collective-permute-start.18
  73.0 1.8 %collective-permute-done.20.x2 = bf16[32,768]{1,0:T(8,128)(2,1)S(1)} collective-permute-done((bf16[32,768]{1,0:T(8,128)(2,1)S(1)}, bf16[32,768]{1,0:T(8,128)(2,1)S(1)}, u32[]{:S(2)}, u32[]{:S(2)}) %collective-permute-start.20) | collective-permute-done | bytes 49184 | tf_op jit(solution)/shard_map/ppermute | solution.py:29
  74.8 1.1 %collective-permute-done.19.x3 = bf16[32,768]{1,0:T(8,128)(2,1)S(1)} collective-permute-done((bf16[32,768]{1,0:T(8,128)(2,1)S(1)}, bf16[32,768]{1,0:T(8,128)(2,1)S(1)}, u32[]{:S(2)}, u32[]{:S(2)}) %collective-permute-start.19) | collective-permute-done | bytes 49184 | tf_op jit(solution)/shard_map/ppermute | solution.py:29
  75.9 0.0 collective-permute-done.18.x1
  75.9 0.4 down.1
  76.3 14.3 %all_to_all.11 = bf16[16,8,256]{2,1,0:T(8,128)(2,1)S(1)} all-to-all(bf16[16,8,256]{2,1,0:T(8,128)(2,1)S(1)} %bitcast.7), channel_id=1, replica_groups=mesh['ctx'=16,'exp'=16] {'exp'}, dimensions={0} | all-to-all | bytes 131072 | tf_op jit(solution)/shard_map/all_to_all | solution.py:542
  90.6 0.7 combine.1
  (11 shorter events, 0.1 us)
Async XLA Ops:
  0.6 6.8 %copy-start.4 = (s32[8]{0:T(128)S(1)}, s32[8]{0:T(128)}, u32[]{:S(2)}) copy-start(s32[8]{0:T(128)} %lengths.1) | copy-start | bytes 100
  0.6 6.9 %copy-start.2 = (f32[8,8]{1,0:T(8,128)S(1)}, f32[8,8]{1,0:T(8,128)}, u32[]{:S(2)}) copy-start(f32[8,8]{1,0:T(8,128)} %gates.1) | copy-start | bytes 772
  0.7 6.9 %copy-start.1 = (s32[8,8]{1,0:T(8,128)S(1)}, s32[8,8]{1,0:T(8,128)}, u32[]{:S(2)}) copy-start(s32[8,8]{1,0:T(8,128)} %routes.1) | copy-start | bytes 772
  2.8 7.1 %collective-permute-start.2 = (f16[8,5248]{1,0:T(8,128)(2,1)S(1)}, f16[8,5248]{1,0:T(8,128)(2,1)S(1)}, u32[]{:S(2)}, u32[]{:S(2)}) collective-permute-start(f16[8,5248]{1,0:T(8,128)(2,1)S(1)} %convert_element_type.40), channel_id=1, source_target_pairs={{0,32},{1,129},{2,34},{3,131},{4,36},{5,133},{6,38},{7,135},{8,40}... | collective-permute-start | bytes 251912 | tf_op jit(solution)/shard_map/ppermute | solution.py:29
  6.6 4.8 %collective-permute-start.1 = (f16[8,5248]{1,0:T(8,128)(2,1)S(1)}, f16[8,5248]{1,0:T(8,128)(2,1)S(1)}, u32[]{:S(2)}, u32[]{:S(2)}) collective-permute-start(f16[8,5248]{1,0:T(8,128)(2,1)S(1)} %convert_element_type.40), channel_id=1, source_target_pairs={{0,48},{1,193},{2,50},{3,195},{4,52},{5,197},{6,54},{7,199},{8,56}... | collective-permute-start | bytes 251912 | tf_op jit(solution)/shard_map/ppermute | solution.py:29
  7.4 4.0 %collective-permute-start = (f16[8,5248]{1,0:T(8,128)(2,1)S(1)}, f16[8,5248]{1,0:T(8,128)(2,1)S(1)}, u32[]{:S(2)}, u32[]{:S(2)}) collective-permute-start(f16[8,5248]{1,0:T(8,128)(2,1)S(1)} %convert_element_type.40), channel_id=1, source_target_pairs={{0,16},{1,65},{2,18},{3,67},{4,20},{5,69},{6,22},{7,71},{8,24},{9,... | collective-permute-start | bytes 251912 | tf_op jit(solution)/shard_map/ppermute | solution.py:29
  11.5 5.1 %collective-permute-start.5 = (f16[8,5248]{1,0:T(8,128)(2,1)S(1)}, f16[8,5248]{1,0:T(8,128)(2,1)S(1)}, u32[]{:S(2)}, u32[]{:S(2)}) collective-permute-start(f16[8,5248]{1,0:T(8,128)(2,1)S(1)} %get-tuple-element.32), channel_id=1, source_target_pairs={{0,128},{1,33},{2,130},{3,35},{4,132},{5,37},{6,134},{7,39},{8,136... | collective-permute-start | bytes 251912 | tf_op jit(solution)/shard_map/ppermute | solution.py:29
  14.0 4.8 %collective-permute-start.4 = (f16[8,5248]{1,0:T(8,128)(2,1)S(1)}, f16[8,5248]{1,0:T(8,128)(2,1)S(1)}, u32[]{:S(2)}, u32[]{:S(2)}) collective-permute-start(f16[8,5248]{1,0:T(8,128)(2,1)S(1)} %get-tuple-element.32), channel_id=1, source_target_pairs={{0,192},{1,49},{2,194},{3,51},{4,196},{5,53},{6,198},{7,55},{8,200... | collective-permute-start | bytes 251912 | tf_op jit(solution)/shard_map/ppermute | solution.py:29
  14.9 3.9 %collective-permute-start.3 = (f16[8,5248]{1,0:T(8,128)(2,1)S(1)}, f16[8,5248]{1,0:T(8,128)(2,1)S(1)}, u32[]{:S(2)}, u32[]{:S(2)}) collective-permute-start(f16[8,5248]{1,0:T(8,128)(2,1)S(1)} %get-tuple-element.32), channel_id=1, source_target_pairs={{0,64},{1,17},{2,66},{3,19},{4,68},{5,21},{6,70},{7,23},{8,72},{9,... | collective-permute-start | bytes 251912 | tf_op jit(solution)/shard_map/ppermute | solution.py:29
  19.9 4.8 %collective-permute-start.8 = (bf16[288,128]{1,0:T(8,128)(2,1)S(1)}, bf16[288,128]{1,0:T(8,128)(2,1)S(1)}, u32[]{:S(2)}, u32[]{:S(2)}) collective-permute-start(bf16[288,128]{1,0:T(8,128)(2,1)S(1)} %attend.1.after.p0), channel_id=1, source_target_pairs={{0,32},{1,129},{2,34},{3,131},{4,36},{5,133},{6,38},{7,135},{8,40}... | collective-permute-start | bytes 221192 | tf_op jit(solution)/shard_map/ppermute | solution.py:29
  21.6 4.4 %collective-permute-start.7 = (bf16[288,128]{1,0:T(8,128)(2,1)S(1)}, bf16[288,128]{1,0:T(8,128)(2,1)S(1)}, u32[]{:S(2)}, u32[]{:S(2)}) collective-permute-start(bf16[288,128]{1,0:T(8,128)(2,1)S(1)} %attend.1.after.p0), channel_id=1, source_target_pairs={{0,48},{1,193},{2,50},{3,195},{4,52},{5,197},{6,54},{7,199},{8,56}... | collective-permute-start | bytes 221192 | tf_op jit(solution)/shard_map/ppermute | solution.py:29
  22.3 3.6 %collective-permute-start.6 = (bf16[288,128]{1,0:T(8,128)(2,1)S(1)}, bf16[288,128]{1,0:T(8,128)(2,1)S(1)}, u32[]{:S(2)}, u32[]{:S(2)}) collective-permute-start(bf16[288,128]{1,0:T(8,128)(2,1)S(1)} %attend.1.after.p0), channel_id=1, source_target_pairs={{0,16},{1,65},{2,18},{3,67},{4,20},{5,69},{6,22},{7,71},{8,24},{9,... | collective-permute-start | bytes 221192 | tf_op jit(solution)/shard_map/ppermute | solution.py:29
  24.5 8.0 %copy-start = (bf16[8,256]{1,0:T(8,128)(2,1)S(1)}, bf16[8,256]{1,0:T(8,128)(2,1)}, u32[]{:S(2)}) copy-start(bf16[8,256]{1,0:T(8,128)(2,1)} %tokens.1) | copy-start | bytes 12292
  26.3 28.6 %copy-start.3 = (f32[256]{0:T(256)S(1)}, f32[256]{0:T(256)}, u32[]{:S(2)}) copy-start(f32[256]{0:T(256)} %param.19) | copy-start | bytes 3076
  26.3 5.6 %collective-permute-start.11 = (bf16[288,128]{1,0:T(8,128)(2,1)S(1)}, bf16[288,128]{1,0:T(8,128)(2,1)S(1)}, u32[]{:S(2)}, u32[]{:S(2)}) collective-permute-start(bf16[288,128]{1,0:T(8,128)(2,1)S(1)} %merge.1.p0), channel_id=1, source_target_pairs={{0,128},{1,33},{2,130},{3,35},{4,132},{5,37},{6,134},{7,39},{8,136... | collective-permute-start | bytes 221192 | tf_op jit(solution)/shard_map/ppermute | solution.py:29
  27.9 4.6 %collective-permute-start.10 = (bf16[288,128]{1,0:T(8,128)(2,1)S(1)}, bf16[288,128]{1,0:T(8,128)(2,1)S(1)}, u32[]{:S(2)}, u32[]{:S(2)}) collective-permute-start(bf16[288,128]{1,0:T(8,128)(2,1)S(1)} %merge.1.p0), channel_id=1, source_target_pairs={{0,192},{1,49},{2,194},{3,51},{4,196},{5,53},{6,198},{7,55},{8,200... | collective-permute-start | bytes 221192 | tf_op jit(solution)/shard_map/ppermute | solution.py:29
  28.8 3.7 %collective-permute-start.9 = (bf16[288,128]{1,0:T(8,128)(2,1)S(1)}, bf16[288,128]{1,0:T(8,128)(2,1)S(1)}, u32[]{:S(2)}, u32[]{:S(2)}) collective-permute-start(bf16[288,128]{1,0:T(8,128)(2,1)S(1)} %merge.1.p0), channel_id=1, source_target_pairs={{0,64},{1,17},{2,66},{3,19},{4,68},{5,21},{6,70},{7,23},{8,72},{9,... | collective-permute-start | bytes 221192 | tf_op jit(solution)/shard_map/ppermute | solution.py:29
  55.5 5.4 %collective-permute-start.12 = (bf16[32,1664]{1,0:T(8,128)(2,1)S(1)}, bf16[32,1664]{1,0:T(8,128)(2,1)S(1)}, u32[]{:S(2)}, u32[]{:S(2)}) collective-permute-start(bf16[32,1664]{1,0:T(8,128)(2,1)S(1)} %get-tuple-element.28), channel_id=1, source_target_pairs={{0,128},{1,33},{2,130},{3,35},{4,132},{5,37},{6,134},{7,39},{8,136... | collective-permute-start | bytes 319496 | tf_op jit(solution)/shard_map/ppermute | solution.py:29
  58.1 5.1 %collective-permute-start.13 = (bf16[32,1664]{1,0:T(8,128)(2,1)S(1)}, bf16[32,1664]{1,0:T(8,128)(2,1)S(1)}, u32[]{:S(2)}, u32[]{:S(2)}) collective-permute-start(bf16[32,1664]{1,0:T(8,128)(2,1)S(1)} %get-tuple-element.29), channel_id=1, source_target_pairs={{0,192},{1,49},{2,194},{3,51},{4,196},{5,53},{6,198},{7,55},{8,200... | collective-permute-start | bytes 319496 | tf_op jit(solution)/shard_map/ppermute | solution.py:29
  58.4 4.7 %collective-permute-start.14 = (bf16[32,1664]{1,0:T(8,128)(2,1)S(1)}, bf16[32,1664]{1,0:T(8,128)(2,1)S(1)}, u32[]{:S(2)}, u32[]{:S(2)}) collective-permute-start(bf16[32,1664]{1,0:T(8,128)(2,1)S(1)} %get-tuple-element.30), channel_id=1, source_target_pairs={{0,64},{1,17},{2,66},{3,19},{4,68},{5,21},{6,70},{7,23},{8,72},{9,... | collective-permute-start | bytes 319496 | tf_op jit(solution)/shard_map/ppermute | solution.py:29
  63.3 5.1 %collective-permute-start.17 = (bf16[32,1664]{1,0:T(8,128)(2,1)S(1)}, bf16[32,1664]{1,0:T(8,128)(2,1)S(1)}, u32[]{:S(2)}, u32[]{:S(2)}) collective-permute-start(bf16[32,1664]{1,0:T(8,128)(2,1)S(1)} %add_rows.1.m0), channel_id=1, source_target_pairs={{0,32},{1,129},{2,34},{3,131},{4,36},{5,133},{6,38},{7,135},{8,40}... | collective-permute-start | bytes 319496 | tf_op jit(solution)/shard_map/ppermute | solution.py:29
  65.1 5.0 %collective-permute-start.16 = (bf16[32,1664]{1,0:T(8,128)(2,1)S(1)}, bf16[32,1664]{1,0:T(8,128)(2,1)S(1)}, u32[]{:S(2)}, u32[]{:S(2)}) collective-permute-start(bf16[32,1664]{1,0:T(8,128)(2,1)S(1)} %add_rows.1.m0), channel_id=1, source_target_pairs={{0,48},{1,193},{2,50},{3,195},{4,52},{5,197},{6,54},{7,199},{8,56}... | collective-permute-start | bytes 319496 | tf_op jit(solution)/shard_map/ppermute | solution.py:29
  66.1 4.0 %collective-permute-start.15 = (bf16[32,1664]{1,0:T(8,128)(2,1)S(1)}, bf16[32,1664]{1,0:T(8,128)(2,1)S(1)}, u32[]{:S(2)}, u32[]{:S(2)}) collective-permute-start(bf16[32,1664]{1,0:T(8,128)(2,1)S(1)} %add_rows.1.m0), channel_id=1, source_target_pairs={{0,16},{1,65},{2,18},{3,67},{4,20},{5,69},{6,22},{7,71},{8,24},{9,... | collective-permute-start | bytes 319496 | tf_op jit(solution)/shard_map/ppermute | solution.py:29
  70.3 4.5 %collective-permute-start.20 = (bf16[32,768]{1,0:T(8,128)(2,1)S(1)}, bf16[32,768]{1,0:T(8,128)(2,1)S(1)}, u32[]{:S(2)}, u32[]{:S(2)}) collective-permute-start(bf16[32,768]{1,0:T(8,128)(2,1)S(1)} %activate.1.x0), channel_id=1, source_target_pairs={{0,128},{1,33},{2,130},{3,35},{4,132},{5,37},{6,134},{7,39},{8,136... | collective-permute-start | bytes 147464 | tf_op jit(solution)/shard_map/ppermute | solution.py:29
  71.7 4.2 %collective-permute-start.19 = (bf16[32,768]{1,0:T(8,128)(2,1)S(1)}, bf16[32,768]{1,0:T(8,128)(2,1)S(1)}, u32[]{:S(2)}, u32[]{:S(2)}) collective-permute-start(bf16[32,768]{1,0:T(8,128)(2,1)S(1)} %activate.1.x0), channel_id=1, source_target_pairs={{0,192},{1,49},{2,194},{3,51},{4,196},{5,53},{6,198},{7,55},{8,200... | collective-permute-start | bytes 147464 | tf_op jit(solution)/shard_map/ppermute | solution.py:29
  72.9 3.0 %collective-permute-start.18 = (bf16[32,768]{1,0:T(8,128)(2,1)S(1)}, bf16[32,768]{1,0:T(8,128)(2,1)S(1)}, u32[]{:S(2)}, u32[]{:S(2)}) collective-permute-start(bf16[32,768]{1,0:T(8,128)(2,1)S(1)} %activate.1.x0), channel_id=1, source_target_pairs={{0,64},{1,17},{2,66},{3,19},{4,68},{5,21},{6,70},{7,23},{8,72},{9,... | collective-permute-start | bytes 147464 | tf_op jit(solution)/shard_map/ppermute | solution.py:29
